TPU v7x, 256 devices: a whole 4x4x8 slice. The times are simulated.
256 devices in a mesh: mem: 16 (over z_hi, x, core), lat: 4 (over z_lo), lon: 4 (over y).
Axes of the slice: x: 4, y: 4, z: 8 (z_hi: 2, z_lo: 4; z = z_hi * 4 + z_lo), core: 2. Of those that a mesh axis runs over, the one named last changes fastest.
Arguments:
- control: bfloat16 [64, 256, 128, 128], P('mem', 'lat', 'lon'), may hold values from -21 to 21
- ensemble: bfloat16 [64, 256, 128, 128], P('mem', 'lat', 'lon'), may hold values from -3 to 3
- precision: float32 [256, 128, 128], P('lat', 'lon'), may hold values from 0.5 to 8
- lat_taps: float32 [9], replicated, may hold values from 0.05 to 0.3
- lon_taps: float32 [9], replicated, may hold values from 0.05 to 0.3
- vertical: bfloat16 [128, 128], replicated, may hold values from -0.5 to 0.5
Outputs:
- hessian: float32 [64, 256, 128, 128], P('mem', 'lat', 'lon')
- curvature: float32 [], replicated
All inputs are finite; a program needn't handle non-finite values.
Results may differ from a plain program's by a relative error of at most 0.0038.
Values may be sent and summed in bfloat16 or wider, within the bound.
No kernel may reach another device: no remote copies, remote signals or barrier semaphores. Data moves between devices by JAX's collectives and lax.ppermute only.
A program may use at most 64 MiB of HBM per device.

v0:
```python
import jax
import jax.numpy as jnp
from jax import lax
from jax.sharding import Mesh
from jax.sharding import PartitionSpec as P

MEM = ("mem_0", "mem_1", "mem_2")
MEM_LAT_LON = ("mem_0", "mem_1", "mem_2", "lat", "lon")


def extended_2(value, sides, width):
    for axis, dim in sides:
        peers, length = (lax.axis_size(axis), value.shape[dim])
        up = [(i, (i + 1) % peers) for i in range(peers)]
        down = [(j, i) for i, j in up]
        last = lax.slice_in_dim(value, length - width, length, axis=dim)
        initial = lax.slice_in_dim(value, 0, width, axis=dim)
        before = lax.ppermute(last, axis, up)
        after = lax.ppermute(initial, axis, down)
        value = jnp.concatenate([before, value, after], axis=dim)
    return value


def in_blocks(value, dim, peers):
    before, after = (value.shape[:dim], value.shape[dim + 1 :])
    return jnp.moveaxis(value.reshape(*before, peers, -1, *after), dim, 0)


def sum_at_owner(value, axis, dim):
    peers = lax.axis_size(axis)
    pieces = lax.all_to_all(in_blocks(value, dim, peers), axis, 0, 0, tiled=True)
    return jnp.sum(pieces, axis=0)


def in_order(pieces, dim):
    pieces = jnp.moveaxis(pieces, 0, dim)
    shape = pieces.shape
    return pieces.reshape(*shape[:dim], shape[dim] * shape[dim + 1], *shape[dim + 2 :])


def copy_for_each(value, axis):
    copies = jnp.broadcast_to(value, (lax.axis_size(axis), *value.shape))
    return lax.all_to_all(copies, axis, split_axis=0, concat_axis=0, tiled=True)


def collect(value, axis, dim):
    return in_order(copy_for_each(value, axis), dim)


def by_axis(value, axes):
    for axis in axes:
        value = lax.psum(value, axis)
    return value


def smooth_block(extended, first_taps, second_taps, tile_rows, tile_cols):
    across = first_taps[0] * extended[:, 0:tile_rows]
    for offset in range(1, first_taps.shape[0]):
        across = across + first_taps[offset] * extended[:, offset : offset + tile_rows]
    result = second_taps[0] * across[:, :, 0:tile_cols]
    for offset in range(1, second_taps.shape[0]):
        result = result + second_taps[offset] * across[:, :, offset : offset + tile_cols]
    return result


def clear_edges(extended, tile_rows):
    lat_pos = lax.axis_index("lat")
    lat_count = lax.axis_size("lat")
    row_index = jnp.arange(tile_rows + 8)
    outside = jnp.logical_or(
        jnp.logical_and(row_index < 4, lat_pos == 0),
        jnp.logical_and(row_index >= tile_rows + 4, lat_pos == lat_count - 1),
    )
    return jnp.where(outside[None, :, None, None], jnp.zeros((), extended.dtype), extended)


def per_device(control, ensemble, precision, lat_taps, lon_taps, vertical):
    tile_rows = control.shape[1]
    tile_cols = control.shape[2]
    levels = control.shape[3]
    entries = control.size * lax.axis_size(MEM) * lax.axis_size("lat") * lax.axis_size("lon")
    extended = extended_2(control, (("lat", 1), ("lon", 2)), 4)
    extended = clear_edges(extended, tile_rows)
    smoothed = smooth_block(extended, lat_taps, lon_taps, tile_rows, tile_cols).astype(jnp.bfloat16)
    leveled = jnp.dot(
        smoothed.reshape(-1, levels), vertical, preferred_element_type=jnp.float32
    ).reshape(smoothed.shape)
    partial_value = jnp.sum(ensemble * leveled, axis=0)
    cell_count = tile_rows * tile_cols
    share_rows = cell_count // lax.axis_size(MEM)
    flat_partial = partial_value.reshape(cell_count, levels)
    inc_share = sum_at_owner(flat_partial, MEM, 0)
    prec_share = lax.dynamic_slice_in_dim(
        precision.reshape(cell_count, levels), lax.axis_index(MEM) * share_rows, share_rows, 0
    )
    weighted_share = prec_share * inc_share
    weighted = collect(weighted_share, MEM, 0).reshape(tile_rows, tile_cols, levels)
    member_part = (ensemble * weighted[None]).astype(jnp.bfloat16)
    adjoint_lev = lax.dot_general(
        member_part.reshape(-1, levels),
        vertical,
        (((1,), (1,)), ((), ())),
        preferred_element_type=jnp.float32,
    )
    adjoint_lev = adjoint_lev.reshape(member_part.shape).astype(jnp.bfloat16)
    adjoint_ext = extended_2(adjoint_lev, (("lat", 1), ("lon", 2)), 4)
    adjoint_ext = clear_edges(adjoint_ext, tile_rows)
    back = smooth_block(adjoint_ext, lat_taps[::-1], lon_taps[::-1], tile_rows, tile_cols)
    hessian = control + back
    curvature = by_axis(jnp.sum(control * hessian), MEM_LAT_LON) / entries
    return (hessian, curvature)


def solution(mesh):
    split = Mesh(
        mesh.devices.reshape(2, 4, 2, mesh.shape["lat"], mesh.shape["lon"]),
        ("mem_0", "mem_1", "mem_2", "lat", "lon"),
    )
    return jax.shard_map(
        per_device,
        mesh=split,
        in_specs=(
            P(MEM, "lat", "lon", None),
            P(MEM, "lat", "lon", None),
            P("lat", "lon", None),
            P(),
            P(),
            P(),
        ),
        out_specs=(P(MEM, "lat", "lon", None), P()),
        check_vma=False,
    )
```

profile of v0, /device:TPU:2, one launch (start us, length us, event | category | flops | bytes accessed | tf_op | source)
XLA Modules:
  0.0 241.0 jit_solution(936113620788499879)
XLA Ops:
  0.6 0.0 copy-start
  0.6 0.0 copy-start.3
  0.7 0.0 copy-start.4
  0.7 1.0 fusion.31
  1.7 2.0 collective-permute-start
  3.7 2.8 %collective-permute-start.1 = (bf16[4,4,32,128]{3,2,1,0:T(8,128)(2,1)S(1)}, bf16[4,4,32,128]{3,2,1,0:T(8,128)(2,1)S(1)}, u32[]{:S(2)}, u32[]{:S(2)}) collective-permute-start(bf16[4,4,32,128]{3,2,1,0:T(8,128)(2,1)S(1)} %get-tuple-element.10), channel_id=1, source_target_pairs={{4,0},{8,4},{12,8},{0,12},{5,1},{9,5},{13,9},{1,13},{6,2},{10,6},{... | collective-permute-start | bytes 393224 | tf_op jit(solution)/shard_map/ppermute | solution.py:19
  6.5 4.3 %collective-permute-done = bf16[4,4,32,128]{3,2,1,0:T(8,128)(2,1)S(1)} collective-permute-done((bf16[4,4,32,128]{3,2,1,0:T(8,128)(2,1)S(1)}, bf16[4,4,32,128]{3,2,1,0:T(8,128)(2,1)S(1)}, u32[]{:S(2)}, u32[]{:S(2)}) %collective-permute-start) | collective-permute-done | bytes 131104 | tf_op jit(solution)/shard_map/ppermute | solution.py:18
  10.7 2.2 constant_dynamic-update-slice_fusion.1
  12.9 0.0 collective-permute-done.1
  13.0 0.2 fusion.29
  13.2 1.7 collective-permute-start.2
  14.8 1.7 collective-permute-start.3
  16.5 0.0 copy-done.3
  16.5 0.7 fusion.33
  17.2 0.0 copy-done.4
  17.2 0.7 fusion.32
  17.9 4.0 %collective-permute-done.2 = bf16[4,72,4,128]{3,2,1,0:T(4,128)(2,1)S(1)} collective-permute-done((bf16[4,72,4,128]{3,2,1,0:T(4,128)(2,1)S(1)}, bf16[4,72,4,128]{3,2,1,0:T(4,128)(2,1)S(1)}, u32[]{:S(2)}, u32[]{:S(2)}) %collective-permute-start.2) | collective-permute-done | bytes 294944 | tf_op jit(solution)/shard_map/ppermute | solution.py:18
  21.9 0.0 collective-permute-done.3
  21.9 2.2 maximum_select_fusion
  24.2 0.0 copy-start.2
  24.2 11.4 %multiply_add_fusion.1 = f32[4,64,40,128]{3,2,1,0:T(8,128)} fusion(bf16[4,72,40,128]{3,2,1,0:T(8,128)(2,1)S(1)} %maximum_select_fusion, f32[]{:T(128)} %bitcast.11, f32[]{:T(128)} %bitcast.10, f32[]{:T(128)} %bitcast.9, f32[]{:T(128)} %bitcast.8, f32[]{:T(128)} %bitcast.7, f32[]{:T(128)} %bitcast.6, f32[]{:T(128)} %bitcast.5, f32[]{:T(128)} %bitcast.4, f32[]{:T(128)} %bitcast.1), kind=kLoop, calls=%fused_computation.5 | loop fusion | flops 34078720 | bytes 28835876 | tf_op jit(solution)/shard_map/add | solution.py:59
  35.6 0.0 copy-done.2
  35.6 23.5 %fusion.1 = f32[64,32,128]{2,1,0:T(8,128)} fusion(bf16[4,64,32,128]{3,2,1,0:T(8,128)(2,1)S(1)} %copy-done.2, f32[4,64,40,128]{3,2,1,0:T(8,128)} %multiply_add_fusion.1, f32[]{:T(128)} %bitcast.18, f32[]{:T(128)} %bitcast.17, f32[]{:T(128)} %bitcast.16, f32[]{:T(128)} %bitcast.15, f32[]{:T(128)} %bitcast.14, f32[]{:T(128)} %bitcast.13, f32[]{:T(128)} %bitcast.12, ...), kind=kOutput, calls=%fused_computation.7 | convolution fusion | flops 290193408 | bytes 40931840 | tf_op jit(solution)/shard_map/dot_general | solution.py:85
  59.1 10.3 %all-to-all-start = ((f32[16,128,128]{2,1,0:T(8,128)}), f32[16,128,128]{2,1,0:T(8,128)S(1)}, u32[]{:S(2)}, u32[]{:S(2)}) async-start(f32[16,128,128]{2,1,0:T(8,128)} %bitcast.29), calls=%async_computation | async-start | bytes 2097152 | tf_op jit(solution)/shard_map/all_to_all | solution.py:31
  69.4 18.9 %all-to-all-done = f32[16,128,128]{2,1,0:T(8,128)S(1)} async-done(((f32[16,128,128]{2,1,0:T(8,128)}), f32[16,128,128]{2,1,0:T(8,128)S(1)}, u32[]{:S(2)}, u32[]{:S(2)}) %all-to-all-start) | async-done | bytes 1048608 | tf_op jit(solution)/shard_map/all_to_all | solution.py:31
  88.4 0.1 reduce_sum.28
  88.4 0.9 dynamic-slice_multiply_fusion
  89.3 0.1 broadcast_in_dim.23
  89.4 29.5 %all_to_all.10 = f32[16,128,128]{2,1,0:T(8,128)S(1)} all-to-all(f32[16,128,128]{2,1,0:T(8,128)S(1)} %broadcast_in_dim.23), channel_id=1, replica_groups=mesh['mem_0'=2,'mem_1'=4,'mem_2'=2,'lat'=4,'lon'=4] {'mem_0','mem_1','me..., dimensions={0} | all-to-all | bytes 2097152 | tf_op jit(solution)/shard_map/all_to_all | solution.py:43
  118.9 0.7 fusion.24
  119.7 14.3 %collective-permute-start.4 = (bf16[4,4,32,128]{3,2,1,0:T(8,128)(2,1)S(1)}, bf16[4,4,32,128]{3,2,1,0:T(8,128)(2,1)S(1)}, u32[]{:S(2)}, u32[]{:S(2)}) collective-permute-start(bf16[4,4,32,128]{3,2,1,0:T(8,128)(2,1)S(1)} %get-tuple-element.8), channel_id=1, source_target_pairs={{0,4},{4,8},{8,12},{12,0},{1,5},{5,9},{9,13},{13,1},{2,6},{6,10},{... | collective-permute-start | bytes 393224 | tf_op jit(solution)/shard_map/ppermute | solution.py:18
  134.0 0.0 collective-permute-start.5
  134.0 3.9 %collective-permute-done.4 = bf16[4,4,32,128]{3,2,1,0:T(8,128)(2,1)S(1)} collective-permute-done((bf16[4,4,32,128]{3,2,1,0:T(8,128)(2,1)S(1)}, bf16[4,4,32,128]{3,2,1,0:T(8,128)(2,1)S(1)}, u32[]{:S(2)}, u32[]{:S(2)}) %collective-permute-start.4) | collective-permute-done | bytes 131104 | tf_op jit(solution)/shard_map/ppermute | solution.py:18
  137.9 1.7 collective-permute-done.5
  139.6 0.2 pad_maximum_fusion.2
  139.8 1.7 collective-permute-start.6
  141.5 1.7 collective-permute-start.7
  143.2 6.0 %collective-permute-done.6 = bf16[4,72,4,128]{3,2,1,0:T(4,128)(2,1)S(1)} collective-permute-done((bf16[4,72,4,128]{3,2,1,0:T(4,128)(2,1)S(1)}, bf16[4,72,4,128]{3,2,1,0:T(4,128)(2,1)S(1)}, u32[]{:S(2)}, u32[]{:S(2)}) %collective-permute-start.6) | collective-permute-done | bytes 294944 | tf_op jit(solution)/shard_map/ppermute | solution.py:18
  149.1 0.0 collective-permute-done.7
  149.2 3.5 %maximum_select_fusion.1 = bf16[4,72,40,128]{3,2,1,0:T(8,128)(2,1)S(1)} fusion(bf16[4,72,4,128]{3,2,1,0:T(4,128)(2,1)S(1)} %collective-permute-done.7, bf16[4,4,32,128]{3,2,1,0:T(8,128)(2,1)S(1)} %collective-permute-done.5, bf16[4,64,32,128]{3,2,1,0:T(8,128)(2,1)S(1)} %fusion.24, bf16[4,4,32,128]{3,2,1,0:T(8,128)(2,1)S(1)} %collective-permute-done.4, ...), kind=kLoop, calls=%fused_computation.45 | loop fusion | flops 16220160 | bytes 5898312 | tf_op jit(solution)/shard_map/jit(_where)/select_n | solution.py:74
  152.6 0.0 copy-start.1
  152.6 11.4 %multiply_add_fusion = f32[4,64,40,128]{3,2,1,0:T(8,128)} fusion(bf16[4,72,40,128]{3,2,1,0:T(8,128)(2,1)S(1)} %maximum_select_fusion.1, f32[]{:T(128)} %bitcast.11, f32[]{:T(128)} %bitcast.10, f32[]{:T(128)} %bitcast.9, f32[]{:T(128)} %bitcast.8, f32[]{:T(128)} %bitcast.7, f32[]{:T(128)} %bitcast.6, f32[]{:T(128)} %bitcast.5, f32[]{:T(128)} %bitcast.4, f32[]{:T(128)} %bitcast.1), kind=kLoop, calls=%fused_computation.4 | loop fusion | flops 34078720 | bytes 28835876 | tf_op jit(solution)/shard_map/add | solution.py:59
  164.0 26.9 %fusion = (f32[]{:T(128)}, f32[4,64,32,128]{3,2,1,0:T(8,128)}) fusion(bf16[4,64,32,128]{3,2,1,0:T(8,128)(2,1)S(1)} %copy-done.1, f32[4,64,40,128]{3,2,1,0:T(8,128)} %multiply_add_fusion, f32[]{:T(128)} %bitcast.3, f32[]{:T(128)} %bitcast.12, f32[]{:T(128)} %bitcast.13, f32[]{:T(128)} %bitcast.14, f32[]{:T(128)} %bitcast.15, f32[]{:T(128)} %bitcast.16, ...), kind=kLoop, calls=%fused_computation.6 | loop fusion | flops 22020096 | bytes 44040232 | tf_op jit(solution)/shard_map/reduce_sum | solution.py:110
  190.8 9.5 %psum.35 = f32[]{:T(128)} all-reduce(f32[]{:T(128)} %get-tuple-element.2), channel_id=1, replica_groups=mesh['mem_0'=2,'mem_1'=4,'mem_2'=2,'lat'=4,'lon'=4] {'mem_0'}, use_global_device_ids=true, to_apply=%region_3.4 | all-reduce | flops 1 | bytes 8 | tf_op jit(solution)/shard_map/psum | solution.py:52
  200.3 11.2 %psum.36 = f32[]{:T(128)} all-reduce(f32[]{:T(128)} %psum.35), channel_id=1, replica_groups=mesh['mem_0'=2,'mem_1'=4,'mem_2'=2,'lat'=4,'lon'=4] {'mem_1'}, use_global_device_ids=true, to_apply=%region_4.5 | all-reduce | flops 1 | bytes 8 | tf_op jit(solution)/shard_map/psum | solution.py:52
  211.5 3.1 %psum.37 = f32[]{:T(128)} all-reduce(f32[]{:T(128)} %psum.36), channel_id=1, replica_groups=mesh['mem_0'=2,'mem_1'=4,'mem_2'=2,'lat'=4,'lon'=4] {'mem_2'}, use_global_device_ids=true, to_apply=%region_5.6 | all-reduce | flops 1 | bytes 8 | tf_op jit(solution)/shard_map/psum | solution.py:52
  214.6 13.2 %psum.38 = f32[]{:T(128)} all-reduce(f32[]{:T(128)} %psum.37), channel_id=1, replica_groups=mesh['mem_0'=2,'mem_1'=4,'mem_2'=2,'lat'=4,'lon'=4] {'lat'}, use_global_device_ids=true, to_apply=%region_6.7 | all-reduce | flops 1 | bytes 8 | tf_op jit(solution)/shard_map/psum | solution.py:52
  227.9 11.3 %psum.39 = f32[]{:T(128)} all-reduce(f32[]{:T(128)} %psum.38), channel_id=1, replica_groups=mesh['mem_0'=2,'mem_1'=4,'mem_2'=2,'lat'=4,'lon'=4] {'lon'}, use_global_device_ids=true, to_apply=%region_7.8 | all-reduce | flops 1 | bytes 8 | tf_op jit(solution)/shard_map/psum | solution.py:52
  (6 shorter events, 0.1 us)
Async XLA Ops:
  0.6 34.9 %copy-start = (bf16[128,128]{1,0:T(8,128)(2,1)S(1)}, bf16[128,128]{1,0:T(8,128)(2,1)}, u32[]{:S(2)}) copy-start(bf16[128,128]{1,0:T(8,128)(2,1)} %param.11) | copy-start | bytes 98308
  0.6 15.9 %copy-start.3 = (f32[9]{0:T(128)S(1)}, f32[9]{0:T(128)}, u32[]{:S(2)}) copy-start(f32[9]{0:T(128)} %param.9) | copy-start | bytes 112
  0.7 16.6 %copy-start.4 = (f32[9]{0:T(128)S(1)}, f32[9]{0:T(128)}, u32[]{:S(2)}) copy-start(f32[9]{0:T(128)} %param.10) | copy-start | bytes 112
  1.7 9.1 %collective-permute-start = (bf16[4,4,32,128]{3,2,1,0:T(8,128)(2,1)S(1)}, bf16[4,4,32,128]{3,2,1,0:T(8,128)(2,1)S(1)}, u32[]{:S(2)}, u32[]{:S(2)}) collective-permute-start(bf16[4,4,32,128]{3,2,1,0:T(8,128)(2,1)S(1)} %get-tuple-element.11), channel_id=1, source_target_pairs={{0,4},{4,8},{8,12},{12,0},{1,5},{5,9},{9,13},{13,1},{2,6},{6,10},{... | collective-permute-start | bytes 393224 | tf_op jit(solution)/shard_map/ppermute | solution.py:18
  3.7 9.2 %collective-permute-start.1 = (bf16[4,4,32,128]{3,2,1,0:T(8,128)(2,1)S(1)}, bf16[4,4,32,128]{3,2,1,0:T(8,128)(2,1)S(1)}, u32[]{:S(2)}, u32[]{:S(2)}) collective-permute-start(bf16[4,4,32,128]{3,2,1,0:T(8,128)(2,1)S(1)} %get-tuple-element.10), channel_id=1, source_target_pairs={{4,0},{8,4},{12,8},{0,12},{5,1},{9,5},{13,9},{1,13},{6,2},{10,6},{... | collective-permute-start | bytes 393224 | tf_op jit(solution)/shard_map/ppermute | solution.py:19
  13.2 8.7 %collective-permute-start.2 = (bf16[4,72,4,128]{3,2,1,0:T(4,128)(2,1)S(1)}, bf16[4,72,4,128]{3,2,1,0:T(4,128)(2,1)S(1)}, u32[]{:S(2)}, u32[]{:S(2)}) collective-permute-start(bf16[4,72,4,128]{3,2,1,0:T(4,128)(2,1)S(1)} %get-tuple-element.6), channel_id=1, source_target_pairs={{0,1},{1,2},{2,3},{3,0},{4,5},{5,6},{6,7},{7,4},{8,9},{9,10},{10,1... | collective-permute-start | bytes 884744 | tf_op jit(solution)/shard_map/ppermute | solution.py:18
  14.8 7.1 %collective-permute-start.3 = (bf16[4,72,4,128]{3,2,1,0:T(4,128)(2,1)S(1)}, bf16[4,72,4,128]{3,2,1,0:T(4,128)(2,1)S(1)}, u32[]{:S(2)}, u32[]{:S(2)}) collective-permute-start(bf16[4,72,4,128]{3,2,1,0:T(4,128)(2,1)S(1)} %get-tuple-element.7), channel_id=1, source_target_pairs={{1,0},{2,1},{3,2},{0,3},{5,4},{6,5},{7,6},{4,7},{9,8},{10,9},{11,1... | collective-permute-start | bytes 884744 | tf_op jit(solution)/shard_map/ppermute | solution.py:19
  24.2 11.4 %copy-start.2 = (bf16[4,64,32,128]{3,2,1,0:T(8,128)(2,1)S(1)}, bf16[4,64,32,128]{3,2,1,0:T(8,128)(2,1)}, u32[]{:S(2)}) copy-start(bf16[4,64,32,128]{3,2,1,0:T(8,128)(2,1)} %param.7) | copy-start | bytes 6291460
  59.1 29.3 %all-to-all-start = ((f32[16,128,128]{2,1,0:T(8,128)}), f32[16,128,128]{2,1,0:T(8,128)S(1)}, u32[]{:S(2)}, u32[]{:S(2)}) async-start(f32[16,128,128]{2,1,0:T(8,128)} %bitcast.29), calls=%async_computation | async-start | bytes 2097152 | tf_op jit(solution)/shard_map/all_to_all | solution.py:31
  119.7 18.2 %collective-permute-start.4 = (bf16[4,4,32,128]{3,2,1,0:T(8,128)(2,1)S(1)}, bf16[4,4,32,128]{3,2,1,0:T(8,128)(2,1)S(1)}, u32[]{:S(2)}, u32[]{:S(2)}) collective-permute-start(bf16[4,4,32,128]{3,2,1,0:T(8,128)(2,1)S(1)} %get-tuple-element.8), channel_id=1, source_target_pairs={{0,4},{4,8},{8,12},{12,0},{1,5},{5,9},{9,13},{13,1},{2,6},{6,10},{... | collective-permute-start | bytes 393224 | tf_op jit(solution)/shard_map/ppermute | solution.py:18
  134.0 5.6 %collective-permute-start.5 = (bf16[4,4,32,128]{3,2,1,0:T(8,128)(2,1)S(1)}, bf16[4,4,32,128]{3,2,1,0:T(8,128)(2,1)S(1)}, u32[]{:S(2)}, u32[]{:S(2)}) collective-permute-start(bf16[4,4,32,128]{3,2,1,0:T(8,128)(2,1)S(1)} %get-tuple-element.9), channel_id=1, source_target_pairs={{4,0},{8,4},{12,8},{0,12},{5,1},{9,5},{13,9},{1,13},{6,2},{10,6},{... | collective-permute-start | bytes 393224 | tf_op jit(solution)/shard_map/ppermute | solution.py:19
  139.8 9.3 %collective-permute-start.6 = (bf16[4,72,4,128]{3,2,1,0:T(4,128)(2,1)S(1)}, bf16[4,72,4,128]{3,2,1,0:T(4,128)(2,1)S(1)}, u32[]{:S(2)}, u32[]{:S(2)}) collective-permute-start(bf16[4,72,4,128]{3,2,1,0:T(4,128)(2,1)S(1)} %get-tuple-element.4), channel_id=1, source_target_pairs={{0,1},{1,2},{2,3},{3,0},{4,5},{5,6},{6,7},{7,4},{8,9},{9,10},{10,1... | collective-permute-start | bytes 884744 | tf_op jit(solution)/shard_map/ppermute | solution.py:18
  141.5 7.7 %collective-permute-start.7 = (bf16[4,72,4,128]{3,2,1,0:T(4,128)(2,1)S(1)}, bf16[4,72,4,128]{3,2,1,0:T(4,128)(2,1)S(1)}, u32[]{:S(2)}, u32[]{:S(2)}) collective-permute-start(bf16[4,72,4,128]{3,2,1,0:T(4,128)(2,1)S(1)} %get-tuple-element.5), channel_id=1, source_target_pairs={{1,0},{2,1},{3,2},{0,3},{5,4},{6,5},{7,6},{4,7},{9,8},{10,9},{11,1... | collective-permute-start | bytes 884744 | tf_op jit(solution)/shard_map/ppermute | solution.py:19
  152.6 11.4 %copy-start.1 = (bf16[4,64,32,128]{3,2,1,0:T(8,128)(2,1)S(1)}, bf16[4,64,32,128]{3,2,1,0:T(8,128)(2,1)}, u32[]{:S(2)}) copy-start(bf16[4,64,32,128]{3,2,1,0:T(8,128)(2,1)} %param.6) | copy-start | bytes 6291460
where the time goes:
time: 242 us; the launch traced here: 241 us
  blocking collectives  77.9 us (32%)
  other arithmetic  56.4 us (23%)
  waiting for transfers between devices  38.9 us (16%)
  starting transfers between devices  36.1 us (15%)
  matrix products  24.3 us (10%)
  local copies, waits for them, and re-layouts  4.95 us (2%)
  between operations  2.55 us (1%)
    psum x5, blocking collectives, by_axis(): value = lax.psum(value, axis)  48.4 us
    all_to_all x1, blocking collectives, copy_for_each(): return lax.all_to_all(copies, axis, split_axis=0, concat_axis=0, tiled=True)  29.5 us
    reduce_sum x1, other arithmetic, per_device(): curvature = by_axis(jnp.sum(control * hessian), MEM_LAT_LON) / entries  26.9 us
    dot_general x1, matrix products, per_device(): jnp.dot(smoothed.reshape(-1, levels), vertical, preferred_element_type=jn...  23.5 us
    add x2, other arithmetic, smooth_block(): across + first_taps[offset] * extended[:, offset:offset + tile_rows]  22.7 us
    ppermute x4, starting transfers between devices, extended_2(): before = lax.ppermute(last, axis, up)  19.6 us
    all_to_all x1, waiting for transfers between devices, sum_at_owner(): lax.all_to_all(in_blocks(value, dim, peers), axis, 0, 0, tiled=True)  18.9 us
    ppermute x4, waiting for transfers between devices, extended_2(): before = lax.ppermute(last, axis, up)  18.1 us
  transfers between devices with their start and end apart: 9, of which 6 were waited for; matrix products, arithmetic and copies ran while one was open for 1% of the time, Pallas kernels for 0%

commit v1 on v0

v1 whole, which is shorter than its diff:
```python
import functools

import jax
import jax.numpy as jnp
from jax import lax
from jax.experimental import pallas as pl
from jax.experimental.pallas import tpu as pltpu
from jax.sharding import Mesh
from jax.sharding import PartitionSpec as P

MEM = ("zh", "x", "core")
BF = jnp.bfloat16
F32 = jnp.float32
HALO = 4
TAPS = 9
ROWS = 8
VMEM = pl.BlockSpec(memory_space=pltpu.VMEM)
SMEM = pl.BlockSpec(memory_space=pltpu.SMEM)


def ring(axis, step):
    n = lax.axis_size(axis)
    return [(i, (i + step) % n) for i in range(n)]


def line(axis, step):
    n = lax.axis_size(axis)
    return [(i, i + step) for i in range(n) if 0 <= i + step < n]


def params():
    return pltpu.CompilerParams(vmem_limit_bytes=40 * 2**20)


def cost(flops, size):
    return pl.CostEstimate(flops=flops, bytes_accessed=size, transcendentals=0)


def band_kernel(cols, lat_taps, lon_taps, fwd, rev):
    width = fwd.shape[1]
    span = ROWS + 2 * HALO
    centre, side = span * cols, span * HALO
    k = lax.broadcasted_iota(jnp.int32, (cols, width), 1)
    j = lax.broadcasted_iota(jnp.int32, (cols, width), 0)
    west = k - centre
    east = west - side
    in_centre, in_west = k < centre, west < side
    p = jnp.where(in_centre, k // cols, jnp.where(in_west, west // HALO, east // HALO))
    q = jnp.where(in_centre, k % cols + HALO, jnp.where(in_west, west % HALO, east % HALO + cols + HALO))
    b = q - j
    fwd_b, rev_b = (jnp.zeros((cols, width), F32),) * 2
    for t in range(TAPS):
        fwd_b = jnp.where(b == t, lon_taps[t], fwd_b)
        rev_b = jnp.where(b == t, lon_taps[TAPS - 1 - t], rev_b)
    for i in range(ROWS):
        a = p - i
        fwd_a, rev_a = (jnp.zeros((cols, width), F32),) * 2
        for t in range(TAPS):
            fwd_a = jnp.where(a == t, lat_taps[t], fwd_a)
            rev_a = jnp.where(a == t, lat_taps[TAPS - 1 - t], rev_a)
        for out, value in ((fwd, fwd_a * fwd_b), (rev, rev_a * rev_b)):
            high = value.astype(BF)
            low = (value - high.astype(F32)).astype(BF)
            out[i * cols : (i + 1) * cols, :] = high
            out[(ROWS + i) * cols : (ROWS + i + 1) * cols, :] = low


def bands(lat_taps, lon_taps, cols):
    span = ROWS + 2 * HALO
    shape = jax.ShapeDtypeStruct((2 * ROWS * cols, span * (cols + 2 * HALO)), BF)
    return pl.pallas_call(
        functools.partial(band_kernel, cols),
        out_shape=(shape, shape),
        in_specs=[SMEM, SMEM],
        out_specs=(VMEM, VMEM),
        compiler_params=params(),
        cost_estimate=cost(2_000_000, 4 * shape.shape[0] * shape.shape[1]),
        name="bands",
    )(lat_taps, lon_taps)


def around(own, south, north, west, east, member, block, cols):
    blocks = own.shape[1] // (ROWS * cols)
    lo = (block * ROWS - HALO) * cols
    hi = (block * ROWS + ROWS + HALO) * cols
    parts = []
    if block == 0:
        parts.append(south[member])
    parts.append(own[member, max(lo, 0) : min(hi, own.shape[1]), :])
    if block == blocks - 1:
        parts.append(north[member])
    side = slice(block * ROWS * HALO, (block * ROWS + ROWS + 2 * HALO) * HALO)
    parts += [west[member, side, :], east[member, side, :]]
    return jnp.concatenate(parts, axis=0)


def filtered(band, own, south, north, west, east, members, block, cols):
    cells = jnp.concatenate(
        [around(own, south, north, west, east, m, block, cols) for m in members], axis=1
    )
    both = jnp.dot(band[...], cells, preferred_element_type=F32)
    size = both.shape[0] // 2
    both = both[:size] + both[size:]
    levels = own.shape[2]
    return [both[:, n * levels : (n + 1) * levels] for n in range(len(members))]


def forward_kernel(cols, own, south, north, west, east, band, vertical, ensemble, keep, send, square):
    members = own.shape[0]
    size = ROWS * cols
    blocks = own.shape[1] // size
    core = lax.axis_index("core")
    total = jnp.zeros((8, own.shape[2]), F32)
    for block in range(blocks):
        rows = slice(block * size, (block + 1) * size)
        increment = jnp.zeros((size, own.shape[2]), F32)
        for first in range(0, members, 2):
            pair = range(first, first + 2)
            for m, value in zip(pair, filtered(band, own, south, north, west, east, pair, block, cols)):
                leveled = jnp.dot(value.astype(BF), vertical[...], preferred_element_type=F32)
                increment = increment + ensemble[m, rows, :].astype(F32) * leveled
                c = own[m, rows, :].astype(F32)
                total = total + jnp.sum((c * c).reshape(size // 8, 8, own.shape[2]), axis=0)
        half, at = block // (blocks // 2), block % (blocks // 2)
        place = slice(at * size, (at + 1) * size)
        increment = increment.astype(BF)

        @pl.when(core == half)
        def _():
            keep[place, :] = increment

        @pl.when(core != half)
        def _():
            send[place, :] = increment

    square[...] = total


def forward(own, south, north, west, east, band, vertical, ensemble, cols):
    members, cells, levels = own.shape
    half = jax.ShapeDtypeStruct((cells // 2, levels), BF)
    return pl.pallas_call(
        functools.partial(forward_kernel, cols),
        out_shape=(half, half, jax.ShapeDtypeStruct((8, levels), F32)),
        in_specs=[VMEM] * 8,
        out_specs=(VMEM,) * 3,
        compiler_params=params(),
        cost_estimate=cost(4_000_000_000, 6_000_000),
        name="forward",
    )(own, south, north, west, east, band, vertical, ensemble)


def level_kernel(weighted, ensemble, vertical, adjoint):
    size = 256
    for start in range(0, weighted.shape[0], size):
        rows = slice(start, start + size)
        w = weighted[rows, :].astype(F32)
        for m in range(ensemble.shape[0]):
            part = (ensemble[m, rows, :].astype(F32) * w).astype(BF)
            adjoint[m, rows, :] = lax.dot_general(
                part, vertical[...], (((1,), (1,)), ((), ())), preferred_element_type=F32
            ).astype(BF)


def level(weighted, ensemble, vertical):
    return pl.pallas_call(
        level_kernel,
        out_shape=jax.ShapeDtypeStruct(ensemble.shape, BF),
        in_specs=[VMEM] * 3,
        out_specs=VMEM,
        compiler_params=params(),
        cost_estimate=cost(300_000_000, 4_500_000),
        name="level",
    )(weighted, ensemble, vertical)


def backward_kernel(cols, own, south, north, west, east, band, control, hessian):
    members = own.shape[0]
    size = ROWS * cols
    for block in range(own.shape[1] // size):
        rows = slice(block * size, (block + 1) * size)
        for first in range(0, members, 2):
            pair = range(first, first + 2)
            for m, value in zip(pair, filtered(band, own, south, north, west, east, pair, block, cols)):
                hessian[m, rows, :] = control[m, rows, :].astype(F32) + value


def backward(own, south, north, west, east, band, control, cols):
    return pl.pallas_call(
        functools.partial(backward_kernel, cols),
        out_shape=jax.ShapeDtypeStruct(control.shape, F32),
        in_specs=[VMEM] * 7,
        out_specs=VMEM,
        compiler_params=params(),
        cost_estimate=cost(3_500_000_000, 9_000_000),
        name="backward",
    )(own, south, north, west, east, band, control)


def halo(tile):
    members, rows, cols, levels = tile.shape
    south = lax.ppermute(tile[:, rows - HALO :], "lat", line("lat", 1))
    north = lax.ppermute(tile[:, :HALO], "lat", line("lat", -1))

    def side(lo):
        cut = slice(lo, lo + HALO)
        return jnp.concatenate([south[:, :, cut], tile[:, :, cut], north[:, :, cut]], axis=1).reshape(
            members, (rows + 2 * HALO) * HALO, levels
        )

    west = lax.ppermute(side(cols - HALO), "lon", ring("lon", 1))
    east = lax.ppermute(side(0), "lon", ring("lon", -1))
    flat = (members, HALO * cols, levels)
    return south.reshape(flat), north.reshape(flat), west, east


def split3(value):
    parts = []
    for _ in range(3):
        part = lax.reduce_precision(value, 8, 7)
        parts.append(part.astype(BF))
        value = value - part
    return jnp.concatenate(parts + [jnp.zeros((13, value.shape[1]), BF)], axis=0)


def join3(rows):
    rows = rows.astype(F32)
    return (rows[0:1] + rows[1:2]) + rows[2:3]


def total_of_four(value, axis):
    n = lax.axis_size(axis)
    value = value + lax.ppermute(value, axis, [(i, i ^ 1) for i in range(n)])
    return value + lax.ppermute(value, axis, [(i, n - 1 - i) for i in range(n)])


def per_device(control, ensemble, precision, lat_taps, lon_taps, vertical):
    members, tile_rows, tile_cols, levels = control.shape
    cells = tile_rows * tile_cols
    entries = control.size * lax.axis_size(MEM) * lax.axis_size("lat") * lax.axis_size("lon")
    core, x = lax.axis_index("core"), lax.axis_index("x")
    flat = (members, cells, levels)
    own, spread = control.reshape(flat), ensemble.reshape(flat)
    share = cells // 8

    south, north, west, east = halo(control)
    band, band_back = bands(lat_taps, lon_taps, tile_cols)
    keep, send, square = forward(own, south, north, west, east, band, vertical, spread, tile_cols)

    got = lax.ppermute(send, "core", ring("core", 1))
    half = (keep.astype(F32) + got.astype(F32)).astype(BF).reshape(4, share, levels)

    def pick(step):
        return lax.dynamic_index_in_dim(half, (x + step) % 4, 0, keepdims=False)

    one, three, two = [lax.ppermute(pick(k), "x", ring("x", k)) for k in (1, 3, 2)]
    part = ((one.astype(F32) + three.astype(F32)) + (pick(0).astype(F32) + two.astype(F32))).astype(BF)
    square = jnp.sum(square, axis=0, keepdims=True)
    message = jnp.concatenate([part, split3(square)], axis=0)
    other = lax.ppermute(message, "zh", ring("zh", 1))
    increment = message[:share].astype(F32) + other[:share].astype(F32)
    squares = join3(message[share:]) + join3(other[share:])
    start = (core * 4 + x) * share
    mine = lax.dynamic_slice_in_dim(precision.reshape(cells, levels), start, share, 0)
    weighted = mine * increment
    inner = squares + jnp.sum(weighted * increment, axis=0, keepdims=True)

    message = jnp.concatenate([weighted.astype(BF), split3(inner)], axis=0)
    three, two, one = [lax.ppermute(message, "x", ring("x", k)) for k in (3, 2, 1)]
    inner = (join3(one[share:]) + join3(three[share:])) + (join3(message[share:]) + join3(two[share:]))
    shares = [v[:share] for v in (message, three, two, one)]
    shares = lax.dynamic_slice_in_dim(jnp.stack(shares + shares), (4 - x) % 4, 4, 0).reshape(cells // 2, levels)
    message = jnp.concatenate([shares, split3(inner)], axis=0)
    other = lax.ppermute(message, "core", ring("core", 1))
    inner = join3(message[cells // 2 :]) + join3(other[cells // 2 :])
    first = jnp.where(core == 0, message[: cells // 2], other[: cells // 2])
    second = jnp.where(core == 0, other[: cells // 2], message[: cells // 2])
    weighted = jnp.concatenate([first, second], axis=0)

    adjoint = level(weighted, spread, vertical)
    south, north, west, east = halo(adjoint.reshape(control.shape))
    inner = total_of_four(total_of_four(inner, "lat"), "lon")
    hessian = backward(adjoint, south, north, west, east, band_back, own, tile_cols)
    return hessian.reshape(control.shape), jnp.sum(inner) / entries


def solution(mesh):
    split = Mesh(
        mesh.devices.reshape(2, 4, 2, mesh.shape["lat"], mesh.shape["lon"]),
        ("zh", "x", "core", "lat", "lon"),
    )
    return jax.shard_map(
        per_device,
        mesh=split,
        in_specs=(
            P(MEM, "lat", "lon", None),
            P(MEM, "lat", "lon", None),
            P("lat", "lon", None),
            P(),
            P(),
            P(),
        ),
        out_specs=(P(MEM, "lat", "lon", None), P()),
        check_vma=False,
    )
```

time: 242 us -> 109 us (0.45)
  blocking collectives: 77.9 us -> 0 us
  other arithmetic: 56.4 us -> 3.68 us
  matrix products: 24.3 us -> 0 us
  Pallas kernels: 0 us -> 17.3 us
  waiting for transfers between devices: 38.9 us -> 28 us
  starting transfers between devices: 36.1 us -> 45 us
  local copies, waits for them, and re-layouts: 4.95 us -> 10.3 us
    psum x5 -> x0, blocking collectives: 48.4 us -> none  [by_axis(): value = lax.psum(value, axis)]
    all_to_all x1 -> x0, blocking collectives: 29.5 us -> none  [copy_for_each(): return lax.all_to_all(copies, axis, split_axis=0, concat_axis=0, tiled=True)]
    reduce_sum x2 -> x3, other arithmetic: 26.9 us -> 1.57 us  [the longest x1 0.96 us: per_device(): inner = squares + jnp.sum(weighted * increment, axis=0, keepdims=True)]
    dot_general x2 -> x0, matrix products: 24.3 us -> none  [the longest x1 23.5 us: per_device(): jnp.dot(smoothed.reshape(-1, levels), vertical, preferred_element_type=jn...]
    add x2 -> x4, other arithmetic: 22.7 us -> 0.02 us  [the longest x1 0.01 us: per_device(): inner = join3(message[cells // 2:]) + join3(other[cells // 2:])]
    ppermute x8 -> x21, starting transfers between devices: 25.7 us -> 45 us  [the longest x2 9.11 us: halo(): south = lax.ppermute(tile[:, rows - HALO:], 'lat', line('lat', 1))]
    all_to_all x1 -> x0, waiting for transfers between devices: 18.9 us -> none  [sum_at_owner(): lax.all_to_all(in_blocks(value, dim, peers), axis, 0, 0, tiled=True)]
    pallas_call x0 -> x4, Pallas kernels: none -> 17.3 us  [the longest x1 10.1 us: forward(): pl.pallas_call(functools.partial(forward_kernel, cols), out_shape=(half,...]
  transfers between devices with their start and end apart: 9 -> 21, of which waited for: 6 -> 15; matrix products, arithmetic and copies ran while one was open for 1% -> 2% of each run, Pallas kernels for 0% -> 1%
where the time goes in v1:
time: 109 us; the launch traced here: 107 us
  starting transfers between devices  45 us (41%)
  waiting for transfers between devices  28 us (26%)
  Pallas kernels  17.3 us (16%)
  local copies, waits for them, and re-layouts  10.3 us (9%)
  other arithmetic  3.68 us (3%)
  between operations  2.88 us (3%)
    pallas_call x1, Pallas kernels, forward(): pl.pallas_call(functools.partial(forward_kernel, cols), out_shape=(half,...  10.1 us
    ppermute x2, starting transfers between devices, halo(): south = lax.ppermute(tile[:, rows - HALO:], 'lat', line('lat', 1))  9.11 us
    ppermute x1, starting transfers between devices, per_device(): other = lax.ppermute(message, 'zh', ring('zh', 1))  6.81 us
    unnamed x24, local copies, waits for them, and re-layouts  6.79 us
    ppermute x2, starting transfers between devices, total_of_four(): return value + lax.ppermute(value, axis, [(i, n - 1 - i) for i in range(n)])  5.99 us
    ppermute x3, starting transfers between devices, per_device(): lax.ppermute(message, 'x', ring('x', k))  5.8 us
    pallas_call x1, Pallas kernels, backward(): pl.pallas_call(functools.partial(backward_kernel, cols), out_shape=jax.Sh...  5.43 us
    ppermute x3, starting transfers between devices, per_device(): lax.ppermute(pick(k), 'x', ring('x', k))  4.83 us
  transfers between devices with their start and end apart: 21, of which 15 were waited for; matrix products, arithmetic and copies ran while one was open for 2% of the time, Pallas kernels for 1%

profile of v1, /device:TPU:2, one launch (start us, length us, event | category | flops | bytes accessed | tf_op | source)
XLA Modules:
  0.0 107.1 jit_solution(11428936424700902604)
XLA Ops:
  0.7 1.1 %fusion.30 = (bf16[4,4,32,128]{3,2,1,0:T(8,128)(2,1)S(1)}, bf16[4,4,32,128]{3,2,1,0:T(8,128)(2,1)S(1)}) fusion(bf16[4,64,32,128]{3,2,1,0:T(8,128)(2,1)} %param.6), kind=kLoop, calls=%fused_computation.85 | loop fusion | bytes 524288 | tf_op jit(solution)/shard_map/slice | solution.py:203
  1.8 1.3 %collective-permute-start.1 = (bf16[4,4,32,128]{3,2,1,0:T(8,128)(2,1)S(1)}, bf16[4,4,32,128]{3,2,1,0:T(8,128)(2,1)S(1)}, u32[]{:S(2)}, u32[]{:S(2)}) collective-permute-start(bf16[4,4,32,128]{3,2,1,0:T(8,128)(2,1)S(1)} %get-tuple-element.24), channel_id=1, source_target_pairs={{4,0},{8,4},{12,8},{5,1},{9,5},{13,9},{6,2},{10,6},{14,10},{7,3},{... | collective-permute-start | bytes 393224 | tf_op jit(solution)/shard_map/ppermute | solution.py:203
  3.1 4.6 %collective-permute-start = (bf16[4,4,32,128]{3,2,1,0:T(8,128)(2,1)S(1)}, bf16[4,4,32,128]{3,2,1,0:T(8,128)(2,1)S(1)}, u32[]{:S(2)}, u32[]{:S(2)}) collective-permute-start(bf16[4,4,32,128]{3,2,1,0:T(8,128)(2,1)S(1)} %get-tuple-element.25), channel_id=1, source_target_pairs={{0,4},{4,8},{8,12},{1,5},{5,9},{9,13},{2,6},{6,10},{10,14},{3,7},{... | collective-permute-start | bytes 393224 | tf_op jit(solution)/shard_map/ppermute | solution.py:202
  7.7 1.4 %fusion.29 = (bf16[4,64,4,128]{3,2,1,0:T(4,128)(2,1)S(1)}, bf16[4,64,4,128]{3,2,1,0:T(4,128)(2,1)S(1)}) fusion(bf16[4,64,32,128]{3,2,1,0:T(8,128)(2,1)} %param.6), kind=kLoop, calls=%fused_computation.84 | loop fusion | bytes 1048576 | tf_op jit(solution)/shard_map/slice | solution.py:207
  9.2 1.2 %collective-permute-done = bf16[4,4,32,128]{3,2,1,0:T(8,128)(2,1)S(1)} collective-permute-done((bf16[4,4,32,128]{3,2,1,0:T(8,128)(2,1)S(1)}, bf16[4,4,32,128]{3,2,1,0:T(8,128)(2,1)S(1)}, u32[]{:S(2)}, u32[]{:S(2)}) %collective-permute-start) | collective-permute-done | bytes 131104 | tf_op jit(solution)/shard_map/ppermute | solution.py:202
  10.6 1.7 %collective-permute-start.2 = (bf16[4,288,128]{2,1,0:T(8,128)(2,1)S(1)}, bf16[4,288,128]{2,1,0:T(8,128)(2,1)S(1)}, u32[]{:S(2)}, u32[]{:S(2)}) collective-permute-start(bf16[4,288,128]{2,1,0:T(8,128)(2,1)S(1)} %bitcast.72), channel_id=1, source_target_pairs={{0,1},{1,2},{2,3},{3,0},{4,5},{5,6},{6,7},{7,4},{8,9},{9,10},{10,1... | collective-permute-start | bytes 884744 | tf_op jit(solution)/shard_map/ppermute | solution.py:211
  12.4 1.7 %collective-permute-start.3 = (bf16[4,288,128]{2,1,0:T(8,128)(2,1)S(1)}, bf16[4,288,128]{2,1,0:T(8,128)(2,1)S(1)}, u32[]{:S(2)}, u32[]{:S(2)}) collective-permute-start(bf16[4,288,128]{2,1,0:T(8,128)(2,1)S(1)} %bitcast.73), channel_id=1, source_target_pairs={{0,3},{1,0},{2,1},{3,2},{4,7},{5,4},{6,5},{7,6},{8,11},{9,8},{10,9... | collective-permute-start | bytes 884744 | tf_op jit(solution)/shard_map/ppermute | solution.py:212
  14.2 1.0 bands.1
  15.2 0.8 copy-done.7
  16.0 3.6 %collective-permute-done.2.west = bf16[4,288,128]{2,1,0:T(8,128)(2,1)S(1)} collective-permute-done((bf16[4,288,128]{2,1,0:T(8,128)(2,1)S(1)}, bf16[4,288,128]{2,1,0:T(8,128)(2,1)S(1)}, u32[]{:S(2)}, u32[]{:S(2)}) %collective-permute-start.2) | collective-permute-done | bytes 294944 | tf_op jit(solution)/shard_map/ppermute | solution.py:211
  19.6 0.3 collective-permute-done.3.east
  19.9 1.6 %copy-done.2 = bf16[4,64,32,128]{3,2,1,0:T(8,128)(2,1)S(1)} copy-done((bf16[4,64,32,128]{3,2,1,0:T(8,128)(2,1)S(1)}, bf16[4,64,32,128]{3,2,1,0:T(8,128)(2,1)}, u32[]{:S(2)}) %copy-start.2) | copy-done | bytes 2097176
  21.5 10.1 %forward.1 = (bf16[1024,128]{1,0:T(8,128)(2,1)S(1)}, bf16[1024,128]{1,0:T(8,128)(2,1)S(1)}, f32[8,128]{1,0:T(8,128)S(1)}) custom-call(bf16[4,2048,128]{2,1,0:T(8,128)(2,1)S(1)} %bitcast.61, bf16[4,128,128]{2,1,0:T(8,128)(2,1)S(1)} %bitcast.66, bf16[4,128,128]{2,1,0:T(8,128)(2,1)S(1)} %bitcast.65, bf16[4,288,128]{2,1,0:T(8,128)(2,1)S(1)} %collective-permute-done.2.west, ...), custom_call_target="tpu_custom_call" | custom-call | flops 4000000000 | bytes 6000000 | tf_op jit(solution)/shard_map/forward/pallas_call | solution.py:142
  31.8 1.4 %collective-permute-done.4 = bf16[1024,128]{1,0:T(8,128)(2,1)S(1)} collective-permute-done((bf16[1024,128]{1,0:T(8,128)(2,1)S(1)}, bf16[1024,128]{1,0:T(8,128)(2,1)S(1)}, u32[]{:S(2)}, u32[]{:S(2)}) %collective-permute-start.4) | collective-permute-done | bytes 262176 | tf_op jit(solution)/shard_map/ppermute | solution.py:250
  33.4 1.6 %collective-permute-start.5 = (bf16[256,128]{1,0:T(8,128)(2,1)S(1)}, bf16[256,128]{1,0:T(8,128)(2,1)S(1)}, u32[]{:S(2)}, u32[]{:S(2)}) collective-permute-start(bf16[256,128]{1,0:T(8,128)(2,1)S(1)} %get-tuple-element.28), channel_id=1, source_target_pairs={{0,32},{32,64},{64,96},{96,0},{1,33},{33,65},{65,97},{97,1},{2,34}... | collective-permute-start | bytes 196616 | tf_op jit(solution)/shard_map/ppermute | solution.py:256
  34.9 1.4 %collective-permute-start.7 = (bf16[256,128]{1,0:T(8,128)(2,1)S(1)}, bf16[256,128]{1,0:T(8,128)(2,1)S(1)}, u32[]{:S(2)}, u32[]{:S(2)}) collective-permute-start(bf16[256,128]{1,0:T(8,128)(2,1)S(1)} %get-tuple-element.29), channel_id=1, source_target_pairs={{0,64},{32,96},{64,0},{96,32},{1,65},{33,97},{65,1},{97,33},{2,66}... | collective-permute-start | bytes 196616 | tf_op jit(solution)/shard_map/ppermute | solution.py:256
  36.3 1.9 %collective-permute-start.6 = (bf16[256,128]{1,0:T(8,128)(2,1)S(1)}, bf16[256,128]{1,0:T(8,128)(2,1)S(1)}, u32[]{:S(2)}, u32[]{:S(2)}) collective-permute-start(bf16[256,128]{1,0:T(8,128)(2,1)S(1)} %get-tuple-element.30), channel_id=1, source_target_pairs={{0,96},{32,0},{64,32},{96,64},{1,97},{33,1},{65,33},{97,65},{2,98}... | collective-permute-start | bytes 196616 | tf_op jit(solution)/shard_map/ppermute | solution.py:256
  38.2 2.8 %collective-permute-done.7 = bf16[256,128]{1,0:T(8,128)(2,1)S(1)} collective-permute-done((bf16[256,128]{1,0:T(8,128)(2,1)S(1)}, bf16[256,128]{1,0:T(8,128)(2,1)S(1)}, u32[]{:S(2)}, u32[]{:S(2)}) %collective-permute-start.7) | collective-permute-done | bytes 65568 | tf_op jit(solution)/shard_map/ppermute | solution.py:256
  41.0 0.3 collective-permute-done.6
  41.5 6.8 %collective-permute-start.8 = (bf16[272,128]{1,0:T(8,128)(2,1)S(1)}, bf16[272,128]{1,0:T(8,128)(2,1)S(1)}, u32[]{:S(2)}, u32[]{:S(2)}) collective-permute-start(bf16[272,128]{1,0:T(8,128)(2,1)S(1)} %concatenate.38), channel_id=1, source_target_pairs={{0,128},{128,0},{1,129},{129,1},{2,130},{130,2},{3,131},{131,3},{4... | collective-permute-start | bytes 208904 | tf_op jit(solution)/shard_map/ppermute | solution.py:260
  48.4 2.6 %collective-permute-done.8 = bf16[272,128]{1,0:T(8,128)(2,1)S(1)} collective-permute-done((bf16[272,128]{1,0:T(8,128)(2,1)S(1)}, bf16[272,128]{1,0:T(8,128)(2,1)S(1)}, u32[]{:S(2)}, u32[]{:S(2)}) %collective-permute-start.8) | collective-permute-done | bytes 69664 | tf_op jit(solution)/shard_map/ppermute | solution.py:260
  51.0 1.0 multiply_reduce_fusion
  51.9 0.9 bitcast_dynamic-update-slice_fusion
  53.0 1.5 %collective-permute-start.11 = (bf16[272,128]{1,0:T(8,128)(2,1)S(1)}, bf16[272,128]{1,0:T(8,128)(2,1)S(1)}, u32[]{:S(2)}, u32[]{:S(2)}) collective-permute-start(bf16[272,128]{1,0:T(8,128)(2,1)S(1)} %concatenate.40), channel_id=1, source_target_pairs={{0,32},{32,64},{64,96},{96,0},{1,33},{33,65},{65,97},{97,1},{2,34}... | collective-permute-start | bytes 208904 | tf_op jit(solution)/shard_map/ppermute | solution.py:269
  54.5 2.3 %collective-permute-start.10 = (bf16[272,128]{1,0:T(8,128)(2,1)S(1)}, bf16[272,128]{1,0:T(8,128)(2,1)S(1)}, u32[]{:S(2)}, u32[]{:S(2)}) collective-permute-start(bf16[272,128]{1,0:T(8,128)(2,1)S(1)} %concatenate.40), channel_id=1, source_target_pairs={{0,64},{32,96},{64,0},{96,32},{1,65},{33,97},{65,1},{97,33},{2,66}... | collective-permute-start | bytes 208904 | tf_op jit(solution)/shard_map/ppermute | solution.py:269
  56.8 2.0 %collective-permute-start.9 = (bf16[272,128]{1,0:T(8,128)(2,1)S(1)}, bf16[272,128]{1,0:T(8,128)(2,1)S(1)}, u32[]{:S(2)}, u32[]{:S(2)}) collective-permute-start(bf16[272,128]{1,0:T(8,128)(2,1)S(1)} %concatenate.40), channel_id=1, source_target_pairs={{0,96},{32,0},{64,32},{96,64},{1,97},{33,1},{65,33},{97,65},{2,98}... | collective-permute-start | bytes 208904 | tf_op jit(solution)/shard_map/ppermute | solution.py:269
  58.9 2.3 %collective-permute-done.9 = bf16[272,128]{1,0:T(8,128)(2,1)S(1)} collective-permute-done((bf16[272,128]{1,0:T(8,128)(2,1)S(1)}, bf16[272,128]{1,0:T(8,128)(2,1)S(1)}, u32[]{:S(2)}, u32[]{:S(2)}) %collective-permute-start.9) | collective-permute-done | bytes 69664 | tf_op jit(solution)/shard_map/ppermute | solution.py:269
  61.7 1.5 %collective-permute-done.12 = bf16[1040,128]{1,0:T(8,128)(2,1)S(1)} collective-permute-done((bf16[1040,128]{1,0:T(8,128)(2,1)S(1)}, bf16[1040,128]{1,0:T(8,128)(2,1)S(1)}, u32[]{:S(2)}, u32[]{:S(2)}) %collective-permute-start.12) | collective-permute-done | bytes 266272 | tf_op jit(solution)/shard_map/ppermute | solution.py:274
  63.4 1.6 %copy-done.1 = bf16[4,64,32,128]{3,2,1,0:T(8,128)(2,1)S(1)} copy-done((bf16[4,64,32,128]{3,2,1,0:T(8,128)(2,1)S(1)}, bf16[4,64,32,128]{3,2,1,0:T(8,128)(2,1)}, u32[]{:S(2)}) %copy-start.1) | copy-done | bytes 2097176
  65.0 0.7 level.1.own
  65.9 1.3 %collective-permute-start.14 = (bf16[4,4,32,128]{3,2,1,0:T(8,128)(2,1)S(1)}, bf16[4,4,32,128]{3,2,1,0:T(8,128)(2,1)S(1)}, u32[]{:S(2)}, u32[]{:S(2)}) collective-permute-start(bf16[4,4,32,128]{3,2,1,0:T(8,128)(2,1)S(1)} %get-tuple-element.20), channel_id=1, source_target_pairs={{4,0},{8,4},{12,8},{5,1},{9,5},{13,9},{6,2},{10,6},{14,10},{7,3},{... | collective-permute-start | bytes 393224 | tf_op jit(solution)/shard_map/ppermute | solution.py:203
  67.2 4.6 %collective-permute-start.13 = (bf16[4,4,32,128]{3,2,1,0:T(8,128)(2,1)S(1)}, bf16[4,4,32,128]{3,2,1,0:T(8,128)(2,1)S(1)}, u32[]{:S(2)}, u32[]{:S(2)}) collective-permute-start(bf16[4,4,32,128]{3,2,1,0:T(8,128)(2,1)S(1)} %get-tuple-element.21), channel_id=1, source_target_pairs={{0,4},{4,8},{8,12},{1,5},{5,9},{9,13},{2,6},{6,10},{10,14},{3,7},{... | collective-permute-start | bytes 393224 | tf_op jit(solution)/shard_map/ppermute | solution.py:202
  71.8 1.7 %collective-permute-done.14 = bf16[4,4,32,128]{3,2,1,0:T(8,128)(2,1)S(1)} collective-permute-done((bf16[4,4,32,128]{3,2,1,0:T(8,128)(2,1)S(1)}, bf16[4,4,32,128]{3,2,1,0:T(8,128)(2,1)S(1)}, u32[]{:S(2)}, u32[]{:S(2)}) %collective-permute-start.14) | collective-permute-done | bytes 131104 | tf_op jit(solution)/shard_map/ppermute | solution.py:203
  73.5 1.2 %collective-permute-done.13 = bf16[4,4,32,128]{3,2,1,0:T(8,128)(2,1)S(1)} collective-permute-done((bf16[4,4,32,128]{3,2,1,0:T(8,128)(2,1)S(1)}, bf16[4,4,32,128]{3,2,1,0:T(8,128)(2,1)S(1)}, u32[]{:S(2)}, u32[]{:S(2)}) %collective-permute-start.13) | collective-permute-done | bytes 131104 | tf_op jit(solution)/shard_map/ppermute | solution.py:202
  74.9 1.7 %collective-permute-start.15 = (bf16[4,288,128]{2,1,0:T(8,128)(2,1)S(1)}, bf16[4,288,128]{2,1,0:T(8,128)(2,1)S(1)}, u32[]{:S(2)}, u32[]{:S(2)}) collective-permute-start(bf16[4,288,128]{2,1,0:T(8,128)(2,1)S(1)} %bitcast.70), channel_id=1, source_target_pairs={{0,1},{1,2},{2,3},{3,0},{4,5},{5,6},{6,7},{7,4},{8,9},{9,10},{10,1... | collective-permute-start | bytes 884744 | tf_op jit(solution)/shard_map/ppermute | solution.py:211
  76.7 1.7 %collective-permute-start.16 = (bf16[4,288,128]{2,1,0:T(8,128)(2,1)S(1)}, bf16[4,288,128]{2,1,0:T(8,128)(2,1)S(1)}, u32[]{:S(2)}, u32[]{:S(2)}) collective-permute-start(bf16[4,288,128]{2,1,0:T(8,128)(2,1)S(1)} %bitcast.71), channel_id=1, source_target_pairs={{0,3},{1,0},{2,1},{3,2},{4,7},{5,4},{6,5},{7,6},{8,11},{9,8},{10,9... | collective-permute-start | bytes 884744 | tf_op jit(solution)/shard_map/ppermute | solution.py:212
  78.5 2.5 %collective-permute-start.17 = (f32[1,128]{1,0:T(1,128)S(1)}, f32[1,128]{1,0:T(1,128)S(1)}, u32[]{:S(2)}, u32[]{:S(2)}) collective-permute-start(f32[1,128]{1,0:T(1,128)S(1)} %fusion.18), channel_id=1, source_target_pairs={{0,4},{4,0},{8,12},{12,8},{1,5},{5,1},{9,13},{13,9},{2,6},{6,2},{1... | collective-permute-start | bytes 1544 | tf_op jit(solution)/shard_map/ppermute | solution.py:233
  81.0 1.5 %collective-permute-done.17 = f32[1,128]{1,0:T(1,128)S(1)} collective-permute-done((f32[1,128]{1,0:T(1,128)S(1)}, f32[1,128]{1,0:T(1,128)S(1)}, u32[]{:S(2)}, u32[]{:S(2)}) %collective-permute-start.17) | collective-permute-done | bytes 544 | tf_op jit(solution)/shard_map/ppermute | solution.py:233
  82.5 4.3 %collective-permute-start.18 = (f32[1,128]{1,0:T(1,128)S(1)}, f32[1,128]{1,0:T(1,128)S(1)}, u32[]{:S(2)}, u32[]{:S(2)}) collective-permute-start(f32[1,128]{1,0:T(1,128)S(1)} %add.182), channel_id=1, source_target_pairs={{0,12},{4,8},{8,4},{12,0},{1,13},{5,9},{9,5},{13,1},{2,14},{6,10},... | collective-permute-start | bytes 1544 | tf_op jit(solution)/shard_map/ppermute | solution.py:234
  86.8 1.5 %collective-permute-done.18 = f32[1,128]{1,0:T(1,128)S(1)} collective-permute-done((f32[1,128]{1,0:T(1,128)S(1)}, f32[1,128]{1,0:T(1,128)S(1)}, u32[]{:S(2)}, u32[]{:S(2)}) %collective-permute-start.18) | collective-permute-done | bytes 544 | tf_op jit(solution)/shard_map/ppermute | solution.py:234
  88.3 0.4 collective-permute-start.19
  88.6 3.2 %collective-permute-done.19 = f32[1,128]{1,0:T(1,128)S(1)} collective-permute-done((f32[1,128]{1,0:T(1,128)S(1)}, f32[1,128]{1,0:T(1,128)S(1)}, u32[]{:S(2)}, u32[]{:S(2)}) %collective-permute-start.19) | collective-permute-done | bytes 544 | tf_op jit(solution)/shard_map/ppermute | solution.py:233
  91.8 1.7 %collective-permute-start.20 = (f32[1,128]{1,0:T(1,128)S(1)}, f32[1,128]{1,0:T(1,128)S(1)}, u32[]{:S(2)}, u32[]{:S(2)}) collective-permute-start(f32[1,128]{1,0:T(1,128)S(1)} %add.184), channel_id=1, source_target_pairs={{0,3},{1,2},{2,1},{3,0},{4,7},{5,6},{6,5},{7,4},{8,11},{9,10},{10,... | collective-permute-start | bytes 1544 | tf_op jit(solution)/shard_map/ppermute | solution.py:234
  93.6 3.0 %collective-permute-done.20 = f32[1,128]{1,0:T(1,128)S(1)} collective-permute-done((f32[1,128]{1,0:T(1,128)S(1)}, f32[1,128]{1,0:T(1,128)S(1)}, u32[]{:S(2)}, u32[]{:S(2)}) %collective-permute-start.20) | collective-permute-done | bytes 544 | tf_op jit(solution)/shard_map/ppermute | solution.py:234
  96.6 0.6 add_reduce_fusion
  97.9 1.6 %copy-done.3 = bf16[4,64,32,128]{3,2,1,0:T(8,128)(2,1)S(1)} copy-done((bf16[4,64,32,128]{3,2,1,0:T(8,128)(2,1)S(1)}, bf16[4,64,32,128]{3,2,1,0:T(8,128)(2,1)}, u32[]{:S(2)}) %copy-start.3) | copy-done | bytes 2097176
  99.4 1.1 %copy-done.8 = bf16[512,640]{1,0:T(8,128)(2,1)S(1)} copy-done((bf16[512,640]{1,0:T(8,128)(2,1)S(1)}, bf16[512,640]{1,0:T(8,128)(2,1)}, u32[]{:S(2)}) %copy-start.8) | copy-done | bytes 655384
  100.5 5.4 %backward.1 = f32[4,2048,128]{2,1,0:T(8,128)} custom-call(bf16[4,2048,128]{2,1,0:T(8,128)(2,1)S(1)} %level.1.own, bf16[4,128,128]{2,1,0:T(8,128)(2,1)S(1)} %bitcast.64, bf16[4,128,128]{2,1,0:T(8,128)(2,1)S(1)} %bitcast.63, bf16[4,288,128]{2,1,0:T(8,128)(2,1)S(1)} %collective-permute-done.15.west, bf16[4,288,128]{2,1,0:T(8,128)(2,1)S(1)} %collective-permute-done.16.east, ...), custom_call_target="tpu_custom_call" | custom-call | flops 3500000000 | bytes 9000000 | tf_op jit(solution)/shard_map/backward/pallas_call | solution.py:189
  (66 shorter events, 2.5 us)
Async XLA Ops:
  0.6 13.5 %copy-start.6 = (f32[9]{0:T(128)S(1)}, f32[9]{0:T(128)}, u32[]{:S(2)}) copy-start(f32[9]{0:T(128)} %lon_taps.1) | copy-start | bytes 112
  0.6 13.5 %copy-start.5 = (f32[9]{0:T(128)S(1)}, f32[9]{0:T(128)}, u32[]{:S(2)}) copy-start(f32[9]{0:T(128)} %lat_taps.1) | copy-start | bytes 112
  0.7 19.2 %copy-start.4 = (bf16[128,128]{1,0:T(8,128)(2,1)S(1)}, bf16[128,128]{1,0:T(8,128)(2,1)}, u32[]{:S(2)}) copy-start(bf16[128,128]{1,0:T(8,128)(2,1)} %vertical.3) | copy-start | bytes 98308
  0.7 19.2 %copy-start = (bf16[4,64,32,128]{3,2,1,0:T(8,128)(2,1)S(1)}, bf16[4,64,32,128]{3,2,1,0:T(8,128)(2,1)}, u32[]{:S(2)}) copy-start(bf16[4,64,32,128]{3,2,1,0:T(8,128)(2,1)} %param.7) | copy-start | bytes 6291460
  1.8 7.3 %collective-permute-start.1 = (bf16[4,4,32,128]{3,2,1,0:T(8,128)(2,1)S(1)}, bf16[4,4,32,128]{3,2,1,0:T(8,128)(2,1)S(1)}, u32[]{:S(2)}, u32[]{:S(2)}) collective-permute-start(bf16[4,4,32,128]{3,2,1,0:T(8,128)(2,1)S(1)} %get-tuple-element.24), channel_id=1, source_target_pairs={{4,0},{8,4},{12,8},{5,1},{9,5},{13,9},{6,2},{10,6},{14,10},{7,3},{... | collective-permute-start | bytes 393224 | tf_op jit(solution)/shard_map/ppermute | solution.py:203
  3.1 7.2 %collective-permute-start = (bf16[4,4,32,128]{3,2,1,0:T(8,128)(2,1)S(1)}, bf16[4,4,32,128]{3,2,1,0:T(8,128)(2,1)S(1)}, u32[]{:S(2)}, u32[]{:S(2)}) collective-permute-start(bf16[4,4,32,128]{3,2,1,0:T(8,128)(2,1)S(1)} %get-tuple-element.25), channel_id=1, source_target_pairs={{0,4},{4,8},{8,12},{1,5},{5,9},{9,13},{2,6},{6,10},{10,14},{3,7},{... | collective-permute-start | bytes 393224 | tf_op jit(solution)/shard_map/ppermute | solution.py:202
  10.6 9.0 %collective-permute-start.2 = (bf16[4,288,128]{2,1,0:T(8,128)(2,1)S(1)}, bf16[4,288,128]{2,1,0:T(8,128)(2,1)S(1)}, u32[]{:S(2)}, u32[]{:S(2)}) collective-permute-start(bf16[4,288,128]{2,1,0:T(8,128)(2,1)S(1)} %bitcast.72), channel_id=1, source_target_pairs={{0,1},{1,2},{2,3},{3,0},{4,5},{5,6},{6,7},{7,4},{8,9},{9,10},{10,1... | collective-permute-start | bytes 884744 | tf_op jit(solution)/shard_map/ppermute | solution.py:211
  12.4 7.5 %collective-permute-start.3 = (bf16[4,288,128]{2,1,0:T(8,128)(2,1)S(1)}, bf16[4,288,128]{2,1,0:T(8,128)(2,1)S(1)}, u32[]{:S(2)}, u32[]{:S(2)}) collective-permute-start(bf16[4,288,128]{2,1,0:T(8,128)(2,1)S(1)} %bitcast.73), channel_id=1, source_target_pairs={{0,3},{1,0},{2,1},{3,2},{4,7},{5,4},{6,5},{7,6},{8,11},{9,8},{10,9... | collective-permute-start | bytes 884744 | tf_op jit(solution)/shard_map/ppermute | solution.py:212
  15.1 0.8 copy-start.7
  19.9 1.6 %copy-start.2 = (bf16[4,64,32,128]{3,2,1,0:T(8,128)(2,1)S(1)}, bf16[4,64,32,128]{3,2,1,0:T(8,128)(2,1)}, u32[]{:S(2)}) copy-start(bf16[4,64,32,128]{3,2,1,0:T(8,128)(2,1)} %param.6) | copy-start | bytes 6291460
  31.6 1.6 %collective-permute-start.4 = (bf16[1024,128]{1,0:T(8,128)(2,1)S(1)}, bf16[1024,128]{1,0:T(8,128)(2,1)S(1)}, u32[]{:S(2)}, u32[]{:S(2)}) collective-permute-start(bf16[1024,128]{1,0:T(8,128)(2,1)S(1)} %get-tuple-element.9), channel_id=1, source_target_pairs={{0,16},{16,0},{1,17},{17,1},{2,18},{18,2},{3,19},{19,3},{4,20},{20... | collective-permute-start | bytes 786440 | tf_op jit(solution)/shard_map/ppermute | solution.py:250
  33.4 4.8 %collective-permute-start.5 = (bf16[256,128]{1,0:T(8,128)(2,1)S(1)}, bf16[256,128]{1,0:T(8,128)(2,1)S(1)}, u32[]{:S(2)}, u32[]{:S(2)}) collective-permute-start(bf16[256,128]{1,0:T(8,128)(2,1)S(1)} %get-tuple-element.28), channel_id=1, source_target_pairs={{0,32},{32,64},{64,96},{96,0},{1,33},{33,65},{65,97},{97,1},{2,34}... | collective-permute-start | bytes 196616 | tf_op jit(solution)/shard_map/ppermute | solution.py:256
  34.9 6.1 %collective-permute-start.7 = (bf16[256,128]{1,0:T(8,128)(2,1)S(1)}, bf16[256,128]{1,0:T(8,128)(2,1)S(1)}, u32[]{:S(2)}, u32[]{:S(2)}) collective-permute-start(bf16[256,128]{1,0:T(8,128)(2,1)S(1)} %get-tuple-element.29), channel_id=1, source_target_pairs={{0,64},{32,96},{64,0},{96,32},{1,65},{33,97},{65,1},{97,33},{2,66}... | collective-permute-start | bytes 196616 | tf_op jit(solution)/shard_map/ppermute | solution.py:256
  36.3 5.0 %collective-permute-start.6 = (bf16[256,128]{1,0:T(8,128)(2,1)S(1)}, bf16[256,128]{1,0:T(8,128)(2,1)S(1)}, u32[]{:S(2)}, u32[]{:S(2)}) collective-permute-start(bf16[256,128]{1,0:T(8,128)(2,1)S(1)} %get-tuple-element.30), channel_id=1, source_target_pairs={{0,96},{32,0},{64,32},{96,64},{1,97},{33,1},{65,33},{97,65},{2,98}... | collective-permute-start | bytes 196616 | tf_op jit(solution)/shard_map/ppermute | solution.py:256
  41.5 9.4 %collective-permute-start.8 = (bf16[272,128]{1,0:T(8,128)(2,1)S(1)}, bf16[272,128]{1,0:T(8,128)(2,1)S(1)}, u32[]{:S(2)}, u32[]{:S(2)}) collective-permute-start(bf16[272,128]{1,0:T(8,128)(2,1)S(1)} %concatenate.38), channel_id=1, source_target_pairs={{0,128},{128,0},{1,129},{129,1},{2,130},{130,2},{3,131},{131,3},{4... | collective-permute-start | bytes 208904 | tf_op jit(solution)/shard_map/ppermute | solution.py:260
  53.0 8.1 %collective-permute-start.11 = (bf16[272,128]{1,0:T(8,128)(2,1)S(1)}, bf16[272,128]{1,0:T(8,128)(2,1)S(1)}, u32[]{:S(2)}, u32[]{:S(2)}) collective-permute-start(bf16[272,128]{1,0:T(8,128)(2,1)S(1)} %concatenate.40), channel_id=1, source_target_pairs={{0,32},{32,64},{64,96},{96,0},{1,33},{33,65},{65,97},{97,1},{2,34}... | collective-permute-start | bytes 208904 | tf_op jit(solution)/shard_map/ppermute | solution.py:269
  54.5 6.6 %collective-permute-start.10 = (bf16[272,128]{1,0:T(8,128)(2,1)S(1)}, bf16[272,128]{1,0:T(8,128)(2,1)S(1)}, u32[]{:S(2)}, u32[]{:S(2)}) collective-permute-start(bf16[272,128]{1,0:T(8,128)(2,1)S(1)} %concatenate.40), channel_id=1, source_target_pairs={{0,64},{32,96},{64,0},{96,32},{1,65},{33,97},{65,1},{97,33},{2,66}... | collective-permute-start | bytes 208904 | tf_op jit(solution)/shard_map/ppermute | solution.py:269
  56.8 4.3 %collective-permute-start.9 = (bf16[272,128]{1,0:T(8,128)(2,1)S(1)}, bf16[272,128]{1,0:T(8,128)(2,1)S(1)}, u32[]{:S(2)}, u32[]{:S(2)}) collective-permute-start(bf16[272,128]{1,0:T(8,128)(2,1)S(1)} %concatenate.40), channel_id=1, source_target_pairs={{0,96},{32,0},{64,32},{96,64},{1,97},{33,1},{65,33},{97,65},{2,98}... | collective-permute-start | bytes 208904 | tf_op jit(solution)/shard_map/ppermute | solution.py:269
  61.6 1.6 %collective-permute-start.12 = (bf16[1040,128]{1,0:T(8,128)(2,1)S(1)}, bf16[1040,128]{1,0:T(8,128)(2,1)S(1)}, u32[]{:S(2)}, u32[]{:S(2)}) collective-permute-start(bf16[1040,128]{1,0:T(8,128)(2,1)S(1)} %concatenate.42), channel_id=1, source_target_pairs={{0,16},{16,0},{1,17},{17,1},{2,18},{18,2},{3,19},{19,3},{4,20},{20... | collective-permute-start | bytes 798728 | tf_op jit(solution)/shard_map/ppermute | solution.py:274
  63.4 1.6 %copy-start.1 = (bf16[4,64,32,128]{3,2,1,0:T(8,128)(2,1)S(1)}, bf16[4,64,32,128]{3,2,1,0:T(8,128)(2,1)}, u32[]{:S(2)}) copy-start(bf16[4,64,32,128]{3,2,1,0:T(8,128)(2,1)} %param.7) | copy-start | bytes 6291460
  65.9 7.5 %collective-permute-start.14 = (bf16[4,4,32,128]{3,2,1,0:T(8,128)(2,1)S(1)}, bf16[4,4,32,128]{3,2,1,0:T(8,128)(2,1)S(1)}, u32[]{:S(2)}, u32[]{:S(2)}) collective-permute-start(bf16[4,4,32,128]{3,2,1,0:T(8,128)(2,1)S(1)} %get-tuple-element.20), channel_id=1, source_target_pairs={{4,0},{8,4},{12,8},{5,1},{9,5},{13,9},{6,2},{10,6},{14,10},{7,3},{... | collective-permute-start | bytes 393224 | tf_op jit(solution)/shard_map/ppermute | solution.py:203
  67.2 7.4 %collective-permute-start.13 = (bf16[4,4,32,128]{3,2,1,0:T(8,128)(2,1)S(1)}, bf16[4,4,32,128]{3,2,1,0:T(8,128)(2,1)S(1)}, u32[]{:S(2)}, u32[]{:S(2)}) collective-permute-start(bf16[4,4,32,128]{3,2,1,0:T(8,128)(2,1)S(1)} %get-tuple-element.21), channel_id=1, source_target_pairs={{0,4},{4,8},{8,12},{1,5},{5,9},{9,13},{2,6},{6,10},{10,14},{3,7},{... | collective-permute-start | bytes 393224 | tf_op jit(solution)/shard_map/ppermute | solution.py:202
  74.9 22.9 %collective-permute-start.15 = (bf16[4,288,128]{2,1,0:T(8,128)(2,1)S(1)}, bf16[4,288,128]{2,1,0:T(8,128)(2,1)S(1)}, u32[]{:S(2)}, u32[]{:S(2)}) collective-permute-start(bf16[4,288,128]{2,1,0:T(8,128)(2,1)S(1)} %bitcast.70), channel_id=1, source_target_pairs={{0,1},{1,2},{2,3},{3,0},{4,5},{5,6},{6,7},{7,4},{8,9},{9,10},{10,1... | collective-permute-start | bytes 884744 | tf_op jit(solution)/shard_map/ppermute | solution.py:211
  76.7 21.1 %collective-permute-start.16 = (bf16[4,288,128]{2,1,0:T(8,128)(2,1)S(1)}, bf16[4,288,128]{2,1,0:T(8,128)(2,1)S(1)}, u32[]{:S(2)}, u32[]{:S(2)}) collective-permute-start(bf16[4,288,128]{2,1,0:T(8,128)(2,1)S(1)} %bitcast.71), channel_id=1, source_target_pairs={{0,3},{1,0},{2,1},{3,2},{4,7},{5,4},{6,5},{7,6},{8,11},{9,8},{10,9... | collective-permute-start | bytes 884744 | tf_op jit(solution)/shard_map/ppermute | solution.py:212
  78.5 4.0 %collective-permute-start.17 = (f32[1,128]{1,0:T(1,128)S(1)}, f32[1,128]{1,0:T(1,128)S(1)}, u32[]{:S(2)}, u32[]{:S(2)}) collective-permute-start(f32[1,128]{1,0:T(1,128)S(1)} %fusion.18), channel_id=1, source_target_pairs={{0,4},{4,0},{8,12},{12,8},{1,5},{5,1},{9,13},{13,9},{2,6},{6,2},{1... | collective-permute-start | bytes 1544 | tf_op jit(solution)/shard_map/ppermute | solution.py:233
  82.5 5.8 %collective-permute-start.18 = (f32[1,128]{1,0:T(1,128)S(1)}, f32[1,128]{1,0:T(1,128)S(1)}, u32[]{:S(2)}, u32[]{:S(2)}) collective-permute-start(f32[1,128]{1,0:T(1,128)S(1)} %add.182), channel_id=1, source_target_pairs={{0,12},{4,8},{8,4},{12,0},{1,13},{5,9},{9,5},{13,1},{2,14},{6,10},... | collective-permute-start | bytes 1544 | tf_op jit(solution)/shard_map/ppermute | solution.py:234
  88.3 3.5 %collective-permute-start.19 = (f32[1,128]{1,0:T(1,128)S(1)}, f32[1,128]{1,0:T(1,128)S(1)}, u32[]{:S(2)}, u32[]{:S(2)}) collective-permute-start(f32[1,128]{1,0:T(1,128)S(1)} %add.183), channel_id=1, source_target_pairs={{0,1},{1,0},{2,3},{3,2},{4,5},{5,4},{6,7},{7,6},{8,9},{9,8},{10,11... | collective-permute-start | bytes 1544 | tf_op jit(solution)/shard_map/ppermute | solution.py:233
  91.8 4.8 %collective-permute-start.20 = (f32[1,128]{1,0:T(1,128)S(1)}, f32[1,128]{1,0:T(1,128)S(1)}, u32[]{:S(2)}, u32[]{:S(2)}) collective-permute-start(f32[1,128]{1,0:T(1,128)S(1)} %add.184), channel_id=1, source_target_pairs={{0,3},{1,2},{2,1},{3,0},{4,7},{5,6},{6,5},{7,4},{8,11},{9,10},{10,... | collective-permute-start | bytes 1544 | tf_op jit(solution)/shard_map/ppermute | solution.py:234
  97.8 1.6 %copy-start.3 = (bf16[4,64,32,128]{3,2,1,0:T(8,128)(2,1)S(1)}, bf16[4,64,32,128]{3,2,1,0:T(8,128)(2,1)}, u32[]{:S(2)}) copy-start(bf16[4,64,32,128]{3,2,1,0:T(8,128)(2,1)} %param.6) | copy-start | bytes 6291460
  99.4 1.1 %copy-start.8 = (bf16[512,640]{1,0:T(8,128)(2,1)S(1)}, bf16[512,640]{1,0:T(8,128)(2,1)}, u32[]{:S(2)}) copy-start(bf16[512,640]{1,0:T(8,128)(2,1)} %copy-done.7) | copy-start | bytes 1966084

commit v2 on v0

v2 whole, which is shorter than its diff:
```python
import functools

import jax
import jax.numpy as jnp
from jax import lax
from jax.experimental import pallas as pl
from jax.experimental.pallas import tpu as pltpu
from jax.sharding import Mesh
from jax.sharding import PartitionSpec as P

MEM = ("zh", "x", "core")
BF = jnp.bfloat16
F32 = jnp.float32
HALO = 4
TAPS = 9
ROWS = 8
VMEM = pl.BlockSpec(memory_space=pltpu.VMEM)
SMEM = pl.BlockSpec(memory_space=pltpu.SMEM)
HBM = pl.BlockSpec(memory_space=pltpu.HBM)
EXTRA = 16


def swap(axis, bits):
    return [(i, i ^ bits) for i in range(lax.axis_size(axis))]


def params(mib=12):
    return pltpu.CompilerParams(vmem_limit_bytes=mib * 2**20)


def cost(flops, size):
    return pl.CostEstimate(flops=flops, bytes_accessed=size, transcendentals=0)


def is_odd(axis):
    return lax.rem(lax.axis_index(axis), 2) == 1


def taps_at(index, taps, flip):
    value = jnp.zeros(index.shape, F32)
    for t in range(TAPS):
        value = jnp.where(index == t, taps[TAPS - 1 - t if flip else t], value)
    return value


def put_halves(out, row, value):
    high = value.astype(BF)
    size = value.shape[0]
    out[row : row + size, :] = high
    out[row + out.shape[0] // 2 : row + out.shape[0] // 2 + size, :] = (value - high.astype(F32)).astype(BF)


def band_kernel(cols, lat_taps, lon_taps, centre, centre_back, side, side_back):
    k = lax.broadcasted_iota(jnp.int32, (cols, centre.shape[1]), 1)
    j = lax.broadcasted_iota(jnp.int32, (cols, centre.shape[1]), 0)
    row, shift = k // cols, k % cols - j + HALO
    k2 = lax.broadcasted_iota(jnp.int32, (16, side.shape[1]), 1)
    j2 = lax.broadcasted_iota(jnp.int32, (16, side.shape[1]), 0)
    half = side.shape[1] // 2
    in_west = k2 < half
    row2 = jnp.where(in_west, k2, k2 - half) // HALO
    column = k2 % HALO
    target = jnp.where(j2 < 8, j2, j2 + cols - 16)
    shift2 = jnp.where(in_west, column, column + cols + HALO) - target
    for flip, wide, narrow in ((False, centre, side), (True, centre_back, side_back)):
        across = taps_at(shift, lon_taps, flip)
        across2 = taps_at(shift2, lon_taps, flip)
        for i in range(ROWS):
            put_halves(wide, i * cols, taps_at(row - i, lat_taps, flip) * across)
            put_halves(narrow, i * 16, taps_at(row2 - i, lat_taps, flip) * across2)


def bands(lat_taps, lon_taps, cols):
    span = ROWS + 2 * HALO
    wide = jax.ShapeDtypeStruct((2 * ROWS * cols, span * cols), BF)
    narrow = jax.ShapeDtypeStruct((2 * ROWS * 16, 2 * span * HALO), BF)
    return pl.pallas_call(
        functools.partial(band_kernel, cols),
        out_shape=(wide, wide, narrow, narrow),
        in_specs=[SMEM, SMEM],
        out_specs=(VMEM,) * 4,
        compiler_params=params(),
        cost_estimate=cost(2_000_000, 1_200_000),
        name="bands",
    )(lat_taps, lon_taps)


def south_north(first, second, rows):
    odd = is_odd("lat")
    at = lax.axis_index("lat")
    zero = jnp.zeros((rows.stop - rows.start, first.shape[1]), BF)
    one, two = first[rows, :], second[rows, :]
    south = jnp.where(at == 0, zero, jnp.where(odd, one, two))
    north = jnp.where(at == lax.axis_size("lat") - 1, zero, jnp.where(odd, two, one))
    return south, north


def centre_kernel(cols, with_square, own, first, second, band, out, *square):
    members, cells, levels = own.shape
    size, edge = ROWS * cols, HALO * cols
    total = jnp.zeros((8, levels), F32)
    for start in range(0, members, 2):
        pair = (start, start + 1)
        edges = [south_north(first, second, slice(m * edge, (m + 1) * edge)) for m in pair]
        for row in range(0, cells, size):
            lo, hi = max(row - edge, 0), min(row + size + edge, cells)
            parts = []
            for m, (south, north) in zip(pair, edges):
                part = [south] if row == 0 else []
                part.append(own[m, lo:hi, :])
                if row + size == cells:
                    part.append(north)
                parts.append(jnp.concatenate(part, axis=0) if len(part) > 1 else part[0])
                if with_square:
                    c = own[m, row : row + size, :].astype(F32)
                    total = total + jnp.sum((c * c).reshape(size // 8, 8, levels), axis=0)
            both = jnp.dot(band[...], jnp.concatenate(parts, axis=1), preferred_element_type=F32)
            both = both[:size] + both[size:]
            for n, m in enumerate(pair):
                out[m, row : row + size, :] = both[:, n * levels : (n + 1) * levels]
    if with_square:
        square[0][...] = total


def centre(own, first, second, band, cols, with_square):
    members, cells, levels = own.shape
    shapes = [jax.ShapeDtypeStruct(own.shape, F32)]
    if with_square:
        shapes.append(jax.ShapeDtypeStruct((8, levels), F32))
    return pl.pallas_call(
        functools.partial(centre_kernel, cols, with_square),
        out_shape=shapes,
        in_specs=[VMEM] * 4,
        out_specs=[VMEM] * len(shapes),
        compiler_params=params(),
        cost_estimate=cost(3_000_000_000, 7_000_000),
        name="centre_forward" if with_square else "centre_back",
    )(own, first, second, band)


def side_rows(cells, cols):
    return (cells // cols + 2 * HALO) * HALO


def sides(band, first, second, pair, row, cols, stride):
    odd = is_odd("lon")
    count = (ROWS + 2 * HALO) * HALO
    parts = []
    for m in pair:
        at = slice(m * stride + row // cols * HALO, m * stride + row // cols * HALO + count)
        one, two = first[at, :], second[at, :]
        parts.append(jnp.concatenate([jnp.where(odd, one, two), jnp.where(odd, two, one)], axis=0))
    both = jnp.dot(band[...], jnp.concatenate(parts, axis=1), preferred_element_type=F32)
    size = both.shape[0] // 2
    both = both[:size] + both[size:]
    levels = both.shape[1] // len(pair)
    return [both[:, n * levels : (n + 1) * levels] for n in range(len(pair))]


def with_sides(value, side, cols):
    levels = value.shape[1]
    value = value.reshape(ROWS, cols, levels)
    side = side.reshape(ROWS, 16, levels)
    return jnp.concatenate(
        [value[:, :8] + side[:, :8], value[:, 8 : cols - 8], value[:, cols - 8 :] + side[:, 8:]], axis=1
    ).reshape(ROWS * cols, levels)


def forward_kernel(cols, inner, first, second, band, vertical, ensemble, keep, send):
    members, cells, levels = inner.shape
    size = ROWS * cols
    blocks = cells // size
    core = lax.axis_index("core")
    for block in range(blocks):
        row = block * size
        rows = slice(row, row + size)
        increment = jnp.zeros((size, levels), F32)
        for start in range(0, members, 2):
            pair = (start, start + 1)
            for m, side in zip(pair, sides(band, first, second, pair, row, cols, side_rows(cells, cols))):
                smoothed = with_sides(inner[m, rows, :], side, cols).astype(BF)
                leveled = jnp.dot(smoothed, vertical[...], preferred_element_type=F32)
                increment = increment + ensemble[m, rows, :].astype(F32) * leveled
        half, at = block // (blocks // 2), block % (blocks // 2)
        place = slice(at * size, (at + 1) * size)
        increment = increment.astype(BF)

        @pl.when(core == half)
        def _():
            keep[place, :] = increment

        @pl.when(core != half)
        def _():
            send[place, :] = increment


def forward(inner, first, second, band, vertical, ensemble, cols):
    members, cells, levels = inner.shape
    half = jax.ShapeDtypeStruct((cells // 2, levels), BF)
    return pl.pallas_call(
        functools.partial(forward_kernel, cols),
        out_shape=(half, half),
        in_specs=[VMEM] * 6,
        out_specs=(VMEM,) * 2,
        compiler_params=params(),
        cost_estimate=cost(1_500_000_000, 7_000_000),
        name="forward",
    )(inner, first, second, band, vertical, ensemble)


def put_sums(message, sums):
    row = lax.broadcasted_iota(jnp.int32, (EXTRA, sums.shape[1]), 0)
    parts = jnp.zeros(row.shape, F32)
    for n in range(3):
        part = sums.astype(BF).astype(F32)
        parts = jnp.where(row == n, part, parts)
        sums = sums - part
    message[message.shape[0] - EXTRA :, :] = parts.astype(BF)


def get_sums(message):
    return jnp.sum(message[message.shape[0] - EXTRA :, :].astype(F32), axis=0, keepdims=True)


def share_of(bits):
    return lax.axis_index("x") ^ bits


def call(kernel, name, shapes, inputs, in_specs=None, scratch=(), flops=1_000_000, size=1_000_000, out_specs=None, mib=12):
    return pl.pallas_call(
        kernel,
        out_shape=tuple(shapes),
        in_specs=in_specs or [VMEM] * len(inputs),
        out_specs=out_specs or (VMEM,) * len(shapes),
        scratch_shapes=scratch,
        compiler_params=params(mib),
        cost_estimate=cost(flops, size),
        name=name,
    )(*inputs)


def edges_kernel(edge, share, control, precision, first, second, mine, done):
    members, cells, _ = control.shape
    start = jnp.where(is_odd("lat"), 0, (cells - edge) // 128) * 128
    copies = []
    for out, at in ((first, start), (second, cells - edge - start)):
        at = pl.multiple_of(at, 128)
        for m in range(members):
            copies.append((control.at[m, pl.ds(at, edge), :], out.at[pl.ds(m * edge, edge), :]))
    at = pl.multiple_of((lax.axis_index("core") * 4 + lax.axis_index("x")) * share, share)
    copies.append((precision.at[pl.ds(at, share), :], mine))
    copies = [pltpu.make_async_copy(*pair, done.at[n]) for n, pair in enumerate(copies)]
    for copy in copies:
        copy.start()
    for copy in copies:
        copy.wait()


def edges(control, precision, edge):
    members, cells, levels = control.shape
    message = jax.ShapeDtypeStruct((members * edge, levels), BF)
    share = cells // 8
    return call(
        functools.partial(edges_kernel, edge, share),
        "edges",
        (message, message, jax.ShapeDtypeStruct((share, levels), F32)),
        (control, precision),
        in_specs=[HBM, HBM],
        scratch=(pltpu.SemaphoreType.DMA((2 * members + 1,)),),
        mib=56,
    )


def picker(lat_rows, cols):
    count = lat_rows * HALO
    row = lax.broadcasted_iota(jnp.int32, (2 * count, lat_rows * cols), 0)
    cell = lax.broadcasted_iota(jnp.int32, (2 * count, lat_rows * cols), 1)
    low = row < count
    at = jnp.where(low, row, row - count)
    wanted = at // HALO * cols + at % HALO + jnp.where(low, 0, cols - HALO)
    return jnp.where(cell == wanted, 1.0, 0.0).astype(BF)


def lon_kernel(cols, tile, first, second, *refs):
    members, cells, levels = tile.shape
    if len(refs) > 2:
        sums, far, west_out, east_out, total = refs
        value = (sums[0:1, :] + get_sums(first)) + (far[0:1, :] + get_sums(second))
        total[...] = jnp.broadcast_to(value, total.shape)
        put_sums(west_out, value)
        put_sums(east_out, value)
    else:
        west_out, east_out = refs
    odd = is_odd("lon")
    edge, block = HALO * cols, 16
    stride = side_rows(cells, cols)
    narrow, wide = picker(HALO, cols), picker(block, cols)

    def put(pick, parts, pair, at):
        got = jnp.dot(pick, jnp.concatenate(parts, axis=1), preferred_element_type=F32).astype(BF)
        half = got.shape[0] // 2
        low, high = got[:half], got[half:]
        one, two = jnp.where(odd, low, high), jnp.where(odd, high, low)
        for n, m in enumerate(pair):
            lanes = slice(n * levels, (n + 1) * levels)
            place = slice(m * stride + at, m * stride + at + half)
            west_out[place, :] = one[:, lanes]
            east_out[place, :] = two[:, lanes]

    for start in range(0, members, 2):
        pair = (start, start + 1)
        ends = [south_north(first, second, slice(m * edge, (m + 1) * edge)) for m in pair]
        put(narrow, [south for south, _ in ends], pair, 0)
        for row in range(0, cells, block * cols):
            put(wide, [tile[m, row : row + block * cols, :] for m in pair], pair, row // cols * HALO + HALO * HALO)
        put(narrow, [north for _, north in ends], pair, stride - HALO * HALO)


def lon_messages(tile, first, second, cols, *sums):
    members, cells, levels = tile.shape
    extra = EXTRA if sums else 0
    message = jax.ShapeDtypeStruct((members * side_rows(cells, cols) + extra, levels), BF)
    shapes = [message, message] + [jax.ShapeDtypeStruct(v.shape, F32) for v in sums[:1]]
    return call(
        functools.partial(lon_kernel, cols),
        "lon_messages",
        shapes,
        (tile, first, second, *sums),
        flops=200_000_000,
        size=3_000_000,
    )


def shares_kernel(keep, got, *shares):
    size = shares[0].shape[0]
    for bits, out in enumerate(shares):
        rows = pl.ds(pl.multiple_of(share_of(bits) * size, size), size)
        out[...] = (keep[rows, :].astype(F32) + got[rows, :].astype(F32)).astype(BF)


def part_kernel(zero, one, two, three, square, message):
    size = zero.shape[0]
    message[:size, :] = (
        (zero[...].astype(F32) + one[...].astype(F32)) + (two[...].astype(F32) + three[...].astype(F32))
    ).astype(BF)
    put_sums(message, jnp.sum(square[...], axis=0, keepdims=True))


def weight_kernel(message, other, mine, out):
    size = mine.shape[0]
    increment = message[:size, :].astype(F32) + other[:size, :].astype(F32)
    weighted = mine[...] * increment
    out[:size, :] = weighted.astype(BF)
    put_sums(out, (get_sums(message) + get_sums(other)) + jnp.sum(weighted * increment, axis=0, keepdims=True))


def gather_kernel(zero, one, two, three, out):
    size = zero.shape[0] - EXTRA
    for n, ref in enumerate((zero, one, two, three)):
        out[n * size : (n + 1) * size, :] = ref[:size, :]
    put_sums(out, (get_sums(zero) + get_sums(one)) + (get_sums(two) + get_sums(three)))


def level_kernel(mine, other, ensemble, vertical, adjoint, first, second, sums):
    members, cells, levels = adjoint.shape
    share = cells // 8
    edge = (first.shape[0] - EXTRA) // members
    core = lax.axis_index("core")
    for which, half in ((mine, core), (other, 1 - core)):
        for k in range(4):
            rows = pl.ds(pl.multiple_of((half * 4 + share_of(k)) * share, share), share)
            w = which[k * share : (k + 1) * share, :].astype(F32)
            for m in range(members):
                part = (ensemble[m, rows, :].astype(F32) * w).astype(BF)
                adjoint[m, rows, :] = lax.dot_general(
                    part, vertical[...], (((1,), (1,)), ((), ())), preferred_element_type=F32
                ).astype(BF)
    odd = is_odd("lat")
    for m in range(members):
        low, high = adjoint[m, :edge, :], adjoint[m, cells - edge :, :]
        first[m * edge : (m + 1) * edge, :] = jnp.where(odd, low, high)
        second[m * edge : (m + 1) * edge, :] = jnp.where(odd, high, low)
    value = get_sums(mine) + get_sums(other)
    put_sums(first, value)
    put_sums(second, value)
    sums[...] = jnp.broadcast_to(value, sums.shape)


def backward_kernel(cols, entries, inner, first, second, band, control, sums, far, hessian, curvature, result, done):
    members, cells, levels = inner.shape
    size = ROWS * cols
    copies = []
    for start in range(0, members, 2):
        pair = (start, start + 1)
        for row in range(0, cells, size):
            rows = slice(row, row + size)
            for m, side in zip(pair, sides(band, first, second, pair, row, cols, side_rows(cells, cols))):
                result[m, rows, :] = control[m, rows, :].astype(F32) + with_sides(inner[m, rows, :], side, cols)
            if (row + size) % (cells // 4) == 0:
                for m in pair:
                    part = pl.ds(row + size - cells // 4, cells // 4)
                    copy = pltpu.make_async_copy(
                        result.at[m, part, :], hessian.at[m, part, :], done.at[len(copies)]
                    )
                    copy.start()
                    copies.append(copy)
    value = (sums[0:1, :] + get_sums(first)) + (far[0:1, :] + get_sums(second))
    curvature[0, 0] = jnp.sum(value) / entries
    for copy in copies:
        copy.wait()


def exchange(first, second, axis):
    return lax.ppermute(first, axis, swap(axis, 1)), lax.ppermute(second, axis, swap(axis, 3))


def per_device(control, ensemble, precision, lat_taps, lon_taps, vertical):
    members, tile_rows, cols, levels = control.shape
    cells = tile_rows * cols
    entries = control.size * lax.axis_size(MEM) * lax.axis_size("lat") * lax.axis_size("lon")
    own, spread = control.reshape(members, cells, levels), ensemble.reshape(members, cells, levels)
    share = cells // 8
    row = jax.ShapeDtypeStruct((8, levels), F32)

    def rows(count):
        return jax.ShapeDtypeStruct((count, levels), BF)

    first, second, mine = edges(own, precision.reshape(cells, levels), HALO * cols)
    one, two = exchange(first, second, "lat")
    west, east = exchange(*lon_messages(own, one, two, cols), "lon")
    band, band_back, band_side, band_side_back = bands(lat_taps, lon_taps, cols)
    inner, square = centre(own, one, two, band, cols, True)
    keep, send = forward(inner, west, east, band_side, vertical, spread, cols)

    got = lax.ppermute(send, "core", swap("core", 1))
    zero, one, two, three = call(shares_kernel, "shares", [rows(share)] * 4, (keep, got))
    two, one, three = [lax.ppermute(v, "x", swap("x", k)) for v, k in ((two, 2), (one, 1), (three, 3))]
    (message,) = call(part_kernel, "part", [rows(share + EXTRA)], (zero, one, two, three, square))
    other = lax.ppermute(message, "zh", swap("zh", 1))
    (zero,) = call(weight_kernel, "weight", [rows(share + EXTRA)], (message, other, mine))
    two, one, three = [lax.ppermute(zero, "x", swap("x", k)) for k in (2, 1, 3)]
    (message,) = call(gather_kernel, "gather", [rows(cells // 2 + EXTRA)], (zero, one, two, three))
    other = lax.ppermute(message, "core", swap("core", 1))

    edge = rows(members * HALO * cols + EXTRA)
    adjoint, first, second, sums = call(
        level_kernel,
        "level",
        [jax.ShapeDtypeStruct(own.shape, BF), edge, edge, row],
        (message, other, spread, vertical),
        flops=300_000_000,
        size=4_500_000,
    )
    one, two = exchange(first, second, "lat")
    far = lax.ppermute(sums, "lat", swap("lat", 2))
    west, east, sums = lon_messages(adjoint, one, two, cols, sums, far)
    west, east = exchange(west, east, "lon")
    far = lax.ppermute(sums, "lon", swap("lon", 2))
    inner = centre(adjoint, one, two, band_back, cols, False)[0]
    hessian, curvature = call(
        functools.partial(backward_kernel, cols, entries),
        "backward",
        [jax.ShapeDtypeStruct(own.shape, F32), jax.ShapeDtypeStruct((1, 1), F32)],
        (inner, west, east, band_side_back, own, sums, far),
        scratch=(pltpu.VMEM(own.shape, F32), pltpu.SemaphoreType.DMA((4 * members,))),
        out_specs=(pl.BlockSpec(memory_space=pl.ANY), SMEM),
        flops=1_000_000_000,
        size=9_000_000,
    )
    return hessian.reshape(control.shape), curvature.reshape(())


def solution(mesh):
    split = Mesh(
        mesh.devices.reshape(2, 4, 2, mesh.shape["lat"], mesh.shape["lon"]),
        ("zh", "x", "core", "lat", "lon"),
    )
    return jax.shard_map(
        per_device,
        mesh=split,
        in_specs=(
            P(MEM, "lat", "lon", None),
            P(MEM, "lat", "lon", None),
            P("lat", "lon", None),
            P(),
            P(),
            P(),
        ),
        out_specs=(P(MEM, "lat", "lon", None), P()),
        check_vma=False,
    )
```

time: 242 us -> 82.1 us (0.34)
  blocking collectives: 77.9 us -> 0 us
  other arithmetic: 56.4 us -> 0 us
  matrix products: 24.3 us -> 0 us
  Pallas kernels: 0 us -> 16.1 us
  starting transfers between devices: 36.1 us -> 30.7 us
  local copies, waits for them, and re-layouts: 4.95 us -> 0.03 us
  waiting for transfers between devices: 38.9 us -> 34.3 us
    psum x5 -> x0, blocking collectives: 48.4 us -> none  [by_axis(): value = lax.psum(value, axis)]
    all_to_all x1 -> x0, blocking collectives: 29.5 us -> none  [copy_for_each(): return lax.all_to_all(copies, axis, split_axis=0, concat_axis=0, tiled=True)]
    reduce_sum x2 -> x0, other arithmetic: 26.9 us -> none  [the longest x1 26.9 us: per_device(): curvature = by_axis(jnp.sum(control * hessian), MEM_LAT_LON) / entries]
    dot_general x2 -> x0, matrix products: 24.3 us -> none  [the longest x1 23.5 us: per_device(): jnp.dot(smoothed.reshape(-1, levels), vertical, preferred_element_type=jn...]
    add x2 -> x0, other arithmetic: 22.7 us -> none  [smooth_block(): across + first_taps[offset] * extended[:, offset:offset + tile_rows]]
    all_to_all x1 -> x0, waiting for transfers between devices: 18.9 us -> none  [sum_at_owner(): lax.all_to_all(in_blocks(value, dim, peers), axis, 0, 0, tiled=True)]
    pallas_call x0 -> x13, Pallas kernels: none -> 16.1 us  [the longest x9 6.94 us: call(): pl.pallas_call(kernel, out_shape=tuple(shapes), in_specs=in_specs or [VME...]
    ppermute x8 -> x19, waiting for transfers between devices: 19.9 us -> 34.3 us  [the longest x4 8.13 us: exchange(): lax.ppermute(second, axis, swap(axis, 3))]
  transfers between devices with their start and end apart: 9 -> 19, of which waited for: 6 -> 14; matrix products, arithmetic and copies ran while one was open for 1% -> 0% of each run, Pallas kernels for 0% -> 7%
where the time goes in v2:
time: 82.1 us; the launch traced here: 82 us
  waiting for transfers between devices  34.3 us (42%)
  starting transfers between devices  30.7 us (37%)
  Pallas kernels  16.1 us (20%)
  between operations  0.95 us (1%)
    ppermute x4, starting transfers between devices, exchange(): lax.ppermute(second, axis, swap(axis, 3))  10.3 us
    ppermute x4, waiting for transfers between devices, exchange(): lax.ppermute(second, axis, swap(axis, 3))  8.13 us
    pallas_call x9, Pallas kernels, call(): pl.pallas_call(kernel, out_shape=tuple(shapes), in_specs=in_specs or [VME...  6.94 us
    ppermute x1, waiting for transfers between devices, per_device(): far = lax.ppermute(sums, 'lat', swap('lat', 2))  6.39 us
    ppermute x3, starting transfers between devices, per_device(): two, one, three = [lax.ppermute(zero, 'x', swap('x', k)) for k in (2, 1, 3)]  5.42 us
    ppermute x1, starting transfers between devices, per_device(): other = lax.ppermute(message, 'zh', swap('zh', 1))  5.1 us
    pallas_call x2, Pallas kernels, centre(): pl.pallas_call(functools.partial(centre_kernel, cols, with_square), out_s...  4.69 us
    ppermute x3, waiting for transfers between devices, per_device(): two, one, three = [lax.ppermute(zero, 'x', swap('x', k)) for k in (2, 1, 3)]  4.31 us
  transfers between devices with their start and end apart: 19, of which 14 were waited for; matrix products, arithmetic and copies ran while one was open for 0% of the time, Pallas kernels for 7%

profile of v2, /device:TPU:2, one launch (start us, length us, event | category | flops | bytes accessed | tf_op | source)
XLA Modules:
  0.0 82.0 jit_solution(4509435501782020322)
XLA Ops:
  0.7 2.0 %edges.1 = (bf16[512,128]{1,0:T(8,128)(2,1)}, bf16[512,128]{1,0:T(8,128)(2,1)}, f32[256,128]{1,0:T(8,128)}) custom-call(bf16[4,2048,128]{2,1,0:T(8,128)(2,1)} %bitcast.5, f32[2048,128]{1,0:T(8,128)} %bitcast.11), custom_call_target="tpu_custom_call" | custom-call | flops 1000000 | bytes 1000000 | tf_op jit(solution)/shard_map/edges/pallas_call | solution.py:230
  2.7 2.0 %collective-permute-start = (bf16[512,128]{1,0:T(8,128)(2,1)}, bf16[512,128]{1,0:T(8,128)(2,1)S(1)}, u32[]{:S(2)}, u32[]{:S(2)}) collective-permute-start(bf16[512,128]{1,0:T(8,128)(2,1)} %get-tuple-element.28), channel_id=1, source_target_pairs={{0,4},{4,0},{8,12},{12,8},{1,5},{5,1},{9,13},{13,9},{2,6},{6,2},{1... | collective-permute-start | bytes 393224 | tf_op jit(solution)/shard_map/ppermute | solution.py:414
  4.7 2.8 %collective-permute-start.1 = (bf16[512,128]{1,0:T(8,128)(2,1)}, bf16[512,128]{1,0:T(8,128)(2,1)S(1)}, u32[]{:S(2)}, u32[]{:S(2)}) collective-permute-start(bf16[512,128]{1,0:T(8,128)(2,1)} %get-tuple-element.29), channel_id=1, source_target_pairs={{0,12},{4,8},{8,4},{12,0},{1,13},{5,9},{9,5},{13,1},{2,14},{6,10},... | collective-permute-start | bytes 393224 | tf_op jit(solution)/shard_map/ppermute | solution.py:414
  7.5 0.9 %collective-permute-done.first = bf16[512,128]{1,0:T(8,128)(2,1)S(1)} collective-permute-done((bf16[512,128]{1,0:T(8,128)(2,1)}, bf16[512,128]{1,0:T(8,128)(2,1)S(1)}, u32[]{:S(2)}, u32[]{:S(2)}) %collective-permute-start) | collective-permute-done | bytes 131104 | tf_op jit(solution)/shard_map/ppermute | solution.py:414
  8.4 5.6 %collective-permute-done.1.second = bf16[512,128]{1,0:T(8,128)(2,1)S(1)} collective-permute-done((bf16[512,128]{1,0:T(8,128)(2,1)}, bf16[512,128]{1,0:T(8,128)(2,1)S(1)}, u32[]{:S(2)}, u32[]{:S(2)}) %collective-permute-start.1) | collective-permute-done | bytes 131104 | tf_op jit(solution)/shard_map/ppermute | solution.py:414
  14.0 0.5 lon_messages.2
  14.5 1.7 %collective-permute-start.2 = (bf16[1152,128]{1,0:T(8,128)(2,1)S(1)}, bf16[1152,128]{1,0:T(8,128)(2,1)S(1)}, u32[]{:S(2)}, u32[]{:S(2)}) collective-permute-start(bf16[1152,128]{1,0:T(8,128)(2,1)S(1)} %get-tuple-element.32), channel_id=1, source_target_pairs={{0,1},{1,0},{2,3},{3,2},{4,5},{5,4},{6,7},{7,6},{8,9},{9,8},{10,11... | collective-permute-start | bytes 884744 | tf_op jit(solution)/shard_map/ppermute | solution.py:414
  16.2 2.2 %collective-permute-start.3 = (bf16[1152,128]{1,0:T(8,128)(2,1)S(1)}, bf16[1152,128]{1,0:T(8,128)(2,1)S(1)}, u32[]{:S(2)}, u32[]{:S(2)}) collective-permute-start(bf16[1152,128]{1,0:T(8,128)(2,1)S(1)} %get-tuple-element.33), channel_id=1, source_target_pairs={{0,3},{1,2},{2,1},{3,0},{4,7},{5,6},{6,5},{7,4},{8,11},{9,10},{10,... | collective-permute-start | bytes 884744 | tf_op jit(solution)/shard_map/ppermute | solution.py:414
  18.4 1.0 %bands.1 = (bf16[512,512]{1,0:T(8,128)(2,1)S(1)}, bf16[512,512]{1,0:T(8,128)(2,1)S(1)}, bf16[256,128]{1,0:T(8,128)(2,1)S(1)}, bf16[256,128]{1,0:T(8,128)(2,1)S(1)}) custom-call(f32[9]{0:T(128)S(1)} %copy-done.4, f32[9]{0:T(128)S(1)} %copy-done.5), custom_call_target="tpu_custom_call" | custom-call | flops 2000000 | bytes 1200000 | tf_op jit(solution)/shard_map/bands/pallas_call | solution.py:77
  19.4 0.0 copy-start.1
  19.4 0.0 copy-start.2
  19.4 2.3 %centre_forward.1 = (f32[4,2048,128]{2,1,0:T(8,128)S(1)}, f32[8,128]{1,0:T(8,128)S(1)}) custom-call(bf16[4,2048,128]{2,1,0:T(8,128)(2,1)S(1)} %bitcast.7, bf16[512,128]{1,0:T(8,128)(2,1)S(1)} %collective-permute-done.first, bf16[512,128]{1,0:T(8,128)(2,1)S(1)} %collective-permute-done.1.second, bf16[512,512]{1,0:T(8,128)(2,1)S(1)} %get-tuple-element.30.band), custom_call_target="tpu_custom_call" | custom-call | flops 3000000000 | bytes 7000000 | tf_op jit(solution)/shard_map/centre_forward/pallas_call | solution.py:130
  21.8 0.8 collective-permute-done.2.first
  22.6 2.5 %collective-permute-done.3.second = bf16[1152,128]{1,0:T(8,128)(2,1)S(1)} collective-permute-done((bf16[1152,128]{1,0:T(8,128)(2,1)S(1)}, bf16[1152,128]{1,0:T(8,128)(2,1)S(1)}, u32[]{:S(2)}, u32[]{:S(2)}) %collective-permute-start.3) | collective-permute-done | bytes 294944 | tf_op jit(solution)/shard_map/ppermute | solution.py:414
  25.1 3.4 %forward.1 = (bf16[1024,128]{1,0:T(8,128)(2,1)S(1)}, bf16[1024,128]{1,0:T(8,128)(2,1)S(1)}) custom-call(f32[4,2048,128]{2,1,0:T(8,128)S(1)} %get-tuple-element.31.inner, bf16[1152,128]{1,0:T(8,128)(2,1)S(1)} %collective-permute-done.2.first, bf16[1152,128]{1,0:T(8,128)(2,1)S(1)} %collective-permute-done.3.second, ...), custom_call_target="tpu_custom_call" | custom-call | flops 1500000000 | bytes 7000000 | tf_op jit(solution)/shard_map/forward/pallas_call | solution.py:200
  28.5 0.1 collective-permute-start.4
  28.6 1.5 %collective-permute-done.4.got = bf16[1024,128]{1,0:T(8,128)(2,1)S(1)} collective-permute-done((bf16[1024,128]{1,0:T(8,128)(2,1)S(1)}, bf16[1024,128]{1,0:T(8,128)(2,1)S(1)}, u32[]{:S(2)}, u32[]{:S(2)}) %collective-permute-start.4) | collective-permute-done | bytes 262176 | tf_op jit(solution)/shard_map/ppermute | solution.py:435
  30.1 0.1 shares.1
  30.2 0.6 collective-permute-start.5
  30.8 2.4 %collective-permute-start.6 = (bf16[256,128]{1,0:T(8,128)(2,1)S(1)}, bf16[256,128]{1,0:T(8,128)(2,1)S(1)}, u32[]{:S(2)}, u32[]{:S(2)}) collective-permute-start(bf16[256,128]{1,0:T(8,128)(2,1)S(1)} %get-tuple-element.39), channel_id=1, source_target_pairs={{0,64},{32,96},{64,0},{96,32},{1,65},{33,97},{65,1},{97,33},{2,66}... | collective-permute-start | bytes 196616 | tf_op jit(solution)/shard_map/ppermute | solution.py:437
  33.3 0.5 collective-permute-start.7
  33.8 0.8 collective-permute-done.5.one
  34.6 2.4 %collective-permute-done.6.two = bf16[256,128]{1,0:T(8,128)(2,1)S(1)} collective-permute-done((bf16[256,128]{1,0:T(8,128)(2,1)S(1)}, bf16[256,128]{1,0:T(8,128)(2,1)S(1)}, u32[]{:S(2)}, u32[]{:S(2)}) %collective-permute-start.6) | collective-permute-done | bytes 65568 | tf_op jit(solution)/shard_map/ppermute | solution.py:437
  37.0 0.9 %collective-permute-done.7.three = bf16[256,128]{1,0:T(8,128)(2,1)S(1)} collective-permute-done((bf16[256,128]{1,0:T(8,128)(2,1)S(1)}, bf16[256,128]{1,0:T(8,128)(2,1)S(1)}, u32[]{:S(2)}, u32[]{:S(2)}) %collective-permute-start.7) | collective-permute-done | bytes 65568 | tf_op jit(solution)/shard_map/ppermute | solution.py:437
  38.0 5.1 %collective-permute-start.8 = (bf16[272,128]{1,0:T(8,128)(2,1)S(1)}, bf16[272,128]{1,0:T(8,128)(2,1)S(1)}, u32[]{:S(2)}, u32[]{:S(2)}) collective-permute-start(bf16[272,128]{1,0:T(8,128)(2,1)S(1)} %part.1.message), channel_id=1, source_target_pairs={{0,128},{128,0},{1,129},{129,1},{2,130},{130,2},{3,131},{131,3},{4... | collective-permute-start | bytes 208904 | tf_op jit(solution)/shard_map/ppermute | solution.py:439
  43.1 3.3 %collective-permute-done.8.other = bf16[272,128]{1,0:T(8,128)(2,1)S(1)} collective-permute-done((bf16[272,128]{1,0:T(8,128)(2,1)S(1)}, bf16[272,128]{1,0:T(8,128)(2,1)S(1)}, u32[]{:S(2)}, u32[]{:S(2)}) %collective-permute-start.8) | collective-permute-done | bytes 69664 | tf_op jit(solution)/shard_map/ppermute | solution.py:439
  46.4 0.1 weight.1.zero
  46.4 1.9 %collective-permute-start.11 = (bf16[272,128]{1,0:T(8,128)(2,1)S(1)}, bf16[272,128]{1,0:T(8,128)(2,1)S(1)}, u32[]{:S(2)}, u32[]{:S(2)}) collective-permute-start(bf16[272,128]{1,0:T(8,128)(2,1)S(1)} %weight.1.zero), channel_id=1, source_target_pairs={{0,96},{32,64},{64,32},{96,0},{1,97},{33,65},{65,33},{97,1},{2,98}... | collective-permute-start | bytes 208904 | tf_op jit(solution)/shard_map/ppermute | solution.py:441
  48.3 3.6 %collective-permute-start.10 = (bf16[272,128]{1,0:T(8,128)(2,1)S(1)}, bf16[272,128]{1,0:T(8,128)(2,1)S(1)}, u32[]{:S(2)}, u32[]{:S(2)}) collective-permute-start(bf16[272,128]{1,0:T(8,128)(2,1)S(1)} %weight.1.zero), channel_id=1, source_target_pairs={{0,64},{32,96},{64,0},{96,32},{1,65},{33,97},{65,1},{97,33},{2,66}... | collective-permute-start | bytes 208904 | tf_op jit(solution)/shard_map/ppermute | solution.py:441
  51.8 0.0 collective-permute-start.9
  51.9 2.3 %collective-permute-done.10.two = bf16[272,128]{1,0:T(8,128)(2,1)S(1)} collective-permute-done((bf16[272,128]{1,0:T(8,128)(2,1)S(1)}, bf16[272,128]{1,0:T(8,128)(2,1)S(1)}, u32[]{:S(2)}, u32[]{:S(2)}) %collective-permute-start.10) | collective-permute-done | bytes 69664 | tf_op jit(solution)/shard_map/ppermute | solution.py:441
  54.1 2.0 %collective-permute-done.9.one = bf16[272,128]{1,0:T(8,128)(2,1)S(1)} collective-permute-done((bf16[272,128]{1,0:T(8,128)(2,1)S(1)}, bf16[272,128]{1,0:T(8,128)(2,1)S(1)}, u32[]{:S(2)}, u32[]{:S(2)}) %collective-permute-start.9) | collective-permute-done | bytes 69664 | tf_op jit(solution)/shard_map/ppermute | solution.py:441
  56.2 0.1 collective-permute-start.12
  56.3 1.5 %collective-permute-done.12.other = bf16[1040,128]{1,0:T(8,128)(2,1)S(1)} collective-permute-done((bf16[1040,128]{1,0:T(8,128)(2,1)S(1)}, bf16[1040,128]{1,0:T(8,128)(2,1)S(1)}, u32[]{:S(2)}, u32[]{:S(2)}) %collective-permute-start.12) | collective-permute-done | bytes 266272 | tf_op jit(solution)/shard_map/ppermute | solution.py:443
  57.8 0.8 level.1
  58.6 0.1 collective-permute-start.13
  58.7 3.0 %collective-permute-start.14 = (bf16[528,128]{1,0:T(8,128)(2,1)S(1)}, bf16[528,128]{1,0:T(8,128)(2,1)S(1)}, u32[]{:S(2)}, u32[]{:S(2)}) collective-permute-start(bf16[528,128]{1,0:T(8,128)(2,1)S(1)} %get-tuple-element.45), channel_id=1, source_target_pairs={{0,12},{4,8},{8,4},{12,0},{1,13},{5,9},{9,5},{13,1},{2,14},{6,10},... | collective-permute-start | bytes 405512 | tf_op jit(solution)/shard_map/ppermute | solution.py:414
  61.7 0.5 collective-permute-start.15
  62.2 6.4 %collective-permute-done.15.refs_1_ = f32[8,128]{1,0:T(8,128)S(1)} collective-permute-done((f32[8,128]{1,0:T(8,128)S(1)}, f32[8,128]{1,0:T(8,128)S(1)}, u32[]{:S(2)}, u32[]{:S(2)}) %collective-permute-start.15) | collective-permute-done | bytes 4128 | tf_op jit(solution)/shard_map/ppermute | solution.py:455
  68.6 0.0 collective-permute-done.13.first
  68.6 0.0 collective-permute-done.14.second
  68.6 0.5 lon_messages.3
  69.1 0.1 collective-permute-start.16
  69.2 2.3 %collective-permute-start.17 = (bf16[1168,128]{1,0:T(8,128)(2,1)S(1)}, bf16[1168,128]{1,0:T(8,128)(2,1)S(1)}, u32[]{:S(2)}, u32[]{:S(2)}) collective-permute-start(bf16[1168,128]{1,0:T(8,128)(2,1)S(1)} %get-tuple-element.49), channel_id=1, source_target_pairs={{0,3},{1,2},{2,1},{3,0},{4,7},{5,6},{6,5},{7,4},{8,11},{9,10},{10,... | collective-permute-start | bytes 897032 | tf_op jit(solution)/shard_map/ppermute | solution.py:414
  71.5 1.8 %collective-permute-start.18 = (f32[8,128]{1,0:T(8,128)S(1)}, f32[8,128]{1,0:T(8,128)S(1)}, u32[]{:S(2)}, u32[]{:S(2)}) collective-permute-start(f32[8,128]{1,0:T(8,128)S(1)} %get-tuple-element.51.sums), channel_id=1, source_target_pairs={{0,2},{1,3},{2,0},{3,1},{4,6},{5,7},{6,4},{7,5},{8,10},{9,11},{10,... | collective-permute-start | bytes 12296 | tf_op jit(solution)/shard_map/ppermute | solution.py:458
  73.3 2.4 %centre_back.1.inner = f32[4,2048,128]{2,1,0:T(8,128)S(1)} custom-call(bf16[4,2048,128]{2,1,0:T(8,128)(2,1)S(1)} %get-tuple-element.43.own.tile, bf16[528,128]{1,0:T(8,128)(2,1)S(1)} %collective-permute-done.13.first, bf16[528,128]{1,0:T(8,128)(2,1)S(1)} %collective-permute-done.14.second, bf16[512,512]{1,0:T(8,128)(2,1)S(1)} %get-tuple-element.46.band), custom_call_target="tpu_custom_call" | custom-call | flops 3000000000 | bytes 7000000 | tf_op jit(solution)/shard_map/centre_back/pallas_call | solution.py:130
  75.7 3.3 %collective-permute-done.18.far = f32[8,128]{1,0:T(8,128)S(1)} collective-permute-done((f32[8,128]{1,0:T(8,128)S(1)}, f32[8,128]{1,0:T(8,128)S(1)}, u32[]{:S(2)}, u32[]{:S(2)}) %collective-permute-start.18) | collective-permute-done | bytes 4128 | tf_op jit(solution)/shard_map/ppermute | solution.py:458
  78.9 2.9 %backward.1 = (f32[4,2048,128]{2,1,0:T(8,128)}, f32[1,1]{1,0:T(1,128)}) custom-call(f32[4,2048,128]{2,1,0:T(8,128)S(1)} %centre_back.1.inner, bf16[1168,128]{1,0:T(8,128)(2,1)S(1)} %collective-permute-done.16.first, bf16[1168,128]{1,0:T(8,128)(2,1)S(1)} %collective-permute-done.17.second, bf16[256,128]{1,0:T(8,128)(2,1)S(1)} %get-tuple-element.50.band, ...), custom_call_target="tpu_custom_call" | custom-call | flops 1000000000 | bytes 9000000 | tf_op jit(solution)/shard_map/backward/pallas_call | solution.py:230
  (15 shorter events, 0.1 us)
Async XLA Ops:
  0.6 13.4 %copy-start = (bf16[4,64,32,128]{3,2,1,0:T(8,128)(2,1)S(1)}, bf16[4,64,32,128]{3,2,1,0:T(8,128)(2,1)}, u32[]{:S(2)}) copy-start(bf16[4,64,32,128]{3,2,1,0:T(8,128)(2,1)} %param.6) | copy-start | bytes 6291460
  0.6 17.7 %copy-start.5 = (f32[9]{0:T(128)S(1)}, f32[9]{0:T(128)}, u32[]{:S(2)}) copy-start(f32[9]{0:T(128)} %lon_taps.1) | copy-start | bytes 112
  0.7 17.7 %copy-start.4 = (f32[9]{0:T(128)S(1)}, f32[9]{0:T(128)}, u32[]{:S(2)}) copy-start(f32[9]{0:T(128)} %lat_taps.1) | copy-start | bytes 112
  2.7 5.7 %collective-permute-start = (bf16[512,128]{1,0:T(8,128)(2,1)}, bf16[512,128]{1,0:T(8,128)(2,1)S(1)}, u32[]{:S(2)}, u32[]{:S(2)}) collective-permute-start(bf16[512,128]{1,0:T(8,128)(2,1)} %get-tuple-element.28), channel_id=1, source_target_pairs={{0,4},{4,0},{8,12},{12,8},{1,5},{5,1},{9,13},{13,9},{2,6},{6,2},{1... | collective-permute-start | bytes 393224 | tf_op jit(solution)/shard_map/ppermute | solution.py:414
  4.7 9.3 %collective-permute-start.1 = (bf16[512,128]{1,0:T(8,128)(2,1)}, bf16[512,128]{1,0:T(8,128)(2,1)S(1)}, u32[]{:S(2)}, u32[]{:S(2)}) collective-permute-start(bf16[512,128]{1,0:T(8,128)(2,1)} %get-tuple-element.29), channel_id=1, source_target_pairs={{0,12},{4,8},{8,4},{12,0},{1,13},{5,9},{9,5},{13,1},{2,14},{6,10},... | collective-permute-start | bytes 393224 | tf_op jit(solution)/shard_map/ppermute | solution.py:414
  14.5 8.1 %collective-permute-start.2 = (bf16[1152,128]{1,0:T(8,128)(2,1)S(1)}, bf16[1152,128]{1,0:T(8,128)(2,1)S(1)}, u32[]{:S(2)}, u32[]{:S(2)}) collective-permute-start(bf16[1152,128]{1,0:T(8,128)(2,1)S(1)} %get-tuple-element.32), channel_id=1, source_target_pairs={{0,1},{1,0},{2,3},{3,2},{4,5},{5,4},{6,7},{7,6},{8,9},{9,8},{10,11... | collective-permute-start | bytes 884744 | tf_op jit(solution)/shard_map/ppermute | solution.py:414
  16.2 8.9 %collective-permute-start.3 = (bf16[1152,128]{1,0:T(8,128)(2,1)S(1)}, bf16[1152,128]{1,0:T(8,128)(2,1)S(1)}, u32[]{:S(2)}, u32[]{:S(2)}) collective-permute-start(bf16[1152,128]{1,0:T(8,128)(2,1)S(1)} %get-tuple-element.33), channel_id=1, source_target_pairs={{0,3},{1,2},{2,1},{3,0},{4,7},{5,6},{6,5},{7,4},{8,11},{9,10},{10,... | collective-permute-start | bytes 884744 | tf_op jit(solution)/shard_map/ppermute | solution.py:414
  19.4 5.7 %copy-start.1 = (bf16[4,64,32,128]{3,2,1,0:T(8,128)(2,1)S(1)}, bf16[4,64,32,128]{3,2,1,0:T(8,128)(2,1)}, u32[]{:S(2)}) copy-start(bf16[4,64,32,128]{3,2,1,0:T(8,128)(2,1)} %param.7) | copy-start | bytes 6291460
  19.4 5.7 %copy-start.2 = (bf16[128,128]{1,0:T(8,128)(2,1)S(1)}, bf16[128,128]{1,0:T(8,128)(2,1)}, u32[]{:S(2)}) copy-start(bf16[128,128]{1,0:T(8,128)(2,1)} %vertical.3) | copy-start | bytes 98308
  21.8 24.6 %copy-start.3 = (f32[256,128]{1,0:T(8,128)S(1)}, f32[256,128]{1,0:T(8,128)}, u32[]{:S(2)}) copy-start(f32[256,128]{1,0:T(8,128)} %get-tuple-element.42.mine) | copy-start | bytes 393220
  28.5 1.6 %collective-permute-start.4 = (bf16[1024,128]{1,0:T(8,128)(2,1)S(1)}, bf16[1024,128]{1,0:T(8,128)(2,1)S(1)}, u32[]{:S(2)}, u32[]{:S(2)}) collective-permute-start(bf16[1024,128]{1,0:T(8,128)(2,1)S(1)} %get-tuple-element.36), channel_id=1, source_target_pairs={{0,16},{16,0},{1,17},{17,1},{2,18},{18,2},{3,19},{19,3},{4,20},{20... | collective-permute-start | bytes 786440 | tf_op jit(solution)/shard_map/ppermute | solution.py:435
  30.2 4.4 %collective-permute-start.5 = (bf16[256,128]{1,0:T(8,128)(2,1)S(1)}, bf16[256,128]{1,0:T(8,128)(2,1)S(1)}, u32[]{:S(2)}, u32[]{:S(2)}) collective-permute-start(bf16[256,128]{1,0:T(8,128)(2,1)S(1)} %get-tuple-element.38), channel_id=1, source_target_pairs={{0,32},{32,0},{64,96},{96,64},{1,33},{33,1},{65,97},{97,65},{2,34}... | collective-permute-start | bytes 196616 | tf_op jit(solution)/shard_map/ppermute | solution.py:437
  30.8 6.2 %collective-permute-start.6 = (bf16[256,128]{1,0:T(8,128)(2,1)S(1)}, bf16[256,128]{1,0:T(8,128)(2,1)S(1)}, u32[]{:S(2)}, u32[]{:S(2)}) collective-permute-start(bf16[256,128]{1,0:T(8,128)(2,1)S(1)} %get-tuple-element.39), channel_id=1, source_target_pairs={{0,64},{32,96},{64,0},{96,32},{1,65},{33,97},{65,1},{97,33},{2,66}... | collective-permute-start | bytes 196616 | tf_op jit(solution)/shard_map/ppermute | solution.py:437
  33.3 4.7 %collective-permute-start.7 = (bf16[256,128]{1,0:T(8,128)(2,1)S(1)}, bf16[256,128]{1,0:T(8,128)(2,1)S(1)}, u32[]{:S(2)}, u32[]{:S(2)}) collective-permute-start(bf16[256,128]{1,0:T(8,128)(2,1)S(1)} %get-tuple-element.40), channel_id=1, source_target_pairs={{0,96},{32,64},{64,32},{96,0},{1,97},{33,65},{65,33},{97,1},{2,98}... | collective-permute-start | bytes 196616 | tf_op jit(solution)/shard_map/ppermute | solution.py:437
  38.0 8.4 %collective-permute-start.8 = (bf16[272,128]{1,0:T(8,128)(2,1)S(1)}, bf16[272,128]{1,0:T(8,128)(2,1)S(1)}, u32[]{:S(2)}, u32[]{:S(2)}) collective-permute-start(bf16[272,128]{1,0:T(8,128)(2,1)S(1)} %part.1.message), channel_id=1, source_target_pairs={{0,128},{128,0},{1,129},{129,1},{2,130},{130,2},{3,131},{131,3},{4... | collective-permute-start | bytes 208904 | tf_op jit(solution)/shard_map/ppermute | solution.py:439
  46.4 5.4 %collective-permute-start.11 = (bf16[272,128]{1,0:T(8,128)(2,1)S(1)}, bf16[272,128]{1,0:T(8,128)(2,1)S(1)}, u32[]{:S(2)}, u32[]{:S(2)}) collective-permute-start(bf16[272,128]{1,0:T(8,128)(2,1)S(1)} %weight.1.zero), channel_id=1, source_target_pairs={{0,96},{32,64},{64,32},{96,0},{1,97},{33,65},{65,33},{97,1},{2,98}... | collective-permute-start | bytes 208904 | tf_op jit(solution)/shard_map/ppermute | solution.py:441
  48.3 5.8 %collective-permute-start.10 = (bf16[272,128]{1,0:T(8,128)(2,1)S(1)}, bf16[272,128]{1,0:T(8,128)(2,1)S(1)}, u32[]{:S(2)}, u32[]{:S(2)}) collective-permute-start(bf16[272,128]{1,0:T(8,128)(2,1)S(1)} %weight.1.zero), channel_id=1, source_target_pairs={{0,64},{32,96},{64,0},{96,32},{1,65},{33,97},{65,1},{97,33},{2,66}... | collective-permute-start | bytes 208904 | tf_op jit(solution)/shard_map/ppermute | solution.py:441
  51.8 4.3 %collective-permute-start.9 = (bf16[272,128]{1,0:T(8,128)(2,1)S(1)}, bf16[272,128]{1,0:T(8,128)(2,1)S(1)}, u32[]{:S(2)}, u32[]{:S(2)}) collective-permute-start(bf16[272,128]{1,0:T(8,128)(2,1)S(1)} %weight.1.zero), channel_id=1, source_target_pairs={{0,32},{32,0},{64,96},{96,64},{1,33},{33,1},{65,97},{97,65},{2,34}... | collective-permute-start | bytes 208904 | tf_op jit(solution)/shard_map/ppermute | solution.py:441
  56.2 1.6 %collective-permute-start.12 = (bf16[1040,128]{1,0:T(8,128)(2,1)S(1)}, bf16[1040,128]{1,0:T(8,128)(2,1)S(1)}, u32[]{:S(2)}, u32[]{:S(2)}) collective-permute-start(bf16[1040,128]{1,0:T(8,128)(2,1)S(1)} %gather.1.mine), channel_id=1, source_target_pairs={{0,16},{16,0},{1,17},{17,1},{2,18},{18,2},{3,19},{19,3},{4,20},{20... | collective-permute-start | bytes 798728 | tf_op jit(solution)/shard_map/ppermute | solution.py:443
  58.6 10.0 %collective-permute-start.13 = (bf16[528,128]{1,0:T(8,128)(2,1)S(1)}, bf16[528,128]{1,0:T(8,128)(2,1)S(1)}, u32[]{:S(2)}, u32[]{:S(2)}) collective-permute-start(bf16[528,128]{1,0:T(8,128)(2,1)S(1)} %get-tuple-element.44), channel_id=1, source_target_pairs={{0,4},{4,0},{8,12},{12,8},{1,5},{5,1},{9,13},{13,9},{2,6},{6,2},{1... | collective-permute-start | bytes 405512 | tf_op jit(solution)/shard_map/ppermute | solution.py:414
  58.7 9.9 %collective-permute-start.14 = (bf16[528,128]{1,0:T(8,128)(2,1)S(1)}, bf16[528,128]{1,0:T(8,128)(2,1)S(1)}, u32[]{:S(2)}, u32[]{:S(2)}) collective-permute-start(bf16[528,128]{1,0:T(8,128)(2,1)S(1)} %get-tuple-element.45), channel_id=1, source_target_pairs={{0,12},{4,8},{8,4},{12,0},{1,13},{5,9},{9,5},{13,1},{2,14},{6,10},... | collective-permute-start | bytes 405512 | tf_op jit(solution)/shard_map/ppermute | solution.py:414
  61.7 6.8 %collective-permute-start.15 = (f32[8,128]{1,0:T(8,128)S(1)}, f32[8,128]{1,0:T(8,128)S(1)}, u32[]{:S(2)}, u32[]{:S(2)}) collective-permute-start(f32[8,128]{1,0:T(8,128)S(1)} %get-tuple-element.47.refs_0_), channel_id=1, source_target_pairs={{0,8},{4,12},{8,0},{12,4},{1,9},{5,13},{9,1},{13,5},{2,10},{6,14},... | collective-permute-start | bytes 12296 | tf_op jit(solution)/shard_map/ppermute | solution.py:455
  69.1 9.8 %collective-permute-start.16 = (bf16[1168,128]{1,0:T(8,128)(2,1)S(1)}, bf16[1168,128]{1,0:T(8,128)(2,1)S(1)}, u32[]{:S(2)}, u32[]{:S(2)}) collective-permute-start(bf16[1168,128]{1,0:T(8,128)(2,1)S(1)} %get-tuple-element.48), channel_id=1, source_target_pairs={{0,1},{1,0},{2,3},{3,2},{4,5},{5,4},{6,7},{7,6},{8,9},{9,8},{10,11... | collective-permute-start | bytes 897032 | tf_op jit(solution)/shard_map/ppermute | solution.py:414
  69.2 9.7 %collective-permute-start.17 = (bf16[1168,128]{1,0:T(8,128)(2,1)S(1)}, bf16[1168,128]{1,0:T(8,128)(2,1)S(1)}, u32[]{:S(2)}, u32[]{:S(2)}) collective-permute-start(bf16[1168,128]{1,0:T(8,128)(2,1)S(1)} %get-tuple-element.49), channel_id=1, source_target_pairs={{0,3},{1,2},{2,1},{3,0},{4,7},{5,6},{6,5},{7,4},{8,11},{9,10},{10,... | collective-permute-start | bytes 897032 | tf_op jit(solution)/shard_map/ppermute | solution.py:414
  71.5 7.4 %collective-permute-start.18 = (f32[8,128]{1,0:T(8,128)S(1)}, f32[8,128]{1,0:T(8,128)S(1)}, u32[]{:S(2)}, u32[]{:S(2)}) collective-permute-start(f32[8,128]{1,0:T(8,128)S(1)} %get-tuple-element.51.sums), channel_id=1, source_target_pairs={{0,2},{1,3},{2,0},{3,1},{4,6},{5,7},{6,4},{7,5},{8,10},{9,11},{10,... | collective-permute-start | bytes 12296 | tf_op jit(solution)/shard_map/ppermute | solution.py:458

commit v3 on v2

--- a/solution.py
+++ b/solution.py
@@ -16,7 +16,6 @@
 ROWS = 8
 VMEM = pl.BlockSpec(memory_space=pltpu.VMEM)
 SMEM = pl.BlockSpec(memory_space=pltpu.SMEM)
-HBM = pl.BlockSpec(memory_space=pltpu.HBM)
 EXTRA = 16
 
 
@@ -138,17 +137,24 @@
     )(own, first, second, band)
 
 
-def side_rows(cells, cols):
-    return (cells // cols + 2 * HALO) * HALO
-
-
-def sides(band, first, second, pair, row, cols, stride):
+def beside(own, corner, member, row, cols, cells):
+    length = cells // cols * HALO
+    edge = HALO * HALO
+    lo = member * length + row // cols * HALO - edge
+    hi = lo + (ROWS + 2 * HALO) * HALO
+    parts = [own[max(lo, member * length) : min(hi, (member + 1) * length), :]]
+    if row == 0:
+        parts.insert(0, corner[2 * member * edge : (2 * member + 1) * edge, :])
+    if row + ROWS * cols == cells:
+        parts.append(corner[(2 * member + 1) * edge : (2 * member + 2) * edge, :])
+    return jnp.concatenate(parts, axis=0) if len(parts) > 1 else parts[0]
+
+
+def sides(band, strips, corners, pair, row, cols, cells):
     odd = is_odd("lon")
-    count = (ROWS + 2 * HALO) * HALO
     parts = []
     for m in pair:
-        at = slice(m * stride + row // cols * HALO, m * stride + row // cols * HALO + count)
-        one, two = first[at, :], second[at, :]
+        one, two = (beside(own, corner, m, row, cols, cells) for own, corner in zip(strips, corners))
         parts.append(jnp.concatenate([jnp.where(odd, one, two), jnp.where(odd, two, one)], axis=0))
     both = jnp.dot(band[...], jnp.concatenate(parts, axis=1), preferred_element_type=F32)
     size = both.shape[0] // 2
@@ -166,7 +172,7 @@
     ).reshape(ROWS * cols, levels)
 
 
-def forward_kernel(cols, inner, first, second, band, vertical, ensemble, keep, send):
+def forward_kernel(cols, inner, first, second, first_corner, second_corner, band, vertical, ensemble, keep, send):
     members, cells, levels = inner.shape
     size = ROWS * cols
     blocks = cells // size
@@ -177,7 +183,7 @@
         increment = jnp.zeros((size, levels), F32)
         for start in range(0, members, 2):
             pair = (start, start + 1)
-            for m, side in zip(pair, sides(band, first, second, pair, row, cols, side_rows(cells, cols))):
+            for m, side in zip(pair, sides(band, (first, second), (first_corner, second_corner), pair, row, cols, cells)):
                 smoothed = with_sides(inner[m, rows, :], side, cols).astype(BF)
                 leveled = jnp.dot(smoothed, vertical[...], preferred_element_type=F32)
                 increment = increment + ensemble[m, rows, :].astype(F32) * leveled
@@ -194,18 +200,18 @@
             send[place, :] = increment
 
 
-def forward(inner, first, second, band, vertical, ensemble, cols):
+def forward(inner, strips, corners, band, vertical, ensemble, cols):
     members, cells, levels = inner.shape
     half = jax.ShapeDtypeStruct((cells // 2, levels), BF)
     return pl.pallas_call(
         functools.partial(forward_kernel, cols),
         out_shape=(half, half),
-        in_specs=[VMEM] * 6,
+        in_specs=[VMEM] * 8,
         out_specs=(VMEM,) * 2,
         compiler_params=params(),
         cost_estimate=cost(1_500_000_000, 7_000_000),
         name="forward",
-    )(inner, first, second, band, vertical, ensemble)
+    )(inner, *strips, *corners, band, vertical, ensemble)
 
 
 def put_sums(message, sums):
@@ -239,38 +245,6 @@
     )(*inputs)
 
 
-def edges_kernel(edge, share, control, precision, first, second, mine, done):
-    members, cells, _ = control.shape
-    start = jnp.where(is_odd("lat"), 0, (cells - edge) // 128) * 128
-    copies = []
-    for out, at in ((first, start), (second, cells - edge - start)):
-        at = pl.multiple_of(at, 128)
-        for m in range(members):
-            copies.append((control.at[m, pl.ds(at, edge), :], out.at[pl.ds(m * edge, edge), :]))
-    at = pl.multiple_of((lax.axis_index("core") * 4 + lax.axis_index("x")) * share, share)
-    copies.append((precision.at[pl.ds(at, share), :], mine))
-    copies = [pltpu.make_async_copy(*pair, done.at[n]) for n, pair in enumerate(copies)]
-    for copy in copies:
-        copy.start()
-    for copy in copies:
-        copy.wait()
-
-
-def edges(control, precision, edge):
-    members, cells, levels = control.shape
-    message = jax.ShapeDtypeStruct((members * edge, levels), BF)
-    share = cells // 8
-    return call(
-        functools.partial(edges_kernel, edge, share),
-        "edges",
-        (message, message, jax.ShapeDtypeStruct((share, levels), F32)),
-        (control, precision),
-        in_specs=[HBM, HBM],
-        scratch=(pltpu.SemaphoreType.DMA((2 * members + 1,)),),
-        mib=56,
-    )
-
-
 def picker(lat_rows, cols):
     count = lat_rows * HALO
     row = lax.broadcasted_iota(jnp.int32, (2 * count, lat_rows * cols), 0)
@@ -281,54 +255,61 @@
     return jnp.where(cell == wanted, 1.0, 0.0).astype(BF)
 
 
-def lon_kernel(cols, tile, first, second, *refs):
+def put_picked(pick, parts, place, out, odd):
+    got = jnp.dot(pick, jnp.concatenate(parts, axis=1), preferred_element_type=F32).astype(BF)
+    half = got.shape[0] // 2
+    levels = got.shape[1] // len(parts)
+    low, high = got[:half], got[half:]
+    for ref, value in zip(out, (jnp.where(odd, low, high), jnp.where(odd, high, low))):
+        for n, at in enumerate(place):
+            ref[at : at + half, :] = value[:, n * levels : (n + 1) * levels]
+
+
+def strips_kernel(cols, tile, *out):
+    members, cells, _ = tile.shape
+    odd = is_odd("lon")
+    block = 16
+    pick = picker(block, cols)
+    length = cells // cols * HALO
+    for start in range(0, members, 2):
+        pair = (start, start + 1)
+        for row in range(0, cells, block * cols):
+            parts = [tile[m, row : row + block * cols, :] for m in pair]
+            put_picked(pick, parts, [m * length + row // cols * HALO for m in pair], out, odd)
+
+
+def strips(tile, cols):
     members, cells, levels = tile.shape
+    message = jax.ShapeDtypeStruct((members * (cells // cols) * HALO, levels), BF)
+    return call(
+        functools.partial(strips_kernel, cols), "strips", [message] * 2, (tile,), flops=300_000_000, size=3_000_000
+    )
+
+
+def corners_kernel(cols, members, first, second, *refs):
     if len(refs) > 2:
-        sums, far, west_out, east_out, total = refs
+        sums, far, *out, total = refs
         value = (sums[0:1, :] + get_sums(first)) + (far[0:1, :] + get_sums(second))
         total[...] = jnp.broadcast_to(value, total.shape)
-        put_sums(west_out, value)
-        put_sums(east_out, value)
+        for ref in out:
+            put_sums(ref, value)
     else:
-        west_out, east_out = refs
+        out = refs
     odd = is_odd("lon")
-    edge, block = HALO * cols, 16
-    stride = side_rows(cells, cols)
-    narrow, wide = picker(HALO, cols), picker(block, cols)
-
-    def put(pick, parts, pair, at):
-        got = jnp.dot(pick, jnp.concatenate(parts, axis=1), preferred_element_type=F32).astype(BF)
-        half = got.shape[0] // 2
-        low, high = got[:half], got[half:]
-        one, two = jnp.where(odd, low, high), jnp.where(odd, high, low)
-        for n, m in enumerate(pair):
-            lanes = slice(n * levels, (n + 1) * levels)
-            place = slice(m * stride + at, m * stride + at + half)
-            west_out[place, :] = one[:, lanes]
-            east_out[place, :] = two[:, lanes]
-
+    edge, corner = HALO * cols, HALO * HALO
+    pick = picker(HALO, cols)
     for start in range(0, members, 2):
         pair = (start, start + 1)
         ends = [south_north(first, second, slice(m * edge, (m + 1) * edge)) for m in pair]
-        put(narrow, [south for south, _ in ends], pair, 0)
-        for row in range(0, cells, block * cols):
-            put(wide, [tile[m, row : row + block * cols, :] for m in pair], pair, row // cols * HALO + HALO * HALO)
-        put(narrow, [north for _, north in ends], pair, stride - HALO * HALO)
-
-
-def lon_messages(tile, first, second, cols, *sums):
-    members, cells, levels = tile.shape
+        for n in range(2):
+            put_picked(pick, [end[n] for end in ends], [(2 * m + n) * corner for m in pair], out, odd)
+
+
+def corners(first, second, cols, members, *sums):
     extra = EXTRA if sums else 0
-    message = jax.ShapeDtypeStruct((members * side_rows(cells, cols) + extra, levels), BF)
+    message = jax.ShapeDtypeStruct((members * 2 * HALO * HALO + extra, first.shape[1]), BF)
     shapes = [message, message] + [jax.ShapeDtypeStruct(v.shape, F32) for v in sums[:1]]
-    return call(
-        functools.partial(lon_kernel, cols),
-        "lon_messages",
-        shapes,
-        (tile, first, second, *sums),
-        flops=200_000_000,
-        size=3_000_000,
-    )
+    return call(functools.partial(corners_kernel, cols, members), "corners", shapes, (first, second, *sums))
 
 
 def shares_kernel(keep, got, *shares):
@@ -346,10 +327,12 @@
     put_sums(message, jnp.sum(square[...], axis=0, keepdims=True))
 
 
-def weight_kernel(message, other, mine, out):
-    size = mine.shape[0]
+def weight_kernel(message, other, precision, out):
+    size = precision.shape[0] // 8
+    share = lax.axis_index("core") * 4 + lax.axis_index("x")
+    mine = precision[pl.ds(pl.multiple_of(share * size, size), size), :]
     increment = message[:size, :].astype(F32) + other[:size, :].astype(F32)
-    weighted = mine[...] * increment
+    weighted = mine * increment
     out[:size, :] = weighted.astype(BF)
     put_sums(out, (get_sums(message) + get_sums(other)) + jnp.sum(weighted * increment, axis=0, keepdims=True))
 
@@ -386,7 +369,10 @@
     sums[...] = jnp.broadcast_to(value, sums.shape)
 
 
-def backward_kernel(cols, entries, inner, first, second, band, control, sums, far, hessian, curvature, result, done):
+def backward_kernel(
+    cols, entries, inner, first, second, first_corner, second_corner, band, control, sums, far,
+    hessian, curvature, result, done,
+):
     members, cells, levels = inner.shape
     size = ROWS * cols
     copies = []
@@ -394,7 +380,7 @@
         pair = (start, start + 1)
         for row in range(0, cells, size):
             rows = slice(row, row + size)
-            for m, side in zip(pair, sides(band, first, second, pair, row, cols, side_rows(cells, cols))):
+            for m, side in zip(pair, sides(band, (first, second), (first_corner, second_corner), pair, row, cols, cells)):
                 result[m, rows, :] = control[m, rows, :].astype(F32) + with_sides(inner[m, rows, :], side, cols)
             if (row + size) % (cells // 4) == 0:
                 for m in pair:
@@ -404,7 +390,7 @@
                     )
                     copy.start()
                     copies.append(copy)
-    value = (sums[0:1, :] + get_sums(first)) + (far[0:1, :] + get_sums(second))
+    value = (sums[0:1, :] + get_sums(first_corner)) + (far[0:1, :] + get_sums(second_corner))
     curvature[0, 0] = jnp.sum(value) / entries
     for copy in copies:
         copy.wait()
@@ -425,19 +411,21 @@
     def rows(count):
         return jax.ShapeDtypeStruct((count, levels), BF)
 
-    first, second, mine = edges(own, precision.reshape(cells, levels), HALO * cols)
-    one, two = exchange(first, second, "lat")
-    west, east = exchange(*lon_messages(own, one, two, cols), "lon")
+    odd = is_odd("lat")
+    low, high = control[:, :HALO].reshape(-1, levels), control[:, tile_rows - HALO :].reshape(-1, levels)
+    one, two = exchange(jnp.where(odd, low, high), jnp.where(odd, high, low), "lat")
+    beside_it = exchange(*strips(own, cols), "lon")
+    corner = exchange(*corners(one, two, cols, members), "lon")
     band, band_back, band_side, band_side_back = bands(lat_taps, lon_taps, cols)
     inner, square = centre(own, one, two, band, cols, True)
-    keep, send = forward(inner, west, east, band_side, vertical, spread, cols)
+    keep, send = forward(inner, beside_it, corner, band_side, vertical, spread, cols)
 
     got = lax.ppermute(send, "core", swap("core", 1))
     zero, one, two, three = call(shares_kernel, "shares", [rows(share)] * 4, (keep, got))
     two, one, three = [lax.ppermute(v, "x", swap("x", k)) for v, k in ((two, 2), (one, 1), (three, 3))]
     (message,) = call(part_kernel, "part", [rows(share + EXTRA)], (zero, one, two, three, square))
     other = lax.ppermute(message, "zh", swap("zh", 1))
-    (zero,) = call(weight_kernel, "weight", [rows(share + EXTRA)], (message, other, mine))
+    (zero,) = call(weight_kernel, "weight", [rows(share + EXTRA)], (message, other, precision.reshape(cells, levels)))
     two, one, three = [lax.ppermute(zero, "x", swap("x", k)) for k in (2, 1, 3)]
     (message,) = call(gather_kernel, "gather", [rows(cells // 2 + EXTRA)], (zero, one, two, three))
     other = lax.ppermute(message, "core", swap("core", 1))
@@ -453,15 +441,16 @@
     )
     one, two = exchange(first, second, "lat")
     far = lax.ppermute(sums, "lat", swap("lat", 2))
-    west, east, sums = lon_messages(adjoint, one, two, cols, sums, far)
-    west, east = exchange(west, east, "lon")
+    beside_it = exchange(*strips(adjoint, cols), "lon")
+    *corner, sums = corners(one, two, cols, members, sums, far)
+    corner = exchange(*corner, "lon")
     far = lax.ppermute(sums, "lon", swap("lon", 2))
     inner = centre(adjoint, one, two, band_back, cols, False)[0]
     hessian, curvature = call(
         functools.partial(backward_kernel, cols, entries),
         "backward",
         [jax.ShapeDtypeStruct(own.shape, F32), jax.ShapeDtypeStruct((1, 1), F32)],
-        (inner, west, east, band_side_back, own, sums, far),
+        (inner, *beside_it, *corner, band_side_back, own, sums, far),
         scratch=(pltpu.VMEM(own.shape, F32), pltpu.SemaphoreType.DMA((4 * members,))),
         out_specs=(pl.BlockSpec(memory_space=pl.ANY), SMEM),
         flops=1_000_000_000,

time: 82.1 us -> 75.3 us (0.917)
  waiting for transfers between devices: 34.3 us -> 20.7 us
  starting transfers between devices: 30.7 us -> 36.5 us
  Pallas kernels: 16.1 us -> 14.4 us
  local copies, waits for them, and re-layouts: 0.03 us -> 1.62 us
  other arithmetic: 0 us -> 1 us
    ppermute x1, waiting for transfers between devices: 6.39 us -> 2.09 us  [per_device(): far = lax.ppermute(sums, 'lat', swap('lat', 2))]
    ppermute x4 -> x6, waiting for transfers between devices: 8.13 us -> 3.97 us  [exchange(): lax.ppermute(second, axis, swap(axis, 3))]
    ppermute x4 -> x6, starting transfers between devices: 10.3 us -> 13.7 us  [exchange(): lax.ppermute(second, axis, swap(axis, 3))]
    ppermute x1, waiting for transfers between devices: 3.25 us -> 0.01 us  [per_device(): far = lax.ppermute(sums, 'lon', swap('lon', 2))]
    ppermute x4 -> x6, starting transfers between devices: 3.86 us -> 6.98 us  [exchange(): lax.ppermute(first, axis, swap(axis, 1))]
    pallas_call x9 -> x10, Pallas kernels: 6.94 us -> 5.19 us  [call(): pl.pallas_call(kernel, out_shape=tuple(shapes), in_specs=in_specs or [VME...]
    ppermute x4 -> x6, waiting for transfers between devices: 1.7 us -> 0.02 us  [exchange(): lax.ppermute(first, axis, swap(axis, 1))]
    unnamed x12 -> x14, local copies, waits for them, and re-layouts: 0.03 us -> 1.62 us
  transfers between devices with their start and end apart: 19 -> 23, of which waited for: 14 -> 12; matrix products, arithmetic and copies ran while one was open for 0% -> 0% of each run, Pallas kernels for 7% -> 9%
where the time goes in v3:
time: 75.3 us; the launch traced here: 75.1 us
  starting transfers between devices  36.5 us (48%)
  waiting for transfers between devices  20.7 us (27%)
  Pallas kernels  14.4 us (19%)
  local copies, waits for them, and re-layouts  1.62 us (2%)
  other arithmetic  1 us (1%)
  between operations  0.99 us (1%)
    ppermute x6, starting transfers between devices, exchange(): lax.ppermute(second, axis, swap(axis, 3))  13.7 us
    ppermute x6, starting transfers between devices, exchange(): lax.ppermute(first, axis, swap(axis, 1))  6.98 us
    ppermute x1, starting transfers between devices, per_device(): other = lax.ppermute(message, 'zh', swap('zh', 1))  5.3 us
    pallas_call x10, Pallas kernels, call(): pl.pallas_call(kernel, out_shape=tuple(shapes), in_specs=in_specs or [VME...  5.19 us
    ppermute x3, starting transfers between devices, per_device(): two, one, three = [lax.ppermute(zero, 'x', swap('x', k)) for k in (2, 1, 3)]  4.95 us
    pallas_call x2, Pallas kernels, centre(): pl.pallas_call(functools.partial(centre_kernel, cols, with_square), out_s...  4.71 us
    ppermute x3, waiting for transfers between devices, per_device(): two, one, three = [lax.ppermute(zero, 'x', swap('x', k)) for k in (2, 1, 3)]  4.31 us
    ppermute x3, waiting for transfers between devices, per_device(): lax.ppermute(v, 'x', swap('x', k))  4.12 us
  transfers between devices with their start and end apart: 23, of which 12 were waited for; matrix products, arithmetic and copies ran while one was open for 0% of the time, Pallas kernels for 9%

profile of v3, /device:TPU:2, one launch (start us, length us, event | category | flops | bytes accessed | tf_op | source)
XLA Modules:
  0.0 75.1 jit_solution(17652517656884439511)
XLA Ops:
  0.7 1.0 %broadcast_select_fusion = (bf16[4,4,32,128]{3,2,1,0:T(8,128)(2,1)S(1)}, bf16[4,4,32,128]{3,2,1,0:T(8,128)(2,1)S(1)}) fusion(pred[]{:T(512)S(6)} %eq.3, bf16[4,64,32,128]{3,2,1,0:T(8,128)(2,1)} %param.6), kind=kLoop, calls=%fused_computation | loop fusion | flops 131072 | bytes 524289 | tf_op jit(solution)/shard_map/jit(_where)/select_n | solution.py:416
  1.7 2.0 %collective-permute-start = (bf16[512,128]{1,0:T(8,128)(2,1)S(1)}, bf16[512,128]{1,0:T(8,128)(2,1)S(1)}, u32[]{:S(2)}, u32[]{:S(2)}) collective-permute-start(bf16[512,128]{1,0:T(8,128)(2,1)S(1)} %bitcast.14), channel_id=1, source_target_pairs={{0,4},{4,0},{8,12},{12,8},{1,5},{5,1},{9,13},{13,9},{2,6},{6,2},{1... | collective-permute-start | bytes 393224 | tf_op jit(solution)/shard_map/ppermute | solution.py:400
  3.7 2.8 %collective-permute-start.1 = (bf16[512,128]{1,0:T(8,128)(2,1)S(1)}, bf16[512,128]{1,0:T(8,128)(2,1)S(1)}, u32[]{:S(2)}, u32[]{:S(2)}) collective-permute-start(bf16[512,128]{1,0:T(8,128)(2,1)S(1)} %bitcast.13), channel_id=1, source_target_pairs={{0,12},{4,8},{8,4},{12,0},{1,13},{5,9},{9,5},{13,1},{2,14},{6,10},... | collective-permute-start | bytes 393224 | tf_op jit(solution)/shard_map/ppermute | solution.py:400
  6.5 1.6 %copy-done = bf16[4,64,32,128]{3,2,1,0:T(8,128)(2,1)S(1)} copy-done((bf16[4,64,32,128]{3,2,1,0:T(8,128)(2,1)S(1)}, bf16[4,64,32,128]{3,2,1,0:T(8,128)(2,1)}, u32[]{:S(2)}) %copy-start) | copy-done | bytes 2097176
  8.1 0.5 strips.2
  8.5 1.7 %collective-permute-start.2 = (bf16[1024,128]{1,0:T(8,128)(2,1)S(1)}, bf16[1024,128]{1,0:T(8,128)(2,1)S(1)}, u32[]{:S(2)}, u32[]{:S(2)}) collective-permute-start(bf16[1024,128]{1,0:T(8,128)(2,1)S(1)} %get-tuple-element.31), channel_id=1, source_target_pairs={{0,1},{1,0},{2,3},{3,2},{4,5},{5,4},{6,7},{7,6},{8,9},{9,8},{10,11... | collective-permute-start | bytes 786440 | tf_op jit(solution)/shard_map/ppermute | solution.py:400
  10.2 2.2 %collective-permute-start.3 = (bf16[1024,128]{1,0:T(8,128)(2,1)S(1)}, bf16[1024,128]{1,0:T(8,128)(2,1)S(1)}, u32[]{:S(2)}, u32[]{:S(2)}) collective-permute-start(bf16[1024,128]{1,0:T(8,128)(2,1)S(1)} %get-tuple-element.32), channel_id=1, source_target_pairs={{0,3},{1,2},{2,1},{3,0},{4,7},{5,6},{6,5},{7,4},{8,11},{9,10},{10,... | collective-permute-start | bytes 786440 | tf_op jit(solution)/shard_map/ppermute | solution.py:400
  12.4 1.0 %bands.1 = (bf16[512,512]{1,0:T(8,128)(2,1)S(1)}, bf16[512,512]{1,0:T(8,128)(2,1)S(1)}, bf16[256,128]{1,0:T(8,128)(2,1)S(1)}, bf16[256,128]{1,0:T(8,128)(2,1)S(1)}) custom-call(f32[9]{0:T(128)S(1)} %copy-done.5, f32[9]{0:T(128)S(1)} %copy-done.6), custom_call_target="tpu_custom_call" | custom-call | flops 2000000 | bytes 1200000 | tf_op jit(solution)/shard_map/bands/pallas_call | solution.py:76
  13.4 0.2 corners.2
  13.6 1.0 %collective-permute-start.4 = (bf16[128,128]{1,0:T(8,128)(2,1)S(1)}, bf16[128,128]{1,0:T(8,128)(2,1)S(1)}, u32[]{:S(2)}, u32[]{:S(2)}) collective-permute-start(bf16[128,128]{1,0:T(8,128)(2,1)S(1)} %get-tuple-element.33), channel_id=1, source_target_pairs={{0,1},{1,0},{2,3},{3,2},{4,5},{5,4},{6,7},{7,6},{8,9},{9,8},{10,11... | collective-permute-start | bytes 98312 | tf_op jit(solution)/shard_map/ppermute | solution.py:400
  14.6 2.2 %collective-permute-start.5 = (bf16[128,128]{1,0:T(8,128)(2,1)S(1)}, bf16[128,128]{1,0:T(8,128)(2,1)S(1)}, u32[]{:S(2)}, u32[]{:S(2)}) collective-permute-start(bf16[128,128]{1,0:T(8,128)(2,1)S(1)} %get-tuple-element.34), channel_id=1, source_target_pairs={{0,3},{1,2},{2,1},{3,0},{4,7},{5,6},{6,5},{7,4},{8,11},{9,10},{10,... | collective-permute-start | bytes 98312 | tf_op jit(solution)/shard_map/ppermute | solution.py:400
  16.8 2.3 %centre_forward.1 = (f32[4,2048,128]{2,1,0:T(8,128)S(1)}, f32[8,128]{1,0:T(8,128)S(1)}) custom-call(bf16[4,2048,128]{2,1,0:T(8,128)(2,1)S(1)} %bitcast.8, bf16[512,128]{1,0:T(8,128)(2,1)S(1)} %collective-permute-done.first, bf16[512,128]{1,0:T(8,128)(2,1)S(1)} %collective-permute-done.1.second, bf16[512,512]{1,0:T(8,128)(2,1)S(1)} %get-tuple-element.29.band), custom_call_target="tpu_custom_call" | custom-call | flops 3000000000 | bytes 7000000 | tf_op jit(solution)/shard_map/centre_forward/pallas_call | solution.py:129
  19.2 0.6 collective-permute-done.5.second_corner
  19.8 0.0 copy-start.3
  19.8 3.4 %forward.1 = (bf16[1024,128]{1,0:T(8,128)(2,1)S(1)}, bf16[1024,128]{1,0:T(8,128)(2,1)S(1)}) custom-call(f32[4,2048,128]{2,1,0:T(8,128)S(1)} %get-tuple-element.30.inner, bf16[1024,128]{1,0:T(8,128)(2,1)S(1)} %collective-permute-done.2.first, bf16[1024,128]{1,0:T(8,128)(2,1)S(1)} %collective-permute-done.3.second, ...), custom_call_target="tpu_custom_call" | custom-call | flops 1500000000 | bytes 7000000 | tf_op jit(solution)/shard_map/forward/pallas_call | solution.py:206
  23.2 0.1 collective-permute-start.6
  23.3 1.5 %collective-permute-done.6.got = bf16[1024,128]{1,0:T(8,128)(2,1)S(1)} collective-permute-done((bf16[1024,128]{1,0:T(8,128)(2,1)S(1)}, bf16[1024,128]{1,0:T(8,128)(2,1)S(1)}, u32[]{:S(2)}, u32[]{:S(2)}) %collective-permute-start.6) | collective-permute-done | bytes 262176 | tf_op jit(solution)/shard_map/ppermute | solution.py:423
  24.9 0.1 shares.1
  24.9 0.6 collective-permute-start.7
  25.5 2.4 %collective-permute-start.8 = (bf16[256,128]{1,0:T(8,128)(2,1)S(1)}, bf16[256,128]{1,0:T(8,128)(2,1)S(1)}, u32[]{:S(2)}, u32[]{:S(2)}) collective-permute-start(bf16[256,128]{1,0:T(8,128)(2,1)S(1)} %get-tuple-element.40), channel_id=1, source_target_pairs={{0,64},{32,96},{64,0},{96,32},{1,65},{33,97},{65,1},{97,33},{2,66}... | collective-permute-start | bytes 196616 | tf_op jit(solution)/shard_map/ppermute | solution.py:425
  28.0 0.5 collective-permute-start.9
  28.5 0.8 %collective-permute-done.7.one = bf16[256,128]{1,0:T(8,128)(2,1)S(1)} collective-permute-done((bf16[256,128]{1,0:T(8,128)(2,1)S(1)}, bf16[256,128]{1,0:T(8,128)(2,1)S(1)}, u32[]{:S(2)}, u32[]{:S(2)}) %collective-permute-start.7) | collective-permute-done | bytes 65568 | tf_op jit(solution)/shard_map/ppermute | solution.py:425
  29.3 2.4 %collective-permute-done.8.two = bf16[256,128]{1,0:T(8,128)(2,1)S(1)} collective-permute-done((bf16[256,128]{1,0:T(8,128)(2,1)S(1)}, bf16[256,128]{1,0:T(8,128)(2,1)S(1)}, u32[]{:S(2)}, u32[]{:S(2)}) %collective-permute-start.8) | collective-permute-done | bytes 65568 | tf_op jit(solution)/shard_map/ppermute | solution.py:425
  31.7 0.9 %collective-permute-done.9.three = bf16[256,128]{1,0:T(8,128)(2,1)S(1)} collective-permute-done((bf16[256,128]{1,0:T(8,128)(2,1)S(1)}, bf16[256,128]{1,0:T(8,128)(2,1)S(1)}, u32[]{:S(2)}, u32[]{:S(2)}) %collective-permute-start.9) | collective-permute-done | bytes 65568 | tf_op jit(solution)/shard_map/ppermute | solution.py:425
  32.7 5.3 %collective-permute-start.10 = (bf16[272,128]{1,0:T(8,128)(2,1)S(1)}, bf16[272,128]{1,0:T(8,128)(2,1)S(1)}, u32[]{:S(2)}, u32[]{:S(2)}) collective-permute-start(bf16[272,128]{1,0:T(8,128)(2,1)S(1)} %part.1.message), channel_id=1, source_target_pairs={{0,128},{128,0},{1,129},{129,1},{2,130},{130,2},{3,131},{131,3},{4... | collective-permute-start | bytes 208904 | tf_op jit(solution)/shard_map/ppermute | solution.py:427
  38.0 3.1 %collective-permute-done.10.other = bf16[272,128]{1,0:T(8,128)(2,1)S(1)} collective-permute-done((bf16[272,128]{1,0:T(8,128)(2,1)S(1)}, bf16[272,128]{1,0:T(8,128)(2,1)S(1)}, u32[]{:S(2)}, u32[]{:S(2)}) %collective-permute-start.10) | collective-permute-done | bytes 69664 | tf_op jit(solution)/shard_map/ppermute | solution.py:427
  41.1 0.1 weight.1.zero
  41.1 1.4 %collective-permute-start.13 = (bf16[272,128]{1,0:T(8,128)(2,1)S(1)}, bf16[272,128]{1,0:T(8,128)(2,1)S(1)}, u32[]{:S(2)}, u32[]{:S(2)}) collective-permute-start(bf16[272,128]{1,0:T(8,128)(2,1)S(1)} %weight.1.zero), channel_id=1, source_target_pairs={{0,96},{32,64},{64,32},{96,0},{1,97},{33,65},{65,33},{97,1},{2,98}... | collective-permute-start | bytes 208904 | tf_op jit(solution)/shard_map/ppermute | solution.py:429
  42.5 3.6 %collective-permute-start.12 = (bf16[272,128]{1,0:T(8,128)(2,1)S(1)}, bf16[272,128]{1,0:T(8,128)(2,1)S(1)}, u32[]{:S(2)}, u32[]{:S(2)}) collective-permute-start(bf16[272,128]{1,0:T(8,128)(2,1)S(1)} %weight.1.zero), channel_id=1, source_target_pairs={{0,64},{32,96},{64,0},{96,32},{1,65},{33,97},{65,1},{97,33},{2,66}... | collective-permute-start | bytes 208904 | tf_op jit(solution)/shard_map/ppermute | solution.py:429
  46.1 2.3 %collective-permute-done.12.two = bf16[272,128]{1,0:T(8,128)(2,1)S(1)} collective-permute-done((bf16[272,128]{1,0:T(8,128)(2,1)S(1)}, bf16[272,128]{1,0:T(8,128)(2,1)S(1)}, u32[]{:S(2)}, u32[]{:S(2)}) %collective-permute-start.12) | collective-permute-done | bytes 69664 | tf_op jit(solution)/shard_map/ppermute | solution.py:429
  48.4 2.0 %collective-permute-done.11.one = bf16[272,128]{1,0:T(8,128)(2,1)S(1)} collective-permute-done((bf16[272,128]{1,0:T(8,128)(2,1)S(1)}, bf16[272,128]{1,0:T(8,128)(2,1)S(1)}, u32[]{:S(2)}, u32[]{:S(2)}) %collective-permute-start.11) | collective-permute-done | bytes 69664 | tf_op jit(solution)/shard_map/ppermute | solution.py:429
  50.4 0.1 collective-permute-start.14
  50.5 1.5 %collective-permute-done.14.other = bf16[1040,128]{1,0:T(8,128)(2,1)S(1)} collective-permute-done((bf16[1040,128]{1,0:T(8,128)(2,1)S(1)}, bf16[1040,128]{1,0:T(8,128)(2,1)S(1)}, u32[]{:S(2)}, u32[]{:S(2)}) %collective-permute-start.14) | collective-permute-done | bytes 266272 | tf_op jit(solution)/shard_map/ppermute | solution.py:431
  52.1 0.8 %level.1 = (bf16[4,2048,128]{2,1,0:T(8,128)(2,1)S(1)}, bf16[528,128]{1,0:T(8,128)(2,1)S(1)}, bf16[528,128]{1,0:T(8,128)(2,1)S(1)}, f32[8,128]{1,0:T(8,128)S(1)}) custom-call(bf16[1040,128]{1,0:T(8,128)(2,1)S(1)} %gather.1.mine, bf16[1040,128]{1,0:T(8,128)(2,1)S(1)} %collective-permute-done.14.other, bf16[4,2048,128]{2,1,0:T(8,128)(2,1)S(1)} %bitcast.11, ...), custom_call_target="tpu_custom_call" | custom-call | flops 300000000 | bytes 4500000 | tf_op jit(solution)/shard_map/level/pallas_call | solution.py:236
  52.9 0.7 collective-permute-start.15
  53.6 3.4 %collective-permute-start.16 = (bf16[528,128]{1,0:T(8,128)(2,1)S(1)}, bf16[528,128]{1,0:T(8,128)(2,1)S(1)}, u32[]{:S(2)}, u32[]{:S(2)}) collective-permute-start(bf16[528,128]{1,0:T(8,128)(2,1)S(1)} %get-tuple-element.45), channel_id=1, source_target_pairs={{0,12},{4,8},{8,4},{12,0},{1,13},{5,9},{9,5},{13,1},{2,14},{6,10},... | collective-permute-start | bytes 405512 | tf_op jit(solution)/shard_map/ppermute | solution.py:400
  57.0 0.5 strips.3
  57.5 0.2 collective-permute-start.17
  57.7 2.1 %collective-permute-start.18 = (bf16[1024,128]{1,0:T(8,128)(2,1)S(1)}, bf16[1024,128]{1,0:T(8,128)(2,1)S(1)}, u32[]{:S(2)}, u32[]{:S(2)}) collective-permute-start(bf16[1024,128]{1,0:T(8,128)(2,1)S(1)} %get-tuple-element.48), channel_id=1, source_target_pairs={{0,3},{1,2},{2,1},{3,0},{4,7},{5,6},{6,5},{7,4},{8,11},{9,10},{10,... | collective-permute-start | bytes 786440 | tf_op jit(solution)/shard_map/ppermute | solution.py:400
  59.8 2.1 %collective-permute-done.19.refs_1_ = f32[8,128]{1,0:T(8,128)S(1)} collective-permute-done((f32[8,128]{1,0:T(8,128)S(1)}, f32[8,128]{1,0:T(8,128)S(1)}, u32[]{:S(2)}, u32[]{:S(2)}) %collective-permute-start.19) | collective-permute-done | bytes 4128 | tf_op jit(solution)/shard_map/ppermute | solution.py:443
  61.9 1.7 %collective-permute-done.16.second = bf16[528,128]{1,0:T(8,128)(2,1)S(1)} collective-permute-done((bf16[528,128]{1,0:T(8,128)(2,1)S(1)}, bf16[528,128]{1,0:T(8,128)(2,1)S(1)}, u32[]{:S(2)}, u32[]{:S(2)}) %collective-permute-start.16) | collective-permute-done | bytes 135200 | tf_op jit(solution)/shard_map/ppermute | solution.py:400
  63.6 0.2 corners.3
  63.8 1.8 %collective-permute-start.22 = (f32[8,128]{1,0:T(8,128)S(1)}, f32[8,128]{1,0:T(8,128)S(1)}, u32[]{:S(2)}, u32[]{:S(2)}) collective-permute-start(f32[8,128]{1,0:T(8,128)S(1)} %get-tuple-element.53.sums), channel_id=1, source_target_pairs={{0,2},{1,3},{2,0},{3,1},{4,6},{5,7},{6,4},{7,5},{8,10},{9,11},{10,... | collective-permute-start | bytes 12296 | tf_op jit(solution)/shard_map/ppermute | solution.py:447
  65.5 1.3 %collective-permute-start.20 = (bf16[144,128]{1,0:T(8,128)(2,1)S(1)}, bf16[144,128]{1,0:T(8,128)(2,1)S(1)}, u32[]{:S(2)}, u32[]{:S(2)}) collective-permute-start(bf16[144,128]{1,0:T(8,128)(2,1)S(1)} %get-tuple-element.50), channel_id=1, source_target_pairs={{0,1},{1,0},{2,3},{3,2},{4,5},{5,4},{6,7},{7,6},{8,9},{9,8},{10,11... | collective-permute-start | bytes 110600 | tf_op jit(solution)/shard_map/ppermute | solution.py:400
  66.9 1.1 %collective-permute-start.21 = (bf16[144,128]{1,0:T(8,128)(2,1)S(1)}, bf16[144,128]{1,0:T(8,128)(2,1)S(1)}, u32[]{:S(2)}, u32[]{:S(2)}) collective-permute-start(bf16[144,128]{1,0:T(8,128)(2,1)S(1)} %get-tuple-element.51), channel_id=1, source_target_pairs={{0,3},{1,2},{2,1},{3,0},{4,7},{5,6},{6,5},{7,4},{8,11},{9,10},{10,... | collective-permute-start | bytes 110600 | tf_op jit(solution)/shard_map/ppermute | solution.py:400
  67.9 2.4 %centre_back.1.inner = f32[4,2048,128]{2,1,0:T(8,128)S(1)} custom-call(bf16[4,2048,128]{2,1,0:T(8,128)(2,1)S(1)} %get-tuple-element.43.own.tile, bf16[528,128]{1,0:T(8,128)(2,1)S(1)} %collective-permute-done.15.first, bf16[528,128]{1,0:T(8,128)(2,1)S(1)} %collective-permute-done.16.second, bf16[512,512]{1,0:T(8,128)(2,1)S(1)} %get-tuple-element.46.band), custom_call_target="tpu_custom_call" | custom-call | flops 3000000000 | bytes 7000000 | tf_op jit(solution)/shard_map/centre_back/pallas_call | solution.py:129
  70.3 1.7 %collective-permute-done.21.second_corner = bf16[144,128]{1,0:T(8,128)(2,1)S(1)} collective-permute-done((bf16[144,128]{1,0:T(8,128)(2,1)S(1)}, bf16[144,128]{1,0:T(8,128)(2,1)S(1)}, u32[]{:S(2)}, u32[]{:S(2)}) %collective-permute-start.21) | collective-permute-done | bytes 36896 | tf_op jit(solution)/shard_map/ppermute | solution.py:400
  72.1 2.9 %backward.1 = (f32[4,2048,128]{2,1,0:T(8,128)}, f32[1,1]{1,0:T(1,128)}) custom-call(f32[4,2048,128]{2,1,0:T(8,128)S(1)} %centre_back.1.inner, bf16[1024,128]{1,0:T(8,128)(2,1)S(1)} %collective-permute-done.17.first, bf16[1024,128]{1,0:T(8,128)(2,1)S(1)} %collective-permute-done.18.second, bf16[144,128]{1,0:T(8,128)(2,1)S(1)} %collective-permute-done.20.first_corner, ...), custom_call_target="tpu_custom_call" | custom-call | flops 1000000000 | bytes 9000000 | tf_op jit(solution)/shard_map/backward/pallas_call | solution.py:236
  (27 shorter events, 0.1 us)
Async XLA Ops:
  0.6 11.7 %copy-start.6 = (f32[9]{0:T(128)S(1)}, f32[9]{0:T(128)}, u32[]{:S(2)}) copy-start(f32[9]{0:T(128)} %lon_taps.1) | copy-start | bytes 112
  0.6 11.7 %copy-start.5 = (f32[9]{0:T(128)S(1)}, f32[9]{0:T(128)}, u32[]{:S(2)}) copy-start(f32[9]{0:T(128)} %lat_taps.1) | copy-start | bytes 112
  1.7 11.8 %collective-permute-start = (bf16[512,128]{1,0:T(8,128)(2,1)S(1)}, bf16[512,128]{1,0:T(8,128)(2,1)S(1)}, u32[]{:S(2)}, u32[]{:S(2)}) collective-permute-start(bf16[512,128]{1,0:T(8,128)(2,1)S(1)} %bitcast.14), channel_id=1, source_target_pairs={{0,4},{4,0},{8,12},{12,8},{1,5},{5,1},{9,13},{13,9},{2,6},{6,2},{1... | collective-permute-start | bytes 393224 | tf_op jit(solution)/shard_map/ppermute | solution.py:400
  3.7 9.8 %collective-permute-start.1 = (bf16[512,128]{1,0:T(8,128)(2,1)S(1)}, bf16[512,128]{1,0:T(8,128)(2,1)S(1)}, u32[]{:S(2)}, u32[]{:S(2)}) collective-permute-start(bf16[512,128]{1,0:T(8,128)(2,1)S(1)} %bitcast.13), channel_id=1, source_target_pairs={{0,12},{4,8},{8,4},{12,0},{1,13},{5,9},{9,5},{13,1},{2,14},{6,10},... | collective-permute-start | bytes 393224 | tf_op jit(solution)/shard_map/ppermute | solution.py:400
  6.5 1.6 %copy-start = (bf16[4,64,32,128]{3,2,1,0:T(8,128)(2,1)S(1)}, bf16[4,64,32,128]{3,2,1,0:T(8,128)(2,1)}, u32[]{:S(2)}) copy-start(bf16[4,64,32,128]{3,2,1,0:T(8,128)(2,1)} %param.6) | copy-start | bytes 6291460
  8.1 8.8 %copy-start.1 = (bf16[4,64,32,128]{3,2,1,0:T(8,128)(2,1)S(1)}, bf16[4,64,32,128]{3,2,1,0:T(8,128)(2,1)}, u32[]{:S(2)}) copy-start(bf16[4,64,32,128]{3,2,1,0:T(8,128)(2,1)} %param.6) | copy-start | bytes 6291460
  8.5 11.2 %collective-permute-start.2 = (bf16[1024,128]{1,0:T(8,128)(2,1)S(1)}, bf16[1024,128]{1,0:T(8,128)(2,1)S(1)}, u32[]{:S(2)}, u32[]{:S(2)}) collective-permute-start(bf16[1024,128]{1,0:T(8,128)(2,1)S(1)} %get-tuple-element.31), channel_id=1, source_target_pairs={{0,1},{1,0},{2,3},{3,2},{4,5},{5,4},{6,7},{7,6},{8,9},{9,8},{10,11... | collective-permute-start | bytes 786440 | tf_op jit(solution)/shard_map/ppermute | solution.py:400
  10.2 9.6 %collective-permute-start.3 = (bf16[1024,128]{1,0:T(8,128)(2,1)S(1)}, bf16[1024,128]{1,0:T(8,128)(2,1)S(1)}, u32[]{:S(2)}, u32[]{:S(2)}) collective-permute-start(bf16[1024,128]{1,0:T(8,128)(2,1)S(1)} %get-tuple-element.32), channel_id=1, source_target_pairs={{0,3},{1,2},{2,1},{3,0},{4,7},{5,6},{6,5},{7,4},{8,11},{9,10},{10,... | collective-permute-start | bytes 786440 | tf_op jit(solution)/shard_map/ppermute | solution.py:400
  13.6 5.5 %collective-permute-start.4 = (bf16[128,128]{1,0:T(8,128)(2,1)S(1)}, bf16[128,128]{1,0:T(8,128)(2,1)S(1)}, u32[]{:S(2)}, u32[]{:S(2)}) collective-permute-start(bf16[128,128]{1,0:T(8,128)(2,1)S(1)} %get-tuple-element.33), channel_id=1, source_target_pairs={{0,1},{1,0},{2,3},{3,2},{4,5},{5,4},{6,7},{7,6},{8,9},{9,8},{10,11... | collective-permute-start | bytes 98312 | tf_op jit(solution)/shard_map/ppermute | solution.py:400
  14.6 5.1 %collective-permute-start.5 = (bf16[128,128]{1,0:T(8,128)(2,1)S(1)}, bf16[128,128]{1,0:T(8,128)(2,1)S(1)}, u32[]{:S(2)}, u32[]{:S(2)}) collective-permute-start(bf16[128,128]{1,0:T(8,128)(2,1)S(1)} %get-tuple-element.34), channel_id=1, source_target_pairs={{0,3},{1,2},{2,1},{3,0},{4,7},{5,6},{6,5},{7,4},{8,11},{9,10},{10,... | collective-permute-start | bytes 98312 | tf_op jit(solution)/shard_map/ppermute | solution.py:400
  16.8 3.0 %copy-start.2 = (bf16[4,64,32,128]{3,2,1,0:T(8,128)(2,1)S(1)}, bf16[4,64,32,128]{3,2,1,0:T(8,128)(2,1)}, u32[]{:S(2)}) copy-start(bf16[4,64,32,128]{3,2,1,0:T(8,128)(2,1)} %param.7) | copy-start | bytes 6291460
  16.8 3.0 %copy-start.4 = (bf16[128,128]{1,0:T(8,128)(2,1)S(1)}, bf16[128,128]{1,0:T(8,128)(2,1)}, u32[]{:S(2)}) copy-start(bf16[128,128]{1,0:T(8,128)(2,1)} %vertical.3) | copy-start | bytes 98308
  19.8 21.3 %copy-start.3 = (f32[64,32,128]{2,1,0:T(8,128)S(1)}, f32[64,32,128]{2,1,0:T(8,128)}, u32[]{:S(2)}) copy-start(f32[64,32,128]{2,1,0:T(8,128)} %param.8) | copy-start | bytes 3145732
  23.2 1.6 %collective-permute-start.6 = (bf16[1024,128]{1,0:T(8,128)(2,1)S(1)}, bf16[1024,128]{1,0:T(8,128)(2,1)S(1)}, u32[]{:S(2)}, u32[]{:S(2)}) collective-permute-start(bf16[1024,128]{1,0:T(8,128)(2,1)S(1)} %get-tuple-element.37), channel_id=1, source_target_pairs={{0,16},{16,0},{1,17},{17,1},{2,18},{18,2},{3,19},{19,3},{4,20},{20... | collective-permute-start | bytes 786440 | tf_op jit(solution)/shard_map/ppermute | solution.py:423
  24.9 4.4 %collective-permute-start.7 = (bf16[256,128]{1,0:T(8,128)(2,1)S(1)}, bf16[256,128]{1,0:T(8,128)(2,1)S(1)}, u32[]{:S(2)}, u32[]{:S(2)}) collective-permute-start(bf16[256,128]{1,0:T(8,128)(2,1)S(1)} %get-tuple-element.39), channel_id=1, source_target_pairs={{0,32},{32,0},{64,96},{96,64},{1,33},{33,1},{65,97},{97,65},{2,34}... | collective-permute-start | bytes 196616 | tf_op jit(solution)/shard_map/ppermute | solution.py:425
  25.5 6.2 %collective-permute-start.8 = (bf16[256,128]{1,0:T(8,128)(2,1)S(1)}, bf16[256,128]{1,0:T(8,128)(2,1)S(1)}, u32[]{:S(2)}, u32[]{:S(2)}) collective-permute-start(bf16[256,128]{1,0:T(8,128)(2,1)S(1)} %get-tuple-element.40), channel_id=1, source_target_pairs={{0,64},{32,96},{64,0},{96,32},{1,65},{33,97},{65,1},{97,33},{2,66}... | collective-permute-start | bytes 196616 | tf_op jit(solution)/shard_map/ppermute | solution.py:425
  28.0 4.7 %collective-permute-start.9 = (bf16[256,128]{1,0:T(8,128)(2,1)S(1)}, bf16[256,128]{1,0:T(8,128)(2,1)S(1)}, u32[]{:S(2)}, u32[]{:S(2)}) collective-permute-start(bf16[256,128]{1,0:T(8,128)(2,1)S(1)} %get-tuple-element.41), channel_id=1, source_target_pairs={{0,96},{32,64},{64,32},{96,0},{1,97},{33,65},{65,33},{97,1},{2,98}... | collective-permute-start | bytes 196616 | tf_op jit(solution)/shard_map/ppermute | solution.py:425
  32.7 8.4 %collective-permute-start.10 = (bf16[272,128]{1,0:T(8,128)(2,1)S(1)}, bf16[272,128]{1,0:T(8,128)(2,1)S(1)}, u32[]{:S(2)}, u32[]{:S(2)}) collective-permute-start(bf16[272,128]{1,0:T(8,128)(2,1)S(1)} %part.1.message), channel_id=1, source_target_pairs={{0,128},{128,0},{1,129},{129,1},{2,130},{130,2},{3,131},{131,3},{4... | collective-permute-start | bytes 208904 | tf_op jit(solution)/shard_map/ppermute | solution.py:427
  41.1 5.0 %collective-permute-start.13 = (bf16[272,128]{1,0:T(8,128)(2,1)S(1)}, bf16[272,128]{1,0:T(8,128)(2,1)S(1)}, u32[]{:S(2)}, u32[]{:S(2)}) collective-permute-start(bf16[272,128]{1,0:T(8,128)(2,1)S(1)} %weight.1.zero), channel_id=1, source_target_pairs={{0,96},{32,64},{64,32},{96,0},{1,97},{33,65},{65,33},{97,1},{2,98}... | collective-permute-start | bytes 208904 | tf_op jit(solution)/shard_map/ppermute | solution.py:429
  42.5 5.8 %collective-permute-start.12 = (bf16[272,128]{1,0:T(8,128)(2,1)S(1)}, bf16[272,128]{1,0:T(8,128)(2,1)S(1)}, u32[]{:S(2)}, u32[]{:S(2)}) collective-permute-start(bf16[272,128]{1,0:T(8,128)(2,1)S(1)} %weight.1.zero), channel_id=1, source_target_pairs={{0,64},{32,96},{64,0},{96,32},{1,65},{33,97},{65,1},{97,33},{2,66}... | collective-permute-start | bytes 208904 | tf_op jit(solution)/shard_map/ppermute | solution.py:429
  46.1 4.3 %collective-permute-start.11 = (bf16[272,128]{1,0:T(8,128)(2,1)S(1)}, bf16[272,128]{1,0:T(8,128)(2,1)S(1)}, u32[]{:S(2)}, u32[]{:S(2)}) collective-permute-start(bf16[272,128]{1,0:T(8,128)(2,1)S(1)} %weight.1.zero), channel_id=1, source_target_pairs={{0,32},{32,0},{64,96},{96,64},{1,33},{33,1},{65,97},{97,65},{2,34}... | collective-permute-start | bytes 208904 | tf_op jit(solution)/shard_map/ppermute | solution.py:429
  50.4 1.6 %collective-permute-start.14 = (bf16[1040,128]{1,0:T(8,128)(2,1)S(1)}, bf16[1040,128]{1,0:T(8,128)(2,1)S(1)}, u32[]{:S(2)}, u32[]{:S(2)}) collective-permute-start(bf16[1040,128]{1,0:T(8,128)(2,1)S(1)} %gather.1.mine), channel_id=1, source_target_pairs={{0,16},{16,0},{1,17},{17,1},{2,18},{18,2},{3,19},{19,3},{4,20},{20... | collective-permute-start | bytes 798728 | tf_op jit(solution)/shard_map/ppermute | solution.py:431
  52.9 9.0 %collective-permute-start.15 = (bf16[528,128]{1,0:T(8,128)(2,1)S(1)}, bf16[528,128]{1,0:T(8,128)(2,1)S(1)}, u32[]{:S(2)}, u32[]{:S(2)}) collective-permute-start(bf16[528,128]{1,0:T(8,128)(2,1)S(1)} %get-tuple-element.44), channel_id=1, source_target_pairs={{0,4},{4,0},{8,12},{12,8},{1,5},{5,1},{9,13},{13,9},{2,6},{6,2},{1... | collective-permute-start | bytes 405512 | tf_op jit(solution)/shard_map/ppermute | solution.py:400
  53.6 9.9 %collective-permute-start.16 = (bf16[528,128]{1,0:T(8,128)(2,1)S(1)}, bf16[528,128]{1,0:T(8,128)(2,1)S(1)}, u32[]{:S(2)}, u32[]{:S(2)}) collective-permute-start(bf16[528,128]{1,0:T(8,128)(2,1)S(1)} %get-tuple-element.45), channel_id=1, source_target_pairs={{0,12},{4,8},{8,4},{12,0},{1,13},{5,9},{9,5},{13,1},{2,14},{6,10},... | collective-permute-start | bytes 405512 | tf_op jit(solution)/shard_map/ppermute | solution.py:400
  57.0 4.9 %collective-permute-start.19 = (f32[8,128]{1,0:T(8,128)S(1)}, f32[8,128]{1,0:T(8,128)S(1)}, u32[]{:S(2)}, u32[]{:S(2)}) collective-permute-start(f32[8,128]{1,0:T(8,128)S(1)} %get-tuple-element.49.refs_0_), channel_id=1, source_target_pairs={{0,8},{4,12},{8,0},{12,4},{1,9},{5,13},{9,1},{13,5},{2,10},{6,14},... | collective-permute-start | bytes 12296 | tf_op jit(solution)/shard_map/ppermute | solution.py:443
  57.5 14.6 %collective-permute-start.17 = (bf16[1024,128]{1,0:T(8,128)(2,1)S(1)}, bf16[1024,128]{1,0:T(8,128)(2,1)S(1)}, u32[]{:S(2)}, u32[]{:S(2)}) collective-permute-start(bf16[1024,128]{1,0:T(8,128)(2,1)S(1)} %get-tuple-element.47), channel_id=1, source_target_pairs={{0,1},{1,0},{2,3},{3,2},{4,5},{5,4},{6,7},{7,6},{8,9},{9,8},{10,11... | collective-permute-start | bytes 786440 | tf_op jit(solution)/shard_map/ppermute | solution.py:400
  57.7 14.4 %collective-permute-start.18 = (bf16[1024,128]{1,0:T(8,128)(2,1)S(1)}, bf16[1024,128]{1,0:T(8,128)(2,1)S(1)}, u32[]{:S(2)}, u32[]{:S(2)}) collective-permute-start(bf16[1024,128]{1,0:T(8,128)(2,1)S(1)} %get-tuple-element.48), channel_id=1, source_target_pairs={{0,3},{1,2},{2,1},{3,0},{4,7},{5,6},{6,5},{7,4},{8,11},{9,10},{10,... | collective-permute-start | bytes 786440 | tf_op jit(solution)/shard_map/ppermute | solution.py:400
  63.8 6.6 %collective-permute-start.22 = (f32[8,128]{1,0:T(8,128)S(1)}, f32[8,128]{1,0:T(8,128)S(1)}, u32[]{:S(2)}, u32[]{:S(2)}) collective-permute-start(f32[8,128]{1,0:T(8,128)S(1)} %get-tuple-element.53.sums), channel_id=1, source_target_pairs={{0,2},{1,3},{2,0},{3,1},{4,6},{5,7},{6,4},{7,5},{8,10},{9,11},{10,... | collective-permute-start | bytes 12296 | tf_op jit(solution)/shard_map/ppermute | solution.py:447
  65.5 4.8 %collective-permute-start.20 = (bf16[144,128]{1,0:T(8,128)(2,1)S(1)}, bf16[144,128]{1,0:T(8,128)(2,1)S(1)}, u32[]{:S(2)}, u32[]{:S(2)}) collective-permute-start(bf16[144,128]{1,0:T(8,128)(2,1)S(1)} %get-tuple-element.50), channel_id=1, source_target_pairs={{0,1},{1,0},{2,3},{3,2},{4,5},{5,4},{6,7},{7,6},{8,9},{9,8},{10,11... | collective-permute-start | bytes 110600 | tf_op jit(solution)/shard_map/ppermute | solution.py:400
  66.9 5.2 %collective-permute-start.21 = (bf16[144,128]{1,0:T(8,128)(2,1)S(1)}, bf16[144,128]{1,0:T(8,128)(2,1)S(1)}, u32[]{:S(2)}, u32[]{:S(2)}) collective-permute-start(bf16[144,128]{1,0:T(8,128)(2,1)S(1)} %get-tuple-element.51), channel_id=1, source_target_pairs={{0,3},{1,2},{2,1},{3,0},{4,7},{5,6},{6,5},{7,4},{8,11},{9,10},{10,... | collective-permute-start | bytes 110600 | tf_op jit(solution)/shard_map/ppermute | solution.py:400

commit v4 on v3

--- a/solution.py
+++ b/solution.py
@@ -49,39 +49,39 @@
     out[row + out.shape[0] // 2 : row + out.shape[0] // 2 + size, :] = (value - high.astype(F32)).astype(BF)
 
 
-def band_kernel(cols, lat_taps, lon_taps, centre, centre_back, side, side_back):
-    k = lax.broadcasted_iota(jnp.int32, (cols, centre.shape[1]), 1)
-    j = lax.broadcasted_iota(jnp.int32, (cols, centre.shape[1]), 0)
+def band_kernel(cols, flip, lat_taps, lon_taps, *refs):
+    wide, narrow = refs[-2:]
+    k = lax.broadcasted_iota(jnp.int32, (cols, wide.shape[1]), 1)
+    j = lax.broadcasted_iota(jnp.int32, (cols, wide.shape[1]), 0)
     row, shift = k // cols, k % cols - j + HALO
-    k2 = lax.broadcasted_iota(jnp.int32, (16, side.shape[1]), 1)
-    j2 = lax.broadcasted_iota(jnp.int32, (16, side.shape[1]), 0)
-    half = side.shape[1] // 2
+    k2 = lax.broadcasted_iota(jnp.int32, (16, narrow.shape[1]), 1)
+    j2 = lax.broadcasted_iota(jnp.int32, (16, narrow.shape[1]), 0)
+    half = narrow.shape[1] // 2
     in_west = k2 < half
     row2 = jnp.where(in_west, k2, k2 - half) // HALO
     column = k2 % HALO
     target = jnp.where(j2 < 8, j2, j2 + cols - 16)
     shift2 = jnp.where(in_west, column, column + cols + HALO) - target
-    for flip, wide, narrow in ((False, centre, side), (True, centre_back, side_back)):
-        across = taps_at(shift, lon_taps, flip)
-        across2 = taps_at(shift2, lon_taps, flip)
-        for i in range(ROWS):
-            put_halves(wide, i * cols, taps_at(row - i, lat_taps, flip) * across)
-            put_halves(narrow, i * 16, taps_at(row2 - i, lat_taps, flip) * across2)
-
-
-def bands(lat_taps, lon_taps, cols):
+    across = taps_at(shift, lon_taps, flip)
+    across2 = taps_at(shift2, lon_taps, flip)
+    for i in range(ROWS):
+        put_halves(wide, i * cols, taps_at(row - i, lat_taps, flip) * across)
+        put_halves(narrow, i * 16, taps_at(row2 - i, lat_taps, flip) * across2)
+
+
+def bands(lat_taps, lon_taps, cols, flip, *after):
     span = ROWS + 2 * HALO
     wide = jax.ShapeDtypeStruct((2 * ROWS * cols, span * cols), BF)
     narrow = jax.ShapeDtypeStruct((2 * ROWS * 16, 2 * span * HALO), BF)
     return pl.pallas_call(
-        functools.partial(band_kernel, cols),
-        out_shape=(wide, wide, narrow, narrow),
-        in_specs=[SMEM, SMEM],
-        out_specs=(VMEM,) * 4,
+        functools.partial(band_kernel, cols, flip),
+        out_shape=(wide, narrow),
+        in_specs=[SMEM, SMEM] + [VMEM] * len(after),
+        out_specs=(VMEM,) * 2,
         compiler_params=params(),
-        cost_estimate=cost(2_000_000, 1_200_000),
-        name="bands",
-    )(lat_taps, lon_taps)
+        cost_estimate=cost(2_000_000, 600_000),
+        name="bands_back" if flip else "bands",
+    )(lat_taps, lon_taps, *after)
 
 
 def south_north(first, second, rows):
@@ -137,25 +137,32 @@
     )(own, first, second, band)
 
 
-def beside(own, corner, member, row, cols, cells):
+def joined(strips, corners, out, members, cols, cells):
+    odd = is_odd("lon")
+    edge = HALO * HALO
     length = cells // cols * HALO
-    edge = HALO * HALO
-    lo = member * length + row // cols * HALO - edge
-    hi = lo + (ROWS + 2 * HALO) * HALO
-    parts = [own[max(lo, member * length) : min(hi, (member + 1) * length), :]]
-    if row == 0:
-        parts.insert(0, corner[2 * member * edge : (2 * member + 1) * edge, :])
-    if row + ROWS * cols == cells:
-        parts.append(corner[(2 * member + 1) * edge : (2 * member + 2) * edge, :])
-    return jnp.concatenate(parts, axis=0) if len(parts) > 1 else parts[0]
-
-
-def sides(band, strips, corners, pair, row, cols, cells):
-    odd = is_odd("lon")
+    for m in range(members):
+        at = m * (length + 2 * edge)
+        for place, refs, start, size in (
+            (at, corners, 2 * m * edge, edge),
+            (at + edge, strips, m * length, length),
+            (at + edge + length, corners, (2 * m + 1) * edge, edge),
+        ):
+            one, two = (ref[start : start + size, :] for ref in refs)
+            out[0][place : place + size, :] = jnp.where(odd, one, two)
+            out[1][place : place + size, :] = jnp.where(odd, two, one)
+
+
+def side_rows(cells, cols):
+    return (cells // cols + 2 * HALO) * HALO
+
+
+def sides(band, west, east, pair, block, stride):
+    count = (ROWS + 2 * HALO) * HALO
     parts = []
     for m in pair:
-        one, two = (beside(own, corner, m, row, cols, cells) for own, corner in zip(strips, corners))
-        parts.append(jnp.concatenate([jnp.where(odd, one, two), jnp.where(odd, two, one)], axis=0))
+        at = pl.ds(pl.multiple_of(m * stride + block * ROWS * HALO, 32), count)
+        parts.append(jnp.concatenate([west[at, :], east[at, :]], axis=0))
     both = jnp.dot(band[...], jnp.concatenate(parts, axis=1), preferred_element_type=F32)
     size = both.shape[0] // 2
     both = both[:size] + both[size:]
@@ -172,46 +179,32 @@
     ).reshape(ROWS * cols, levels)
 
 
-def forward_kernel(cols, inner, first, second, first_corner, second_corner, band, vertical, ensemble, keep, send):
+def half_forward(cols, half, inner, west, east, band, vertical, ensemble, out):
     members, cells, levels = inner.shape
     size = ROWS * cols
-    blocks = cells // size
-    core = lax.axis_index("core")
-    for block in range(blocks):
-        row = block * size
-        rows = slice(row, row + size)
+    count = cells // size // 2
+    stride = side_rows(cells, cols)
+    for n in range(count):
+        block = half * count + n
+        rows = pl.ds(pl.multiple_of(block * size, size), size)
         increment = jnp.zeros((size, levels), F32)
         for start in range(0, members, 2):
             pair = (start, start + 1)
-            for m, side in zip(pair, sides(band, (first, second), (first_corner, second_corner), pair, row, cols, cells)):
+            for m, side in zip(pair, sides(band, west, east, pair, block, stride)):
                 smoothed = with_sides(inner[m, rows, :], side, cols).astype(BF)
                 leveled = jnp.dot(smoothed, vertical[...], preferred_element_type=F32)
                 increment = increment + ensemble[m, rows, :].astype(F32) * leveled
-        half, at = block // (blocks // 2), block % (blocks // 2)
-        place = slice(at * size, (at + 1) * size)
-        increment = increment.astype(BF)
-
-        @pl.when(core == half)
-        def _():
-            keep[place, :] = increment
-
-        @pl.when(core != half)
-        def _():
-            send[place, :] = increment
-
-
-def forward(inner, strips, corners, band, vertical, ensemble, cols):
-    members, cells, levels = inner.shape
-    half = jax.ShapeDtypeStruct((cells // 2, levels), BF)
-    return pl.pallas_call(
-        functools.partial(forward_kernel, cols),
-        out_shape=(half, half),
-        in_specs=[VMEM] * 8,
-        out_specs=(VMEM,) * 2,
-        compiler_params=params(),
-        cost_estimate=cost(1_500_000_000, 7_000_000),
-        name="forward",
-    )(inner, *strips, *corners, band, vertical, ensemble)
+        out[n * size : (n + 1) * size, :] = increment.astype(BF)
+
+
+def send_kernel(cols, inner, one, two, one_corner, two_corner, band, vertical, ensemble, out, west, east):
+    members, cells, _ = inner.shape
+    joined((one, two), (one_corner, two_corner), (west, east), members, cols, cells)
+    half_forward(cols, 1 - lax.axis_index("core"), inner, west, east, band, vertical, ensemble, out)
+
+
+def keep_kernel(cols, inner, west, east, band, vertical, ensemble, out):
+    half_forward(cols, lax.axis_index("core"), inner, west, east, band, vertical, ensemble, out)
 
 
 def put_sums(message, sums):
@@ -243,6 +236,16 @@
         cost_estimate=cost(flops, size),
         name=name,
     )(*inputs)
+
+
+def edges_kernel(tile, first, second):
+    members, cells, _ = tile.shape
+    edge = first.shape[0] // members
+    odd = is_odd("lat")
+    for m in range(members):
+        low, high = tile[m, :edge, :], tile[m, cells - edge :, :]
+        first[m * edge : (m + 1) * edge, :] = jnp.where(odd, low, high)
+        second[m * edge : (m + 1) * edge, :] = jnp.where(odd, high, low)
 
 
 def picker(lat_rows, cols):
@@ -327,7 +330,7 @@
     put_sums(message, jnp.sum(square[...], axis=0, keepdims=True))
 
 
-def weight_kernel(message, other, precision, out):
+def weight_kernel(message, other, precision, _, out):
     size = precision.shape[0] // 8
     share = lax.axis_index("core") * 4 + lax.axis_index("x")
     mine = precision[pl.ds(pl.multiple_of(share * size, size), size), :]
@@ -344,43 +347,60 @@
     put_sums(out, (get_sums(zero) + get_sums(one)) + (get_sums(two) + get_sums(three)))
 
 
-def level_kernel(mine, other, ensemble, vertical, adjoint, first, second, sums):
-    members, cells, levels = adjoint.shape
+def adjoint_of(ensemble, weighted, vertical):
+    return lax.dot_general(
+        (ensemble.astype(F32) * weighted).astype(BF),
+        vertical[...],
+        (((1,), (1,)), ((), ())),
+        preferred_element_type=F32,
+    ).astype(BF)
+
+
+def level_edges_kernel(mine, other, ensemble, vertical, first, second):
+    members, cells, _ = ensemble.shape
     share = cells // 8
     edge = (first.shape[0] - EXTRA) // members
-    core = lax.axis_index("core")
-    for which, half in ((mine, core), (other, 1 - core)):
-        for k in range(4):
-            rows = pl.ds(pl.multiple_of((half * 4 + share_of(k)) * share, share), share)
-            w = which[k * share : (k + 1) * share, :].astype(F32)
-            for m in range(members):
-                part = (ensemble[m, rows, :].astype(F32) * w).astype(BF)
-                adjoint[m, rows, :] = lax.dot_general(
-                    part, vertical[...], (((1,), (1,)), ((), ())), preferred_element_type=F32
-                ).astype(BF)
-    odd = is_odd("lat")
+    core, odd = lax.axis_index("core"), is_odd("lat")
+    south = pl.ds(pl.multiple_of(share_of(0) * share, edge), edge)
+    north = pl.ds(pl.multiple_of(share_of(3) * share + share - edge, edge), edge)
+    low_weight = jnp.where(core == 0, mine[south, :], other[south, :]).astype(F32)
+    high_weight = jnp.where(core == 0, other[north, :], mine[north, :]).astype(F32)
     for m in range(members):
-        low, high = adjoint[m, :edge, :], adjoint[m, cells - edge :, :]
+        low = adjoint_of(ensemble[m, :edge, :], low_weight, vertical)
+        high = adjoint_of(ensemble[m, cells - edge :, :], high_weight, vertical)
         first[m * edge : (m + 1) * edge, :] = jnp.where(odd, low, high)
         second[m * edge : (m + 1) * edge, :] = jnp.where(odd, high, low)
     value = get_sums(mine) + get_sums(other)
     put_sums(first, value)
     put_sums(second, value)
-    sums[...] = jnp.broadcast_to(value, sums.shape)
+
+
+def level_kernel(mine, other, ensemble, vertical, adjoint, sums):
+    sums[...] = jnp.broadcast_to(get_sums(mine) + get_sums(other), sums.shape)
+    members, cells, _ = adjoint.shape
+    share = cells // 8
+    core = lax.axis_index("core")
+    for which, half in ((mine, core), (other, 1 - core)):
+        for k in range(4):
+            rows = pl.ds(pl.multiple_of((half * 4 + share_of(k)) * share, share), share)
+            weighted = which[k * share : (k + 1) * share, :].astype(F32)
+            for m in range(members):
+                adjoint[m, rows, :] = adjoint_of(ensemble[m, rows, :], weighted, vertical)
 
 
 def backward_kernel(
-    cols, entries, inner, first, second, first_corner, second_corner, band, control, sums, far,
-    hessian, curvature, result, done,
+    cols, entries, inner, one, two, one_corner, two_corner, band, control, sums, far,
+    hessian, curvature, result, west, east, done,
 ):
     members, cells, levels = inner.shape
     size = ROWS * cols
+    joined((one, two), (one_corner, two_corner), (west, east), members, cols, cells)
     copies = []
     for start in range(0, members, 2):
         pair = (start, start + 1)
         for row in range(0, cells, size):
             rows = slice(row, row + size)
-            for m, side in zip(pair, sides(band, (first, second), (first_corner, second_corner), pair, row, cols, cells)):
+            for m, side in zip(pair, sides(band, west, east, pair, row // size, side_rows(cells, cols))):
                 result[m, rows, :] = control[m, rows, :].astype(F32) + with_sides(inner[m, rows, :], side, cols)
             if (row + size) % (cells // 4) == 0:
                 for m in pair:
@@ -390,7 +410,7 @@
                     )
                     copy.start()
                     copies.append(copy)
-    value = (sums[0:1, :] + get_sums(first_corner)) + (far[0:1, :] + get_sums(second_corner))
+    value = (sums[0:1, :] + get_sums(one_corner)) + (far[0:1, :] + get_sums(two_corner))
     curvature[0, 0] = jnp.sum(value) / entries
     for copy in copies:
         copy.wait()
@@ -411,30 +431,50 @@
     def rows(count):
         return jax.ShapeDtypeStruct((count, levels), BF)
 
-    odd = is_odd("lat")
-    low, high = control[:, :HALO].reshape(-1, levels), control[:, tile_rows - HALO :].reshape(-1, levels)
-    one, two = exchange(jnp.where(odd, low, high), jnp.where(odd, high, low), "lat")
+    edge = HALO * cols
+    first, second = call(edges_kernel, "edges", [rows(members * edge)] * 2, (own,))
+    one, two = exchange(first, second, "lat")
     beside_it = exchange(*strips(own, cols), "lon")
     corner = exchange(*corners(one, two, cols, members), "lon")
-    band, band_back, band_side, band_side_back = bands(lat_taps, lon_taps, cols)
+    band, band_side = bands(lat_taps, lon_taps, cols, False)
     inner, square = centre(own, one, two, band, cols, True)
-    keep, send = forward(inner, beside_it, corner, band_side, vertical, spread, cols)
+    joint = rows(members * side_rows(cells, cols))
+    send, west, east = call(
+        functools.partial(send_kernel, cols),
+        "forward_send",
+        [rows(cells // 2), joint, joint],
+        (inner, *beside_it, *corner, band_side, vertical, spread),
+        flops=700_000_000,
+        size=3_000_000,
+    )
+    (keep,) = call(
+        functools.partial(keep_kernel, cols),
+        "forward_keep",
+        [rows(cells // 2)],
+        (inner, west, east, band_side, vertical, spread),
+        flops=700_000_000,
+        size=3_000_000,
+    )
 
     got = lax.ppermute(send, "core", swap("core", 1))
     zero, one, two, three = call(shares_kernel, "shares", [rows(share)] * 4, (keep, got))
     two, one, three = [lax.ppermute(v, "x", swap("x", k)) for v, k in ((two, 2), (one, 1), (three, 3))]
+    band_back, band_side_back = bands(lat_taps, lon_taps, cols, True, three)
     (message,) = call(part_kernel, "part", [rows(share + EXTRA)], (zero, one, two, three, square))
     other = lax.ppermute(message, "zh", swap("zh", 1))
-    (zero,) = call(weight_kernel, "weight", [rows(share + EXTRA)], (message, other, precision.reshape(cells, levels)))
+    (zero,) = call(weight_kernel, "weight", [rows(share + EXTRA)], (message, other, precision.reshape(cells, levels), band_side_back))
     two, one, three = [lax.ppermute(zero, "x", swap("x", k)) for k in (2, 1, 3)]
     (message,) = call(gather_kernel, "gather", [rows(cells // 2 + EXTRA)], (zero, one, two, three))
     other = lax.ppermute(message, "core", swap("core", 1))
 
-    edge = rows(members * HALO * cols + EXTRA)
-    adjoint, first, second, sums = call(
+    message_shape = rows(members * edge + EXTRA)
+    first, second = call(
+        level_edges_kernel, "level_edges", [message_shape, message_shape], (message, other, spread, vertical)
+    )
+    adjoint, sums = call(
         level_kernel,
         "level",
-        [jax.ShapeDtypeStruct(own.shape, BF), edge, edge, row],
+        [jax.ShapeDtypeStruct(own.shape, BF), row],
         (message, other, spread, vertical),
         flops=300_000_000,
         size=4_500_000,
@@ -451,7 +491,12 @@
         "backward",
         [jax.ShapeDtypeStruct(own.shape, F32), jax.ShapeDtypeStruct((1, 1), F32)],
         (inner, *beside_it, *corner, band_side_back, own, sums, far),
-        scratch=(pltpu.VMEM(own.shape, F32), pltpu.SemaphoreType.DMA((4 * members,))),
+        scratch=(
+            pltpu.VMEM(own.shape, F32),
+            pltpu.VMEM((members * side_rows(cells, cols), levels), BF),
+            pltpu.VMEM((members * side_rows(cells, cols), levels), BF),
+            pltpu.SemaphoreType.DMA((4 * members,)),
+        ),
         out_specs=(pl.BlockSpec(memory_space=pl.ANY), SMEM),
         flops=1_000_000_000,
         size=9_000_000,

time: 75.3 us -> 72.7 us (0.965)
  waiting for transfers between devices: 20.7 us -> 19.4 us
  Pallas kernels: 14.4 us -> 13.4 us
  other arithmetic: 1 us -> 0 us
    pallas_call x2, Pallas kernels: 4.45 us -> 1.51 us  [bands(): pl.pallas_call(functools.partial(band_kernel, cols, flip), out_shape=(wid...]
    pallas_call x10 -> x14, Pallas kernels: 5.19 us -> 7.25 us  [call(): pl.pallas_call(kernel, out_shape=tuple(shapes), in_specs=in_specs or [VME...]
    select_n x1 -> x0, other arithmetic: 1 us -> none  [per_device(): jnp.where(odd, high, low)]
    ppermute x1, waiting for transfers between devices: 1.52 us -> 0.65 us  [per_device(): got = lax.ppermute(send, 'core', swap('core', 1))]
    ppermute x1, waiting for transfers between devices: 3.1 us -> 2.34 us  [per_device(): other = lax.ppermute(message, 'zh', swap('zh', 1))]
  transfers between devices with their start and end apart: 23 -> 23, of which waited for: 12 -> 13; matrix products, arithmetic and copies ran while one was open for 0% -> 0% of each run, Pallas kernels for 9% -> 12%
where the time goes in v4:
time: 72.7 us; the launch traced here: 72.6 us
  starting transfers between devices  37.1 us (51%)
  waiting for transfers between devices  19.4 us (27%)
  Pallas kernels  13.4 us (18%)
  local copies, waits for them, and re-layouts  1.62 us (2%)
  between operations  1.01 us (1%)
    ppermute x6, starting transfers between devices, exchange(): lax.ppermute(second, axis, swap(axis, 3))  13.8 us
    ppermute x6, starting transfers between devices, exchange(): lax.ppermute(first, axis, swap(axis, 1))  7.62 us
    pallas_call x14, Pallas kernels, call(): pl.pallas_call(kernel, out_shape=tuple(shapes), in_specs=in_specs or [VME...  7.25 us
    ppermute x1, starting transfers between devices, per_device(): other = lax.ppermute(message, 'zh', swap('zh', 1))  5.3 us
    ppermute x3, starting transfers between devices, per_device(): two, one, three = [lax.ppermute(zero, 'x', swap('x', k)) for k in (2, 1, 3)]  4.77 us
    pallas_call x2, Pallas kernels, centre(): pl.pallas_call(functools.partial(centre_kernel, cols, with_square), out_s...  4.68 us
    ppermute x6, waiting for transfers between devices, exchange(): lax.ppermute(second, axis, swap(axis, 3))  4.39 us
    ppermute x3, waiting for transfers between devices, per_device(): two, one, three = [lax.ppermute(zero, 'x', swap('x', k)) for k in (2, 1, 3)]  4.31 us
  transfers between devices with their start and end apart: 23, of which 13 were waited for; matrix products, arithmetic and copies ran while one was open for 0% of the time, Pallas kernels for 12%

profile of v4, /device:TPU:2, one launch (start us, length us, event | category | flops | bytes accessed | tf_op | source)
XLA Modules:
  0.0 72.6 jit_solution(17904519379133227410)
XLA Ops:
  0.7 1.6 %copy-done.1 = bf16[4,64,32,128]{3,2,1,0:T(8,128)(2,1)S(1)} copy-done((bf16[4,64,32,128]{3,2,1,0:T(8,128)(2,1)S(1)}, bf16[4,64,32,128]{3,2,1,0:T(8,128)(2,1)}, u32[]{:S(2)}) %copy-start.1) | copy-done | bytes 2097176
  2.3 2.0 %collective-permute-start = (bf16[512,128]{1,0:T(8,128)(2,1)S(1)}, bf16[512,128]{1,0:T(8,128)(2,1)S(1)}, u32[]{:S(2)}, u32[]{:S(2)}) collective-permute-start(bf16[512,128]{1,0:T(8,128)(2,1)S(1)} %get-tuple-element.32), channel_id=1, source_target_pairs={{0,4},{4,0},{8,12},{12,8},{1,5},{5,1},{9,13},{13,9},{2,6},{6,2},{1... | collective-permute-start | bytes 393224 | tf_op jit(solution)/shard_map/ppermute | solution.py:420
  4.3 2.8 %collective-permute-start.1 = (bf16[512,128]{1,0:T(8,128)(2,1)S(1)}, bf16[512,128]{1,0:T(8,128)(2,1)S(1)}, u32[]{:S(2)}, u32[]{:S(2)}) collective-permute-start(bf16[512,128]{1,0:T(8,128)(2,1)S(1)} %get-tuple-element.33), channel_id=1, source_target_pairs={{0,12},{4,8},{8,4},{12,0},{1,13},{5,9},{9,5},{13,1},{2,14},{6,10},... | collective-permute-start | bytes 393224 | tf_op jit(solution)/shard_map/ppermute | solution.py:420
  7.1 0.5 strips.2
  7.6 1.7 %collective-permute-start.2 = (bf16[1024,128]{1,0:T(8,128)(2,1)S(1)}, bf16[1024,128]{1,0:T(8,128)(2,1)S(1)}, u32[]{:S(2)}, u32[]{:S(2)}) collective-permute-start(bf16[1024,128]{1,0:T(8,128)(2,1)S(1)} %get-tuple-element.36), channel_id=1, source_target_pairs={{0,1},{1,0},{2,3},{3,2},{4,5},{5,4},{6,7},{7,6},{8,9},{9,8},{10,11... | collective-permute-start | bytes 786440 | tf_op jit(solution)/shard_map/ppermute | solution.py:420
  9.3 2.2 %collective-permute-start.3 = (bf16[1024,128]{1,0:T(8,128)(2,1)S(1)}, bf16[1024,128]{1,0:T(8,128)(2,1)S(1)}, u32[]{:S(2)}, u32[]{:S(2)}) collective-permute-start(bf16[1024,128]{1,0:T(8,128)(2,1)S(1)} %get-tuple-element.37), channel_id=1, source_target_pairs={{0,3},{1,2},{2,1},{3,0},{4,7},{5,6},{6,5},{7,4},{8,11},{9,10},{10,... | collective-permute-start | bytes 786440 | tf_op jit(solution)/shard_map/ppermute | solution.py:420
  11.4 0.8 %bands.1 = (bf16[512,512]{1,0:T(8,128)(2,1)S(1)}, bf16[256,128]{1,0:T(8,128)(2,1)S(1)}) custom-call(f32[9]{0:T(128)S(1)} %copy-done.5, f32[9]{0:T(128)S(1)} %copy-done.6), custom_call_target="tpu_custom_call" | custom-call | flops 2000000 | bytes 600000 | tf_op jit(solution)/shard_map/bands/pallas_call | solution.py:76
  12.2 1.2 %collective-permute-done.1.second = bf16[512,128]{1,0:T(8,128)(2,1)S(1)} collective-permute-done((bf16[512,128]{1,0:T(8,128)(2,1)S(1)}, bf16[512,128]{1,0:T(8,128)(2,1)S(1)}, u32[]{:S(2)}, u32[]{:S(2)}) %collective-permute-start.1) | collective-permute-done | bytes 131104 | tf_op jit(solution)/shard_map/ppermute | solution.py:420
  13.4 0.2 corners.2
  13.6 1.7 %collective-permute-start.4 = (bf16[128,128]{1,0:T(8,128)(2,1)S(1)}, bf16[128,128]{1,0:T(8,128)(2,1)S(1)}, u32[]{:S(2)}, u32[]{:S(2)}) collective-permute-start(bf16[128,128]{1,0:T(8,128)(2,1)S(1)} %get-tuple-element.38), channel_id=1, source_target_pairs={{0,1},{1,0},{2,3},{3,2},{4,5},{5,4},{6,7},{7,6},{8,9},{9,8},{10,11... | collective-permute-start | bytes 98312 | tf_op jit(solution)/shard_map/ppermute | solution.py:420
  15.3 2.2 %collective-permute-start.5 = (bf16[128,128]{1,0:T(8,128)(2,1)S(1)}, bf16[128,128]{1,0:T(8,128)(2,1)S(1)}, u32[]{:S(2)}, u32[]{:S(2)}) collective-permute-start(bf16[128,128]{1,0:T(8,128)(2,1)S(1)} %get-tuple-element.39), channel_id=1, source_target_pairs={{0,3},{1,2},{2,1},{3,0},{4,7},{5,6},{6,5},{7,4},{8,11},{9,10},{10,... | collective-permute-start | bytes 98312 | tf_op jit(solution)/shard_map/ppermute | solution.py:420
  17.5 2.3 %centre_forward.1 = (f32[4,2048,128]{2,1,0:T(8,128)S(1)}, f32[8,128]{1,0:T(8,128)S(1)}) custom-call(bf16[4,2048,128]{2,1,0:T(8,128)(2,1)S(1)} %bitcast.11, bf16[512,128]{1,0:T(8,128)(2,1)S(1)} %collective-permute-done.first, bf16[512,128]{1,0:T(8,128)(2,1)S(1)} %collective-permute-done.1.second, bf16[512,512]{1,0:T(8,128)(2,1)S(1)} %get-tuple-element.34.band), custom_call_target="tpu_custom_call" | custom-call | flops 3000000000 | bytes 7000000 | tf_op jit(solution)/shard_map/centre_forward/pallas_call | solution.py:129
  19.8 0.6 collective-permute-done.5.two_corner
  20.4 0.9 %forward_send.1 = (bf16[1024,128]{1,0:T(8,128)(2,1)S(1)}, bf16[1152,128]{1,0:T(8,128)(2,1)S(1)}, bf16[1152,128]{1,0:T(8,128)(2,1)S(1)}) custom-call(f32[4,2048,128]{2,1,0:T(8,128)S(1)} %get-tuple-element.35.inner, bf16[1024,128]{1,0:T(8,128)(2,1)S(1)} %collective-permute-done.2.one, bf16[1024,128]{1,0:T(8,128)(2,1)S(1)} %collective-permute-done.3.two, ...), custom_call_target="tpu_custom_call" | custom-call | flops 700000000 | bytes 3000000 | tf_op jit(solution)/shard_map/forward_send/pallas_call | solution.py:229
  21.4 0.1 collective-permute-start.6
  21.5 0.9 %forward_keep.1.keep = bf16[1024,128]{1,0:T(8,128)(2,1)S(1)} custom-call(f32[4,2048,128]{2,1,0:T(8,128)S(1)} %get-tuple-element.35.inner, bf16[1152,128]{1,0:T(8,128)(2,1)S(1)} %get-tuple-element.41.west, bf16[1152,128]{1,0:T(8,128)(2,1)S(1)} %get-tuple-element.42.east, bf16[256,128]{1,0:T(8,128)(2,1)S(1)} %get-tuple-element.40.band, ...), custom_call_target="tpu_custom_call" | custom-call | flops 700000000 | bytes 3000000 | tf_op jit(solution)/shard_map/forward_keep/pallas_call | solution.py:229
  22.3 0.7 collective-permute-done.6.got
  23.0 0.6 collective-permute-start.7
  23.7 2.4 %collective-permute-start.8 = (bf16[256,128]{1,0:T(8,128)(2,1)S(1)}, bf16[256,128]{1,0:T(8,128)(2,1)S(1)}, u32[]{:S(2)}, u32[]{:S(2)}) collective-permute-start(bf16[256,128]{1,0:T(8,128)(2,1)S(1)} %get-tuple-element.46), channel_id=1, source_target_pairs={{0,64},{32,96},{64,0},{96,32},{1,65},{33,97},{65,1},{97,33},{2,66}... | collective-permute-start | bytes 196616 | tf_op jit(solution)/shard_map/ppermute | solution.py:461
  26.1 0.5 collective-permute-start.9
  26.6 0.8 %collective-permute-done.7.one = bf16[256,128]{1,0:T(8,128)(2,1)S(1)} collective-permute-done((bf16[256,128]{1,0:T(8,128)(2,1)S(1)}, bf16[256,128]{1,0:T(8,128)(2,1)S(1)}, u32[]{:S(2)}, u32[]{:S(2)}) %collective-permute-start.7) | collective-permute-done | bytes 65568 | tf_op jit(solution)/shard_map/ppermute | solution.py:461
  27.4 2.4 %collective-permute-done.8.two = bf16[256,128]{1,0:T(8,128)(2,1)S(1)} collective-permute-done((bf16[256,128]{1,0:T(8,128)(2,1)S(1)}, bf16[256,128]{1,0:T(8,128)(2,1)S(1)}, u32[]{:S(2)}, u32[]{:S(2)}) %collective-permute-start.8) | collective-permute-done | bytes 65568 | tf_op jit(solution)/shard_map/ppermute | solution.py:461
  29.8 0.9 %collective-permute-done.9.three.refs_0_ = bf16[256,128]{1,0:T(8,128)(2,1)S(1)} collective-permute-done((bf16[256,128]{1,0:T(8,128)(2,1)S(1)}, bf16[256,128]{1,0:T(8,128)(2,1)S(1)}, u32[]{:S(2)}, u32[]{:S(2)}) %collective-permute-start.9) | collective-permute-done | bytes 65568 | tf_op jit(solution)/shard_map/ppermute | solution.py:461
  30.8 5.3 %collective-permute-start.10 = (bf16[272,128]{1,0:T(8,128)(2,1)S(1)}, bf16[272,128]{1,0:T(8,128)(2,1)S(1)}, u32[]{:S(2)}, u32[]{:S(2)}) collective-permute-start(bf16[272,128]{1,0:T(8,128)(2,1)S(1)} %part.1.message), channel_id=1, source_target_pairs={{0,128},{128,0},{1,129},{129,1},{2,130},{130,2},{3,131},{131,3},{4... | collective-permute-start | bytes 208904 | tf_op jit(solution)/shard_map/ppermute | solution.py:464
  36.1 0.8 %bands_back.1 = (bf16[512,512]{1,0:T(8,128)(2,1)S(1)}, bf16[256,128]{1,0:T(8,128)(2,1)S(1)}) custom-call(f32[9]{0:T(128)S(1)} %copy-done.5, f32[9]{0:T(128)S(1)} %copy-done.6, bf16[256,128]{1,0:T(8,128)(2,1)S(1)} %collective-permute-done.9.three.refs_0_), custom_call_target="tpu_custom_call" | custom-call | flops 2000000 | bytes 600000 | tf_op jit(solution)/shard_map/bands_back/pallas_call | solution.py:76
  36.9 2.3 %collective-permute-done.10.other = bf16[272,128]{1,0:T(8,128)(2,1)S(1)} collective-permute-done((bf16[272,128]{1,0:T(8,128)(2,1)S(1)}, bf16[272,128]{1,0:T(8,128)(2,1)S(1)}, u32[]{:S(2)}, u32[]{:S(2)}) %collective-permute-start.10) | collective-permute-done | bytes 69664 | tf_op jit(solution)/shard_map/ppermute | solution.py:464
  39.3 1.2 %collective-permute-start.13 = (bf16[272,128]{1,0:T(8,128)(2,1)S(1)}, bf16[272,128]{1,0:T(8,128)(2,1)S(1)}, u32[]{:S(2)}, u32[]{:S(2)}) collective-permute-start(bf16[272,128]{1,0:T(8,128)(2,1)S(1)} %weight.1.zero), channel_id=1, source_target_pairs={{0,96},{32,64},{64,32},{96,0},{1,97},{33,65},{65,33},{97,1},{2,98}... | collective-permute-start | bytes 208904 | tf_op jit(solution)/shard_map/ppermute | solution.py:466
  40.5 3.6 %collective-permute-start.12 = (bf16[272,128]{1,0:T(8,128)(2,1)S(1)}, bf16[272,128]{1,0:T(8,128)(2,1)S(1)}, u32[]{:S(2)}, u32[]{:S(2)}) collective-permute-start(bf16[272,128]{1,0:T(8,128)(2,1)S(1)} %weight.1.zero), channel_id=1, source_target_pairs={{0,64},{32,96},{64,0},{96,32},{1,65},{33,97},{65,1},{97,33},{2,66}... | collective-permute-start | bytes 208904 | tf_op jit(solution)/shard_map/ppermute | solution.py:466
  44.0 2.3 %collective-permute-done.12.two = bf16[272,128]{1,0:T(8,128)(2,1)S(1)} collective-permute-done((bf16[272,128]{1,0:T(8,128)(2,1)S(1)}, bf16[272,128]{1,0:T(8,128)(2,1)S(1)}, u32[]{:S(2)}, u32[]{:S(2)}) %collective-permute-start.12) | collective-permute-done | bytes 69664 | tf_op jit(solution)/shard_map/ppermute | solution.py:466
  46.3 2.0 %collective-permute-done.11.one = bf16[272,128]{1,0:T(8,128)(2,1)S(1)} collective-permute-done((bf16[272,128]{1,0:T(8,128)(2,1)S(1)}, bf16[272,128]{1,0:T(8,128)(2,1)S(1)}, u32[]{:S(2)}, u32[]{:S(2)}) %collective-permute-start.11) | collective-permute-done | bytes 69664 | tf_op jit(solution)/shard_map/ppermute | solution.py:466
  48.5 1.5 %collective-permute-done.14.other = bf16[1040,128]{1,0:T(8,128)(2,1)S(1)} collective-permute-done((bf16[1040,128]{1,0:T(8,128)(2,1)S(1)}, bf16[1040,128]{1,0:T(8,128)(2,1)S(1)}, u32[]{:S(2)}, u32[]{:S(2)}) %collective-permute-start.14) | collective-permute-done | bytes 266272 | tf_op jit(solution)/shard_map/ppermute | solution.py:468
  50.0 0.3 level_edges.1
  50.3 0.7 collective-permute-start.15
  51.0 3.4 %collective-permute-start.16 = (bf16[528,128]{1,0:T(8,128)(2,1)S(1)}, bf16[528,128]{1,0:T(8,128)(2,1)S(1)}, u32[]{:S(2)}, u32[]{:S(2)}) collective-permute-start(bf16[528,128]{1,0:T(8,128)(2,1)S(1)} %get-tuple-element.52), channel_id=1, source_target_pairs={{0,12},{4,8},{8,4},{12,0},{1,13},{5,9},{9,5},{13,1},{2,14},{6,10},... | collective-permute-start | bytes 405512 | tf_op jit(solution)/shard_map/ppermute | solution.py:420
  54.4 0.7 level.1
  55.2 0.1 collective-permute-start.19
  55.3 0.5 strips.3
  55.7 0.2 collective-permute-start.17
  55.9 2.2 %collective-permute-start.18 = (bf16[1024,128]{1,0:T(8,128)(2,1)S(1)}, bf16[1024,128]{1,0:T(8,128)(2,1)S(1)}, u32[]{:S(2)}, u32[]{:S(2)}) collective-permute-start(bf16[1024,128]{1,0:T(8,128)(2,1)S(1)} %get-tuple-element.55), channel_id=1, source_target_pairs={{0,3},{1,2},{2,1},{3,0},{4,7},{5,6},{6,5},{7,4},{8,11},{9,10},{10,... | collective-permute-start | bytes 786440 | tf_op jit(solution)/shard_map/ppermute | solution.py:420
  58.1 2.1 %collective-permute-done.19.refs_1_ = f32[8,128]{1,0:T(8,128)S(1)} collective-permute-done((f32[8,128]{1,0:T(8,128)S(1)}, f32[8,128]{1,0:T(8,128)S(1)}, u32[]{:S(2)}, u32[]{:S(2)}) %collective-permute-start.19) | collective-permute-done | bytes 4128 | tf_op jit(solution)/shard_map/ppermute | solution.py:483
  60.2 0.8 %collective-permute-done.16.second = bf16[528,128]{1,0:T(8,128)(2,1)S(1)} collective-permute-done((bf16[528,128]{1,0:T(8,128)(2,1)S(1)}, bf16[528,128]{1,0:T(8,128)(2,1)S(1)}, u32[]{:S(2)}, u32[]{:S(2)}) %collective-permute-start.16) | collective-permute-done | bytes 135200 | tf_op jit(solution)/shard_map/ppermute | solution.py:420
  61.0 0.2 corners.3
  61.2 1.8 %collective-permute-start.22 = (f32[8,128]{1,0:T(8,128)S(1)}, f32[8,128]{1,0:T(8,128)S(1)}, u32[]{:S(2)}, u32[]{:S(2)}) collective-permute-start(f32[8,128]{1,0:T(8,128)S(1)} %get-tuple-element.59.sums), channel_id=1, source_target_pairs={{0,2},{1,3},{2,0},{3,1},{4,6},{5,7},{6,4},{7,5},{8,10},{9,11},{10,... | collective-permute-start | bytes 12296 | tf_op jit(solution)/shard_map/ppermute | solution.py:487
  63.0 1.3 %collective-permute-start.20 = (bf16[144,128]{1,0:T(8,128)(2,1)S(1)}, bf16[144,128]{1,0:T(8,128)(2,1)S(1)}, u32[]{:S(2)}, u32[]{:S(2)}) collective-permute-start(bf16[144,128]{1,0:T(8,128)(2,1)S(1)} %get-tuple-element.57), channel_id=1, source_target_pairs={{0,1},{1,0},{2,3},{3,2},{4,5},{5,4},{6,7},{7,6},{8,9},{9,8},{10,11... | collective-permute-start | bytes 110600 | tf_op jit(solution)/shard_map/ppermute | solution.py:420
  64.3 1.1 %collective-permute-start.21 = (bf16[144,128]{1,0:T(8,128)(2,1)S(1)}, bf16[144,128]{1,0:T(8,128)(2,1)S(1)}, u32[]{:S(2)}, u32[]{:S(2)}) collective-permute-start(bf16[144,128]{1,0:T(8,128)(2,1)S(1)} %get-tuple-element.58), channel_id=1, source_target_pairs={{0,3},{1,2},{2,1},{3,0},{4,7},{5,6},{6,5},{7,4},{8,11},{9,10},{10,... | collective-permute-start | bytes 110600 | tf_op jit(solution)/shard_map/ppermute | solution.py:420
  65.4 2.3 %centre_back.1.inner = f32[4,2048,128]{2,1,0:T(8,128)S(1)} custom-call(bf16[4,2048,128]{2,1,0:T(8,128)(2,1)S(1)} %get-tuple-element.50.own.tile, bf16[528,128]{1,0:T(8,128)(2,1)S(1)} %collective-permute-done.15.first, bf16[528,128]{1,0:T(8,128)(2,1)S(1)} %collective-permute-done.16.second, bf16[512,512]{1,0:T(8,128)(2,1)S(1)} %get-tuple-element.53.band), custom_call_target="tpu_custom_call" | custom-call | flops 3000000000 | bytes 7000000 | tf_op jit(solution)/shard_map/centre_back/pallas_call | solution.py:129
  67.8 1.7 %collective-permute-done.21.two_corner = bf16[144,128]{1,0:T(8,128)(2,1)S(1)} collective-permute-done((bf16[144,128]{1,0:T(8,128)(2,1)S(1)}, bf16[144,128]{1,0:T(8,128)(2,1)S(1)}, u32[]{:S(2)}, u32[]{:S(2)}) %collective-permute-start.21) | collective-permute-done | bytes 36896 | tf_op jit(solution)/shard_map/ppermute | solution.py:420
  69.5 2.9 %backward.1 = (f32[4,2048,128]{2,1,0:T(8,128)}, f32[1,1]{1,0:T(1,128)}) custom-call(f32[4,2048,128]{2,1,0:T(8,128)S(1)} %centre_back.1.inner, bf16[1024,128]{1,0:T(8,128)(2,1)S(1)} %collective-permute-done.17.one, bf16[1024,128]{1,0:T(8,128)(2,1)S(1)} %collective-permute-done.18.two, bf16[144,128]{1,0:T(8,128)(2,1)S(1)} %collective-permute-done.20.one_corner, ...), custom_call_target="tpu_custom_call" | custom-call | flops 1000000000 | bytes 9000000 | tf_op jit(solution)/shard_map/backward/pallas_call | solution.py:229
  (30 shorter events, 0.4 us)
Async XLA Ops:
  0.6 10.8 %copy-start.6 = (f32[9]{0:T(128)S(1)}, f32[9]{0:T(128)}, u32[]{:S(2)}) copy-start(f32[9]{0:T(128)} %lon_taps.3) | copy-start | bytes 112
  0.6 10.8 %copy-start.5 = (f32[9]{0:T(128)S(1)}, f32[9]{0:T(128)}, u32[]{:S(2)}) copy-start(f32[9]{0:T(128)} %lat_taps.3) | copy-start | bytes 112
  0.6 1.6 %copy-start.1 = (bf16[4,64,32,128]{3,2,1,0:T(8,128)(2,1)S(1)}, bf16[4,64,32,128]{3,2,1,0:T(8,128)(2,1)}, u32[]{:S(2)}) copy-start(bf16[4,64,32,128]{3,2,1,0:T(8,128)(2,1)} %param.6) | copy-start | bytes 6291460
  2.3 15.2 %copy-start.2 = (bf16[4,64,32,128]{3,2,1,0:T(8,128)(2,1)S(1)}, bf16[4,64,32,128]{3,2,1,0:T(8,128)(2,1)}, u32[]{:S(2)}) copy-start(bf16[4,64,32,128]{3,2,1,0:T(8,128)(2,1)} %param.6) | copy-start | bytes 6291460
  2.3 9.9 %collective-permute-start = (bf16[512,128]{1,0:T(8,128)(2,1)S(1)}, bf16[512,128]{1,0:T(8,128)(2,1)S(1)}, u32[]{:S(2)}, u32[]{:S(2)}) collective-permute-start(bf16[512,128]{1,0:T(8,128)(2,1)S(1)} %get-tuple-element.32), channel_id=1, source_target_pairs={{0,4},{4,0},{8,12},{12,8},{1,5},{5,1},{9,13},{13,9},{2,6},{6,2},{1... | collective-permute-start | bytes 393224 | tf_op jit(solution)/shard_map/ppermute | solution.py:420
  4.3 9.1 %collective-permute-start.1 = (bf16[512,128]{1,0:T(8,128)(2,1)S(1)}, bf16[512,128]{1,0:T(8,128)(2,1)S(1)}, u32[]{:S(2)}, u32[]{:S(2)}) collective-permute-start(bf16[512,128]{1,0:T(8,128)(2,1)S(1)} %get-tuple-element.33), channel_id=1, source_target_pairs={{0,12},{4,8},{8,4},{12,0},{1,13},{5,9},{9,5},{13,1},{2,14},{6,10},... | collective-permute-start | bytes 393224 | tf_op jit(solution)/shard_map/ppermute | solution.py:420
  7.6 12.8 %collective-permute-start.2 = (bf16[1024,128]{1,0:T(8,128)(2,1)S(1)}, bf16[1024,128]{1,0:T(8,128)(2,1)S(1)}, u32[]{:S(2)}, u32[]{:S(2)}) collective-permute-start(bf16[1024,128]{1,0:T(8,128)(2,1)S(1)} %get-tuple-element.36), channel_id=1, source_target_pairs={{0,1},{1,0},{2,3},{3,2},{4,5},{5,4},{6,7},{7,6},{8,9},{9,8},{10,11... | collective-permute-start | bytes 786440 | tf_op jit(solution)/shard_map/ppermute | solution.py:420
  9.3 11.2 %collective-permute-start.3 = (bf16[1024,128]{1,0:T(8,128)(2,1)S(1)}, bf16[1024,128]{1,0:T(8,128)(2,1)S(1)}, u32[]{:S(2)}, u32[]{:S(2)}) collective-permute-start(bf16[1024,128]{1,0:T(8,128)(2,1)S(1)} %get-tuple-element.37), channel_id=1, source_target_pairs={{0,3},{1,2},{2,1},{3,0},{4,7},{5,6},{6,5},{7,4},{8,11},{9,10},{10,... | collective-permute-start | bytes 786440 | tf_op jit(solution)/shard_map/ppermute | solution.py:420
  13.6 6.2 %collective-permute-start.4 = (bf16[128,128]{1,0:T(8,128)(2,1)S(1)}, bf16[128,128]{1,0:T(8,128)(2,1)S(1)}, u32[]{:S(2)}, u32[]{:S(2)}) collective-permute-start(bf16[128,128]{1,0:T(8,128)(2,1)S(1)} %get-tuple-element.38), channel_id=1, source_target_pairs={{0,1},{1,0},{2,3},{3,2},{4,5},{5,4},{6,7},{7,6},{8,9},{9,8},{10,11... | collective-permute-start | bytes 98312 | tf_op jit(solution)/shard_map/ppermute | solution.py:420
  15.3 5.1 %collective-permute-start.5 = (bf16[128,128]{1,0:T(8,128)(2,1)S(1)}, bf16[128,128]{1,0:T(8,128)(2,1)S(1)}, u32[]{:S(2)}, u32[]{:S(2)}) collective-permute-start(bf16[128,128]{1,0:T(8,128)(2,1)S(1)} %get-tuple-element.39), channel_id=1, source_target_pairs={{0,3},{1,2},{2,1},{3,0},{4,7},{5,6},{6,5},{7,4},{8,11},{9,10},{10,... | collective-permute-start | bytes 98312 | tf_op jit(solution)/shard_map/ppermute | solution.py:420
  17.5 3.0 %copy-start = (bf16[4,64,32,128]{3,2,1,0:T(8,128)(2,1)S(1)}, bf16[4,64,32,128]{3,2,1,0:T(8,128)(2,1)}, u32[]{:S(2)}) copy-start(bf16[4,64,32,128]{3,2,1,0:T(8,128)(2,1)} %param.7) | copy-start | bytes 6291460
  17.5 3.0 %copy-start.4 = (bf16[128,128]{1,0:T(8,128)(2,1)S(1)}, bf16[128,128]{1,0:T(8,128)(2,1)}, u32[]{:S(2)}) copy-start(bf16[128,128]{1,0:T(8,128)(2,1)} %vertical.7) | copy-start | bytes 98308
  21.3 17.9 %copy-start.3 = (f32[64,32,128]{2,1,0:T(8,128)S(1)}, f32[64,32,128]{2,1,0:T(8,128)}, u32[]{:S(2)}) copy-start(f32[64,32,128]{2,1,0:T(8,128)} %param.8) | copy-start | bytes 3145732
  21.4 1.6 %collective-permute-start.6 = (bf16[1024,128]{1,0:T(8,128)(2,1)S(1)}, bf16[1024,128]{1,0:T(8,128)(2,1)S(1)}, u32[]{:S(2)}, u32[]{:S(2)}) collective-permute-start(bf16[1024,128]{1,0:T(8,128)(2,1)S(1)} %get-tuple-element.43), channel_id=1, source_target_pairs={{0,16},{16,0},{1,17},{17,1},{2,18},{18,2},{3,19},{19,3},{4,20},{20... | collective-permute-start | bytes 786440 | tf_op jit(solution)/shard_map/ppermute | solution.py:459
  23.0 4.4 %collective-permute-start.7 = (bf16[256,128]{1,0:T(8,128)(2,1)S(1)}, bf16[256,128]{1,0:T(8,128)(2,1)S(1)}, u32[]{:S(2)}, u32[]{:S(2)}) collective-permute-start(bf16[256,128]{1,0:T(8,128)(2,1)S(1)} %get-tuple-element.45), channel_id=1, source_target_pairs={{0,32},{32,0},{64,96},{96,64},{1,33},{33,1},{65,97},{97,65},{2,34}... | collective-permute-start | bytes 196616 | tf_op jit(solution)/shard_map/ppermute | solution.py:461
  23.7 6.2 %collective-permute-start.8 = (bf16[256,128]{1,0:T(8,128)(2,1)S(1)}, bf16[256,128]{1,0:T(8,128)(2,1)S(1)}, u32[]{:S(2)}, u32[]{:S(2)}) collective-permute-start(bf16[256,128]{1,0:T(8,128)(2,1)S(1)} %get-tuple-element.46), channel_id=1, source_target_pairs={{0,64},{32,96},{64,0},{96,32},{1,65},{33,97},{65,1},{97,33},{2,66}... | collective-permute-start | bytes 196616 | tf_op jit(solution)/shard_map/ppermute | solution.py:461
  26.1 4.7 %collective-permute-start.9 = (bf16[256,128]{1,0:T(8,128)(2,1)S(1)}, bf16[256,128]{1,0:T(8,128)(2,1)S(1)}, u32[]{:S(2)}, u32[]{:S(2)}) collective-permute-start(bf16[256,128]{1,0:T(8,128)(2,1)S(1)} %get-tuple-element.47), channel_id=1, source_target_pairs={{0,96},{32,64},{64,32},{96,0},{1,97},{33,65},{65,33},{97,1},{2,98}... | collective-permute-start | bytes 196616 | tf_op jit(solution)/shard_map/ppermute | solution.py:461
  30.8 8.4 %collective-permute-start.10 = (bf16[272,128]{1,0:T(8,128)(2,1)S(1)}, bf16[272,128]{1,0:T(8,128)(2,1)S(1)}, u32[]{:S(2)}, u32[]{:S(2)}) collective-permute-start(bf16[272,128]{1,0:T(8,128)(2,1)S(1)} %part.1.message), channel_id=1, source_target_pairs={{0,128},{128,0},{1,129},{129,1},{2,130},{130,2},{3,131},{131,3},{4... | collective-permute-start | bytes 208904 | tf_op jit(solution)/shard_map/ppermute | solution.py:464
  39.3 4.8 %collective-permute-start.13 = (bf16[272,128]{1,0:T(8,128)(2,1)S(1)}, bf16[272,128]{1,0:T(8,128)(2,1)S(1)}, u32[]{:S(2)}, u32[]{:S(2)}) collective-permute-start(bf16[272,128]{1,0:T(8,128)(2,1)S(1)} %weight.1.zero), channel_id=1, source_target_pairs={{0,96},{32,64},{64,32},{96,0},{1,97},{33,65},{65,33},{97,1},{2,98}... | collective-permute-start | bytes 208904 | tf_op jit(solution)/shard_map/ppermute | solution.py:466
  40.5 5.8 %collective-permute-start.12 = (bf16[272,128]{1,0:T(8,128)(2,1)S(1)}, bf16[272,128]{1,0:T(8,128)(2,1)S(1)}, u32[]{:S(2)}, u32[]{:S(2)}) collective-permute-start(bf16[272,128]{1,0:T(8,128)(2,1)S(1)} %weight.1.zero), channel_id=1, source_target_pairs={{0,64},{32,96},{64,0},{96,32},{1,65},{33,97},{65,1},{97,33},{2,66}... | collective-permute-start | bytes 208904 | tf_op jit(solution)/shard_map/ppermute | solution.py:466
  44.0 4.3 %collective-permute-start.11 = (bf16[272,128]{1,0:T(8,128)(2,1)S(1)}, bf16[272,128]{1,0:T(8,128)(2,1)S(1)}, u32[]{:S(2)}, u32[]{:S(2)}) collective-permute-start(bf16[272,128]{1,0:T(8,128)(2,1)S(1)} %weight.1.zero), channel_id=1, source_target_pairs={{0,32},{32,0},{64,96},{96,64},{1,33},{33,1},{65,97},{97,65},{2,34}... | collective-permute-start | bytes 208904 | tf_op jit(solution)/shard_map/ppermute | solution.py:466
  48.4 1.6 %collective-permute-start.14 = (bf16[1040,128]{1,0:T(8,128)(2,1)S(1)}, bf16[1040,128]{1,0:T(8,128)(2,1)S(1)}, u32[]{:S(2)}, u32[]{:S(2)}) collective-permute-start(bf16[1040,128]{1,0:T(8,128)(2,1)S(1)} %gather.1.mine), channel_id=1, source_target_pairs={{0,16},{16,0},{1,17},{17,1},{2,18},{18,2},{3,19},{19,3},{4,20},{20... | collective-permute-start | bytes 798728 | tf_op jit(solution)/shard_map/ppermute | solution.py:468
  50.3 9.9 %collective-permute-start.15 = (bf16[528,128]{1,0:T(8,128)(2,1)S(1)}, bf16[528,128]{1,0:T(8,128)(2,1)S(1)}, u32[]{:S(2)}, u32[]{:S(2)}) collective-permute-start(bf16[528,128]{1,0:T(8,128)(2,1)S(1)} %get-tuple-element.51), channel_id=1, source_target_pairs={{0,4},{4,0},{8,12},{12,8},{1,5},{5,1},{9,13},{13,9},{2,6},{6,2},{1... | collective-permute-start | bytes 405512 | tf_op jit(solution)/shard_map/ppermute | solution.py:420
  51.0 10.0 %collective-permute-start.16 = (bf16[528,128]{1,0:T(8,128)(2,1)S(1)}, bf16[528,128]{1,0:T(8,128)(2,1)S(1)}, u32[]{:S(2)}, u32[]{:S(2)}) collective-permute-start(bf16[528,128]{1,0:T(8,128)(2,1)S(1)} %get-tuple-element.52), channel_id=1, source_target_pairs={{0,12},{4,8},{8,4},{12,0},{1,13},{5,9},{9,5},{13,1},{2,14},{6,10},... | collective-permute-start | bytes 405512 | tf_op jit(solution)/shard_map/ppermute | solution.py:420
  55.2 5.0 %collective-permute-start.19 = (f32[8,128]{1,0:T(8,128)S(1)}, f32[8,128]{1,0:T(8,128)S(1)}, u32[]{:S(2)}, u32[]{:S(2)}) collective-permute-start(f32[8,128]{1,0:T(8,128)S(1)} %get-tuple-element.56.refs_0_), channel_id=1, source_target_pairs={{0,8},{4,12},{8,0},{12,4},{1,9},{5,13},{9,1},{13,5},{2,10},{6,14},... | collective-permute-start | bytes 12296 | tf_op jit(solution)/shard_map/ppermute | solution.py:483
  55.7 13.8 %collective-permute-start.17 = (bf16[1024,128]{1,0:T(8,128)(2,1)S(1)}, bf16[1024,128]{1,0:T(8,128)(2,1)S(1)}, u32[]{:S(2)}, u32[]{:S(2)}) collective-permute-start(bf16[1024,128]{1,0:T(8,128)(2,1)S(1)} %get-tuple-element.54), channel_id=1, source_target_pairs={{0,1},{1,0},{2,3},{3,2},{4,5},{5,4},{6,7},{7,6},{8,9},{9,8},{10,11... | collective-permute-start | bytes 786440 | tf_op jit(solution)/shard_map/ppermute | solution.py:420
  55.9 13.6 %collective-permute-start.18 = (bf16[1024,128]{1,0:T(8,128)(2,1)S(1)}, bf16[1024,128]{1,0:T(8,128)(2,1)S(1)}, u32[]{:S(2)}, u32[]{:S(2)}) collective-permute-start(bf16[1024,128]{1,0:T(8,128)(2,1)S(1)} %get-tuple-element.55), channel_id=1, source_target_pairs={{0,3},{1,2},{2,1},{3,0},{4,7},{5,6},{6,5},{7,4},{8,11},{9,10},{10,... | collective-permute-start | bytes 786440 | tf_op jit(solution)/shard_map/ppermute | solution.py:420
  61.2 6.5 %collective-permute-start.22 = (f32[8,128]{1,0:T(8,128)S(1)}, f32[8,128]{1,0:T(8,128)S(1)}, u32[]{:S(2)}, u32[]{:S(2)}) collective-permute-start(f32[8,128]{1,0:T(8,128)S(1)} %get-tuple-element.59.sums), channel_id=1, source_target_pairs={{0,2},{1,3},{2,0},{3,1},{4,6},{5,7},{6,4},{7,5},{8,10},{9,11},{10,... | collective-permute-start | bytes 12296 | tf_op jit(solution)/shard_map/ppermute | solution.py:487
  63.0 4.8 %collective-permute-start.20 = (bf16[144,128]{1,0:T(8,128)(2,1)S(1)}, bf16[144,128]{1,0:T(8,128)(2,1)S(1)}, u32[]{:S(2)}, u32[]{:S(2)}) collective-permute-start(bf16[144,128]{1,0:T(8,128)(2,1)S(1)} %get-tuple-element.57), channel_id=1, source_target_pairs={{0,1},{1,0},{2,3},{3,2},{4,5},{5,4},{6,7},{7,6},{8,9},{9,8},{10,11... | collective-permute-start | bytes 110600 | tf_op jit(solution)/shard_map/ppermute | solution.py:420
  64.3 5.2 %collective-permute-start.21 = (bf16[144,128]{1,0:T(8,128)(2,1)S(1)}, bf16[144,128]{1,0:T(8,128)(2,1)S(1)}, u32[]{:S(2)}, u32[]{:S(2)}) collective-permute-start(bf16[144,128]{1,0:T(8,128)(2,1)S(1)} %get-tuple-element.58), channel_id=1, source_target_pairs={{0,3},{1,2},{2,1},{3,0},{4,7},{5,6},{6,5},{7,4},{8,11},{9,10},{10,... | collective-permute-start | bytes 110600 | tf_op jit(solution)/shard_map/ppermute | solution.py:420

commit v5 on v4

--- a/solution.py
+++ b/solution.py
@@ -94,10 +94,9 @@
     return south, north
 
 
-def centre_kernel(cols, with_square, own, first, second, band, out, *square):
+def centre_blocks(cols, own, first, second, band):
     members, cells, levels = own.shape
     size, edge = ROWS * cols, HALO * cols
-    total = jnp.zeros((8, levels), F32)
     for start in range(0, members, 2):
         pair = (start, start + 1)
         edges = [south_north(first, second, slice(m * edge, (m + 1) * edge)) for m in pair]
@@ -110,31 +109,45 @@
                 if row + size == cells:
                     part.append(north)
                 parts.append(jnp.concatenate(part, axis=0) if len(part) > 1 else part[0])
-                if with_square:
-                    c = own[m, row : row + size, :].astype(F32)
-                    total = total + jnp.sum((c * c).reshape(size // 8, 8, levels), axis=0)
             both = jnp.dot(band[...], jnp.concatenate(parts, axis=1), preferred_element_type=F32)
             both = both[:size] + both[size:]
             for n, m in enumerate(pair):
-                out[m, row : row + size, :] = both[:, n * levels : (n + 1) * levels]
-    if with_square:
-        square[0][...] = total
-
-
-def centre(own, first, second, band, cols, with_square):
+                yield m, row, both[:, n * levels : (n + 1) * levels]
+
+
+def centre_kernel(cols, own, first, second, band, out, square):
+    levels = own.shape[2]
+    size = ROWS * cols
+    total = jnp.zeros((8, levels), F32)
+    for m, row, value in centre_blocks(cols, own, first, second, band):
+        out[m, row : row + size, :] = value
+        c = own[m, row : row + size, :].astype(F32)
+        total = total + jnp.sum((c * c).reshape(size // 8, 8, levels), axis=0)
+    square[...] = total
+
+
+def centre_back_kernel(cols, own, first, second, band, control, sums, hessian, outer, same, middle, done):
     members, cells, levels = own.shape
-    shapes = [jax.ShapeDtypeStruct(own.shape, F32)]
-    if with_square:
-        shapes.append(jax.ShapeDtypeStruct((8, levels), F32))
-    return pl.pallas_call(
-        functools.partial(centre_kernel, cols, with_square),
-        out_shape=shapes,
-        in_specs=[VMEM] * 4,
-        out_specs=[VMEM] * len(shapes),
-        compiler_params=params(),
-        cost_estimate=cost(3_000_000_000, 7_000_000),
-        name="centre_forward" if with_square else "centre_back",
-    )(own, first, second, band)
+    size = ROWS * cols
+    batch = 2 * ROWS
+    copies = []
+    for m, row, value in centre_blocks(cols, own, first, second, band):
+        value = (control[m, row : row + size, :].astype(F32) + value).reshape(ROWS, cols, levels)
+        at = row // cols
+        rows = slice(at, at + ROWS)
+        middle[m, rows, :, :] = value[:, 8 : cols - 8]
+        outer[m, rows, :8, :] = value[:, :8]
+        outer[m, rows, 8:, :] = value[:, cols - 8 :]
+        if (at + ROWS) % batch == 0:
+            rows = pl.ds(at + ROWS - batch, batch)
+            copy = pltpu.make_async_copy(
+                middle.at[m, rows], hessian.at[m, rows, pl.ds(8, cols - 16), :], done.at[len(copies)]
+            )
+            copy.start()
+            copies.append(copy)
+    same[...] = sums[...]
+    for copy in copies:
+        copy.wait()
 
 
 def joined(strips, corners, out, members, cols, cells):
@@ -225,13 +238,14 @@
     return lax.axis_index("x") ^ bits
 
 
-def call(kernel, name, shapes, inputs, in_specs=None, scratch=(), flops=1_000_000, size=1_000_000, out_specs=None, mib=12):
+def call(kernel, name, shapes, inputs, in_specs=None, scratch=(), flops=1_000_000, size=1_000_000, out_specs=None, mib=12, aliases=None):
     return pl.pallas_call(
         kernel,
         out_shape=tuple(shapes),
         in_specs=in_specs or [VMEM] * len(inputs),
         out_specs=out_specs or (VMEM,) * len(shapes),
         scratch_shapes=scratch,
+        input_output_aliases=aliases or {},
         compiler_params=params(mib),
         cost_estimate=cost(flops, size),
         name=name,
@@ -291,8 +305,10 @@
 
 def corners_kernel(cols, members, first, second, *refs):
     if len(refs) > 2:
-        sums, far, *out, total = refs
-        value = (sums[0:1, :] + get_sums(first)) + (far[0:1, :] + get_sums(second))
+        sums, far, around, *out, total = refs
+        at, last = lax.axis_index("lat"), lax.axis_size("lat") - 1
+        other = jnp.where(jnp.logical_or(at == 0, at == last), around[0:1, :], get_sums(second))
+        value = (sums[0:1, :] + get_sums(first)) + (far[0:1, :] + other)
         total[...] = jnp.broadcast_to(value, total.shape)
         for ref in out:
             put_sums(ref, value)
@@ -389,35 +405,45 @@
 
 
 def backward_kernel(
-    cols, entries, inner, one, two, one_corner, two_corner, band, control, sums, far,
-    hessian, curvature, result, west, east, done,
+    cols, outer, one, two, one_corner, two_corner, band, sums, _, hessian, same, result, west, east, done
 ):
-    members, cells, levels = inner.shape
-    size = ROWS * cols
+    members, tile_rows, width, levels = outer.shape
+    cells = tile_rows * cols
+    batch = 2 * ROWS
     joined((one, two), (one_corner, two_corner), (west, east), members, cols, cells)
     copies = []
     for start in range(0, members, 2):
         pair = (start, start + 1)
-        for row in range(0, cells, size):
-            rows = slice(row, row + size)
-            for m, side in zip(pair, sides(band, west, east, pair, row // size, side_rows(cells, cols))):
-                result[m, rows, :] = control[m, rows, :].astype(F32) + with_sides(inner[m, rows, :], side, cols)
-            if (row + size) % (cells // 4) == 0:
+        for block in range(tile_rows // ROWS):
+            rows = slice(block * ROWS, (block + 1) * ROWS)
+            for m, side in zip(pair, sides(band, west, east, pair, block, side_rows(cells, cols))):
+                result[m, rows, :, :] = outer[m, rows, :, :] + side.reshape(ROWS, width, levels)
+            if (block + 1) * ROWS % batch == 0:
+                rows = pl.ds((block + 1) * ROWS - batch, batch)
                 for m in pair:
-                    part = pl.ds(row + size - cells // 4, cells // 4)
-                    copy = pltpu.make_async_copy(
-                        result.at[m, part, :], hessian.at[m, part, :], done.at[len(copies)]
-                    )
-                    copy.start()
-                    copies.append(copy)
+                    for source, target in ((0, 0), (8, cols - 8)):
+                        copy = pltpu.make_async_copy(
+                            result.at[m, rows, pl.ds(source, 8), :],
+                            hessian.at[m, rows, pl.ds(target, 8), :],
+                            done.at[len(copies)],
+                        )
+                        copy.start()
+                        copies.append(copy)
+    same[...] = sums[...]
+    for copy in copies:
+        copy.wait()
+
+
+def finish_kernel(entries, sums, far, one_corner, two_corner, curvature):
     value = (sums[0:1, :] + get_sums(one_corner)) + (far[0:1, :] + get_sums(two_corner))
     curvature[0, 0] = jnp.sum(value) / entries
-    for copy in copies:
-        copy.wait()
 
 
 def exchange(first, second, axis):
-    return lax.ppermute(first, axis, swap(axis, 1)), lax.ppermute(second, axis, swap(axis, 3))
+    other = swap(axis, 3)
+    if axis == "lat":
+        other = [(i, j) for i, j in other if abs(i - j) == 1]
+    return lax.ppermute(first, axis, swap(axis, 1)), lax.ppermute(second, axis, other)
 
 
 def per_device(control, ensemble, precision, lat_taps, lon_taps, vertical):
@@ -437,7 +463,14 @@
     beside_it = exchange(*strips(own, cols), "lon")
     corner = exchange(*corners(one, two, cols, members), "lon")
     band, band_side = bands(lat_taps, lon_taps, cols, False)
-    inner, square = centre(own, one, two, band, cols, True)
+    inner, square = call(
+        functools.partial(centre_kernel, cols),
+        "centre",
+        [jax.ShapeDtypeStruct(own.shape, F32), row],
+        (own, one, two, band),
+        flops=3_000_000_000,
+        size=7_000_000,
+    )
     joint = rows(members * side_rows(cells, cols))
     send, west, east = call(
         functools.partial(send_kernel, cols),
@@ -480,28 +513,52 @@
         size=4_500_000,
     )
     one, two = exchange(first, second, "lat")
+    last = lax.axis_size("lat") - 1
     far = lax.ppermute(sums, "lat", swap("lat", 2))
+    around = lax.ppermute(sums, "lat", [(0, last), (last, 0)])
     beside_it = exchange(*strips(adjoint, cols), "lon")
-    *corner, sums = corners(one, two, cols, members, sums, far)
+    *corner, sums = corners(one, two, cols, members, sums, far, around)
     corner = exchange(*corner, "lon")
+    outer_shape = (members, tile_rows, 16, levels)
+    hessian, outer, sums = call(
+        functools.partial(centre_back_kernel, cols),
+        "centre_back",
+        [jax.ShapeDtypeStruct(control.shape, F32), jax.ShapeDtypeStruct(outer_shape, F32), row],
+        (adjoint, one, two, band_back, own, sums),
+        out_specs=(pl.BlockSpec(memory_space=pl.ANY), VMEM, VMEM),
+        scratch=(
+            pltpu.VMEM((members, tile_rows, cols - 16, levels), F32),
+            pltpu.SemaphoreType.DMA((members * tile_rows // (2 * ROWS),)),
+        ),
+        flops=3_000_000_000,
+        size=7_000_000,
+    )
     far = lax.ppermute(sums, "lon", swap("lon", 2))
-    inner = centre(adjoint, one, two, band_back, cols, False)[0]
-    hessian, curvature = call(
-        functools.partial(backward_kernel, cols, entries),
+    hessian, sums = call(
+        functools.partial(backward_kernel, cols),
         "backward",
-        [jax.ShapeDtypeStruct(own.shape, F32), jax.ShapeDtypeStruct((1, 1), F32)],
-        (inner, *beside_it, *corner, band_side_back, own, sums, far),
+        [jax.ShapeDtypeStruct(control.shape, F32), row],
+        (outer, *beside_it, *corner, band_side_back, sums, hessian),
+        in_specs=[VMEM] * 7 + [pl.BlockSpec(memory_space=pl.ANY)],
         scratch=(
-            pltpu.VMEM(own.shape, F32),
-            pltpu.VMEM((members * side_rows(cells, cols), levels), BF),
-            pltpu.VMEM((members * side_rows(cells, cols), levels), BF),
-            pltpu.SemaphoreType.DMA((4 * members,)),
+            pltpu.VMEM(outer_shape, F32),
+            pltpu.VMEM(joint.shape, BF),
+            pltpu.VMEM(joint.shape, BF),
+            pltpu.SemaphoreType.DMA((2 * members * tile_rows // (2 * ROWS),)),
         ),
-        out_specs=(pl.BlockSpec(memory_space=pl.ANY), SMEM),
+        out_specs=(pl.BlockSpec(memory_space=pl.ANY), VMEM),
+        aliases={7: 0},
         flops=1_000_000_000,
         size=9_000_000,
     )
-    return hessian.reshape(control.shape), curvature.reshape(())
+    (curvature,) = call(
+        functools.partial(finish_kernel, entries),
+        "finish",
+        [jax.ShapeDtypeStruct((1, 1), F32)],
+        (sums, far, *corner),
+        out_specs=(SMEM,),
+    )
+    return hessian, curvature.reshape(())
 
 
 def solution(mesh):

time: 72.7 us -> 72.9 us (level)
  waiting for transfers between devices: 19.4 us -> 18.1 us
  starting transfers between devices: 37.1 us -> 38.1 us
    pallas_call x14 -> x17, Pallas kernels: 7.25 us -> 12.4 us  [call(): pl.pallas_call(kernel, out_shape=tuple(shapes), in_specs=in_specs or [VME...]
    pallas_call x2 -> x0, Pallas kernels: 4.68 us -> none  [centre(): pl.pallas_call(functools.partial(centre_kernel, cols, with_square), out_s...]
    ppermute x6 -> x7, starting transfers between devices: 13.8 us -> 11.1 us  [the longest x6 7.63 us: exchange(): lax.ppermute(second, axis, other)]
    ppermute x1, waiting for transfers between devices: 2.06 us -> 0.01 us  [per_device(): far = lax.ppermute(sums, 'lat', swap('lat', 2))]
    ppermute x6, starting transfers between devices: 7.62 us -> 9.14 us  [exchange(): lax.ppermute(first, axis, swap(axis, 1))]
    ppermute x1, starting transfers between devices: 1.78 us -> 3.02 us  [per_device(): far = lax.ppermute(sums, 'lon', swap('lon', 2))]
    ppermute x1, starting transfers between devices: 5.3 us -> 6.38 us  [per_device(): other = lax.ppermute(message, 'zh', swap('zh', 1))]
    ppermute x6 -> x7, waiting for transfers between devices: 4.39 us -> 5.27 us  [the longest x1 3.03 us: per_device(): around = lax.ppermute(sums, 'lat', [(0, last), (last, 0)])]
  transfers between devices with their start and end apart: 23 -> 24, of which waited for: 13 -> 12; matrix products, arithmetic and copies ran while one was open for 0% -> 0% of each run, Pallas kernels for 12% -> 16%
where the time goes in v5:
time: 72.9 us; the launch traced here: 72.8 us
  starting transfers between devices  38.1 us (52%)
  waiting for transfers between devices  18.1 us (25%)
  Pallas kernels  13.9 us (19%)
  local copies, waits for them, and re-layouts  1.61 us (2%)
  between operations  1.03 us (1%)
    pallas_call x17, Pallas kernels, call(): pl.pallas_call(kernel, out_shape=tuple(shapes), in_specs=in_specs or [VME...  12.4 us
    ppermute x6, starting transfers between devices, exchange(): lax.ppermute(first, axis, swap(axis, 1))  9.14 us
    ppermute x6, starting transfers between devices, exchange(): lax.ppermute(second, axis, other)  7.63 us
    ppermute x1, starting transfers between devices, per_device(): other = lax.ppermute(message, 'zh', swap('zh', 1))  6.38 us
    ppermute x3, starting transfers between devices, per_device(): two, one, three = [lax.ppermute(zero, 'x', swap('x', k)) for k in (2, 1, 3)]  4.55 us
    ppermute x3, waiting for transfers between devices, per_device(): two, one, three = [lax.ppermute(zero, 'x', swap('x', k)) for k in (2, 1, 3)]  4.31 us
    ppermute x3, waiting for transfers between devices, per_device(): lax.ppermute(v, 'x', swap('x', k))  4.12 us
    ppermute x3, starting transfers between devices, per_device(): lax.ppermute(v, 'x', swap('x', k))  3.58 us
  transfers between devices with their start and end apart: 24, of which 12 were waited for; matrix products, arithmetic and copies ran while one was open for 0% of the time, Pallas kernels for 16%

profile of v5, /device:TPU:2, one launch (start us, length us, event | category | flops | bytes accessed | tf_op | source)
XLA Modules:
  0.0 72.8 jit_solution(5690904039494971244)
XLA Ops:
  0.6 1.6 %copy-done.1 = bf16[4,64,32,128]{3,2,1,0:T(8,128)(2,1)S(1)} copy-done((bf16[4,64,32,128]{3,2,1,0:T(8,128)(2,1)S(1)}, bf16[4,64,32,128]{3,2,1,0:T(8,128)(2,1)}, u32[]{:S(2)}) %copy-start.1) | copy-done | bytes 2097176
  2.3 2.0 %collective-permute-start = (bf16[512,128]{1,0:T(8,128)(2,1)S(1)}, bf16[512,128]{1,0:T(8,128)(2,1)S(1)}, u32[]{:S(2)}, u32[]{:S(2)}) collective-permute-start(bf16[512,128]{1,0:T(8,128)(2,1)S(1)} %get-tuple-element.35), channel_id=1, source_target_pairs={{0,4},{4,0},{8,12},{12,8},{1,5},{5,1},{9,13},{13,9},{2,6},{6,2},{1... | collective-permute-start | bytes 393224 | tf_op jit(solution)/shard_map/ppermute | solution.py:446
  4.3 0.7 collective-permute-start.1
  5.0 0.5 strips.2
  5.4 1.7 %collective-permute-start.2 = (bf16[1024,128]{1,0:T(8,128)(2,1)S(1)}, bf16[1024,128]{1,0:T(8,128)(2,1)S(1)}, u32[]{:S(2)}, u32[]{:S(2)}) collective-permute-start(bf16[1024,128]{1,0:T(8,128)(2,1)S(1)} %get-tuple-element.39), channel_id=1, source_target_pairs={{0,1},{1,0},{2,3},{3,2},{4,5},{5,4},{6,7},{7,6},{8,9},{9,8},{10,11... | collective-permute-start | bytes 786440 | tf_op jit(solution)/shard_map/ppermute | solution.py:446
  7.1 2.2 %collective-permute-start.3 = (bf16[1024,128]{1,0:T(8,128)(2,1)S(1)}, bf16[1024,128]{1,0:T(8,128)(2,1)S(1)}, u32[]{:S(2)}, u32[]{:S(2)}) collective-permute-start(bf16[1024,128]{1,0:T(8,128)(2,1)S(1)} %get-tuple-element.40), channel_id=1, source_target_pairs={{0,3},{1,2},{2,1},{3,0},{4,7},{5,6},{6,5},{7,4},{8,11},{9,10},{10,... | collective-permute-start | bytes 786440 | tf_op jit(solution)/shard_map/ppermute | solution.py:446
  9.3 0.8 %bands.1 = (bf16[512,512]{1,0:T(8,128)(2,1)S(1)}, bf16[256,128]{1,0:T(8,128)(2,1)S(1)}) custom-call(f32[9]{0:T(128)S(1)} %copy-done.5, f32[9]{0:T(128)S(1)} %copy-done.6), custom_call_target="tpu_custom_call" | custom-call | flops 2000000 | bytes 600000 | tf_op jit(solution)/shard_map/bands/pallas_call | solution.py:76
  10.1 0.2 corners.2
  10.3 0.8 %collective-permute-start.4 = (bf16[128,128]{1,0:T(8,128)(2,1)S(1)}, bf16[128,128]{1,0:T(8,128)(2,1)S(1)}, u32[]{:S(2)}, u32[]{:S(2)}) collective-permute-start(bf16[128,128]{1,0:T(8,128)(2,1)S(1)} %get-tuple-element.41), channel_id=1, source_target_pairs={{0,1},{1,0},{2,3},{3,2},{4,5},{5,4},{6,7},{7,6},{8,9},{9,8},{10,11... | collective-permute-start | bytes 98312 | tf_op jit(solution)/shard_map/ppermute | solution.py:446
  11.0 0.8 %collective-permute-start.5 = (bf16[128,128]{1,0:T(8,128)(2,1)S(1)}, bf16[128,128]{1,0:T(8,128)(2,1)S(1)}, u32[]{:S(2)}, u32[]{:S(2)}) collective-permute-start(bf16[128,128]{1,0:T(8,128)(2,1)S(1)} %get-tuple-element.42), channel_id=1, source_target_pairs={{0,3},{1,2},{2,1},{3,0},{4,7},{5,6},{6,5},{7,4},{8,11},{9,10},{10,... | collective-permute-start | bytes 98312 | tf_op jit(solution)/shard_map/ppermute | solution.py:446
  11.8 2.3 %centre.1 = (f32[4,2048,128]{2,1,0:T(8,128)S(1)}, f32[8,128]{1,0:T(8,128)S(1)}) custom-call(bf16[4,2048,128]{2,1,0:T(8,128)(2,1)S(1)} %bitcast.10, bf16[512,128]{1,0:T(8,128)(2,1)S(1)} %collective-permute-done.first, bf16[512,128]{1,0:T(8,128)(2,1)S(1)} %collective-permute-done.1.second, bf16[512,512]{1,0:T(8,128)(2,1)S(1)} %get-tuple-element.37.band), custom_call_target="tpu_custom_call" | custom-call | flops 3000000000 | bytes 7000000 | tf_op jit(solution)/shard_map/centre/pallas_call | solution.py:242
  14.3 2.2 %collective-permute-done.5.two_corner = bf16[128,128]{1,0:T(8,128)(2,1)S(1)} collective-permute-done((bf16[128,128]{1,0:T(8,128)(2,1)S(1)}, bf16[128,128]{1,0:T(8,128)(2,1)S(1)}, u32[]{:S(2)}, u32[]{:S(2)}) %collective-permute-start.5) | collective-permute-done | bytes 32800 | tf_op jit(solution)/shard_map/ppermute | solution.py:446
  16.5 0.9 %forward_send.1 = (bf16[1024,128]{1,0:T(8,128)(2,1)S(1)}, bf16[1152,128]{1,0:T(8,128)(2,1)S(1)}, bf16[1152,128]{1,0:T(8,128)(2,1)S(1)}) custom-call(f32[4,2048,128]{2,1,0:T(8,128)S(1)} %get-tuple-element.38.inner, bf16[1024,128]{1,0:T(8,128)(2,1)S(1)} %collective-permute-done.2.one, bf16[1024,128]{1,0:T(8,128)(2,1)S(1)} %collective-permute-done.3.two, ...), custom_call_target="tpu_custom_call" | custom-call | flops 700000000 | bytes 3000000 | tf_op jit(solution)/shard_map/forward_send/pallas_call | solution.py:242
  17.4 0.1 collective-permute-start.6
  17.5 0.9 %forward_keep.1.keep = bf16[1024,128]{1,0:T(8,128)(2,1)S(1)} custom-call(f32[4,2048,128]{2,1,0:T(8,128)S(1)} %get-tuple-element.38.inner, bf16[1152,128]{1,0:T(8,128)(2,1)S(1)} %get-tuple-element.44.west, bf16[1152,128]{1,0:T(8,128)(2,1)S(1)} %get-tuple-element.45.east, bf16[256,128]{1,0:T(8,128)(2,1)S(1)} %get-tuple-element.43.band, ...), custom_call_target="tpu_custom_call" | custom-call | flops 700000000 | bytes 3000000 | tf_op jit(solution)/shard_map/forward_keep/pallas_call | solution.py:242
  18.4 0.6 collective-permute-done.6.got
  19.1 0.6 collective-permute-start.7
  19.7 2.4 %collective-permute-start.8 = (bf16[256,128]{1,0:T(8,128)(2,1)S(1)}, bf16[256,128]{1,0:T(8,128)(2,1)S(1)}, u32[]{:S(2)}, u32[]{:S(2)}) collective-permute-start(bf16[256,128]{1,0:T(8,128)(2,1)S(1)} %get-tuple-element.49), channel_id=1, source_target_pairs={{0,64},{32,96},{64,0},{96,32},{1,65},{33,97},{65,1},{97,33},{2,66}... | collective-permute-start | bytes 196616 | tf_op jit(solution)/shard_map/ppermute | solution.py:494
  22.1 0.5 collective-permute-start.9
  22.7 0.8 %collective-permute-done.7.one = bf16[256,128]{1,0:T(8,128)(2,1)S(1)} collective-permute-done((bf16[256,128]{1,0:T(8,128)(2,1)S(1)}, bf16[256,128]{1,0:T(8,128)(2,1)S(1)}, u32[]{:S(2)}, u32[]{:S(2)}) %collective-permute-start.7) | collective-permute-done | bytes 65568 | tf_op jit(solution)/shard_map/ppermute | solution.py:494
  23.4 2.4 %collective-permute-done.8.two = bf16[256,128]{1,0:T(8,128)(2,1)S(1)} collective-permute-done((bf16[256,128]{1,0:T(8,128)(2,1)S(1)}, bf16[256,128]{1,0:T(8,128)(2,1)S(1)}, u32[]{:S(2)}, u32[]{:S(2)}) %collective-permute-start.8) | collective-permute-done | bytes 65568 | tf_op jit(solution)/shard_map/ppermute | solution.py:494
  25.9 0.9 %collective-permute-done.9.three.refs_0_ = bf16[256,128]{1,0:T(8,128)(2,1)S(1)} collective-permute-done((bf16[256,128]{1,0:T(8,128)(2,1)S(1)}, bf16[256,128]{1,0:T(8,128)(2,1)S(1)}, u32[]{:S(2)}, u32[]{:S(2)}) %collective-permute-start.9) | collective-permute-done | bytes 65568 | tf_op jit(solution)/shard_map/ppermute | solution.py:494
  26.8 6.4 %collective-permute-start.10 = (bf16[272,128]{1,0:T(8,128)(2,1)S(1)}, bf16[272,128]{1,0:T(8,128)(2,1)S(1)}, u32[]{:S(2)}, u32[]{:S(2)}) collective-permute-start(bf16[272,128]{1,0:T(8,128)(2,1)S(1)} %part.1.message), channel_id=1, source_target_pairs={{0,128},{128,0},{1,129},{129,1},{2,130},{130,2},{3,131},{131,3},{4... | collective-permute-start | bytes 208904 | tf_op jit(solution)/shard_map/ppermute | solution.py:497
  33.2 0.8 %bands_back.1 = (bf16[512,512]{1,0:T(8,128)(2,1)S(1)}, bf16[256,128]{1,0:T(8,128)(2,1)S(1)}) custom-call(f32[9]{0:T(128)S(1)} %copy-done.5, f32[9]{0:T(128)S(1)} %copy-done.6, bf16[256,128]{1,0:T(8,128)(2,1)S(1)} %collective-permute-done.9.three.refs_0_), custom_call_target="tpu_custom_call" | custom-call | flops 2000000 | bytes 600000 | tf_op jit(solution)/shard_map/bands_back/pallas_call | solution.py:76
  34.0 1.8 %collective-permute-done.10.other = bf16[272,128]{1,0:T(8,128)(2,1)S(1)} collective-permute-done((bf16[272,128]{1,0:T(8,128)(2,1)S(1)}, bf16[272,128]{1,0:T(8,128)(2,1)S(1)}, u32[]{:S(2)}, u32[]{:S(2)}) %collective-permute-start.10) | collective-permute-done | bytes 69664 | tf_op jit(solution)/shard_map/ppermute | solution.py:497
  35.9 1.0 %collective-permute-start.13 = (bf16[272,128]{1,0:T(8,128)(2,1)S(1)}, bf16[272,128]{1,0:T(8,128)(2,1)S(1)}, u32[]{:S(2)}, u32[]{:S(2)}) collective-permute-start(bf16[272,128]{1,0:T(8,128)(2,1)S(1)} %weight.1.zero), channel_id=1, source_target_pairs={{0,96},{32,64},{64,32},{96,0},{1,97},{33,65},{65,33},{97,1},{2,98}... | collective-permute-start | bytes 208904 | tf_op jit(solution)/shard_map/ppermute | solution.py:499
  36.9 3.6 %collective-permute-start.12 = (bf16[272,128]{1,0:T(8,128)(2,1)S(1)}, bf16[272,128]{1,0:T(8,128)(2,1)S(1)}, u32[]{:S(2)}, u32[]{:S(2)}) collective-permute-start(bf16[272,128]{1,0:T(8,128)(2,1)S(1)} %weight.1.zero), channel_id=1, source_target_pairs={{0,64},{32,96},{64,0},{96,32},{1,65},{33,97},{65,1},{97,33},{2,66}... | collective-permute-start | bytes 208904 | tf_op jit(solution)/shard_map/ppermute | solution.py:499
  40.5 2.3 %collective-permute-done.12.two = bf16[272,128]{1,0:T(8,128)(2,1)S(1)} collective-permute-done((bf16[272,128]{1,0:T(8,128)(2,1)S(1)}, bf16[272,128]{1,0:T(8,128)(2,1)S(1)}, u32[]{:S(2)}, u32[]{:S(2)}) %collective-permute-start.12) | collective-permute-done | bytes 69664 | tf_op jit(solution)/shard_map/ppermute | solution.py:499
  42.7 2.0 %collective-permute-done.11.one = bf16[272,128]{1,0:T(8,128)(2,1)S(1)} collective-permute-done((bf16[272,128]{1,0:T(8,128)(2,1)S(1)}, bf16[272,128]{1,0:T(8,128)(2,1)S(1)}, u32[]{:S(2)}, u32[]{:S(2)}) %collective-permute-start.11) | collective-permute-done | bytes 69664 | tf_op jit(solution)/shard_map/ppermute | solution.py:499
  44.9 1.5 %collective-permute-done.14.other = bf16[1040,128]{1,0:T(8,128)(2,1)S(1)} collective-permute-done((bf16[1040,128]{1,0:T(8,128)(2,1)S(1)}, bf16[1040,128]{1,0:T(8,128)(2,1)S(1)}, u32[]{:S(2)}, u32[]{:S(2)}) %collective-permute-start.14) | collective-permute-done | bytes 266272 | tf_op jit(solution)/shard_map/ppermute | solution.py:501
  46.4 0.3 level_edges.1
  46.7 4.4 %collective-permute-start.15 = (bf16[528,128]{1,0:T(8,128)(2,1)S(1)}, bf16[528,128]{1,0:T(8,128)(2,1)S(1)}, u32[]{:S(2)}, u32[]{:S(2)}) collective-permute-start(bf16[528,128]{1,0:T(8,128)(2,1)S(1)} %get-tuple-element.54), channel_id=1, source_target_pairs={{0,4},{4,0},{8,12},{12,8},{1,5},{5,1},{9,13},{13,9},{2,6},{6,2},{1... | collective-permute-start | bytes 405512 | tf_op jit(solution)/shard_map/ppermute | solution.py:446
  51.1 0.7 collective-permute-start.16
  51.8 0.7 level.1
  52.5 3.5 %collective-permute-start.18 = (f32[8,128]{1,0:T(8,128)S(1)}, f32[8,128]{1,0:T(8,128)S(1)}, u32[]{:S(2)}, u32[]{:S(2)}) collective-permute-start(f32[8,128]{1,0:T(8,128)S(1)} %get-tuple-element.57.refs_0_), channel_id=1, source_target_pairs={{0,12},{12,0},{1,13},{13,1},{2,14},{14,2},{3,15},{15,3},{16,28},{2... | collective-permute-start | bytes 12296 | tf_op jit(solution)/shard_map/ppermute | solution.py:518
  56.0 0.1 collective-permute-start.17
  56.2 0.5 strips.3
  56.6 0.2 collective-permute-start.19
  56.8 3.0 %collective-permute-done.18.refs_2_ = f32[8,128]{1,0:T(8,128)S(1)} collective-permute-done((f32[8,128]{1,0:T(8,128)S(1)}, f32[8,128]{1,0:T(8,128)S(1)}, u32[]{:S(2)}, u32[]{:S(2)}) %collective-permute-start.18) | collective-permute-done | bytes 4128 | tf_op jit(solution)/shard_map/ppermute | solution.py:518
  59.8 2.2 %collective-permute-start.20 = (bf16[1024,128]{1,0:T(8,128)(2,1)S(1)}, bf16[1024,128]{1,0:T(8,128)(2,1)S(1)}, u32[]{:S(2)}, u32[]{:S(2)}) collective-permute-start(bf16[1024,128]{1,0:T(8,128)(2,1)S(1)} %get-tuple-element.61), channel_id=1, source_target_pairs={{0,3},{1,2},{2,1},{3,0},{4,7},{5,6},{6,5},{7,4},{8,11},{9,10},{10,... | collective-permute-start | bytes 786440 | tf_op jit(solution)/shard_map/ppermute | solution.py:446
  62.0 0.2 corners.3
  62.2 0.1 collective-permute-start.21
  62.3 1.1 %collective-permute-start.22 = (bf16[144,128]{1,0:T(8,128)(2,1)S(1)}, bf16[144,128]{1,0:T(8,128)(2,1)S(1)}, u32[]{:S(2)}, u32[]{:S(2)}) collective-permute-start(bf16[144,128]{1,0:T(8,128)(2,1)S(1)} %get-tuple-element.63), channel_id=1, source_target_pairs={{0,3},{1,2},{2,1},{3,0},{4,7},{5,6},{6,5},{7,4},{8,11},{9,10},{10,... | collective-permute-start | bytes 110600 | tf_op jit(solution)/shard_map/ppermute | solution.py:446
  63.5 3.3 %centre_back.1 = (f32[4,64,32,128]{3,2,1,0:T(8,128)}, f32[4,64,16,128]{3,2,1,0:T(8,128)S(1)}, f32[8,128]{1,0:T(8,128)S(1)}) custom-call(bf16[4,2048,128]{2,1,0:T(8,128)(2,1)S(1)} %get-tuple-element.53.own.tile, bf16[528,128]{1,0:T(8,128)(2,1)S(1)} %collective-permute-done.15.first, bf16[528,128]{1,0:T(8,128)(2,1)S(1)} %collective-permute-done.16.second, ...), custom_call_target="tpu_custom_call" | custom-call | flops 3000000000 | bytes 7000000 | tf_op jit(solution)/shard_map/centre_back/pallas_call | solution.py:242
  66.8 3.0 %collective-permute-start.23 = (f32[8,128]{1,0:T(8,128)S(1)}, f32[8,128]{1,0:T(8,128)S(1)}, u32[]{:S(2)}, u32[]{:S(2)}) collective-permute-start(f32[8,128]{1,0:T(8,128)S(1)} %get-tuple-element.64.sums), channel_id=1, source_target_pairs={{0,2},{1,3},{2,0},{3,1},{4,6},{5,7},{6,4},{7,5},{8,10},{9,11},{10,... | collective-permute-start | bytes 12296 | tf_op jit(solution)/shard_map/ppermute | solution.py:536
  69.8 1.8 %backward.1 = (f32[4,64,32,128]{3,2,1,0:T(8,128)}, f32[8,128]{1,0:T(8,128)S(1)}) custom-call(f32[4,64,16,128]{3,2,1,0:T(8,128)S(1)} %get-tuple-element.59.outer, bf16[1024,128]{1,0:T(8,128)(2,1)S(1)} %collective-permute-done.19.one, bf16[1024,128]{1,0:T(8,128)(2,1)S(1)} %collective-permute-done.20.two, ...), custom_call_target="tpu_custom_call", output_to_operand_aliasing={{0}: (7, {})} | custom-call | flops 1000000000 | bytes 9000000 | tf_op jit(solution)/shard_map/backward/pallas_call | solution.py:242
  71.7 0.3 collective-permute-done.23.far
  72.0 0.6 finish.1
  (33 shorter events, 0.5 us)
Async XLA Ops:
  0.6 1.6 %copy-start.1 = (bf16[4,64,32,128]{3,2,1,0:T(8,128)(2,1)S(1)}, bf16[4,64,32,128]{3,2,1,0:T(8,128)(2,1)}, u32[]{:S(2)}) copy-start(bf16[4,64,32,128]{3,2,1,0:T(8,128)(2,1)} %param.6) | copy-start | bytes 6291460
  2.2 7.0 %copy-start.5 = (f32[9]{0:T(128)S(1)}, f32[9]{0:T(128)}, u32[]{:S(2)}) copy-start(f32[9]{0:T(128)} %lat_taps.3) | copy-start | bytes 112
  2.2 7.0 %copy-start.6 = (f32[9]{0:T(128)S(1)}, f32[9]{0:T(128)}, u32[]{:S(2)}) copy-start(f32[9]{0:T(128)} %lon_taps.3) | copy-start | bytes 112
  2.2 9.6 %copy-start.2 = (bf16[4,64,32,128]{3,2,1,0:T(8,128)(2,1)S(1)}, bf16[4,64,32,128]{3,2,1,0:T(8,128)(2,1)}, u32[]{:S(2)}) copy-start(bf16[4,64,32,128]{3,2,1,0:T(8,128)(2,1)} %param.6) | copy-start | bytes 6291460
  2.3 7.7 %collective-permute-start = (bf16[512,128]{1,0:T(8,128)(2,1)S(1)}, bf16[512,128]{1,0:T(8,128)(2,1)S(1)}, u32[]{:S(2)}, u32[]{:S(2)}) collective-permute-start(bf16[512,128]{1,0:T(8,128)(2,1)S(1)} %get-tuple-element.35), channel_id=1, source_target_pairs={{0,4},{4,0},{8,12},{12,8},{1,5},{5,1},{9,13},{13,9},{2,6},{6,2},{1... | collective-permute-start | bytes 393224 | tf_op jit(solution)/shard_map/ppermute | solution.py:446
  4.3 5.8 %collective-permute-start.1 = (bf16[512,128]{1,0:T(8,128)(2,1)S(1)}, bf16[512,128]{1,0:T(8,128)(2,1)S(1)}, u32[]{:S(2)}, u32[]{:S(2)}) collective-permute-start(bf16[512,128]{1,0:T(8,128)(2,1)S(1)} %get-tuple-element.36), channel_id=1, source_target_pairs={{4,8},{8,4},{5,9},{9,5},{6,10},{10,6},{7,11},{11,7},{20,24},{24,20... | collective-permute-start | bytes 393224 | tf_op jit(solution)/shard_map/ppermute | solution.py:446
  5.4 11.1 %collective-permute-start.2 = (bf16[1024,128]{1,0:T(8,128)(2,1)S(1)}, bf16[1024,128]{1,0:T(8,128)(2,1)S(1)}, u32[]{:S(2)}, u32[]{:S(2)}) collective-permute-start(bf16[1024,128]{1,0:T(8,128)(2,1)S(1)} %get-tuple-element.39), channel_id=1, source_target_pairs={{0,1},{1,0},{2,3},{3,2},{4,5},{5,4},{6,7},{7,6},{8,9},{9,8},{10,11... | collective-permute-start | bytes 786440 | tf_op jit(solution)/shard_map/ppermute | solution.py:446
  7.1 9.4 %collective-permute-start.3 = (bf16[1024,128]{1,0:T(8,128)(2,1)S(1)}, bf16[1024,128]{1,0:T(8,128)(2,1)S(1)}, u32[]{:S(2)}, u32[]{:S(2)}) collective-permute-start(bf16[1024,128]{1,0:T(8,128)(2,1)S(1)} %get-tuple-element.40), channel_id=1, source_target_pairs={{0,3},{1,2},{2,1},{3,0},{4,7},{5,6},{6,5},{7,4},{8,11},{9,10},{10,... | collective-permute-start | bytes 786440 | tf_op jit(solution)/shard_map/ppermute | solution.py:446
  10.3 4.0 %collective-permute-start.4 = (bf16[128,128]{1,0:T(8,128)(2,1)S(1)}, bf16[128,128]{1,0:T(8,128)(2,1)S(1)}, u32[]{:S(2)}, u32[]{:S(2)}) collective-permute-start(bf16[128,128]{1,0:T(8,128)(2,1)S(1)} %get-tuple-element.41), channel_id=1, source_target_pairs={{0,1},{1,0},{2,3},{3,2},{4,5},{5,4},{6,7},{7,6},{8,9},{9,8},{10,11... | collective-permute-start | bytes 98312 | tf_op jit(solution)/shard_map/ppermute | solution.py:446
  11.0 5.5 %collective-permute-start.5 = (bf16[128,128]{1,0:T(8,128)(2,1)S(1)}, bf16[128,128]{1,0:T(8,128)(2,1)S(1)}, u32[]{:S(2)}, u32[]{:S(2)}) collective-permute-start(bf16[128,128]{1,0:T(8,128)(2,1)S(1)} %get-tuple-element.42), channel_id=1, source_target_pairs={{0,3},{1,2},{2,1},{3,0},{4,7},{5,6},{6,5},{7,4},{8,11},{9,10},{10,... | collective-permute-start | bytes 98312 | tf_op jit(solution)/shard_map/ppermute | solution.py:446
  11.8 4.7 %copy-start = (bf16[4,64,32,128]{3,2,1,0:T(8,128)(2,1)S(1)}, bf16[4,64,32,128]{3,2,1,0:T(8,128)(2,1)}, u32[]{:S(2)}) copy-start(bf16[4,64,32,128]{3,2,1,0:T(8,128)(2,1)} %param.7) | copy-start | bytes 6291460
  11.8 4.7 %copy-start.4 = (bf16[128,128]{1,0:T(8,128)(2,1)S(1)}, bf16[128,128]{1,0:T(8,128)(2,1)}, u32[]{:S(2)}) copy-start(bf16[128,128]{1,0:T(8,128)(2,1)} %vertical.7) | copy-start | bytes 98308
  17.4 1.6 %collective-permute-start.6 = (bf16[1024,128]{1,0:T(8,128)(2,1)S(1)}, bf16[1024,128]{1,0:T(8,128)(2,1)S(1)}, u32[]{:S(2)}, u32[]{:S(2)}) collective-permute-start(bf16[1024,128]{1,0:T(8,128)(2,1)S(1)} %get-tuple-element.46), channel_id=1, source_target_pairs={{0,16},{16,0},{1,17},{17,1},{2,18},{18,2},{3,19},{19,3},{4,20},{20... | collective-permute-start | bytes 786440 | tf_op jit(solution)/shard_map/ppermute | solution.py:492
  17.5 18.3 %copy-start.3 = (f32[64,32,128]{2,1,0:T(8,128)S(1)}, f32[64,32,128]{2,1,0:T(8,128)}, u32[]{:S(2)}) copy-start(f32[64,32,128]{2,1,0:T(8,128)} %param.8) | copy-start | bytes 3145732
  19.1 4.4 %collective-permute-start.7 = (bf16[256,128]{1,0:T(8,128)(2,1)S(1)}, bf16[256,128]{1,0:T(8,128)(2,1)S(1)}, u32[]{:S(2)}, u32[]{:S(2)}) collective-permute-start(bf16[256,128]{1,0:T(8,128)(2,1)S(1)} %get-tuple-element.48), channel_id=1, source_target_pairs={{0,32},{32,0},{64,96},{96,64},{1,33},{33,1},{65,97},{97,65},{2,34}... | collective-permute-start | bytes 196616 | tf_op jit(solution)/shard_map/ppermute | solution.py:494
  19.7 6.2 %collective-permute-start.8 = (bf16[256,128]{1,0:T(8,128)(2,1)S(1)}, bf16[256,128]{1,0:T(8,128)(2,1)S(1)}, u32[]{:S(2)}, u32[]{:S(2)}) collective-permute-start(bf16[256,128]{1,0:T(8,128)(2,1)S(1)} %get-tuple-element.49), channel_id=1, source_target_pairs={{0,64},{32,96},{64,0},{96,32},{1,65},{33,97},{65,1},{97,33},{2,66}... | collective-permute-start | bytes 196616 | tf_op jit(solution)/shard_map/ppermute | solution.py:494
  22.1 4.7 %collective-permute-start.9 = (bf16[256,128]{1,0:T(8,128)(2,1)S(1)}, bf16[256,128]{1,0:T(8,128)(2,1)S(1)}, u32[]{:S(2)}, u32[]{:S(2)}) collective-permute-start(bf16[256,128]{1,0:T(8,128)(2,1)S(1)} %get-tuple-element.50), channel_id=1, source_target_pairs={{0,96},{32,64},{64,32},{96,0},{1,97},{33,65},{65,33},{97,1},{2,98}... | collective-permute-start | bytes 196616 | tf_op jit(solution)/shard_map/ppermute | solution.py:494
  26.8 9.0 %collective-permute-start.10 = (bf16[272,128]{1,0:T(8,128)(2,1)S(1)}, bf16[272,128]{1,0:T(8,128)(2,1)S(1)}, u32[]{:S(2)}, u32[]{:S(2)}) collective-permute-start(bf16[272,128]{1,0:T(8,128)(2,1)S(1)} %part.1.message), channel_id=1, source_target_pairs={{0,128},{128,0},{1,129},{129,1},{2,130},{130,2},{3,131},{131,3},{4... | collective-permute-start | bytes 208904 | tf_op jit(solution)/shard_map/ppermute | solution.py:497
  35.9 4.6 %collective-permute-start.13 = (bf16[272,128]{1,0:T(8,128)(2,1)S(1)}, bf16[272,128]{1,0:T(8,128)(2,1)S(1)}, u32[]{:S(2)}, u32[]{:S(2)}) collective-permute-start(bf16[272,128]{1,0:T(8,128)(2,1)S(1)} %weight.1.zero), channel_id=1, source_target_pairs={{0,96},{32,64},{64,32},{96,0},{1,97},{33,65},{65,33},{97,1},{2,98}... | collective-permute-start | bytes 208904 | tf_op jit(solution)/shard_map/ppermute | solution.py:499
  36.9 5.8 %collective-permute-start.12 = (bf16[272,128]{1,0:T(8,128)(2,1)S(1)}, bf16[272,128]{1,0:T(8,128)(2,1)S(1)}, u32[]{:S(2)}, u32[]{:S(2)}) collective-permute-start(bf16[272,128]{1,0:T(8,128)(2,1)S(1)} %weight.1.zero), channel_id=1, source_target_pairs={{0,64},{32,96},{64,0},{96,32},{1,65},{33,97},{65,1},{97,33},{2,66}... | collective-permute-start | bytes 208904 | tf_op jit(solution)/shard_map/ppermute | solution.py:499
  40.4 4.3 %collective-permute-start.11 = (bf16[272,128]{1,0:T(8,128)(2,1)S(1)}, bf16[272,128]{1,0:T(8,128)(2,1)S(1)}, u32[]{:S(2)}, u32[]{:S(2)}) collective-permute-start(bf16[272,128]{1,0:T(8,128)(2,1)S(1)} %weight.1.zero), channel_id=1, source_target_pairs={{0,32},{32,0},{64,96},{96,64},{1,33},{33,1},{65,97},{97,65},{2,34}... | collective-permute-start | bytes 208904 | tf_op jit(solution)/shard_map/ppermute | solution.py:499
  44.8 1.6 %collective-permute-start.14 = (bf16[1040,128]{1,0:T(8,128)(2,1)S(1)}, bf16[1040,128]{1,0:T(8,128)(2,1)S(1)}, u32[]{:S(2)}, u32[]{:S(2)}) collective-permute-start(bf16[1040,128]{1,0:T(8,128)(2,1)S(1)} %gather.1.mine), channel_id=1, source_target_pairs={{0,16},{16,0},{1,17},{17,1},{2,18},{18,2},{3,19},{19,3},{4,20},{20... | collective-permute-start | bytes 798728 | tf_op jit(solution)/shard_map/ppermute | solution.py:501
  46.7 15.3 %collective-permute-start.15 = (bf16[528,128]{1,0:T(8,128)(2,1)S(1)}, bf16[528,128]{1,0:T(8,128)(2,1)S(1)}, u32[]{:S(2)}, u32[]{:S(2)}) collective-permute-start(bf16[528,128]{1,0:T(8,128)(2,1)S(1)} %get-tuple-element.54), channel_id=1, source_target_pairs={{0,4},{4,0},{8,12},{12,8},{1,5},{5,1},{9,13},{13,9},{2,6},{6,2},{1... | collective-permute-start | bytes 405512 | tf_op jit(solution)/shard_map/ppermute | solution.py:446
  51.1 10.9 %collective-permute-start.16 = (bf16[528,128]{1,0:T(8,128)(2,1)S(1)}, bf16[528,128]{1,0:T(8,128)(2,1)S(1)}, u32[]{:S(2)}, u32[]{:S(2)}) collective-permute-start(bf16[528,128]{1,0:T(8,128)(2,1)S(1)} %get-tuple-element.55), channel_id=1, source_target_pairs={{4,8},{8,4},{5,9},{9,5},{6,10},{10,6},{7,11},{11,7},{20,24},{24,20... | collective-permute-start | bytes 405512 | tf_op jit(solution)/shard_map/ppermute | solution.py:446
  52.5 7.3 %collective-permute-start.18 = (f32[8,128]{1,0:T(8,128)S(1)}, f32[8,128]{1,0:T(8,128)S(1)}, u32[]{:S(2)}, u32[]{:S(2)}) collective-permute-start(f32[8,128]{1,0:T(8,128)S(1)} %get-tuple-element.57.refs_0_), channel_id=1, source_target_pairs={{0,12},{12,0},{1,13},{13,1},{2,14},{14,2},{3,15},{15,3},{16,28},{2... | collective-permute-start | bytes 12296 | tf_op jit(solution)/shard_map/ppermute | solution.py:518
  56.0 6.0 %collective-permute-start.17 = (f32[8,128]{1,0:T(8,128)S(1)}, f32[8,128]{1,0:T(8,128)S(1)}, u32[]{:S(2)}, u32[]{:S(2)}) collective-permute-start(f32[8,128]{1,0:T(8,128)S(1)} %get-tuple-element.57.refs_0_), channel_id=1, source_target_pairs={{0,8},{4,12},{8,0},{12,4},{1,9},{5,13},{9,1},{13,5},{2,10},{6,14},... | collective-permute-start | bytes 12296 | tf_op jit(solution)/shard_map/ppermute | solution.py:517
  56.6 13.2 %collective-permute-start.19 = (bf16[1024,128]{1,0:T(8,128)(2,1)S(1)}, bf16[1024,128]{1,0:T(8,128)(2,1)S(1)}, u32[]{:S(2)}, u32[]{:S(2)}) collective-permute-start(bf16[1024,128]{1,0:T(8,128)(2,1)S(1)} %get-tuple-element.60), channel_id=1, source_target_pairs={{0,1},{1,0},{2,3},{3,2},{4,5},{5,4},{6,7},{7,6},{8,9},{9,8},{10,11... | collective-permute-start | bytes 786440 | tf_op jit(solution)/shard_map/ppermute | solution.py:446
  59.8 10.0 %collective-permute-start.20 = (bf16[1024,128]{1,0:T(8,128)(2,1)S(1)}, bf16[1024,128]{1,0:T(8,128)(2,1)S(1)}, u32[]{:S(2)}, u32[]{:S(2)}) collective-permute-start(bf16[1024,128]{1,0:T(8,128)(2,1)S(1)} %get-tuple-element.61), channel_id=1, source_target_pairs={{0,3},{1,2},{2,1},{3,0},{4,7},{5,6},{6,5},{7,4},{8,11},{9,10},{10,... | collective-permute-start | bytes 786440 | tf_op jit(solution)/shard_map/ppermute | solution.py:446
  62.2 7.5 %collective-permute-start.21 = (bf16[144,128]{1,0:T(8,128)(2,1)S(1)}, bf16[144,128]{1,0:T(8,128)(2,1)S(1)}, u32[]{:S(2)}, u32[]{:S(2)}) collective-permute-start(bf16[144,128]{1,0:T(8,128)(2,1)S(1)} %get-tuple-element.62), channel_id=1, source_target_pairs={{0,1},{1,0},{2,3},{3,2},{4,5},{5,4},{6,7},{7,6},{8,9},{9,8},{10,11... | collective-permute-start | bytes 110600 | tf_op jit(solution)/shard_map/ppermute | solution.py:446
  62.3 7.4 %collective-permute-start.22 = (bf16[144,128]{1,0:T(8,128)(2,1)S(1)}, bf16[144,128]{1,0:T(8,128)(2,1)S(1)}, u32[]{:S(2)}, u32[]{:S(2)}) collective-permute-start(bf16[144,128]{1,0:T(8,128)(2,1)S(1)} %get-tuple-element.63), channel_id=1, source_target_pairs={{0,3},{1,2},{2,1},{3,0},{4,7},{5,6},{6,5},{7,4},{8,11},{9,10},{10,... | collective-permute-start | bytes 110600 | tf_op jit(solution)/shard_map/ppermute | solution.py:446
  66.8 5.2 %collective-permute-start.23 = (f32[8,128]{1,0:T(8,128)S(1)}, f32[8,128]{1,0:T(8,128)S(1)}, u32[]{:S(2)}, u32[]{:S(2)}) collective-permute-start(f32[8,128]{1,0:T(8,128)S(1)} %get-tuple-element.64.sums), channel_id=1, source_target_pairs={{0,2},{1,3},{2,0},{3,1},{4,6},{5,7},{6,4},{7,5},{8,10},{9,11},{10,... | collective-permute-start | bytes 12296 | tf_op jit(solution)/shard_map/ppermute | solution.py:536

commit v6 on v5

--- a/solution.py
+++ b/solution.py
@@ -126,7 +126,7 @@
     square[...] = total
 
 
-def centre_back_kernel(cols, own, first, second, band, control, sums, hessian, outer, same, middle, done):
+def centre_back_kernel(cols, own, first, second, band, control, hessian, outer, middle, done):
     members, cells, levels = own.shape
     size = ROWS * cols
     batch = 2 * ROWS
@@ -145,7 +145,6 @@
             )
             copy.start()
             copies.append(copy)
-    same[...] = sums[...]
     for copy in copies:
         copy.wait()
 
@@ -305,10 +304,8 @@
 
 def corners_kernel(cols, members, first, second, *refs):
     if len(refs) > 2:
-        sums, far, around, *out, total = refs
-        at, last = lax.axis_index("lat"), lax.axis_size("lat") - 1
-        other = jnp.where(jnp.logical_or(at == 0, at == last), around[0:1, :], get_sums(second))
-        value = (sums[0:1, :] + get_sums(first)) + (far[0:1, :] + other)
+        sums, far, *out, total = refs
+        value = (sums[0:1, :] + get_sums(first)) + (far[0:1, :] + get_sums(second))
         total[...] = jnp.broadcast_to(value, total.shape)
         for ref in out:
             put_sums(ref, value)
@@ -405,7 +402,8 @@
 
 
 def backward_kernel(
-    cols, outer, one, two, one_corner, two_corner, band, sums, _, hessian, same, result, west, east, done
+    cols, entries, outer, one, two, one_corner, two_corner, band, sums, far, _,
+    hessian, curvature, result, west, east, done,
 ):
     members, tile_rows, width, levels = outer.shape
     cells = tile_rows * cols
@@ -429,21 +427,21 @@
                         )
                         copy.start()
                         copies.append(copy)
-    same[...] = sums[...]
+    value = (sums[0:1, :] + get_sums(one_corner)) + (far[0:1, :] + get_sums(two_corner))
+    curvature[0, 0] = jnp.sum(value) / entries
     for copy in copies:
         copy.wait()
 
 
-def finish_kernel(entries, sums, far, one_corner, two_corner, curvature):
-    value = (sums[0:1, :] + get_sums(one_corner)) + (far[0:1, :] + get_sums(two_corner))
-    curvature[0, 0] = jnp.sum(value) / entries
-
-
 def exchange(first, second, axis):
-    other = swap(axis, 3)
     if axis == "lat":
-        other = [(i, j) for i, j in other if abs(i - j) == 1]
-    return lax.ppermute(first, axis, swap(axis, 1)), lax.ppermute(second, axis, other)
+        count = lax.axis_size("zh") * lax.axis_size("lat")
+        axis = ("zh", "lat")
+    else:
+        count = lax.axis_size(axis)
+    one = [(i, i ^ 1) for i in range(count)]
+    two = [(i, (i + 1 if i % 2 else i - 1) % count) for i in range(count)]
+    return lax.ppermute(first, axis, one), lax.ppermute(second, axis, two)
 
 
 def per_device(control, ensemble, precision, lat_taps, lon_taps, vertical):
@@ -513,19 +511,18 @@
         size=4_500_000,
     )
     one, two = exchange(first, second, "lat")
-    last = lax.axis_size("lat") - 1
     far = lax.ppermute(sums, "lat", swap("lat", 2))
-    around = lax.ppermute(sums, "lat", [(0, last), (last, 0)])
     beside_it = exchange(*strips(adjoint, cols), "lon")
-    *corner, sums = corners(one, two, cols, members, sums, far, around)
+    *corner, sums = corners(one, two, cols, members, sums, far)
     corner = exchange(*corner, "lon")
     outer_shape = (members, tile_rows, 16, levels)
-    hessian, outer, sums = call(
+    far = lax.ppermute(sums, "lon", swap("lon", 2))
+    hessian, outer = call(
         functools.partial(centre_back_kernel, cols),
         "centre_back",
-        [jax.ShapeDtypeStruct(control.shape, F32), jax.ShapeDtypeStruct(outer_shape, F32), row],
-        (adjoint, one, two, band_back, own, sums),
-        out_specs=(pl.BlockSpec(memory_space=pl.ANY), VMEM, VMEM),
+        [jax.ShapeDtypeStruct(control.shape, F32), jax.ShapeDtypeStruct(outer_shape, F32)],
+        (adjoint, one, two, band_back, own),
+        out_specs=(pl.BlockSpec(memory_space=pl.ANY), VMEM),
         scratch=(
             pltpu.VMEM((members, tile_rows, cols - 16, levels), F32),
             pltpu.SemaphoreType.DMA((members * tile_rows // (2 * ROWS),)),
@@ -533,30 +530,22 @@
         flops=3_000_000_000,
         size=7_000_000,
     )
-    far = lax.ppermute(sums, "lon", swap("lon", 2))
-    hessian, sums = call(
-        functools.partial(backward_kernel, cols),
+    hessian, curvature = call(
+        functools.partial(backward_kernel, cols, entries),
         "backward",
-        [jax.ShapeDtypeStruct(control.shape, F32), row],
-        (outer, *beside_it, *corner, band_side_back, sums, hessian),
-        in_specs=[VMEM] * 7 + [pl.BlockSpec(memory_space=pl.ANY)],
+        [jax.ShapeDtypeStruct(control.shape, F32), jax.ShapeDtypeStruct((1, 1), F32)],
+        (outer, *beside_it, *corner, band_side_back, sums, far, hessian),
+        in_specs=[VMEM] * 8 + [pl.BlockSpec(memory_space=pl.ANY)],
         scratch=(
             pltpu.VMEM(outer_shape, F32),
             pltpu.VMEM(joint.shape, BF),
             pltpu.VMEM(joint.shape, BF),
             pltpu.SemaphoreType.DMA((2 * members * tile_rows // (2 * ROWS),)),
         ),
-        out_specs=(pl.BlockSpec(memory_space=pl.ANY), VMEM),
-        aliases={7: 0},
+        out_specs=(pl.BlockSpec(memory_space=pl.ANY), SMEM),
+        aliases={8: 0},
         flops=1_000_000_000,
         size=9_000_000,
-    )
-    (curvature,) = call(
-        functools.partial(finish_kernel, entries),
-        "finish",
-        [jax.ShapeDtypeStruct((1, 1), F32)],
-        (sums, far, *corner),
-        out_specs=(SMEM,),
     )
     return hessian, curvature.reshape(())
 

time: 72.9 us -> 69 us (0.947)
  starting transfers between devices: 38.1 us -> 34.6 us
    ppermute x1, starting transfers between devices: 6.38 us -> 3.35 us  [per_device(): other = lax.ppermute(message, 'zh', swap('zh', 1))]
    ppermute x13 -> x12, waiting for transfers between devices: 5.36 us -> 2.49 us  [exchange(): return (lax.ppermute(first, axis, one), lax.ppermute(second, axis, two))]
    ppermute x1, waiting for transfers between devices: 1.85 us -> 4.45 us  [per_device(): other = lax.ppermute(message, 'zh', swap('zh', 1))]
    ppermute x1, starting transfers between devices: 0.09 us -> 1.42 us  [per_device(): far = lax.ppermute(sums, 'lat', swap('lat', 2))]
    ppermute x1, starting transfers between devices: 3.02 us -> 1.78 us  [per_device(): far = lax.ppermute(sums, 'lon', swap('lon', 2))]
    ppermute x13 -> x12, starting transfers between devices: 20.3 us -> 19.8 us  [exchange(): return (lax.ppermute(first, axis, one), lax.ppermute(second, axis, two))]
    pallas_call x17 -> x16, Pallas kernels: 12.4 us -> 12.3 us  [call(): pl.pallas_call(kernel, out_shape=tuple(shapes), in_specs=in_specs or [VME...]
  transfers between devices with their start and end apart: 24 -> 23, of which waited for: 12 -> 11; matrix products, arithmetic and copies ran while one was open for 0% -> 0% of each run, Pallas kernels for 16% -> 14%
where the time goes in v6:
time: 69 us; the launch traced here: 68.9 us
  starting transfers between devices  34.6 us (50%)
  waiting for transfers between devices  17.9 us (26%)
  Pallas kernels  13.8 us (20%)
  local copies, waits for them, and re-layouts  1.61 us (2%)
  between operations  1 us (1%)
    ppermute x12, starting transfers between devices, exchange(): return (lax.ppermute(first, axis, one), lax.ppermute(second, axis, two))  19.8 us
    pallas_call x16, Pallas kernels, call(): pl.pallas_call(kernel, out_shape=tuple(shapes), in_specs=in_specs or [VME...  12.3 us
    ppermute x3, starting transfers between devices, per_device(): two, one, three = [lax.ppermute(zero, 'x', swap('x', k)) for k in (2, 1, 3)]  4.52 us
    ppermute x1, waiting for transfers between devices, per_device(): other = lax.ppermute(message, 'zh', swap('zh', 1))  4.45 us
    ppermute x3, waiting for transfers between devices, per_device(): two, one, three = [lax.ppermute(zero, 'x', swap('x', k)) for k in (2, 1, 3)]  4.31 us
    ppermute x3, waiting for transfers between devices, per_device(): lax.ppermute(v, 'x', swap('x', k))  4.12 us
    ppermute x3, starting transfers between devices, per_device(): lax.ppermute(v, 'x', swap('x', k))  3.58 us
    ppermute x1, starting transfers between devices, per_device(): other = lax.ppermute(message, 'zh', swap('zh', 1))  3.35 us
  transfers between devices with their start and end apart: 23, of which 11 were waited for; matrix products, arithmetic and copies ran while one was open for 0% of the time, Pallas kernels for 14%

profile of v6, /device:TPU:2, one launch (start us, length us, event | category | flops | bytes accessed | tf_op | source)
XLA Modules:
  0.0 68.9 jit_solution(5247696993222795207)
XLA Ops:
  0.6 1.6 %copy-done.1 = bf16[4,64,32,128]{3,2,1,0:T(8,128)(2,1)S(1)} copy-done((bf16[4,64,32,128]{3,2,1,0:T(8,128)(2,1)S(1)}, bf16[4,64,32,128]{3,2,1,0:T(8,128)(2,1)}, u32[]{:S(2)}) %copy-start.1) | copy-done | bytes 2097176
  2.3 2.0 %collective-permute-start = (bf16[512,128]{1,0:T(8,128)(2,1)S(1)}, bf16[512,128]{1,0:T(8,128)(2,1)S(1)}, u32[]{:S(2)}, u32[]{:S(2)}) collective-permute-start(bf16[512,128]{1,0:T(8,128)(2,1)S(1)} %get-tuple-element.34), channel_id=1, source_target_pairs={{0,4},{4,0},{8,12},{12,8},{128,132},{132,128},{136,140},{140,136},... | collective-permute-start | bytes 393224 | tf_op jit(solution)/shard_map/ppermute | solution.py:444
  4.3 4.9 %collective-permute-start.1 = (bf16[512,128]{1,0:T(8,128)(2,1)S(1)}, bf16[512,128]{1,0:T(8,128)(2,1)S(1)}, u32[]{:S(2)}, u32[]{:S(2)}) collective-permute-start(bf16[512,128]{1,0:T(8,128)(2,1)S(1)} %get-tuple-element.35), channel_id=1, source_target_pairs={{0,140},{4,8},{8,4},{12,128},{128,12},{132,136},{136,132},{140,0},... | collective-permute-start | bytes 393224 | tf_op jit(solution)/shard_map/ppermute | solution.py:444
  9.2 0.5 strips.2
  9.7 1.7 %collective-permute-start.2 = (bf16[1024,128]{1,0:T(8,128)(2,1)S(1)}, bf16[1024,128]{1,0:T(8,128)(2,1)S(1)}, u32[]{:S(2)}, u32[]{:S(2)}) collective-permute-start(bf16[1024,128]{1,0:T(8,128)(2,1)S(1)} %get-tuple-element.38), channel_id=1, source_target_pairs={{0,1},{1,0},{2,3},{3,2},{4,5},{5,4},{6,7},{7,6},{8,9},{9,8},{10,11... | collective-permute-start | bytes 786440 | tf_op jit(solution)/shard_map/ppermute | solution.py:444
  11.4 2.2 %collective-permute-start.3 = (bf16[1024,128]{1,0:T(8,128)(2,1)S(1)}, bf16[1024,128]{1,0:T(8,128)(2,1)S(1)}, u32[]{:S(2)}, u32[]{:S(2)}) collective-permute-start(bf16[1024,128]{1,0:T(8,128)(2,1)S(1)} %get-tuple-element.39), channel_id=1, source_target_pairs={{0,3},{1,2},{2,1},{3,0},{4,7},{5,6},{6,5},{7,4},{8,11},{9,10},{10,... | collective-permute-start | bytes 786440 | tf_op jit(solution)/shard_map/ppermute | solution.py:444
  13.6 0.8 %bands.1 = (bf16[512,512]{1,0:T(8,128)(2,1)S(1)}, bf16[256,128]{1,0:T(8,128)(2,1)S(1)}) custom-call(f32[9]{0:T(128)S(1)} %copy-done.5, f32[9]{0:T(128)S(1)} %copy-done.6), custom_call_target="tpu_custom_call" | custom-call | flops 2000000 | bytes 600000 | tf_op jit(solution)/shard_map/bands/pallas_call | solution.py:76
  14.3 0.2 corners.2
  14.5 0.8 %collective-permute-start.4 = (bf16[128,128]{1,0:T(8,128)(2,1)S(1)}, bf16[128,128]{1,0:T(8,128)(2,1)S(1)}, u32[]{:S(2)}, u32[]{:S(2)}) collective-permute-start(bf16[128,128]{1,0:T(8,128)(2,1)S(1)} %get-tuple-element.40), channel_id=1, source_target_pairs={{0,1},{1,0},{2,3},{3,2},{4,5},{5,4},{6,7},{7,6},{8,9},{9,8},{10,11... | collective-permute-start | bytes 98312 | tf_op jit(solution)/shard_map/ppermute | solution.py:444
  15.3 1.2 %collective-permute-start.5 = (bf16[128,128]{1,0:T(8,128)(2,1)S(1)}, bf16[128,128]{1,0:T(8,128)(2,1)S(1)}, u32[]{:S(2)}, u32[]{:S(2)}) collective-permute-start(bf16[128,128]{1,0:T(8,128)(2,1)S(1)} %get-tuple-element.41), channel_id=1, source_target_pairs={{0,3},{1,2},{2,1},{3,0},{4,7},{5,6},{6,5},{7,4},{8,11},{9,10},{10,... | collective-permute-start | bytes 98312 | tf_op jit(solution)/shard_map/ppermute | solution.py:444
  16.5 2.3 %centre.1 = (f32[4,2048,128]{2,1,0:T(8,128)S(1)}, f32[8,128]{1,0:T(8,128)S(1)}) custom-call(bf16[4,2048,128]{2,1,0:T(8,128)(2,1)S(1)} %bitcast.10, bf16[512,128]{1,0:T(8,128)(2,1)S(1)} %collective-permute-done.first, bf16[512,128]{1,0:T(8,128)(2,1)S(1)} %collective-permute-done.1.second, bf16[512,512]{1,0:T(8,128)(2,1)S(1)} %get-tuple-element.36.band), custom_call_target="tpu_custom_call" | custom-call | flops 3000000000 | bytes 7000000 | tf_op jit(solution)/shard_map/centre/pallas_call | solution.py:241
  18.9 1.6 %collective-permute-done.5.two_corner = bf16[128,128]{1,0:T(8,128)(2,1)S(1)} collective-permute-done((bf16[128,128]{1,0:T(8,128)(2,1)S(1)}, bf16[128,128]{1,0:T(8,128)(2,1)S(1)}, u32[]{:S(2)}, u32[]{:S(2)}) %collective-permute-start.5) | collective-permute-done | bytes 32800 | tf_op jit(solution)/shard_map/ppermute | solution.py:444
  20.5 0.9 %forward_send.1 = (bf16[1024,128]{1,0:T(8,128)(2,1)S(1)}, bf16[1152,128]{1,0:T(8,128)(2,1)S(1)}, bf16[1152,128]{1,0:T(8,128)(2,1)S(1)}) custom-call(f32[4,2048,128]{2,1,0:T(8,128)S(1)} %get-tuple-element.37.inner, bf16[1024,128]{1,0:T(8,128)(2,1)S(1)} %collective-permute-done.2.one, bf16[1024,128]{1,0:T(8,128)(2,1)S(1)} %collective-permute-done.3.two, ...), custom_call_target="tpu_custom_call" | custom-call | flops 700000000 | bytes 3000000 | tf_op jit(solution)/shard_map/forward_send/pallas_call | solution.py:241
  21.4 0.1 collective-permute-start.6
  21.5 0.9 %forward_keep.1.keep = bf16[1024,128]{1,0:T(8,128)(2,1)S(1)} custom-call(f32[4,2048,128]{2,1,0:T(8,128)S(1)} %get-tuple-element.37.inner, bf16[1152,128]{1,0:T(8,128)(2,1)S(1)} %get-tuple-element.43.west, bf16[1152,128]{1,0:T(8,128)(2,1)S(1)} %get-tuple-element.44.east, bf16[256,128]{1,0:T(8,128)(2,1)S(1)} %get-tuple-element.42.band, ...), custom_call_target="tpu_custom_call" | custom-call | flops 700000000 | bytes 3000000 | tf_op jit(solution)/shard_map/forward_keep/pallas_call | solution.py:241
  22.4 0.6 collective-permute-done.6.got
  23.1 0.6 collective-permute-start.7
  23.7 2.4 %collective-permute-start.8 = (bf16[256,128]{1,0:T(8,128)(2,1)S(1)}, bf16[256,128]{1,0:T(8,128)(2,1)S(1)}, u32[]{:S(2)}, u32[]{:S(2)}) collective-permute-start(bf16[256,128]{1,0:T(8,128)(2,1)S(1)} %get-tuple-element.48), channel_id=1, source_target_pairs={{0,64},{32,96},{64,0},{96,32},{1,65},{33,97},{65,1},{97,33},{2,66}... | collective-permute-start | bytes 196616 | tf_op jit(solution)/shard_map/ppermute | solution.py:492
  26.1 0.5 collective-permute-start.9
  26.7 0.8 %collective-permute-done.7.one = bf16[256,128]{1,0:T(8,128)(2,1)S(1)} collective-permute-done((bf16[256,128]{1,0:T(8,128)(2,1)S(1)}, bf16[256,128]{1,0:T(8,128)(2,1)S(1)}, u32[]{:S(2)}, u32[]{:S(2)}) %collective-permute-start.7) | collective-permute-done | bytes 65568 | tf_op jit(solution)/shard_map/ppermute | solution.py:492
  27.4 2.4 %collective-permute-done.8.two = bf16[256,128]{1,0:T(8,128)(2,1)S(1)} collective-permute-done((bf16[256,128]{1,0:T(8,128)(2,1)S(1)}, bf16[256,128]{1,0:T(8,128)(2,1)S(1)}, u32[]{:S(2)}, u32[]{:S(2)}) %collective-permute-start.8) | collective-permute-done | bytes 65568 | tf_op jit(solution)/shard_map/ppermute | solution.py:492
  29.9 0.9 %collective-permute-done.9.three.refs_0_ = bf16[256,128]{1,0:T(8,128)(2,1)S(1)} collective-permute-done((bf16[256,128]{1,0:T(8,128)(2,1)S(1)}, bf16[256,128]{1,0:T(8,128)(2,1)S(1)}, u32[]{:S(2)}, u32[]{:S(2)}) %collective-permute-start.9) | collective-permute-done | bytes 65568 | tf_op jit(solution)/shard_map/ppermute | solution.py:492
  30.8 3.3 %collective-permute-start.10 = (bf16[272,128]{1,0:T(8,128)(2,1)S(1)}, bf16[272,128]{1,0:T(8,128)(2,1)S(1)}, u32[]{:S(2)}, u32[]{:S(2)}) collective-permute-start(bf16[272,128]{1,0:T(8,128)(2,1)S(1)} %part.1.message), channel_id=1, source_target_pairs={{0,128},{128,0},{1,129},{129,1},{2,130},{130,2},{3,131},{131,3},{4... | collective-permute-start | bytes 208904 | tf_op jit(solution)/shard_map/ppermute | solution.py:495
  34.2 0.8 %bands_back.1 = (bf16[512,512]{1,0:T(8,128)(2,1)S(1)}, bf16[256,128]{1,0:T(8,128)(2,1)S(1)}) custom-call(f32[9]{0:T(128)S(1)} %copy-done.5, f32[9]{0:T(128)S(1)} %copy-done.6, bf16[256,128]{1,0:T(8,128)(2,1)S(1)} %collective-permute-done.9.three.refs_0_), custom_call_target="tpu_custom_call" | custom-call | flops 2000000 | bytes 600000 | tf_op jit(solution)/shard_map/bands_back/pallas_call | solution.py:76
  34.9 4.5 %collective-permute-done.10.other = bf16[272,128]{1,0:T(8,128)(2,1)S(1)} collective-permute-done((bf16[272,128]{1,0:T(8,128)(2,1)S(1)}, bf16[272,128]{1,0:T(8,128)(2,1)S(1)}, u32[]{:S(2)}, u32[]{:S(2)}) %collective-permute-start.10) | collective-permute-done | bytes 69664 | tf_op jit(solution)/shard_map/ppermute | solution.py:495
  39.4 0.1 weight.1.zero
  39.5 1.0 %collective-permute-start.13 = (bf16[272,128]{1,0:T(8,128)(2,1)S(1)}, bf16[272,128]{1,0:T(8,128)(2,1)S(1)}, u32[]{:S(2)}, u32[]{:S(2)}) collective-permute-start(bf16[272,128]{1,0:T(8,128)(2,1)S(1)} %weight.1.zero), channel_id=1, source_target_pairs={{0,96},{32,64},{64,32},{96,0},{1,97},{33,65},{65,33},{97,1},{2,98}... | collective-permute-start | bytes 208904 | tf_op jit(solution)/shard_map/ppermute | solution.py:497
  40.4 3.6 %collective-permute-start.12 = (bf16[272,128]{1,0:T(8,128)(2,1)S(1)}, bf16[272,128]{1,0:T(8,128)(2,1)S(1)}, u32[]{:S(2)}, u32[]{:S(2)}) collective-permute-start(bf16[272,128]{1,0:T(8,128)(2,1)S(1)} %weight.1.zero), channel_id=1, source_target_pairs={{0,64},{32,96},{64,0},{96,32},{1,65},{33,97},{65,1},{97,33},{2,66}... | collective-permute-start | bytes 208904 | tf_op jit(solution)/shard_map/ppermute | solution.py:497
  44.0 2.3 %collective-permute-done.12.two = bf16[272,128]{1,0:T(8,128)(2,1)S(1)} collective-permute-done((bf16[272,128]{1,0:T(8,128)(2,1)S(1)}, bf16[272,128]{1,0:T(8,128)(2,1)S(1)}, u32[]{:S(2)}, u32[]{:S(2)}) %collective-permute-start.12) | collective-permute-done | bytes 69664 | tf_op jit(solution)/shard_map/ppermute | solution.py:497
  46.3 2.0 %collective-permute-done.11.one = bf16[272,128]{1,0:T(8,128)(2,1)S(1)} collective-permute-done((bf16[272,128]{1,0:T(8,128)(2,1)S(1)}, bf16[272,128]{1,0:T(8,128)(2,1)S(1)}, u32[]{:S(2)}, u32[]{:S(2)}) %collective-permute-start.11) | collective-permute-done | bytes 69664 | tf_op jit(solution)/shard_map/ppermute | solution.py:497
  48.3 0.1 collective-permute-start.14
  48.4 1.5 %collective-permute-done.14.other = bf16[1040,128]{1,0:T(8,128)(2,1)S(1)} collective-permute-done((bf16[1040,128]{1,0:T(8,128)(2,1)S(1)}, bf16[1040,128]{1,0:T(8,128)(2,1)S(1)}, u32[]{:S(2)}, u32[]{:S(2)}) %collective-permute-start.14) | collective-permute-done | bytes 266272 | tf_op jit(solution)/shard_map/ppermute | solution.py:499
  50.0 0.3 level_edges.1
  50.3 0.1 collective-permute-start.15
  50.4 2.1 %collective-permute-start.16 = (bf16[528,128]{1,0:T(8,128)(2,1)S(1)}, bf16[528,128]{1,0:T(8,128)(2,1)S(1)}, u32[]{:S(2)}, u32[]{:S(2)}) collective-permute-start(bf16[528,128]{1,0:T(8,128)(2,1)S(1)} %get-tuple-element.54), channel_id=1, source_target_pairs={{0,140},{4,8},{8,4},{12,128},{128,12},{132,136},{136,132},{140,0},... | collective-permute-start | bytes 405512 | tf_op jit(solution)/shard_map/ppermute | solution.py:444
  52.5 0.7 %level.1 = (bf16[4,2048,128]{2,1,0:T(8,128)(2,1)S(1)}, f32[8,128]{1,0:T(8,128)S(1)}) custom-call(bf16[1040,128]{1,0:T(8,128)(2,1)S(1)} %gather.1.mine, bf16[1040,128]{1,0:T(8,128)(2,1)S(1)} %collective-permute-done.14.other, bf16[4,2048,128]{2,1,0:T(8,128)(2,1)S(1)} %bitcast.7, bf16[128,128]{1,0:T(8,128)(2,1)S(1)} %copy-done.4), custom_call_target="tpu_custom_call" | custom-call | flops 300000000 | bytes 4500000 | tf_op jit(solution)/shard_map/level/pallas_call | solution.py:241
  53.2 1.4 %collective-permute-start.19 = (f32[8,128]{1,0:T(8,128)S(1)}, f32[8,128]{1,0:T(8,128)S(1)}, u32[]{:S(2)}, u32[]{:S(2)}) collective-permute-start(f32[8,128]{1,0:T(8,128)S(1)} %get-tuple-element.59.refs_0_), channel_id=1, source_target_pairs={{0,8},{4,12},{8,0},{12,4},{1,9},{5,13},{9,1},{13,5},{2,10},{6,14},... | collective-permute-start | bytes 12296 | tf_op jit(solution)/shard_map/ppermute | solution.py:514
  54.7 0.5 strips.3
  55.1 0.2 collective-permute-start.17
  55.3 2.2 %collective-permute-start.18 = (bf16[1024,128]{1,0:T(8,128)(2,1)S(1)}, bf16[1024,128]{1,0:T(8,128)(2,1)S(1)}, u32[]{:S(2)}, u32[]{:S(2)}) collective-permute-start(bf16[1024,128]{1,0:T(8,128)(2,1)S(1)} %get-tuple-element.58), channel_id=1, source_target_pairs={{0,3},{1,2},{2,1},{3,0},{4,7},{5,6},{6,5},{7,4},{8,11},{9,10},{10,... | collective-permute-start | bytes 786440 | tf_op jit(solution)/shard_map/ppermute | solution.py:444
  57.5 0.3 collective-permute-done.19.refs_1_
  57.8 0.2 corners.3
  58.0 1.8 %collective-permute-start.22 = (f32[8,128]{1,0:T(8,128)S(1)}, f32[8,128]{1,0:T(8,128)S(1)}, u32[]{:S(2)}, u32[]{:S(2)}) collective-permute-start(f32[8,128]{1,0:T(8,128)S(1)} %get-tuple-element.62.sums), channel_id=1, source_target_pairs={{0,2},{1,3},{2,0},{3,1},{4,6},{5,7},{6,4},{7,5},{8,10},{9,11},{10,... | collective-permute-start | bytes 12296 | tf_op jit(solution)/shard_map/ppermute | solution.py:519
  59.8 1.4 %collective-permute-start.20 = (bf16[144,128]{1,0:T(8,128)(2,1)S(1)}, bf16[144,128]{1,0:T(8,128)(2,1)S(1)}, u32[]{:S(2)}, u32[]{:S(2)}) collective-permute-start(bf16[144,128]{1,0:T(8,128)(2,1)S(1)} %get-tuple-element.60), channel_id=1, source_target_pairs={{0,1},{1,0},{2,3},{3,2},{4,5},{5,4},{6,7},{7,6},{8,9},{9,8},{10,11... | collective-permute-start | bytes 110600 | tf_op jit(solution)/shard_map/ppermute | solution.py:444
  61.2 1.0 %collective-permute-start.21 = (bf16[144,128]{1,0:T(8,128)(2,1)S(1)}, bf16[144,128]{1,0:T(8,128)(2,1)S(1)}, u32[]{:S(2)}, u32[]{:S(2)}) collective-permute-start(bf16[144,128]{1,0:T(8,128)(2,1)S(1)} %get-tuple-element.61), channel_id=1, source_target_pairs={{0,3},{1,2},{2,1},{3,0},{4,7},{5,6},{6,5},{7,4},{8,11},{9,10},{10,... | collective-permute-start | bytes 110600 | tf_op jit(solution)/shard_map/ppermute | solution.py:444
  62.2 3.3 %centre_back.1 = (f32[4,64,32,128]{3,2,1,0:T(8,128)}, f32[4,64,16,128]{3,2,1,0:T(8,128)S(1)}) custom-call(bf16[4,2048,128]{2,1,0:T(8,128)(2,1)S(1)} %get-tuple-element.52.own.tile, bf16[528,128]{1,0:T(8,128)(2,1)S(1)} %collective-permute-done.15.first, bf16[528,128]{1,0:T(8,128)(2,1)S(1)} %collective-permute-done.16.second, ...), custom_call_target="tpu_custom_call" | custom-call | flops 3000000000 | bytes 7000000 | tf_op jit(solution)/shard_map/centre_back/pallas_call | solution.py:241
  65.5 0.8 %collective-permute-done.21.two_corner = bf16[144,128]{1,0:T(8,128)(2,1)S(1)} collective-permute-done((bf16[144,128]{1,0:T(8,128)(2,1)S(1)}, bf16[144,128]{1,0:T(8,128)(2,1)S(1)}, u32[]{:S(2)}, u32[]{:S(2)}) %collective-permute-start.21) | collective-permute-done | bytes 36896 | tf_op jit(solution)/shard_map/ppermute | solution.py:444
  66.3 2.3 %backward.1 = (f32[4,64,32,128]{3,2,1,0:T(8,128)}, f32[1,1]{1,0:T(1,128)}) custom-call(f32[4,64,16,128]{3,2,1,0:T(8,128)S(1)} %get-tuple-element.56.outer, bf16[1024,128]{1,0:T(8,128)(2,1)S(1)} %collective-permute-done.17.one, bf16[1024,128]{1,0:T(8,128)(2,1)S(1)} %collective-permute-done.18.two, ...), custom_call_target="tpu_custom_call", output_to_operand_aliasing={{0}: (8, {})} | custom-call | flops 1000000000 | bytes 9000000 | tf_op jit(solution)/shard_map/backward/pallas_call | solution.py:241
  (30 shorter events, 0.3 us)
Async XLA Ops:
  0.6 1.6 %copy-start.1 = (bf16[4,64,32,128]{3,2,1,0:T(8,128)(2,1)S(1)}, bf16[4,64,32,128]{3,2,1,0:T(8,128)(2,1)}, u32[]{:S(2)}) copy-start(bf16[4,64,32,128]{3,2,1,0:T(8,128)(2,1)} %param.6) | copy-start | bytes 6291460
  2.2 11.3 %copy-start.5 = (f32[9]{0:T(128)S(1)}, f32[9]{0:T(128)}, u32[]{:S(2)}) copy-start(f32[9]{0:T(128)} %lat_taps.3) | copy-start | bytes 112
  2.2 11.3 %copy-start.6 = (f32[9]{0:T(128)S(1)}, f32[9]{0:T(128)}, u32[]{:S(2)}) copy-start(f32[9]{0:T(128)} %lon_taps.3) | copy-start | bytes 112
  2.2 14.3 %copy-start.2 = (bf16[4,64,32,128]{3,2,1,0:T(8,128)(2,1)S(1)}, bf16[4,64,32,128]{3,2,1,0:T(8,128)(2,1)}, u32[]{:S(2)}) copy-start(bf16[4,64,32,128]{3,2,1,0:T(8,128)(2,1)} %param.6) | copy-start | bytes 6291460
  2.3 12.0 %collective-permute-start = (bf16[512,128]{1,0:T(8,128)(2,1)S(1)}, bf16[512,128]{1,0:T(8,128)(2,1)S(1)}, u32[]{:S(2)}, u32[]{:S(2)}) collective-permute-start(bf16[512,128]{1,0:T(8,128)(2,1)S(1)} %get-tuple-element.34), channel_id=1, source_target_pairs={{0,4},{4,0},{8,12},{12,8},{128,132},{132,128},{136,140},{140,136},... | collective-permute-start | bytes 393224 | tf_op jit(solution)/shard_map/ppermute | solution.py:444
  4.3 10.0 %collective-permute-start.1 = (bf16[512,128]{1,0:T(8,128)(2,1)S(1)}, bf16[512,128]{1,0:T(8,128)(2,1)S(1)}, u32[]{:S(2)}, u32[]{:S(2)}) collective-permute-start(bf16[512,128]{1,0:T(8,128)(2,1)S(1)} %get-tuple-element.35), channel_id=1, source_target_pairs={{0,140},{4,8},{8,4},{12,128},{128,12},{132,136},{136,132},{140,0},... | collective-permute-start | bytes 393224 | tf_op jit(solution)/shard_map/ppermute | solution.py:444
  9.7 10.8 %collective-permute-start.2 = (bf16[1024,128]{1,0:T(8,128)(2,1)S(1)}, bf16[1024,128]{1,0:T(8,128)(2,1)S(1)}, u32[]{:S(2)}, u32[]{:S(2)}) collective-permute-start(bf16[1024,128]{1,0:T(8,128)(2,1)S(1)} %get-tuple-element.38), channel_id=1, source_target_pairs={{0,1},{1,0},{2,3},{3,2},{4,5},{5,4},{6,7},{7,6},{8,9},{9,8},{10,11... | collective-permute-start | bytes 786440 | tf_op jit(solution)/shard_map/ppermute | solution.py:444
  11.4 9.1 %collective-permute-start.3 = (bf16[1024,128]{1,0:T(8,128)(2,1)S(1)}, bf16[1024,128]{1,0:T(8,128)(2,1)S(1)}, u32[]{:S(2)}, u32[]{:S(2)}) collective-permute-start(bf16[1024,128]{1,0:T(8,128)(2,1)S(1)} %get-tuple-element.39), channel_id=1, source_target_pairs={{0,3},{1,2},{2,1},{3,0},{4,7},{5,6},{6,5},{7,4},{8,11},{9,10},{10,... | collective-permute-start | bytes 786440 | tf_op jit(solution)/shard_map/ppermute | solution.py:444
  14.5 4.3 %collective-permute-start.4 = (bf16[128,128]{1,0:T(8,128)(2,1)S(1)}, bf16[128,128]{1,0:T(8,128)(2,1)S(1)}, u32[]{:S(2)}, u32[]{:S(2)}) collective-permute-start(bf16[128,128]{1,0:T(8,128)(2,1)S(1)} %get-tuple-element.40), channel_id=1, source_target_pairs={{0,1},{1,0},{2,3},{3,2},{4,5},{5,4},{6,7},{7,6},{8,9},{9,8},{10,11... | collective-permute-start | bytes 98312 | tf_op jit(solution)/shard_map/ppermute | solution.py:444
  15.3 5.2 %collective-permute-start.5 = (bf16[128,128]{1,0:T(8,128)(2,1)S(1)}, bf16[128,128]{1,0:T(8,128)(2,1)S(1)}, u32[]{:S(2)}, u32[]{:S(2)}) collective-permute-start(bf16[128,128]{1,0:T(8,128)(2,1)S(1)} %get-tuple-element.41), channel_id=1, source_target_pairs={{0,3},{1,2},{2,1},{3,0},{4,7},{5,6},{6,5},{7,4},{8,11},{9,10},{10,... | collective-permute-start | bytes 98312 | tf_op jit(solution)/shard_map/ppermute | solution.py:444
  16.5 4.0 %copy-start = (bf16[4,64,32,128]{3,2,1,0:T(8,128)(2,1)S(1)}, bf16[4,64,32,128]{3,2,1,0:T(8,128)(2,1)}, u32[]{:S(2)}) copy-start(bf16[4,64,32,128]{3,2,1,0:T(8,128)(2,1)} %param.7) | copy-start | bytes 6291460
  16.5 4.0 %copy-start.4 = (bf16[128,128]{1,0:T(8,128)(2,1)S(1)}, bf16[128,128]{1,0:T(8,128)(2,1)}, u32[]{:S(2)}) copy-start(bf16[128,128]{1,0:T(8,128)(2,1)} %vertical.7) | copy-start | bytes 98308
  21.4 1.6 %collective-permute-start.6 = (bf16[1024,128]{1,0:T(8,128)(2,1)S(1)}, bf16[1024,128]{1,0:T(8,128)(2,1)S(1)}, u32[]{:S(2)}, u32[]{:S(2)}) collective-permute-start(bf16[1024,128]{1,0:T(8,128)(2,1)S(1)} %get-tuple-element.45), channel_id=1, source_target_pairs={{0,16},{16,0},{1,17},{17,1},{2,18},{18,2},{3,19},{19,3},{4,20},{20... | collective-permute-start | bytes 786440 | tf_op jit(solution)/shard_map/ppermute | solution.py:490
  21.5 17.9 %copy-start.3 = (f32[64,32,128]{2,1,0:T(8,128)S(1)}, f32[64,32,128]{2,1,0:T(8,128)}, u32[]{:S(2)}) copy-start(f32[64,32,128]{2,1,0:T(8,128)} %param.8) | copy-start | bytes 3145732
  23.1 4.4 %collective-permute-start.7 = (bf16[256,128]{1,0:T(8,128)(2,1)S(1)}, bf16[256,128]{1,0:T(8,128)(2,1)S(1)}, u32[]{:S(2)}, u32[]{:S(2)}) collective-permute-start(bf16[256,128]{1,0:T(8,128)(2,1)S(1)} %get-tuple-element.47), channel_id=1, source_target_pairs={{0,32},{32,0},{64,96},{96,64},{1,33},{33,1},{65,97},{97,65},{2,34}... | collective-permute-start | bytes 196616 | tf_op jit(solution)/shard_map/ppermute | solution.py:492
  23.7 6.2 %collective-permute-start.8 = (bf16[256,128]{1,0:T(8,128)(2,1)S(1)}, bf16[256,128]{1,0:T(8,128)(2,1)S(1)}, u32[]{:S(2)}, u32[]{:S(2)}) collective-permute-start(bf16[256,128]{1,0:T(8,128)(2,1)S(1)} %get-tuple-element.48), channel_id=1, source_target_pairs={{0,64},{32,96},{64,0},{96,32},{1,65},{33,97},{65,1},{97,33},{2,66}... | collective-permute-start | bytes 196616 | tf_op jit(solution)/shard_map/ppermute | solution.py:492
  26.1 4.7 %collective-permute-start.9 = (bf16[256,128]{1,0:T(8,128)(2,1)S(1)}, bf16[256,128]{1,0:T(8,128)(2,1)S(1)}, u32[]{:S(2)}, u32[]{:S(2)}) collective-permute-start(bf16[256,128]{1,0:T(8,128)(2,1)S(1)} %get-tuple-element.49), channel_id=1, source_target_pairs={{0,96},{32,64},{64,32},{96,0},{1,97},{33,65},{65,33},{97,1},{2,98}... | collective-permute-start | bytes 196616 | tf_op jit(solution)/shard_map/ppermute | solution.py:492
  30.8 8.6 %collective-permute-start.10 = (bf16[272,128]{1,0:T(8,128)(2,1)S(1)}, bf16[272,128]{1,0:T(8,128)(2,1)S(1)}, u32[]{:S(2)}, u32[]{:S(2)}) collective-permute-start(bf16[272,128]{1,0:T(8,128)(2,1)S(1)} %part.1.message), channel_id=1, source_target_pairs={{0,128},{128,0},{1,129},{129,1},{2,130},{130,2},{3,131},{131,3},{4... | collective-permute-start | bytes 208904 | tf_op jit(solution)/shard_map/ppermute | solution.py:495
  39.5 4.5 %collective-permute-start.13 = (bf16[272,128]{1,0:T(8,128)(2,1)S(1)}, bf16[272,128]{1,0:T(8,128)(2,1)S(1)}, u32[]{:S(2)}, u32[]{:S(2)}) collective-permute-start(bf16[272,128]{1,0:T(8,128)(2,1)S(1)} %weight.1.zero), channel_id=1, source_target_pairs={{0,96},{32,64},{64,32},{96,0},{1,97},{33,65},{65,33},{97,1},{2,98}... | collective-permute-start | bytes 208904 | tf_op jit(solution)/shard_map/ppermute | solution.py:497
  40.4 5.8 %collective-permute-start.12 = (bf16[272,128]{1,0:T(8,128)(2,1)S(1)}, bf16[272,128]{1,0:T(8,128)(2,1)S(1)}, u32[]{:S(2)}, u32[]{:S(2)}) collective-permute-start(bf16[272,128]{1,0:T(8,128)(2,1)S(1)} %weight.1.zero), channel_id=1, source_target_pairs={{0,64},{32,96},{64,0},{96,32},{1,65},{33,97},{65,1},{97,33},{2,66}... | collective-permute-start | bytes 208904 | tf_op jit(solution)/shard_map/ppermute | solution.py:497
  44.0 4.3 %collective-permute-start.11 = (bf16[272,128]{1,0:T(8,128)(2,1)S(1)}, bf16[272,128]{1,0:T(8,128)(2,1)S(1)}, u32[]{:S(2)}, u32[]{:S(2)}) collective-permute-start(bf16[272,128]{1,0:T(8,128)(2,1)S(1)} %weight.1.zero), channel_id=1, source_target_pairs={{0,32},{32,0},{64,96},{96,64},{1,33},{33,1},{65,97},{97,65},{2,34}... | collective-permute-start | bytes 208904 | tf_op jit(solution)/shard_map/ppermute | solution.py:497
  48.3 1.6 %collective-permute-start.14 = (bf16[1040,128]{1,0:T(8,128)(2,1)S(1)}, bf16[1040,128]{1,0:T(8,128)(2,1)S(1)}, u32[]{:S(2)}, u32[]{:S(2)}) collective-permute-start(bf16[1040,128]{1,0:T(8,128)(2,1)S(1)} %gather.1.mine), channel_id=1, source_target_pairs={{0,16},{16,0},{1,17},{17,1},{2,18},{18,2},{3,19},{19,3},{4,20},{20... | collective-permute-start | bytes 798728 | tf_op jit(solution)/shard_map/ppermute | solution.py:499
  50.3 7.6 %collective-permute-start.15 = (bf16[528,128]{1,0:T(8,128)(2,1)S(1)}, bf16[528,128]{1,0:T(8,128)(2,1)S(1)}, u32[]{:S(2)}, u32[]{:S(2)}) collective-permute-start(bf16[528,128]{1,0:T(8,128)(2,1)S(1)} %get-tuple-element.53), channel_id=1, source_target_pairs={{0,4},{4,0},{8,12},{12,8},{128,132},{132,128},{136,140},{140,136},... | collective-permute-start | bytes 405512 | tf_op jit(solution)/shard_map/ppermute | solution.py:444
  50.4 7.5 %collective-permute-start.16 = (bf16[528,128]{1,0:T(8,128)(2,1)S(1)}, bf16[528,128]{1,0:T(8,128)(2,1)S(1)}, u32[]{:S(2)}, u32[]{:S(2)}) collective-permute-start(bf16[528,128]{1,0:T(8,128)(2,1)S(1)} %get-tuple-element.54), channel_id=1, source_target_pairs={{0,140},{4,8},{8,4},{12,128},{128,12},{132,136},{136,132},{140,0},... | collective-permute-start | bytes 405512 | tf_op jit(solution)/shard_map/ppermute | solution.py:444
  53.2 4.6 %collective-permute-start.19 = (f32[8,128]{1,0:T(8,128)S(1)}, f32[8,128]{1,0:T(8,128)S(1)}, u32[]{:S(2)}, u32[]{:S(2)}) collective-permute-start(f32[8,128]{1,0:T(8,128)S(1)} %get-tuple-element.59.refs_0_), channel_id=1, source_target_pairs={{0,8},{4,12},{8,0},{12,4},{1,9},{5,13},{9,1},{13,5},{2,10},{6,14},... | collective-permute-start | bytes 12296 | tf_op jit(solution)/shard_map/ppermute | solution.py:514
  55.1 11.2 %collective-permute-start.17 = (bf16[1024,128]{1,0:T(8,128)(2,1)S(1)}, bf16[1024,128]{1,0:T(8,128)(2,1)S(1)}, u32[]{:S(2)}, u32[]{:S(2)}) collective-permute-start(bf16[1024,128]{1,0:T(8,128)(2,1)S(1)} %get-tuple-element.57), channel_id=1, source_target_pairs={{0,1},{1,0},{2,3},{3,2},{4,5},{5,4},{6,7},{7,6},{8,9},{9,8},{10,11... | collective-permute-start | bytes 786440 | tf_op jit(solution)/shard_map/ppermute | solution.py:444
  55.3 11.1 %collective-permute-start.18 = (bf16[1024,128]{1,0:T(8,128)(2,1)S(1)}, bf16[1024,128]{1,0:T(8,128)(2,1)S(1)}, u32[]{:S(2)}, u32[]{:S(2)}) collective-permute-start(bf16[1024,128]{1,0:T(8,128)(2,1)S(1)} %get-tuple-element.58), channel_id=1, source_target_pairs={{0,3},{1,2},{2,1},{3,0},{4,7},{5,6},{6,5},{7,4},{8,11},{9,10},{10,... | collective-permute-start | bytes 786440 | tf_op jit(solution)/shard_map/ppermute | solution.py:444
  58.0 7.5 %collective-permute-start.22 = (f32[8,128]{1,0:T(8,128)S(1)}, f32[8,128]{1,0:T(8,128)S(1)}, u32[]{:S(2)}, u32[]{:S(2)}) collective-permute-start(f32[8,128]{1,0:T(8,128)S(1)} %get-tuple-element.62.sums), channel_id=1, source_target_pairs={{0,2},{1,3},{2,0},{3,1},{4,6},{5,7},{6,4},{7,5},{8,10},{9,11},{10,... | collective-permute-start | bytes 12296 | tf_op jit(solution)/shard_map/ppermute | solution.py:519
  59.8 5.7 %collective-permute-start.20 = (bf16[144,128]{1,0:T(8,128)(2,1)S(1)}, bf16[144,128]{1,0:T(8,128)(2,1)S(1)}, u32[]{:S(2)}, u32[]{:S(2)}) collective-permute-start(bf16[144,128]{1,0:T(8,128)(2,1)S(1)} %get-tuple-element.60), channel_id=1, source_target_pairs={{0,1},{1,0},{2,3},{3,2},{4,5},{5,4},{6,7},{7,6},{8,9},{9,8},{10,11... | collective-permute-start | bytes 110600 | tf_op jit(solution)/shard_map/ppermute | solution.py:444
  61.2 5.2 %collective-permute-start.21 = (bf16[144,128]{1,0:T(8,128)(2,1)S(1)}, bf16[144,128]{1,0:T(8,128)(2,1)S(1)}, u32[]{:S(2)}, u32[]{:S(2)}) collective-permute-start(bf16[144,128]{1,0:T(8,128)(2,1)S(1)} %get-tuple-element.61), channel_id=1, source_target_pairs={{0,3},{1,2},{2,1},{3,0},{4,7},{5,6},{6,5},{7,4},{8,11},{9,10},{10,... | collective-permute-start | bytes 110600 | tf_op jit(solution)/shard_map/ppermute | solution.py:444

commit v7 on v6

--- a/solution.py
+++ b/solution.py
@@ -129,7 +129,7 @@
 def centre_back_kernel(cols, own, first, second, band, control, hessian, outer, middle, done):
     members, cells, levels = own.shape
     size = ROWS * cols
-    batch = 2 * ROWS
+    batch = ROWS
     copies = []
     for m, row, value in centre_blocks(cols, own, first, second, band):
         value = (control[m, row : row + size, :].astype(F32) + value).reshape(ROWS, cols, levels)
@@ -153,7 +153,7 @@
     odd = is_odd("lon")
     edge = HALO * HALO
     length = cells // cols * HALO
-    for m in range(members):
+    for m in members:
         at = m * (length + 2 * edge)
         for place, refs, start, size in (
             (at, corners, 2 * m * edge, edge),
@@ -211,7 +211,7 @@
 
 def send_kernel(cols, inner, one, two, one_corner, two_corner, band, vertical, ensemble, out, west, east):
     members, cells, _ = inner.shape
-    joined((one, two), (one_corner, two_corner), (west, east), members, cols, cells)
+    joined((one, two), (one_corner, two_corner), (west, east), range(members), cols, cells)
     half_forward(cols, 1 - lax.axis_index("core"), inner, west, east, band, vertical, ensemble, out)
 
 
@@ -249,16 +249,6 @@
         cost_estimate=cost(flops, size),
         name=name,
     )(*inputs)
-
-
-def edges_kernel(tile, first, second):
-    members, cells, _ = tile.shape
-    edge = first.shape[0] // members
-    odd = is_odd("lat")
-    for m in range(members):
-        low, high = tile[m, :edge, :], tile[m, cells - edge :, :]
-        first[m * edge : (m + 1) * edge, :] = jnp.where(odd, low, high)
-        second[m * edge : (m + 1) * edge, :] = jnp.where(odd, high, low)
 
 
 def picker(lat_rows, cols):
@@ -408,10 +398,10 @@
     members, tile_rows, width, levels = outer.shape
     cells = tile_rows * cols
     batch = 2 * ROWS
-    joined((one, two), (one_corner, two_corner), (west, east), members, cols, cells)
     copies = []
     for start in range(0, members, 2):
         pair = (start, start + 1)
+        joined((one, two), (one_corner, two_corner), (west, east), pair, cols, cells)
         for block in range(tile_rows // ROWS):
             rows = slice(block * ROWS, (block + 1) * ROWS)
             for m, side in zip(pair, sides(band, west, east, pair, block, side_rows(cells, cols))):
@@ -456,11 +446,13 @@
         return jax.ShapeDtypeStruct((count, levels), BF)
 
     edge = HALO * cols
-    first, second = call(edges_kernel, "edges", [rows(members * edge)] * 2, (own,))
-    one, two = exchange(first, second, "lat")
+    low, high = control[:, :HALO].reshape(-1, levels), control[:, tile_rows - HALO :].reshape(-1, levels)
+    odd = is_odd("lat")
+    one, two = exchange(jnp.where(odd, low, high), jnp.where(odd, high, low), "lat")
     beside_it = exchange(*strips(own, cols), "lon")
-    corner = exchange(*corners(one, two, cols, members), "lon")
-    band, band_side = bands(lat_taps, lon_taps, cols, False)
+    low, high = corners(one, two, cols, members)
+    corner = exchange(low, high, "lon")
+    band, band_side = bands(lat_taps, lon_taps, cols, False, low)
     inner, square = call(
         functools.partial(centre_kernel, cols),
         "centre",
@@ -525,7 +517,7 @@
         out_specs=(pl.BlockSpec(memory_space=pl.ANY), VMEM),
         scratch=(
             pltpu.VMEM((members, tile_rows, cols - 16, levels), F32),
-            pltpu.SemaphoreType.DMA((members * tile_rows // (2 * ROWS),)),
+            pltpu.SemaphoreType.DMA((members * tile_rows // ROWS,)),
         ),
         flops=3_000_000_000,
         size=7_000_000,

time: 69 us -> 69.9 us (1.013)
  starting transfers between devices: 34.6 us -> 32.4 us
  waiting for transfers between devices: 17.9 us -> 19.8 us
  other arithmetic: 0 us -> 1 us
    ppermute x1, starting transfers between devices: 3.35 us -> 1.97 us  [per_device(): other = lax.ppermute(message, 'zh', swap('zh', 1))]
    ppermute x1, waiting for transfers between devices: 4.45 us -> 5.83 us  [per_device(): other = lax.ppermute(message, 'zh', swap('zh', 1))]
    select_n x0 -> x1, other arithmetic: none -> 1 us  [per_device(): jnp.where(odd, high, low)]
    ppermute x12, starting transfers between devices: 19.8 us -> 18.8 us  [exchange(): return (lax.ppermute(first, axis, one), lax.ppermute(second, axis, two))]
    pallas_call x16 -> x15, Pallas kernels: 12.3 us -> 12.4 us  [call(): pl.pallas_call(kernel, out_shape=tuple(shapes), in_specs=in_specs or [VME...]
  transfers between devices with their start and end apart: 23 -> 23, of which waited for: 11 -> 11; matrix products, arithmetic and copies ran while one was open for 0% -> 0% of each run, Pallas kernels for 14% -> 15%
where the time goes in v7:
time: 69.9 us; the launch traced here: 69.7 us
  starting transfers between devices  32.4 us (46%)
  waiting for transfers between devices  19.8 us (28%)
  Pallas kernels  13.9 us (20%)
  local copies, waits for them, and re-layouts  1.62 us (2%)
  between operations  1.03 us (1%)
  other arithmetic  1 us (1%)
    ppermute x12, starting transfers between devices, exchange(): return (lax.ppermute(first, axis, one), lax.ppermute(second, axis, two))  18.8 us
    pallas_call x15, Pallas kernels, call(): pl.pallas_call(kernel, out_shape=tuple(shapes), in_specs=in_specs or [VME...  12.4 us
    ppermute x1, waiting for transfers between devices, per_device(): other = lax.ppermute(message, 'zh', swap('zh', 1))  5.83 us
    ppermute x3, starting transfers between devices, per_device(): two, one, three = [lax.ppermute(zero, 'x', swap('x', k)) for k in (2, 1, 3)]  4.52 us
    ppermute x3, waiting for transfers between devices, per_device(): two, one, three = [lax.ppermute(zero, 'x', swap('x', k)) for k in (2, 1, 3)]  4.31 us
    ppermute x3, waiting for transfers between devices, per_device(): lax.ppermute(v, 'x', swap('x', k))  4.12 us
    ppermute x3, starting transfers between devices, per_device(): lax.ppermute(v, 'x', swap('x', k))  3.58 us
    ppermute x12, waiting for transfers between devices, exchange(): return (lax.ppermute(first, axis, one), lax.ppermute(second, axis, two))  3.12 us
  transfers between devices with their start and end apart: 23, of which 11 were waited for; matrix products, arithmetic and copies ran while one was open for 0% of the time, Pallas kernels for 15%

profile of v7, /device:TPU:2, one launch (start us, length us, event | category | flops | bytes accessed | tf_op | source)
XLA Modules:
  0.0 69.7 jit_solution(15316976191007652245)
XLA Ops:
  0.7 1.0 %broadcast_select_fusion = (bf16[4,4,32,128]{3,2,1,0:T(8,128)(2,1)S(1)}, bf16[4,4,32,128]{3,2,1,0:T(8,128)(2,1)S(1)}) fusion(pred[]{:T(512)S(6)} %eq.3, bf16[4,64,32,128]{3,2,1,0:T(8,128)(2,1)} %param.6), kind=kLoop, calls=%fused_computation | loop fusion | flops 131072 | bytes 524289 | tf_op jit(solution)/shard_map/jit(_where)/select_n | solution.py:451
  1.7 2.0 %collective-permute-start = (bf16[512,128]{1,0:T(8,128)(2,1)S(1)}, bf16[512,128]{1,0:T(8,128)(2,1)S(1)}, u32[]{:S(2)}, u32[]{:S(2)}) collective-permute-start(bf16[512,128]{1,0:T(8,128)(2,1)S(1)} %bitcast.15), channel_id=1, source_target_pairs={{0,4},{4,0},{8,12},{12,8},{128,132},{132,128},{136,140},{140,136},... | collective-permute-start | bytes 393224 | tf_op jit(solution)/shard_map/ppermute | solution.py:434
  3.7 4.9 %collective-permute-start.1 = (bf16[512,128]{1,0:T(8,128)(2,1)S(1)}, bf16[512,128]{1,0:T(8,128)(2,1)S(1)}, u32[]{:S(2)}, u32[]{:S(2)}) collective-permute-start(bf16[512,128]{1,0:T(8,128)(2,1)S(1)} %bitcast.14), channel_id=1, source_target_pairs={{0,140},{4,8},{8,4},{12,128},{128,12},{132,136},{136,132},{140,0},... | collective-permute-start | bytes 393224 | tf_op jit(solution)/shard_map/ppermute | solution.py:434
  8.6 1.6 %copy-done.1 = bf16[4,64,32,128]{3,2,1,0:T(8,128)(2,1)S(1)} copy-done((bf16[4,64,32,128]{3,2,1,0:T(8,128)(2,1)S(1)}, bf16[4,64,32,128]{3,2,1,0:T(8,128)(2,1)}, u32[]{:S(2)}) %copy-start.1) | copy-done | bytes 2097176
  10.2 0.5 strips.2
  10.7 1.7 %collective-permute-start.2 = (bf16[1024,128]{1,0:T(8,128)(2,1)S(1)}, bf16[1024,128]{1,0:T(8,128)(2,1)S(1)}, u32[]{:S(2)}, u32[]{:S(2)}) collective-permute-start(bf16[1024,128]{1,0:T(8,128)(2,1)S(1)} %get-tuple-element.35), channel_id=1, source_target_pairs={{0,1},{1,0},{2,3},{3,2},{4,5},{5,4},{6,7},{7,6},{8,9},{9,8},{10,11... | collective-permute-start | bytes 786440 | tf_op jit(solution)/shard_map/ppermute | solution.py:434
  12.3 2.2 %collective-permute-start.3 = (bf16[1024,128]{1,0:T(8,128)(2,1)S(1)}, bf16[1024,128]{1,0:T(8,128)(2,1)S(1)}, u32[]{:S(2)}, u32[]{:S(2)}) collective-permute-start(bf16[1024,128]{1,0:T(8,128)(2,1)S(1)} %get-tuple-element.36), channel_id=1, source_target_pairs={{0,3},{1,2},{2,1},{3,0},{4,7},{5,6},{6,5},{7,4},{8,11},{9,10},{10,... | collective-permute-start | bytes 786440 | tf_op jit(solution)/shard_map/ppermute | solution.py:434
  14.5 0.2 corners.2
  14.7 1.1 %collective-permute-start.5 = (bf16[128,128]{1,0:T(8,128)(2,1)S(1)}, bf16[128,128]{1,0:T(8,128)(2,1)S(1)}, u32[]{:S(2)}, u32[]{:S(2)}) collective-permute-start(bf16[128,128]{1,0:T(8,128)(2,1)S(1)} %get-tuple-element.37), channel_id=1, source_target_pairs={{0,3},{1,2},{2,1},{3,0},{4,7},{5,6},{6,5},{7,4},{8,11},{9,10},{10,... | collective-permute-start | bytes 98312 | tf_op jit(solution)/shard_map/ppermute | solution.py:434
  15.9 0.8 %bands.1 = (bf16[512,512]{1,0:T(8,128)(2,1)S(1)}, bf16[256,128]{1,0:T(8,128)(2,1)S(1)}) custom-call(f32[9]{0:T(128)S(1)} %copy-done.5, f32[9]{0:T(128)S(1)} %copy-done.6, bf16[128,128]{1,0:T(8,128)(2,1)S(1)} %get-tuple-element.32.refs_0_), custom_call_target="tpu_custom_call" | custom-call | flops 2000000 | bytes 600000 | tf_op jit(solution)/shard_map/bands/pallas_call | solution.py:76
  16.7 2.4 %centre.1 = (f32[4,2048,128]{2,1,0:T(8,128)S(1)}, f32[8,128]{1,0:T(8,128)S(1)}) custom-call(bf16[4,2048,128]{2,1,0:T(8,128)(2,1)S(1)} %bitcast.11, bf16[512,128]{1,0:T(8,128)(2,1)S(1)} %collective-permute-done.first, bf16[512,128]{1,0:T(8,128)(2,1)S(1)} %collective-permute-done.1.second, bf16[512,512]{1,0:T(8,128)(2,1)S(1)} %get-tuple-element.33.band), custom_call_target="tpu_custom_call" | custom-call | flops 3000000000 | bytes 7000000 | tf_op jit(solution)/shard_map/centre/pallas_call | solution.py:241
  19.1 2.4 %collective-permute-done.5.two_corner = bf16[128,128]{1,0:T(8,128)(2,1)S(1)} collective-permute-done((bf16[128,128]{1,0:T(8,128)(2,1)S(1)}, bf16[128,128]{1,0:T(8,128)(2,1)S(1)}, u32[]{:S(2)}, u32[]{:S(2)}) %collective-permute-start.5) | collective-permute-done | bytes 32800 | tf_op jit(solution)/shard_map/ppermute | solution.py:434
  21.5 0.9 %forward_send.1 = (bf16[1024,128]{1,0:T(8,128)(2,1)S(1)}, bf16[1152,128]{1,0:T(8,128)(2,1)S(1)}, bf16[1152,128]{1,0:T(8,128)(2,1)S(1)}) custom-call(f32[4,2048,128]{2,1,0:T(8,128)S(1)} %get-tuple-element.34.inner, bf16[1024,128]{1,0:T(8,128)(2,1)S(1)} %collective-permute-done.2.one, bf16[1024,128]{1,0:T(8,128)(2,1)S(1)} %collective-permute-done.3.two, ...), custom_call_target="tpu_custom_call" | custom-call | flops 700000000 | bytes 3000000 | tf_op jit(solution)/shard_map/forward_send/pallas_call | solution.py:241
  22.4 0.1 collective-permute-start.6
  22.5 0.9 %forward_keep.1.keep = bf16[1024,128]{1,0:T(8,128)(2,1)S(1)} custom-call(f32[4,2048,128]{2,1,0:T(8,128)S(1)} %get-tuple-element.34.inner, bf16[1152,128]{1,0:T(8,128)(2,1)S(1)} %get-tuple-element.39.west, bf16[1152,128]{1,0:T(8,128)(2,1)S(1)} %get-tuple-element.40.east, bf16[256,128]{1,0:T(8,128)(2,1)S(1)} %get-tuple-element.38.band, ...), custom_call_target="tpu_custom_call" | custom-call | flops 700000000 | bytes 3000000 | tf_op jit(solution)/shard_map/forward_keep/pallas_call | solution.py:241
  23.3 0.6 collective-permute-done.6.got
  24.1 0.6 collective-permute-start.7
  24.7 2.4 %collective-permute-start.8 = (bf16[256,128]{1,0:T(8,128)(2,1)S(1)}, bf16[256,128]{1,0:T(8,128)(2,1)S(1)}, u32[]{:S(2)}, u32[]{:S(2)}) collective-permute-start(bf16[256,128]{1,0:T(8,128)(2,1)S(1)} %get-tuple-element.44), channel_id=1, source_target_pairs={{0,64},{32,96},{64,0},{96,32},{1,65},{33,97},{65,1},{97,33},{2,66}... | collective-permute-start | bytes 196616 | tf_op jit(solution)/shard_map/ppermute | solution.py:484
  27.1 0.5 collective-permute-start.9
  27.6 0.8 %collective-permute-done.7.one = bf16[256,128]{1,0:T(8,128)(2,1)S(1)} collective-permute-done((bf16[256,128]{1,0:T(8,128)(2,1)S(1)}, bf16[256,128]{1,0:T(8,128)(2,1)S(1)}, u32[]{:S(2)}, u32[]{:S(2)}) %collective-permute-start.7) | collective-permute-done | bytes 65568 | tf_op jit(solution)/shard_map/ppermute | solution.py:484
  28.4 2.4 %collective-permute-done.8.two = bf16[256,128]{1,0:T(8,128)(2,1)S(1)} collective-permute-done((bf16[256,128]{1,0:T(8,128)(2,1)S(1)}, bf16[256,128]{1,0:T(8,128)(2,1)S(1)}, u32[]{:S(2)}, u32[]{:S(2)}) %collective-permute-start.8) | collective-permute-done | bytes 65568 | tf_op jit(solution)/shard_map/ppermute | solution.py:484
  30.9 0.9 %collective-permute-done.9.three.refs_0_ = bf16[256,128]{1,0:T(8,128)(2,1)S(1)} collective-permute-done((bf16[256,128]{1,0:T(8,128)(2,1)S(1)}, bf16[256,128]{1,0:T(8,128)(2,1)S(1)}, u32[]{:S(2)}, u32[]{:S(2)}) %collective-permute-start.9) | collective-permute-done | bytes 65568 | tf_op jit(solution)/shard_map/ppermute | solution.py:484
  31.8 2.0 %collective-permute-start.10 = (bf16[272,128]{1,0:T(8,128)(2,1)S(1)}, bf16[272,128]{1,0:T(8,128)(2,1)S(1)}, u32[]{:S(2)}, u32[]{:S(2)}) collective-permute-start(bf16[272,128]{1,0:T(8,128)(2,1)S(1)} %part.1.message), channel_id=1, source_target_pairs={{0,128},{128,0},{1,129},{129,1},{2,130},{130,2},{3,131},{131,3},{4... | collective-permute-start | bytes 208904 | tf_op jit(solution)/shard_map/ppermute | solution.py:487
  33.8 0.8 %bands_back.1 = (bf16[512,512]{1,0:T(8,128)(2,1)S(1)}, bf16[256,128]{1,0:T(8,128)(2,1)S(1)}) custom-call(f32[9]{0:T(128)S(1)} %copy-done.5, f32[9]{0:T(128)S(1)} %copy-done.6, bf16[256,128]{1,0:T(8,128)(2,1)S(1)} %collective-permute-done.9.three.refs_0_), custom_call_target="tpu_custom_call" | custom-call | flops 2000000 | bytes 600000 | tf_op jit(solution)/shard_map/bands_back/pallas_call | solution.py:76
  34.5 5.8 %collective-permute-done.10.other = bf16[272,128]{1,0:T(8,128)(2,1)S(1)} collective-permute-done((bf16[272,128]{1,0:T(8,128)(2,1)S(1)}, bf16[272,128]{1,0:T(8,128)(2,1)S(1)}, u32[]{:S(2)}, u32[]{:S(2)}) %collective-permute-start.10) | collective-permute-done | bytes 69664 | tf_op jit(solution)/shard_map/ppermute | solution.py:487
  40.4 0.1 weight.1.zero
  40.4 1.0 %collective-permute-start.13 = (bf16[272,128]{1,0:T(8,128)(2,1)S(1)}, bf16[272,128]{1,0:T(8,128)(2,1)S(1)}, u32[]{:S(2)}, u32[]{:S(2)}) collective-permute-start(bf16[272,128]{1,0:T(8,128)(2,1)S(1)} %weight.1.zero), channel_id=1, source_target_pairs={{0,96},{32,64},{64,32},{96,0},{1,97},{33,65},{65,33},{97,1},{2,98}... | collective-permute-start | bytes 208904 | tf_op jit(solution)/shard_map/ppermute | solution.py:489
  41.4 3.6 %collective-permute-start.12 = (bf16[272,128]{1,0:T(8,128)(2,1)S(1)}, bf16[272,128]{1,0:T(8,128)(2,1)S(1)}, u32[]{:S(2)}, u32[]{:S(2)}) collective-permute-start(bf16[272,128]{1,0:T(8,128)(2,1)S(1)} %weight.1.zero), channel_id=1, source_target_pairs={{0,64},{32,96},{64,0},{96,32},{1,65},{33,97},{65,1},{97,33},{2,66}... | collective-permute-start | bytes 208904 | tf_op jit(solution)/shard_map/ppermute | solution.py:489
  45.0 2.3 %collective-permute-done.12.two = bf16[272,128]{1,0:T(8,128)(2,1)S(1)} collective-permute-done((bf16[272,128]{1,0:T(8,128)(2,1)S(1)}, bf16[272,128]{1,0:T(8,128)(2,1)S(1)}, u32[]{:S(2)}, u32[]{:S(2)}) %collective-permute-start.12) | collective-permute-done | bytes 69664 | tf_op jit(solution)/shard_map/ppermute | solution.py:489
  47.2 2.0 %collective-permute-done.11.one = bf16[272,128]{1,0:T(8,128)(2,1)S(1)} collective-permute-done((bf16[272,128]{1,0:T(8,128)(2,1)S(1)}, bf16[272,128]{1,0:T(8,128)(2,1)S(1)}, u32[]{:S(2)}, u32[]{:S(2)}) %collective-permute-start.11) | collective-permute-done | bytes 69664 | tf_op jit(solution)/shard_map/ppermute | solution.py:489
  49.3 0.1 collective-permute-start.14
  49.4 1.5 %collective-permute-done.14.other = bf16[1040,128]{1,0:T(8,128)(2,1)S(1)} collective-permute-done((bf16[1040,128]{1,0:T(8,128)(2,1)S(1)}, bf16[1040,128]{1,0:T(8,128)(2,1)S(1)}, u32[]{:S(2)}, u32[]{:S(2)}) %collective-permute-start.14) | collective-permute-done | bytes 266272 | tf_op jit(solution)/shard_map/ppermute | solution.py:491
  50.9 0.3 level_edges.1
  51.2 0.1 collective-permute-start.15
  51.3 2.0 %collective-permute-start.16 = (bf16[528,128]{1,0:T(8,128)(2,1)S(1)}, bf16[528,128]{1,0:T(8,128)(2,1)S(1)}, u32[]{:S(2)}, u32[]{:S(2)}) collective-permute-start(bf16[528,128]{1,0:T(8,128)(2,1)S(1)} %get-tuple-element.50), channel_id=1, source_target_pairs={{0,140},{4,8},{8,4},{12,128},{128,12},{132,136},{136,132},{140,0},... | collective-permute-start | bytes 405512 | tf_op jit(solution)/shard_map/ppermute | solution.py:434
  53.4 0.7 %level.1 = (bf16[4,2048,128]{2,1,0:T(8,128)(2,1)S(1)}, f32[8,128]{1,0:T(8,128)S(1)}) custom-call(bf16[1040,128]{1,0:T(8,128)(2,1)S(1)} %gather.1.mine, bf16[1040,128]{1,0:T(8,128)(2,1)S(1)} %collective-permute-done.14.other, bf16[4,2048,128]{2,1,0:T(8,128)(2,1)S(1)} %bitcast.9, bf16[128,128]{1,0:T(8,128)(2,1)S(1)} %copy-done.4), custom_call_target="tpu_custom_call" | custom-call | flops 300000000 | bytes 4500000 | tf_op jit(solution)/shard_map/level/pallas_call | solution.py:241
  54.1 1.5 %collective-permute-start.19 = (f32[8,128]{1,0:T(8,128)S(1)}, f32[8,128]{1,0:T(8,128)S(1)}, u32[]{:S(2)}, u32[]{:S(2)}) collective-permute-start(f32[8,128]{1,0:T(8,128)S(1)} %get-tuple-element.55.refs_0_), channel_id=1, source_target_pairs={{0,8},{4,12},{8,0},{12,4},{1,9},{5,13},{9,1},{13,5},{2,10},{6,14},... | collective-permute-start | bytes 12296 | tf_op jit(solution)/shard_map/ppermute | solution.py:506
  55.6 0.5 strips.3
  56.1 0.1 collective-permute-start.17
  56.2 2.3 %collective-permute-start.18 = (bf16[1024,128]{1,0:T(8,128)(2,1)S(1)}, bf16[1024,128]{1,0:T(8,128)(2,1)S(1)}, u32[]{:S(2)}, u32[]{:S(2)}) collective-permute-start(bf16[1024,128]{1,0:T(8,128)(2,1)S(1)} %get-tuple-element.54), channel_id=1, source_target_pairs={{0,3},{1,2},{2,1},{3,0},{4,7},{5,6},{6,5},{7,4},{8,11},{9,10},{10,... | collective-permute-start | bytes 786440 | tf_op jit(solution)/shard_map/ppermute | solution.py:434
  58.5 0.2 collective-permute-done.19.refs_1_
  58.7 0.2 corners.3
  58.9 1.8 %collective-permute-start.22 = (f32[8,128]{1,0:T(8,128)S(1)}, f32[8,128]{1,0:T(8,128)S(1)}, u32[]{:S(2)}, u32[]{:S(2)}) collective-permute-start(f32[8,128]{1,0:T(8,128)S(1)} %get-tuple-element.58.sums), channel_id=1, source_target_pairs={{0,2},{1,3},{2,0},{3,1},{4,6},{5,7},{6,4},{7,5},{8,10},{9,11},{10,... | collective-permute-start | bytes 12296 | tf_op jit(solution)/shard_map/ppermute | solution.py:511
  60.7 1.4 %collective-permute-start.20 = (bf16[144,128]{1,0:T(8,128)(2,1)S(1)}, bf16[144,128]{1,0:T(8,128)(2,1)S(1)}, u32[]{:S(2)}, u32[]{:S(2)}) collective-permute-start(bf16[144,128]{1,0:T(8,128)(2,1)S(1)} %get-tuple-element.56), channel_id=1, source_target_pairs={{0,1},{1,0},{2,3},{3,2},{4,5},{5,4},{6,7},{7,6},{8,9},{9,8},{10,11... | collective-permute-start | bytes 110600 | tf_op jit(solution)/shard_map/ppermute | solution.py:434
  62.1 1.0 %collective-permute-start.21 = (bf16[144,128]{1,0:T(8,128)(2,1)S(1)}, bf16[144,128]{1,0:T(8,128)(2,1)S(1)}, u32[]{:S(2)}, u32[]{:S(2)}) collective-permute-start(bf16[144,128]{1,0:T(8,128)(2,1)S(1)} %get-tuple-element.57), channel_id=1, source_target_pairs={{0,3},{1,2},{2,1},{3,0},{4,7},{5,6},{6,5},{7,4},{8,11},{9,10},{10,... | collective-permute-start | bytes 110600 | tf_op jit(solution)/shard_map/ppermute | solution.py:434
  63.1 3.4 %centre_back.1 = (f32[4,64,32,128]{3,2,1,0:T(8,128)}, f32[4,64,16,128]{3,2,1,0:T(8,128)S(1)}) custom-call(bf16[4,2048,128]{2,1,0:T(8,128)(2,1)S(1)} %get-tuple-element.48.own.tile, bf16[528,128]{1,0:T(8,128)(2,1)S(1)} %collective-permute-done.15.first, bf16[528,128]{1,0:T(8,128)(2,1)S(1)} %collective-permute-done.16.second, ...), custom_call_target="tpu_custom_call" | custom-call | flops 3000000000 | bytes 7000000 | tf_op jit(solution)/shard_map/centre_back/pallas_call | solution.py:241
  66.5 0.7 %collective-permute-done.21.two_corner = bf16[144,128]{1,0:T(8,128)(2,1)S(1)} collective-permute-done((bf16[144,128]{1,0:T(8,128)(2,1)S(1)}, bf16[144,128]{1,0:T(8,128)(2,1)S(1)}, u32[]{:S(2)}, u32[]{:S(2)}) %collective-permute-start.21) | collective-permute-done | bytes 36896 | tf_op jit(solution)/shard_map/ppermute | solution.py:434
  67.2 2.3 %backward.1 = (f32[4,64,32,128]{3,2,1,0:T(8,128)}, f32[1,1]{1,0:T(1,128)}) custom-call(f32[4,64,16,128]{3,2,1,0:T(8,128)S(1)} %get-tuple-element.52.outer, bf16[1024,128]{1,0:T(8,128)(2,1)S(1)} %collective-permute-done.17.one, bf16[1024,128]{1,0:T(8,128)(2,1)S(1)} %collective-permute-done.18.two, ...), custom_call_target="tpu_custom_call", output_to_operand_aliasing={{0}: (8, {})} | custom-call | flops 1000000000 | bytes 9000000 | tf_op jit(solution)/shard_map/backward/pallas_call | solution.py:241
  (30 shorter events, 0.2 us)
Async XLA Ops:
  0.6 15.2 %copy-start.6 = (f32[9]{0:T(128)S(1)}, f32[9]{0:T(128)}, u32[]{:S(2)}) copy-start(f32[9]{0:T(128)} %lon_taps.3) | copy-start | bytes 112
  0.6 15.2 %copy-start.5 = (f32[9]{0:T(128)S(1)}, f32[9]{0:T(128)}, u32[]{:S(2)}) copy-start(f32[9]{0:T(128)} %lat_taps.3) | copy-start | bytes 112
  1.7 12.9 %collective-permute-start = (bf16[512,128]{1,0:T(8,128)(2,1)S(1)}, bf16[512,128]{1,0:T(8,128)(2,1)S(1)}, u32[]{:S(2)}, u32[]{:S(2)}) collective-permute-start(bf16[512,128]{1,0:T(8,128)(2,1)S(1)} %bitcast.15), channel_id=1, source_target_pairs={{0,4},{4,0},{8,12},{12,8},{128,132},{132,128},{136,140},{140,136},... | collective-permute-start | bytes 393224 | tf_op jit(solution)/shard_map/ppermute | solution.py:434
  3.7 10.9 %collective-permute-start.1 = (bf16[512,128]{1,0:T(8,128)(2,1)S(1)}, bf16[512,128]{1,0:T(8,128)(2,1)S(1)}, u32[]{:S(2)}, u32[]{:S(2)}) collective-permute-start(bf16[512,128]{1,0:T(8,128)(2,1)S(1)} %bitcast.14), channel_id=1, source_target_pairs={{0,140},{4,8},{8,4},{12,128},{128,12},{132,136},{136,132},{140,0},... | collective-permute-start | bytes 393224 | tf_op jit(solution)/shard_map/ppermute | solution.py:434
  8.6 1.6 %copy-start.1 = (bf16[4,64,32,128]{3,2,1,0:T(8,128)(2,1)S(1)}, bf16[4,64,32,128]{3,2,1,0:T(8,128)(2,1)}, u32[]{:S(2)}) copy-start(bf16[4,64,32,128]{3,2,1,0:T(8,128)(2,1)} %param.6) | copy-start | bytes 6291460
  10.2 6.4 %copy-start.2 = (bf16[4,64,32,128]{3,2,1,0:T(8,128)(2,1)S(1)}, bf16[4,64,32,128]{3,2,1,0:T(8,128)(2,1)}, u32[]{:S(2)}) copy-start(bf16[4,64,32,128]{3,2,1,0:T(8,128)(2,1)} %param.6) | copy-start | bytes 6291460
  10.7 10.8 %collective-permute-start.2 = (bf16[1024,128]{1,0:T(8,128)(2,1)S(1)}, bf16[1024,128]{1,0:T(8,128)(2,1)S(1)}, u32[]{:S(2)}, u32[]{:S(2)}) collective-permute-start(bf16[1024,128]{1,0:T(8,128)(2,1)S(1)} %get-tuple-element.35), channel_id=1, source_target_pairs={{0,1},{1,0},{2,3},{3,2},{4,5},{5,4},{6,7},{7,6},{8,9},{9,8},{10,11... | collective-permute-start | bytes 786440 | tf_op jit(solution)/shard_map/ppermute | solution.py:434
  12.3 9.1 %collective-permute-start.3 = (bf16[1024,128]{1,0:T(8,128)(2,1)S(1)}, bf16[1024,128]{1,0:T(8,128)(2,1)S(1)}, u32[]{:S(2)}, u32[]{:S(2)}) collective-permute-start(bf16[1024,128]{1,0:T(8,128)(2,1)S(1)} %get-tuple-element.36), channel_id=1, source_target_pairs={{0,3},{1,2},{2,1},{3,0},{4,7},{5,6},{6,5},{7,4},{8,11},{9,10},{10,... | collective-permute-start | bytes 786440 | tf_op jit(solution)/shard_map/ppermute | solution.py:434
  14.7 6.7 %collective-permute-start.5 = (bf16[128,128]{1,0:T(8,128)(2,1)S(1)}, bf16[128,128]{1,0:T(8,128)(2,1)S(1)}, u32[]{:S(2)}, u32[]{:S(2)}) collective-permute-start(bf16[128,128]{1,0:T(8,128)(2,1)S(1)} %get-tuple-element.37), channel_id=1, source_target_pairs={{0,3},{1,2},{2,1},{3,0},{4,7},{5,6},{6,5},{7,4},{8,11},{9,10},{10,... | collective-permute-start | bytes 98312 | tf_op jit(solution)/shard_map/ppermute | solution.py:434
  15.9 5.6 %collective-permute-start.4 = (bf16[128,128]{1,0:T(8,128)(2,1)S(1)}, bf16[128,128]{1,0:T(8,128)(2,1)S(1)}, u32[]{:S(2)}, u32[]{:S(2)}) collective-permute-start(bf16[128,128]{1,0:T(8,128)(2,1)S(1)} %get-tuple-element.32.refs_0_), channel_id=1, source_target_pairs={{0,1},{1,0},{2,3},{3,2},{4,5},{5,4},{6,7},{7,6},{8,9},{9,8},{10,11... | collective-permute-start | bytes 98312 | tf_op jit(solution)/shard_map/ppermute | solution.py:434
  16.6 4.8 %copy-start = (bf16[4,64,32,128]{3,2,1,0:T(8,128)(2,1)S(1)}, bf16[4,64,32,128]{3,2,1,0:T(8,128)(2,1)}, u32[]{:S(2)}) copy-start(bf16[4,64,32,128]{3,2,1,0:T(8,128)(2,1)} %param.7) | copy-start | bytes 6291460
  16.6 4.8 %copy-start.4 = (bf16[128,128]{1,0:T(8,128)(2,1)S(1)}, bf16[128,128]{1,0:T(8,128)(2,1)}, u32[]{:S(2)}) copy-start(bf16[128,128]{1,0:T(8,128)(2,1)} %vertical.7) | copy-start | bytes 98308
  22.4 1.6 %collective-permute-start.6 = (bf16[1024,128]{1,0:T(8,128)(2,1)S(1)}, bf16[1024,128]{1,0:T(8,128)(2,1)S(1)}, u32[]{:S(2)}, u32[]{:S(2)}) collective-permute-start(bf16[1024,128]{1,0:T(8,128)(2,1)S(1)} %get-tuple-element.41), channel_id=1, source_target_pairs={{0,16},{16,0},{1,17},{17,1},{2,18},{18,2},{3,19},{19,3},{4,20},{20... | collective-permute-start | bytes 786440 | tf_op jit(solution)/shard_map/ppermute | solution.py:482
  22.5 17.9 %copy-start.3 = (f32[64,32,128]{2,1,0:T(8,128)S(1)}, f32[64,32,128]{2,1,0:T(8,128)}, u32[]{:S(2)}) copy-start(f32[64,32,128]{2,1,0:T(8,128)} %param.8) | copy-start | bytes 3145732
  24.1 4.4 %collective-permute-start.7 = (bf16[256,128]{1,0:T(8,128)(2,1)S(1)}, bf16[256,128]{1,0:T(8,128)(2,1)S(1)}, u32[]{:S(2)}, u32[]{:S(2)}) collective-permute-start(bf16[256,128]{1,0:T(8,128)(2,1)S(1)} %get-tuple-element.43), channel_id=1, source_target_pairs={{0,32},{32,0},{64,96},{96,64},{1,33},{33,1},{65,97},{97,65},{2,34}... | collective-permute-start | bytes 196616 | tf_op jit(solution)/shard_map/ppermute | solution.py:484
  24.7 6.2 %collective-permute-start.8 = (bf16[256,128]{1,0:T(8,128)(2,1)S(1)}, bf16[256,128]{1,0:T(8,128)(2,1)S(1)}, u32[]{:S(2)}, u32[]{:S(2)}) collective-permute-start(bf16[256,128]{1,0:T(8,128)(2,1)S(1)} %get-tuple-element.44), channel_id=1, source_target_pairs={{0,64},{32,96},{64,0},{96,32},{1,65},{33,97},{65,1},{97,33},{2,66}... | collective-permute-start | bytes 196616 | tf_op jit(solution)/shard_map/ppermute | solution.py:484
  27.1 4.7 %collective-permute-start.9 = (bf16[256,128]{1,0:T(8,128)(2,1)S(1)}, bf16[256,128]{1,0:T(8,128)(2,1)S(1)}, u32[]{:S(2)}, u32[]{:S(2)}) collective-permute-start(bf16[256,128]{1,0:T(8,128)(2,1)S(1)} %get-tuple-element.45), channel_id=1, source_target_pairs={{0,96},{32,64},{64,32},{96,0},{1,97},{33,65},{65,33},{97,1},{2,98}... | collective-permute-start | bytes 196616 | tf_op jit(solution)/shard_map/ppermute | solution.py:484
  31.8 8.6 %collective-permute-start.10 = (bf16[272,128]{1,0:T(8,128)(2,1)S(1)}, bf16[272,128]{1,0:T(8,128)(2,1)S(1)}, u32[]{:S(2)}, u32[]{:S(2)}) collective-permute-start(bf16[272,128]{1,0:T(8,128)(2,1)S(1)} %part.1.message), channel_id=1, source_target_pairs={{0,128},{128,0},{1,129},{129,1},{2,130},{130,2},{3,131},{131,3},{4... | collective-permute-start | bytes 208904 | tf_op jit(solution)/shard_map/ppermute | solution.py:487
  40.4 4.5 %collective-permute-start.13 = (bf16[272,128]{1,0:T(8,128)(2,1)S(1)}, bf16[272,128]{1,0:T(8,128)(2,1)S(1)}, u32[]{:S(2)}, u32[]{:S(2)}) collective-permute-start(bf16[272,128]{1,0:T(8,128)(2,1)S(1)} %weight.1.zero), channel_id=1, source_target_pairs={{0,96},{32,64},{64,32},{96,0},{1,97},{33,65},{65,33},{97,1},{2,98}... | collective-permute-start | bytes 208904 | tf_op jit(solution)/shard_map/ppermute | solution.py:489
  41.4 5.8 %collective-permute-start.12 = (bf16[272,128]{1,0:T(8,128)(2,1)S(1)}, bf16[272,128]{1,0:T(8,128)(2,1)S(1)}, u32[]{:S(2)}, u32[]{:S(2)}) collective-permute-start(bf16[272,128]{1,0:T(8,128)(2,1)S(1)} %weight.1.zero), channel_id=1, source_target_pairs={{0,64},{32,96},{64,0},{96,32},{1,65},{33,97},{65,1},{97,33},{2,66}... | collective-permute-start | bytes 208904 | tf_op jit(solution)/shard_map/ppermute | solution.py:489
  44.9 4.3 %collective-permute-start.11 = (bf16[272,128]{1,0:T(8,128)(2,1)S(1)}, bf16[272,128]{1,0:T(8,128)(2,1)S(1)}, u32[]{:S(2)}, u32[]{:S(2)}) collective-permute-start(bf16[272,128]{1,0:T(8,128)(2,1)S(1)} %weight.1.zero), channel_id=1, source_target_pairs={{0,32},{32,0},{64,96},{96,64},{1,33},{33,1},{65,97},{97,65},{2,34}... | collective-permute-start | bytes 208904 | tf_op jit(solution)/shard_map/ppermute | solution.py:489
  49.3 1.6 %collective-permute-start.14 = (bf16[1040,128]{1,0:T(8,128)(2,1)S(1)}, bf16[1040,128]{1,0:T(8,128)(2,1)S(1)}, u32[]{:S(2)}, u32[]{:S(2)}) collective-permute-start(bf16[1040,128]{1,0:T(8,128)(2,1)S(1)} %gather.1.mine), channel_id=1, source_target_pairs={{0,16},{16,0},{1,17},{17,1},{2,18},{18,2},{3,19},{19,3},{4,20},{20... | collective-permute-start | bytes 798728 | tf_op jit(solution)/shard_map/ppermute | solution.py:491
  51.2 7.5 %collective-permute-start.15 = (bf16[528,128]{1,0:T(8,128)(2,1)S(1)}, bf16[528,128]{1,0:T(8,128)(2,1)S(1)}, u32[]{:S(2)}, u32[]{:S(2)}) collective-permute-start(bf16[528,128]{1,0:T(8,128)(2,1)S(1)} %get-tuple-element.49), channel_id=1, source_target_pairs={{0,4},{4,0},{8,12},{12,8},{128,132},{132,128},{136,140},{140,136},... | collective-permute-start | bytes 405512 | tf_op jit(solution)/shard_map/ppermute | solution.py:434
  51.3 7.4 %collective-permute-start.16 = (bf16[528,128]{1,0:T(8,128)(2,1)S(1)}, bf16[528,128]{1,0:T(8,128)(2,1)S(1)}, u32[]{:S(2)}, u32[]{:S(2)}) collective-permute-start(bf16[528,128]{1,0:T(8,128)(2,1)S(1)} %get-tuple-element.50), channel_id=1, source_target_pairs={{0,140},{4,8},{8,4},{12,128},{128,12},{132,136},{136,132},{140,0},... | collective-permute-start | bytes 405512 | tf_op jit(solution)/shard_map/ppermute | solution.py:434
  54.1 4.6 %collective-permute-start.19 = (f32[8,128]{1,0:T(8,128)S(1)}, f32[8,128]{1,0:T(8,128)S(1)}, u32[]{:S(2)}, u32[]{:S(2)}) collective-permute-start(f32[8,128]{1,0:T(8,128)S(1)} %get-tuple-element.55.refs_0_), channel_id=1, source_target_pairs={{0,8},{4,12},{8,0},{12,4},{1,9},{5,13},{9,1},{13,5},{2,10},{6,14},... | collective-permute-start | bytes 12296 | tf_op jit(solution)/shard_map/ppermute | solution.py:506
  56.1 11.1 %collective-permute-start.17 = (bf16[1024,128]{1,0:T(8,128)(2,1)S(1)}, bf16[1024,128]{1,0:T(8,128)(2,1)S(1)}, u32[]{:S(2)}, u32[]{:S(2)}) collective-permute-start(bf16[1024,128]{1,0:T(8,128)(2,1)S(1)} %get-tuple-element.53), channel_id=1, source_target_pairs={{0,1},{1,0},{2,3},{3,2},{4,5},{5,4},{6,7},{7,6},{8,9},{9,8},{10,11... | collective-permute-start | bytes 786440 | tf_op jit(solution)/shard_map/ppermute | solution.py:434
  56.2 11.0 %collective-permute-start.18 = (bf16[1024,128]{1,0:T(8,128)(2,1)S(1)}, bf16[1024,128]{1,0:T(8,128)(2,1)S(1)}, u32[]{:S(2)}, u32[]{:S(2)}) collective-permute-start(bf16[1024,128]{1,0:T(8,128)(2,1)S(1)} %get-tuple-element.54), channel_id=1, source_target_pairs={{0,3},{1,2},{2,1},{3,0},{4,7},{5,6},{6,5},{7,4},{8,11},{9,10},{10,... | collective-permute-start | bytes 786440 | tf_op jit(solution)/shard_map/ppermute | solution.py:434
  58.9 7.6 %collective-permute-start.22 = (f32[8,128]{1,0:T(8,128)S(1)}, f32[8,128]{1,0:T(8,128)S(1)}, u32[]{:S(2)}, u32[]{:S(2)}) collective-permute-start(f32[8,128]{1,0:T(8,128)S(1)} %get-tuple-element.58.sums), channel_id=1, source_target_pairs={{0,2},{1,3},{2,0},{3,1},{4,6},{5,7},{6,4},{7,5},{8,10},{9,11},{10,... | collective-permute-start | bytes 12296 | tf_op jit(solution)/shard_map/ppermute | solution.py:511
  60.7 5.8 %collective-permute-start.20 = (bf16[144,128]{1,0:T(8,128)(2,1)S(1)}, bf16[144,128]{1,0:T(8,128)(2,1)S(1)}, u32[]{:S(2)}, u32[]{:S(2)}) collective-permute-start(bf16[144,128]{1,0:T(8,128)(2,1)S(1)} %get-tuple-element.56), channel_id=1, source_target_pairs={{0,1},{1,0},{2,3},{3,2},{4,5},{5,4},{6,7},{7,6},{8,9},{9,8},{10,11... | collective-permute-start | bytes 110600 | tf_op jit(solution)/shard_map/ppermute | solution.py:434
  62.1 5.2 %collective-permute-start.21 = (bf16[144,128]{1,0:T(8,128)(2,1)S(1)}, bf16[144,128]{1,0:T(8,128)(2,1)S(1)}, u32[]{:S(2)}, u32[]{:S(2)}) collective-permute-start(bf16[144,128]{1,0:T(8,128)(2,1)S(1)} %get-tuple-element.57), channel_id=1, source_target_pairs={{0,3},{1,2},{2,1},{3,0},{4,7},{5,6},{6,5},{7,4},{8,11},{9,10},{10,... | collective-permute-start | bytes 110600 | tf_op jit(solution)/shard_map/ppermute | solution.py:434

commit v8 on v6

--- a/solution.py
+++ b/solution.py
@@ -32,7 +32,7 @@
 
 
 def is_odd(axis):
-    return lax.rem(lax.axis_index(axis), 2) == 1
+    return lax.rem(lax.axis_index(axis) + lax.axis_index("core"), 2) == 1
 
 
 def taps_at(index, taps, flip):
@@ -237,6 +237,15 @@
     return lax.axis_index("x") ^ bits
 
 
+def by_core(first, second):
+    return jnp.where(lax.axis_index("core") == 0, first, second)
+
+
+def near_sums(one, two):
+    one, two = get_sums(one), get_sums(two)
+    return by_core(one, two), by_core(two, one)
+
+
 def call(kernel, name, shapes, inputs, in_specs=None, scratch=(), flops=1_000_000, size=1_000_000, out_specs=None, mib=12, aliases=None):
     return pl.pallas_call(
         kernel,
@@ -305,7 +314,8 @@
 def corners_kernel(cols, members, first, second, *refs):
     if len(refs) > 2:
         sums, far, *out, total = refs
-        value = (sums[0:1, :] + get_sums(first)) + (far[0:1, :] + get_sums(second))
+        one, two = near_sums(first, second)
+        value = (sums[0:1, :] + one) + (far[0:1, :] + two)
         total[...] = jnp.broadcast_to(value, total.shape)
         for ref in out:
             put_sums(ref, value)
@@ -330,7 +340,7 @@
 
 def shares_kernel(keep, got, *shares):
     size = shares[0].shape[0]
-    for bits, out in enumerate(shares):
+    for bits, out in zip((0, by_core(1, 3), 2, by_core(3, 1)), shares):
         rows = pl.ds(pl.multiple_of(share_of(bits) * size, size), size)
         out[...] = (keep[rows, :].astype(F32) + got[rows, :].astype(F32)).astype(BF)
 
@@ -355,8 +365,8 @@
 
 def gather_kernel(zero, one, two, three, out):
     size = zero.shape[0] - EXTRA
-    for n, ref in enumerate((zero, one, two, three)):
-        out[n * size : (n + 1) * size, :] = ref[:size, :]
+    for n, ref in ((0, zero), (by_core(1, 3), one), (2, two), (by_core(3, 1), three)):
+        out[pl.ds(pl.multiple_of(n * size, size), size), :] = ref[:size, :]
     put_sums(out, (get_sums(zero) + get_sums(one)) + (get_sums(two) + get_sums(three)))
 
 
@@ -427,21 +437,42 @@
                         )
                         copy.start()
                         copies.append(copy)
-    value = (sums[0:1, :] + get_sums(one_corner)) + (far[0:1, :] + get_sums(two_corner))
+    near, next_door = near_sums(one_corner, two_corner)
+    value = (sums[0:1, :] + near) + (far[0:1, :] + next_door)
     curvature[0, 0] = jnp.sum(value) / entries
     for copy in copies:
         copy.wait()
 
 
 def exchange(first, second, axis):
-    if axis == "lat":
-        count = lax.axis_size("zh") * lax.axis_size("lat")
-        axis = ("zh", "lat")
-    else:
-        count = lax.axis_size(axis)
-    one = [(i, i ^ 1) for i in range(count)]
-    two = [(i, (i + 1 if i % 2 else i - 1) % count) for i in range(count)]
-    return lax.ppermute(first, axis, one), lax.ppermute(second, axis, two)
+    groups = lax.axis_size("zh") if axis == "lat" else 1
+    names = ("zh", "core", "lat") if axis == "lat" else ("core", axis)
+    size = lax.axis_size(axis)
+    count = groups * size
+
+    def place(core, at):
+        return (at // size * 2 + core) * size + at % size
+
+    def near(at):
+        return at ^ 1
+
+    def next_door(at):
+        return (at + 1 if at % 2 else at - 1) % count
+
+    one, two = (
+        [(place(core, at), place(core, way(at))) for core, way in enumerate(ways) for at in range(count)]
+        for ways in ((near, next_door), (next_door, near))
+    )
+    return lax.ppermute(first, names, one), lax.ppermute(second, names, two)
+
+
+def swap_x(value, first, second):
+    bits = (first, second)
+    return lax.ppermute(
+        value,
+        ("x", "core"),
+        [(2 * i + core, 2 * (i ^ bits[core]) + core) for i in range(lax.axis_size("x")) for core in range(2)],
+    )
 
 
 def per_device(control, ensemble, precision, lat_taps, lon_taps, vertical):
@@ -489,12 +520,12 @@
 
     got = lax.ppermute(send, "core", swap("core", 1))
     zero, one, two, three = call(shares_kernel, "shares", [rows(share)] * 4, (keep, got))
-    two, one, three = [lax.ppermute(v, "x", swap("x", k)) for v, k in ((two, 2), (one, 1), (three, 3))]
+    two, one, three = swap_x(two, 2, 2), swap_x(one, 1, 3), swap_x(three, 3, 1)
     band_back, band_side_back = bands(lat_taps, lon_taps, cols, True, three)
     (message,) = call(part_kernel, "part", [rows(share + EXTRA)], (zero, one, two, three, square))
     other = lax.ppermute(message, "zh", swap("zh", 1))
     (zero,) = call(weight_kernel, "weight", [rows(share + EXTRA)], (message, other, precision.reshape(cells, levels), band_side_back))
-    two, one, three = [lax.ppermute(zero, "x", swap("x", k)) for k in (2, 1, 3)]
+    two, one, three = swap_x(zero, 2, 2), swap_x(zero, 1, 3), swap_x(zero, 3, 1)
     (message,) = call(gather_kernel, "gather", [rows(cells // 2 + EXTRA)], (zero, one, two, three))
     other = lax.ppermute(message, "core", swap("core", 1))
 

time: 69 us -> 69.7 us (1.010)
    ppermute x1, waiting for transfers between devices: 0.34 us -> 1.59 us  [per_device(): far = lax.ppermute(sums, 'lat', swap('lat', 2))]
  transfers between devices with their start and end apart: 23 -> 23, of which waited for: 11 -> 13; matrix products, arithmetic and copies ran while one was open for 0% -> 0% of each run, Pallas kernels for 14% -> 14%
where the time goes in v8:
time: 69.7 us; the launch traced here: 69 us
  starting transfers between devices  34.1 us (49%)
  waiting for transfers between devices  18.5 us (27%)
  Pallas kernels  13.8 us (20%)
  local copies, waits for them, and re-layouts  1.61 us (2%)
  between operations  0.99 us (1%)
    ppermute x12, starting transfers between devices, exchange(): return (lax.ppermute(first, names, one), lax.ppermute(second, names, two))  19.6 us
    pallas_call x16, Pallas kernels, call(): pl.pallas_call(kernel, out_shape=tuple(shapes), in_specs=in_specs or [VME...  12.3 us
    ppermute x6, starting transfers between devices, swap_x(): lax.ppermute(value, ('x', 'core'), [(2 * i + core, 2 * (i ^ bits[core]) +...  8.41 us
    ppermute x6, waiting for transfers between devices, swap_x(): lax.ppermute(value, ('x', 'core'), [(2 * i + core, 2 * (i ^ bits[core]) +...  8.37 us
    ppermute x1, waiting for transfers between devices, per_device(): other = lax.ppermute(message, 'zh', swap('zh', 1))  4.14 us
    ppermute x1, starting transfers between devices, per_device(): other = lax.ppermute(message, 'zh', swap('zh', 1))  3.41 us
    ppermute x12, waiting for transfers between devices, exchange(): return (lax.ppermute(first, names, one), lax.ppermute(second, names, two))  2.22 us
    ppermute x1, starting transfers between devices, per_device(): far = lax.ppermute(sums, 'lon', swap('lon', 2))  1.77 us
  transfers between devices with their start and end apart: 23, of which 13 were waited for; matrix products, arithmetic and copies ran while one was open for 0% of the time, Pallas kernels for 14%

profile of v8, /device:TPU:2, one launch (start us, length us, event | category | flops | bytes accessed | tf_op | source)
XLA Modules:
  0.0 69.0 jit_solution(5067799547227642313)
XLA Ops:
  0.6 1.6 %copy-done.1 = bf16[4,64,32,128]{3,2,1,0:T(8,128)(2,1)S(1)} copy-done((bf16[4,64,32,128]{3,2,1,0:T(8,128)(2,1)S(1)}, bf16[4,64,32,128]{3,2,1,0:T(8,128)(2,1)}, u32[]{:S(2)}) %copy-start.1) | copy-done | bytes 2097176
  2.3 2.0 %collective-permute-start = (bf16[512,128]{1,0:T(8,128)(2,1)S(1)}, bf16[512,128]{1,0:T(8,128)(2,1)S(1)}, u32[]{:S(2)}, u32[]{:S(2)}) collective-permute-start(bf16[512,128]{1,0:T(8,128)(2,1)S(1)} %get-tuple-element.34), channel_id=1, source_target_pairs={{0,4},{4,0},{8,12},{12,8},{128,132},{132,128},{136,140},{140,136},... | collective-permute-start | bytes 393224 | tf_op jit(solution)/shard_map/ppermute | solution.py:466
  4.3 4.9 %collective-permute-start.1 = (bf16[512,128]{1,0:T(8,128)(2,1)S(1)}, bf16[512,128]{1,0:T(8,128)(2,1)S(1)}, u32[]{:S(2)}, u32[]{:S(2)}) collective-permute-start(bf16[512,128]{1,0:T(8,128)(2,1)S(1)} %get-tuple-element.35), channel_id=1, source_target_pairs={{0,140},{4,8},{8,4},{12,128},{128,12},{132,136},{136,132},{140,0},... | collective-permute-start | bytes 393224 | tf_op jit(solution)/shard_map/ppermute | solution.py:466
  9.2 0.5 strips.2
  9.7 1.7 %collective-permute-start.2 = (bf16[1024,128]{1,0:T(8,128)(2,1)S(1)}, bf16[1024,128]{1,0:T(8,128)(2,1)S(1)}, u32[]{:S(2)}, u32[]{:S(2)}) collective-permute-start(bf16[1024,128]{1,0:T(8,128)(2,1)S(1)} %get-tuple-element.38), channel_id=1, source_target_pairs={{0,1},{1,0},{2,3},{3,2},{16,19},{17,18},{18,17},{19,16},{4,5},{5,4... | collective-permute-start | bytes 786440 | tf_op jit(solution)/shard_map/ppermute | solution.py:466
  11.4 2.2 %collective-permute-start.3 = (bf16[1024,128]{1,0:T(8,128)(2,1)S(1)}, bf16[1024,128]{1,0:T(8,128)(2,1)S(1)}, u32[]{:S(2)}, u32[]{:S(2)}) collective-permute-start(bf16[1024,128]{1,0:T(8,128)(2,1)S(1)} %get-tuple-element.39), channel_id=1, source_target_pairs={{0,3},{1,2},{2,1},{3,0},{16,17},{17,16},{18,19},{19,18},{4,7},{5,6... | collective-permute-start | bytes 786440 | tf_op jit(solution)/shard_map/ppermute | solution.py:466
  13.6 0.8 %bands.1 = (bf16[512,512]{1,0:T(8,128)(2,1)S(1)}, bf16[256,128]{1,0:T(8,128)(2,1)S(1)}) custom-call(f32[9]{0:T(128)S(1)} %copy-done.5, f32[9]{0:T(128)S(1)} %copy-done.6), custom_call_target="tpu_custom_call" | custom-call | flops 2000000 | bytes 600000 | tf_op jit(solution)/shard_map/bands/pallas_call | solution.py:76
  14.3 0.2 corners.2
  14.5 0.8 %collective-permute-start.4 = (bf16[128,128]{1,0:T(8,128)(2,1)S(1)}, bf16[128,128]{1,0:T(8,128)(2,1)S(1)}, u32[]{:S(2)}, u32[]{:S(2)}) collective-permute-start(bf16[128,128]{1,0:T(8,128)(2,1)S(1)} %get-tuple-element.40), channel_id=1, source_target_pairs={{0,1},{1,0},{2,3},{3,2},{16,19},{17,18},{18,17},{19,16},{4,5},{5,4... | collective-permute-start | bytes 98312 | tf_op jit(solution)/shard_map/ppermute | solution.py:466
  15.3 0.9 %collective-permute-start.5 = (bf16[128,128]{1,0:T(8,128)(2,1)S(1)}, bf16[128,128]{1,0:T(8,128)(2,1)S(1)}, u32[]{:S(2)}, u32[]{:S(2)}) collective-permute-start(bf16[128,128]{1,0:T(8,128)(2,1)S(1)} %get-tuple-element.41), channel_id=1, source_target_pairs={{0,3},{1,2},{2,1},{3,0},{16,17},{17,16},{18,19},{19,18},{4,7},{5,6... | collective-permute-start | bytes 98312 | tf_op jit(solution)/shard_map/ppermute | solution.py:466
  16.2 2.3 %centre.1 = (f32[4,2048,128]{2,1,0:T(8,128)S(1)}, f32[8,128]{1,0:T(8,128)S(1)}) custom-call(bf16[4,2048,128]{2,1,0:T(8,128)(2,1)S(1)} %bitcast.10, bf16[512,128]{1,0:T(8,128)(2,1)S(1)} %collective-permute-done.first, bf16[512,128]{1,0:T(8,128)(2,1)S(1)} %collective-permute-done.1.second, bf16[512,512]{1,0:T(8,128)(2,1)S(1)} %get-tuple-element.36.band), custom_call_target="tpu_custom_call" | custom-call | flops 3000000000 | bytes 7000000 | tf_op jit(solution)/shard_map/centre/pallas_call | solution.py:250
  18.6 0.8 %collective-permute-done.4.one_corner = bf16[128,128]{1,0:T(8,128)(2,1)S(1)} collective-permute-done((bf16[128,128]{1,0:T(8,128)(2,1)S(1)}, bf16[128,128]{1,0:T(8,128)(2,1)S(1)}, u32[]{:S(2)}, u32[]{:S(2)}) %collective-permute-start.4) | collective-permute-done | bytes 32800 | tf_op jit(solution)/shard_map/ppermute | solution.py:466
  19.4 1.1 %collective-permute-done.5.two_corner = bf16[128,128]{1,0:T(8,128)(2,1)S(1)} collective-permute-done((bf16[128,128]{1,0:T(8,128)(2,1)S(1)}, bf16[128,128]{1,0:T(8,128)(2,1)S(1)}, u32[]{:S(2)}, u32[]{:S(2)}) %collective-permute-start.5) | collective-permute-done | bytes 32800 | tf_op jit(solution)/shard_map/ppermute | solution.py:466
  20.4 0.9 %forward_send.1 = (bf16[1024,128]{1,0:T(8,128)(2,1)S(1)}, bf16[1152,128]{1,0:T(8,128)(2,1)S(1)}, bf16[1152,128]{1,0:T(8,128)(2,1)S(1)}) custom-call(f32[4,2048,128]{2,1,0:T(8,128)S(1)} %get-tuple-element.37.inner, bf16[1024,128]{1,0:T(8,128)(2,1)S(1)} %collective-permute-done.2.one, bf16[1024,128]{1,0:T(8,128)(2,1)S(1)} %collective-permute-done.3.two, ...), custom_call_target="tpu_custom_call" | custom-call | flops 700000000 | bytes 3000000 | tf_op jit(solution)/shard_map/forward_send/pallas_call | solution.py:250
  21.4 0.1 collective-permute-start.6
  21.5 0.9 %forward_keep.1.keep = bf16[1024,128]{1,0:T(8,128)(2,1)S(1)} custom-call(f32[4,2048,128]{2,1,0:T(8,128)S(1)} %get-tuple-element.37.inner, bf16[1152,128]{1,0:T(8,128)(2,1)S(1)} %get-tuple-element.43.west, bf16[1152,128]{1,0:T(8,128)(2,1)S(1)} %get-tuple-element.44.east, bf16[256,128]{1,0:T(8,128)(2,1)S(1)} %get-tuple-element.42.band, ...), custom_call_target="tpu_custom_call" | custom-call | flops 700000000 | bytes 3000000 | tf_op jit(solution)/shard_map/forward_keep/pallas_call | solution.py:250
  22.3 0.6 collective-permute-done.6.got
  23.0 0.6 collective-permute-start.7
  23.7 2.4 %collective-permute-start.8 = (bf16[256,128]{1,0:T(8,128)(2,1)S(1)}, bf16[256,128]{1,0:T(8,128)(2,1)S(1)}, u32[]{:S(2)}, u32[]{:S(2)}) collective-permute-start(bf16[256,128]{1,0:T(8,128)(2,1)S(1)} %get-tuple-element.48), channel_id=1, source_target_pairs={{0,64},{16,80},{32,96},{48,112},{64,0},{80,16},{96,32},{112,48},{1... | collective-permute-start | bytes 196616 | tf_op jit(solution)/shard_map/ppermute | solution.py:471
  26.1 0.5 collective-permute-start.9
  26.6 0.8 %collective-permute-done.7.one = bf16[256,128]{1,0:T(8,128)(2,1)S(1)} collective-permute-done((bf16[256,128]{1,0:T(8,128)(2,1)S(1)}, bf16[256,128]{1,0:T(8,128)(2,1)S(1)}, u32[]{:S(2)}, u32[]{:S(2)}) %collective-permute-start.7) | collective-permute-done | bytes 65568 | tf_op jit(solution)/shard_map/ppermute | solution.py:471
  27.4 2.7 %collective-permute-done.8.two = bf16[256,128]{1,0:T(8,128)(2,1)S(1)} collective-permute-done((bf16[256,128]{1,0:T(8,128)(2,1)S(1)}, bf16[256,128]{1,0:T(8,128)(2,1)S(1)}, u32[]{:S(2)}, u32[]{:S(2)}) %collective-permute-start.8) | collective-permute-done | bytes 65568 | tf_op jit(solution)/shard_map/ppermute | solution.py:471
  30.1 0.5 collective-permute-done.9.three.refs_0_
  30.7 3.4 %collective-permute-start.10 = (bf16[272,128]{1,0:T(8,128)(2,1)S(1)}, bf16[272,128]{1,0:T(8,128)(2,1)S(1)}, u32[]{:S(2)}, u32[]{:S(2)}) collective-permute-start(bf16[272,128]{1,0:T(8,128)(2,1)S(1)} %part.1.message), channel_id=1, source_target_pairs={{0,128},{128,0},{1,129},{129,1},{2,130},{130,2},{3,131},{131,3},{4... | collective-permute-start | bytes 208904 | tf_op jit(solution)/shard_map/ppermute | solution.py:526
  34.1 0.8 %bands_back.1 = (bf16[512,512]{1,0:T(8,128)(2,1)S(1)}, bf16[256,128]{1,0:T(8,128)(2,1)S(1)}) custom-call(f32[9]{0:T(128)S(1)} %copy-done.5, f32[9]{0:T(128)S(1)} %copy-done.6, bf16[256,128]{1,0:T(8,128)(2,1)S(1)} %collective-permute-done.9.three.refs_0_), custom_call_target="tpu_custom_call" | custom-call | flops 2000000 | bytes 600000 | tf_op jit(solution)/shard_map/bands_back/pallas_call | solution.py:76
  34.9 4.1 %collective-permute-done.10.other = bf16[272,128]{1,0:T(8,128)(2,1)S(1)} collective-permute-done((bf16[272,128]{1,0:T(8,128)(2,1)S(1)}, bf16[272,128]{1,0:T(8,128)(2,1)S(1)}, u32[]{:S(2)}, u32[]{:S(2)}) %collective-permute-start.10) | collective-permute-done | bytes 69664 | tf_op jit(solution)/shard_map/ppermute | solution.py:526
  39.1 2.2 %collective-permute-start.13 = (bf16[272,128]{1,0:T(8,128)(2,1)S(1)}, bf16[272,128]{1,0:T(8,128)(2,1)S(1)}, u32[]{:S(2)}, u32[]{:S(2)}) collective-permute-start(bf16[272,128]{1,0:T(8,128)(2,1)S(1)} %weight.1.zero), channel_id=1, source_target_pairs={{0,96},{16,48},{32,64},{48,16},{64,32},{80,112},{96,0},{112,80},{1... | collective-permute-start | bytes 208904 | tf_op jit(solution)/shard_map/ppermute | solution.py:471
  41.3 2.7 %collective-permute-start.12 = (bf16[272,128]{1,0:T(8,128)(2,1)S(1)}, bf16[272,128]{1,0:T(8,128)(2,1)S(1)}, u32[]{:S(2)}, u32[]{:S(2)}) collective-permute-start(bf16[272,128]{1,0:T(8,128)(2,1)S(1)} %weight.1.zero), channel_id=1, source_target_pairs={{0,64},{16,80},{32,96},{48,112},{64,0},{80,16},{96,32},{112,48},{1... | collective-permute-start | bytes 208904 | tf_op jit(solution)/shard_map/ppermute | solution.py:471
  43.9 0.5 collective-permute-done.13.three
  44.5 2.6 %collective-permute-done.12.two = bf16[272,128]{1,0:T(8,128)(2,1)S(1)} collective-permute-done((bf16[272,128]{1,0:T(8,128)(2,1)S(1)}, bf16[272,128]{1,0:T(8,128)(2,1)S(1)}, u32[]{:S(2)}, u32[]{:S(2)}) %collective-permute-start.12) | collective-permute-done | bytes 69664 | tf_op jit(solution)/shard_map/ppermute | solution.py:471
  47.1 1.2 %collective-permute-done.11.one = bf16[272,128]{1,0:T(8,128)(2,1)S(1)} collective-permute-done((bf16[272,128]{1,0:T(8,128)(2,1)S(1)}, bf16[272,128]{1,0:T(8,128)(2,1)S(1)}, u32[]{:S(2)}, u32[]{:S(2)}) %collective-permute-start.11) | collective-permute-done | bytes 69664 | tf_op jit(solution)/shard_map/ppermute | solution.py:471
  48.4 1.5 %collective-permute-done.14.other = bf16[1040,128]{1,0:T(8,128)(2,1)S(1)} collective-permute-done((bf16[1040,128]{1,0:T(8,128)(2,1)S(1)}, bf16[1040,128]{1,0:T(8,128)(2,1)S(1)}, u32[]{:S(2)}, u32[]{:S(2)}) %collective-permute-start.14) | collective-permute-done | bytes 266272 | tf_op jit(solution)/shard_map/ppermute | solution.py:530
  49.9 0.3 level_edges.1
  50.2 0.1 collective-permute-start.15
  50.3 2.8 %collective-permute-start.16 = (bf16[528,128]{1,0:T(8,128)(2,1)S(1)}, bf16[528,128]{1,0:T(8,128)(2,1)S(1)}, u32[]{:S(2)}, u32[]{:S(2)}) collective-permute-start(bf16[528,128]{1,0:T(8,128)(2,1)S(1)} %get-tuple-element.54), channel_id=1, source_target_pairs={{0,140},{4,8},{8,4},{12,128},{128,12},{132,136},{136,132},{140,0},... | collective-permute-start | bytes 405512 | tf_op jit(solution)/shard_map/ppermute | solution.py:466
  53.1 0.7 %level.1 = (bf16[4,2048,128]{2,1,0:T(8,128)(2,1)S(1)}, f32[8,128]{1,0:T(8,128)S(1)}) custom-call(bf16[1040,128]{1,0:T(8,128)(2,1)S(1)} %gather.1.mine, bf16[1040,128]{1,0:T(8,128)(2,1)S(1)} %collective-permute-done.14.other, bf16[4,2048,128]{2,1,0:T(8,128)(2,1)S(1)} %bitcast.7, bf16[128,128]{1,0:T(8,128)(2,1)S(1)} %copy-done.4), custom_call_target="tpu_custom_call" | custom-call | flops 300000000 | bytes 4500000 | tf_op jit(solution)/shard_map/level/pallas_call | solution.py:250
  53.9 0.8 %collective-permute-start.19 = (f32[8,128]{1,0:T(8,128)S(1)}, f32[8,128]{1,0:T(8,128)S(1)}, u32[]{:S(2)}, u32[]{:S(2)}) collective-permute-start(f32[8,128]{1,0:T(8,128)S(1)} %get-tuple-element.59.refs_0_), channel_id=1, source_target_pairs={{0,8},{4,12},{8,0},{12,4},{1,9},{5,13},{9,1},{13,5},{2,10},{6,14},... | collective-permute-start | bytes 12296 | tf_op jit(solution)/shard_map/ppermute | solution.py:545
  54.6 0.5 strips.3
  55.1 0.2 collective-permute-start.17
  55.3 1.6 %collective-permute-start.18 = (bf16[1024,128]{1,0:T(8,128)(2,1)S(1)}, bf16[1024,128]{1,0:T(8,128)(2,1)S(1)}, u32[]{:S(2)}, u32[]{:S(2)}) collective-permute-start(bf16[1024,128]{1,0:T(8,128)(2,1)S(1)} %get-tuple-element.58), channel_id=1, source_target_pairs={{0,3},{1,2},{2,1},{3,0},{16,17},{17,16},{18,19},{19,18},{4,7},{5,6... | collective-permute-start | bytes 786440 | tf_op jit(solution)/shard_map/ppermute | solution.py:466
  56.9 1.6 %collective-permute-done.19.refs_1_ = f32[8,128]{1,0:T(8,128)S(1)} collective-permute-done((f32[8,128]{1,0:T(8,128)S(1)}, f32[8,128]{1,0:T(8,128)S(1)}, u32[]{:S(2)}, u32[]{:S(2)}) %collective-permute-start.19) | collective-permute-done | bytes 4128 | tf_op jit(solution)/shard_map/ppermute | solution.py:545
  58.5 0.2 corners.3
  58.7 1.8 %collective-permute-start.22 = (f32[8,128]{1,0:T(8,128)S(1)}, f32[8,128]{1,0:T(8,128)S(1)}, u32[]{:S(2)}, u32[]{:S(2)}) collective-permute-start(f32[8,128]{1,0:T(8,128)S(1)} %get-tuple-element.62.sums), channel_id=1, source_target_pairs={{0,2},{1,3},{2,0},{3,1},{4,6},{5,7},{6,4},{7,5},{8,10},{9,11},{10,... | collective-permute-start | bytes 12296 | tf_op jit(solution)/shard_map/ppermute | solution.py:550
  60.4 0.8 %collective-permute-start.20 = (bf16[144,128]{1,0:T(8,128)(2,1)S(1)}, bf16[144,128]{1,0:T(8,128)(2,1)S(1)}, u32[]{:S(2)}, u32[]{:S(2)}) collective-permute-start(bf16[144,128]{1,0:T(8,128)(2,1)S(1)} %get-tuple-element.60), channel_id=1, source_target_pairs={{0,1},{1,0},{2,3},{3,2},{16,19},{17,18},{18,17},{19,16},{4,5},{5,4... | collective-permute-start | bytes 110600 | tf_op jit(solution)/shard_map/ppermute | solution.py:466
  61.2 1.6 %collective-permute-start.21 = (bf16[144,128]{1,0:T(8,128)(2,1)S(1)}, bf16[144,128]{1,0:T(8,128)(2,1)S(1)}, u32[]{:S(2)}, u32[]{:S(2)}) collective-permute-start(bf16[144,128]{1,0:T(8,128)(2,1)S(1)} %get-tuple-element.61), channel_id=1, source_target_pairs={{0,3},{1,2},{2,1},{3,0},{16,17},{17,16},{18,19},{19,18},{4,7},{5,6... | collective-permute-start | bytes 110600 | tf_op jit(solution)/shard_map/ppermute | solution.py:466
  62.8 3.2 %centre_back.1 = (f32[4,64,32,128]{3,2,1,0:T(8,128)}, f32[4,64,16,128]{3,2,1,0:T(8,128)S(1)}) custom-call(bf16[4,2048,128]{2,1,0:T(8,128)(2,1)S(1)} %get-tuple-element.52.own.tile, bf16[528,128]{1,0:T(8,128)(2,1)S(1)} %collective-permute-done.15.first, bf16[528,128]{1,0:T(8,128)(2,1)S(1)} %collective-permute-done.16.second, ...), custom_call_target="tpu_custom_call" | custom-call | flops 3000000000 | bytes 7000000 | tf_op jit(solution)/shard_map/centre_back/pallas_call | solution.py:250
  66.1 0.3 collective-permute-done.21.two_corner
  66.5 2.3 %backward.1 = (f32[4,64,32,128]{3,2,1,0:T(8,128)}, f32[1,1]{1,0:T(1,128)}) custom-call(f32[4,64,16,128]{3,2,1,0:T(8,128)S(1)} %get-tuple-element.56.outer, bf16[1024,128]{1,0:T(8,128)(2,1)S(1)} %collective-permute-done.17.one, bf16[1024,128]{1,0:T(8,128)(2,1)S(1)} %collective-permute-done.18.two, ...), custom_call_target="tpu_custom_call", output_to_operand_aliasing={{0}: (8, {})} | custom-call | flops 1000000000 | bytes 9000000 | tf_op jit(solution)/shard_map/backward/pallas_call | solution.py:250
  (30 shorter events, 0.4 us)
Async XLA Ops:
  0.6 1.6 %copy-start.1 = (bf16[4,64,32,128]{3,2,1,0:T(8,128)(2,1)S(1)}, bf16[4,64,32,128]{3,2,1,0:T(8,128)(2,1)}, u32[]{:S(2)}) copy-start(bf16[4,64,32,128]{3,2,1,0:T(8,128)(2,1)} %param.6) | copy-start | bytes 6291460
  2.2 11.3 %copy-start.5 = (f32[9]{0:T(128)S(1)}, f32[9]{0:T(128)}, u32[]{:S(2)}) copy-start(f32[9]{0:T(128)} %lat_taps.3) | copy-start | bytes 112
  2.2 11.3 %copy-start.6 = (f32[9]{0:T(128)S(1)}, f32[9]{0:T(128)}, u32[]{:S(2)}) copy-start(f32[9]{0:T(128)} %lon_taps.3) | copy-start | bytes 112
  2.2 14.0 %copy-start.2 = (bf16[4,64,32,128]{3,2,1,0:T(8,128)(2,1)S(1)}, bf16[4,64,32,128]{3,2,1,0:T(8,128)(2,1)}, u32[]{:S(2)}) copy-start(bf16[4,64,32,128]{3,2,1,0:T(8,128)(2,1)} %param.6) | copy-start | bytes 6291460
  2.3 12.0 %collective-permute-start = (bf16[512,128]{1,0:T(8,128)(2,1)S(1)}, bf16[512,128]{1,0:T(8,128)(2,1)S(1)}, u32[]{:S(2)}, u32[]{:S(2)}) collective-permute-start(bf16[512,128]{1,0:T(8,128)(2,1)S(1)} %get-tuple-element.34), channel_id=1, source_target_pairs={{0,4},{4,0},{8,12},{12,8},{128,132},{132,128},{136,140},{140,136},... | collective-permute-start | bytes 393224 | tf_op jit(solution)/shard_map/ppermute | solution.py:466
  4.3 10.0 %collective-permute-start.1 = (bf16[512,128]{1,0:T(8,128)(2,1)S(1)}, bf16[512,128]{1,0:T(8,128)(2,1)S(1)}, u32[]{:S(2)}, u32[]{:S(2)}) collective-permute-start(bf16[512,128]{1,0:T(8,128)(2,1)S(1)} %get-tuple-element.35), channel_id=1, source_target_pairs={{0,140},{4,8},{8,4},{12,128},{128,12},{132,136},{136,132},{140,0},... | collective-permute-start | bytes 393224 | tf_op jit(solution)/shard_map/ppermute | solution.py:466
  9.7 10.7 %collective-permute-start.2 = (bf16[1024,128]{1,0:T(8,128)(2,1)S(1)}, bf16[1024,128]{1,0:T(8,128)(2,1)S(1)}, u32[]{:S(2)}, u32[]{:S(2)}) collective-permute-start(bf16[1024,128]{1,0:T(8,128)(2,1)S(1)} %get-tuple-element.38), channel_id=1, source_target_pairs={{0,1},{1,0},{2,3},{3,2},{16,19},{17,18},{18,17},{19,16},{4,5},{5,4... | collective-permute-start | bytes 786440 | tf_op jit(solution)/shard_map/ppermute | solution.py:466
  11.4 9.1 %collective-permute-start.3 = (bf16[1024,128]{1,0:T(8,128)(2,1)S(1)}, bf16[1024,128]{1,0:T(8,128)(2,1)S(1)}, u32[]{:S(2)}, u32[]{:S(2)}) collective-permute-start(bf16[1024,128]{1,0:T(8,128)(2,1)S(1)} %get-tuple-element.39), channel_id=1, source_target_pairs={{0,3},{1,2},{2,1},{3,0},{16,17},{17,16},{18,19},{19,18},{4,7},{5,6... | collective-permute-start | bytes 786440 | tf_op jit(solution)/shard_map/ppermute | solution.py:466
  14.5 4.8 %collective-permute-start.4 = (bf16[128,128]{1,0:T(8,128)(2,1)S(1)}, bf16[128,128]{1,0:T(8,128)(2,1)S(1)}, u32[]{:S(2)}, u32[]{:S(2)}) collective-permute-start(bf16[128,128]{1,0:T(8,128)(2,1)S(1)} %get-tuple-element.40), channel_id=1, source_target_pairs={{0,1},{1,0},{2,3},{3,2},{16,19},{17,18},{18,17},{19,16},{4,5},{5,4... | collective-permute-start | bytes 98312 | tf_op jit(solution)/shard_map/ppermute | solution.py:466
  15.3 5.1 %collective-permute-start.5 = (bf16[128,128]{1,0:T(8,128)(2,1)S(1)}, bf16[128,128]{1,0:T(8,128)(2,1)S(1)}, u32[]{:S(2)}, u32[]{:S(2)}) collective-permute-start(bf16[128,128]{1,0:T(8,128)(2,1)S(1)} %get-tuple-element.41), channel_id=1, source_target_pairs={{0,3},{1,2},{2,1},{3,0},{16,17},{17,16},{18,19},{19,18},{4,7},{5,6... | collective-permute-start | bytes 98312 | tf_op jit(solution)/shard_map/ppermute | solution.py:466
  16.2 4.2 %copy-start = (bf16[4,64,32,128]{3,2,1,0:T(8,128)(2,1)S(1)}, bf16[4,64,32,128]{3,2,1,0:T(8,128)(2,1)}, u32[]{:S(2)}) copy-start(bf16[4,64,32,128]{3,2,1,0:T(8,128)(2,1)} %param.7) | copy-start | bytes 6291460
  16.2 4.2 %copy-start.4 = (bf16[128,128]{1,0:T(8,128)(2,1)S(1)}, bf16[128,128]{1,0:T(8,128)(2,1)}, u32[]{:S(2)}) copy-start(bf16[128,128]{1,0:T(8,128)(2,1)} %vertical.7) | copy-start | bytes 98308
  21.4 1.6 %collective-permute-start.6 = (bf16[1024,128]{1,0:T(8,128)(2,1)S(1)}, bf16[1024,128]{1,0:T(8,128)(2,1)S(1)}, u32[]{:S(2)}, u32[]{:S(2)}) collective-permute-start(bf16[1024,128]{1,0:T(8,128)(2,1)S(1)} %get-tuple-element.45), channel_id=1, source_target_pairs={{0,16},{16,0},{1,17},{17,1},{2,18},{18,2},{3,19},{19,3},{4,20},{20... | collective-permute-start | bytes 786440 | tf_op jit(solution)/shard_map/ppermute | solution.py:521
  21.5 17.6 %copy-start.3 = (f32[64,32,128]{2,1,0:T(8,128)S(1)}, f32[64,32,128]{2,1,0:T(8,128)}, u32[]{:S(2)}) copy-start(f32[64,32,128]{2,1,0:T(8,128)} %param.8) | copy-start | bytes 3145732
  23.0 4.4 %collective-permute-start.7 = (bf16[256,128]{1,0:T(8,128)(2,1)S(1)}, bf16[256,128]{1,0:T(8,128)(2,1)S(1)}, u32[]{:S(2)}, u32[]{:S(2)}) collective-permute-start(bf16[256,128]{1,0:T(8,128)(2,1)S(1)} %get-tuple-element.47), channel_id=1, source_target_pairs={{0,32},{16,112},{32,0},{48,80},{64,96},{80,48},{96,64},{112,16},{1... | collective-permute-start | bytes 196616 | tf_op jit(solution)/shard_map/ppermute | solution.py:471
  23.7 6.5 %collective-permute-start.8 = (bf16[256,128]{1,0:T(8,128)(2,1)S(1)}, bf16[256,128]{1,0:T(8,128)(2,1)S(1)}, u32[]{:S(2)}, u32[]{:S(2)}) collective-permute-start(bf16[256,128]{1,0:T(8,128)(2,1)S(1)} %get-tuple-element.48), channel_id=1, source_target_pairs={{0,64},{16,80},{32,96},{48,112},{64,0},{80,16},{96,32},{112,48},{1... | collective-permute-start | bytes 196616 | tf_op jit(solution)/shard_map/ppermute | solution.py:471
  26.1 4.6 %collective-permute-start.9 = (bf16[256,128]{1,0:T(8,128)(2,1)S(1)}, bf16[256,128]{1,0:T(8,128)(2,1)S(1)}, u32[]{:S(2)}, u32[]{:S(2)}) collective-permute-start(bf16[256,128]{1,0:T(8,128)(2,1)S(1)} %get-tuple-element.49), channel_id=1, source_target_pairs={{0,96},{16,48},{32,64},{48,16},{64,32},{80,112},{96,0},{112,80},{1... | collective-permute-start | bytes 196616 | tf_op jit(solution)/shard_map/ppermute | solution.py:471
  30.7 8.3 %collective-permute-start.10 = (bf16[272,128]{1,0:T(8,128)(2,1)S(1)}, bf16[272,128]{1,0:T(8,128)(2,1)S(1)}, u32[]{:S(2)}, u32[]{:S(2)}) collective-permute-start(bf16[272,128]{1,0:T(8,128)(2,1)S(1)} %part.1.message), channel_id=1, source_target_pairs={{0,128},{128,0},{1,129},{129,1},{2,130},{130,2},{3,131},{131,3},{4... | collective-permute-start | bytes 208904 | tf_op jit(solution)/shard_map/ppermute | solution.py:526
  39.1 5.4 %collective-permute-start.13 = (bf16[272,128]{1,0:T(8,128)(2,1)S(1)}, bf16[272,128]{1,0:T(8,128)(2,1)S(1)}, u32[]{:S(2)}, u32[]{:S(2)}) collective-permute-start(bf16[272,128]{1,0:T(8,128)(2,1)S(1)} %weight.1.zero), channel_id=1, source_target_pairs={{0,96},{16,48},{32,64},{48,16},{64,32},{80,112},{96,0},{112,80},{1... | collective-permute-start | bytes 208904 | tf_op jit(solution)/shard_map/ppermute | solution.py:471
  41.3 5.8 %collective-permute-start.12 = (bf16[272,128]{1,0:T(8,128)(2,1)S(1)}, bf16[272,128]{1,0:T(8,128)(2,1)S(1)}, u32[]{:S(2)}, u32[]{:S(2)}) collective-permute-start(bf16[272,128]{1,0:T(8,128)(2,1)S(1)} %weight.1.zero), channel_id=1, source_target_pairs={{0,64},{16,80},{32,96},{48,112},{64,0},{80,16},{96,32},{112,48},{1... | collective-permute-start | bytes 208904 | tf_op jit(solution)/shard_map/ppermute | solution.py:471
  43.9 4.3 %collective-permute-start.11 = (bf16[272,128]{1,0:T(8,128)(2,1)S(1)}, bf16[272,128]{1,0:T(8,128)(2,1)S(1)}, u32[]{:S(2)}, u32[]{:S(2)}) collective-permute-start(bf16[272,128]{1,0:T(8,128)(2,1)S(1)} %weight.1.zero), channel_id=1, source_target_pairs={{0,32},{16,112},{32,0},{48,80},{64,96},{80,48},{96,64},{112,16},{1... | collective-permute-start | bytes 208904 | tf_op jit(solution)/shard_map/ppermute | solution.py:471
  48.3 1.6 %collective-permute-start.14 = (bf16[1040,128]{1,0:T(8,128)(2,1)S(1)}, bf16[1040,128]{1,0:T(8,128)(2,1)S(1)}, u32[]{:S(2)}, u32[]{:S(2)}) collective-permute-start(bf16[1040,128]{1,0:T(8,128)(2,1)S(1)} %gather.1.mine), channel_id=1, source_target_pairs={{0,16},{16,0},{1,17},{17,1},{2,18},{18,2},{3,19},{19,3},{4,20},{20... | collective-permute-start | bytes 798728 | tf_op jit(solution)/shard_map/ppermute | solution.py:530
  50.2 8.2 %collective-permute-start.15 = (bf16[528,128]{1,0:T(8,128)(2,1)S(1)}, bf16[528,128]{1,0:T(8,128)(2,1)S(1)}, u32[]{:S(2)}, u32[]{:S(2)}) collective-permute-start(bf16[528,128]{1,0:T(8,128)(2,1)S(1)} %get-tuple-element.53), channel_id=1, source_target_pairs={{0,4},{4,0},{8,12},{12,8},{128,132},{132,128},{136,140},{140,136},... | collective-permute-start | bytes 405512 | tf_op jit(solution)/shard_map/ppermute | solution.py:466
  50.3 8.1 %collective-permute-start.16 = (bf16[528,128]{1,0:T(8,128)(2,1)S(1)}, bf16[528,128]{1,0:T(8,128)(2,1)S(1)}, u32[]{:S(2)}, u32[]{:S(2)}) collective-permute-start(bf16[528,128]{1,0:T(8,128)(2,1)S(1)} %get-tuple-element.54), channel_id=1, source_target_pairs={{0,140},{4,8},{8,4},{12,128},{128,12},{132,136},{136,132},{140,0},... | collective-permute-start | bytes 405512 | tf_op jit(solution)/shard_map/ppermute | solution.py:466
  53.9 4.6 %collective-permute-start.19 = (f32[8,128]{1,0:T(8,128)S(1)}, f32[8,128]{1,0:T(8,128)S(1)}, u32[]{:S(2)}, u32[]{:S(2)}) collective-permute-start(f32[8,128]{1,0:T(8,128)S(1)} %get-tuple-element.59.refs_0_), channel_id=1, source_target_pairs={{0,8},{4,12},{8,0},{12,4},{1,9},{5,13},{9,1},{13,5},{2,10},{6,14},... | collective-permute-start | bytes 12296 | tf_op jit(solution)/shard_map/ppermute | solution.py:545
  55.1 11.4 %collective-permute-start.17 = (bf16[1024,128]{1,0:T(8,128)(2,1)S(1)}, bf16[1024,128]{1,0:T(8,128)(2,1)S(1)}, u32[]{:S(2)}, u32[]{:S(2)}) collective-permute-start(bf16[1024,128]{1,0:T(8,128)(2,1)S(1)} %get-tuple-element.57), channel_id=1, source_target_pairs={{0,1},{1,0},{2,3},{3,2},{16,19},{17,18},{18,17},{19,16},{4,5},{5,4... | collective-permute-start | bytes 786440 | tf_op jit(solution)/shard_map/ppermute | solution.py:466
  55.3 11.2 %collective-permute-start.18 = (bf16[1024,128]{1,0:T(8,128)(2,1)S(1)}, bf16[1024,128]{1,0:T(8,128)(2,1)S(1)}, u32[]{:S(2)}, u32[]{:S(2)}) collective-permute-start(bf16[1024,128]{1,0:T(8,128)(2,1)S(1)} %get-tuple-element.58), channel_id=1, source_target_pairs={{0,3},{1,2},{2,1},{3,0},{16,17},{17,16},{18,19},{19,18},{4,7},{5,6... | collective-permute-start | bytes 786440 | tf_op jit(solution)/shard_map/ppermute | solution.py:466
  58.7 7.4 %collective-permute-start.22 = (f32[8,128]{1,0:T(8,128)S(1)}, f32[8,128]{1,0:T(8,128)S(1)}, u32[]{:S(2)}, u32[]{:S(2)}) collective-permute-start(f32[8,128]{1,0:T(8,128)S(1)} %get-tuple-element.62.sums), channel_id=1, source_target_pairs={{0,2},{1,3},{2,0},{3,1},{4,6},{5,7},{6,4},{7,5},{8,10},{9,11},{10,... | collective-permute-start | bytes 12296 | tf_op jit(solution)/shard_map/ppermute | solution.py:550
  60.4 5.7 %collective-permute-start.20 = (bf16[144,128]{1,0:T(8,128)(2,1)S(1)}, bf16[144,128]{1,0:T(8,128)(2,1)S(1)}, u32[]{:S(2)}, u32[]{:S(2)}) collective-permute-start(bf16[144,128]{1,0:T(8,128)(2,1)S(1)} %get-tuple-element.60), channel_id=1, source_target_pairs={{0,1},{1,0},{2,3},{3,2},{16,19},{17,18},{18,17},{19,16},{4,5},{5,4... | collective-permute-start | bytes 110600 | tf_op jit(solution)/shard_map/ppermute | solution.py:466
  61.2 5.3 %collective-permute-start.21 = (bf16[144,128]{1,0:T(8,128)(2,1)S(1)}, bf16[144,128]{1,0:T(8,128)(2,1)S(1)}, u32[]{:S(2)}, u32[]{:S(2)}) collective-permute-start(bf16[144,128]{1,0:T(8,128)(2,1)S(1)} %get-tuple-element.61), channel_id=1, source_target_pairs={{0,3},{1,2},{2,1},{3,0},{16,17},{17,16},{18,19},{19,18},{4,7},{5,6... | collective-permute-start | bytes 110600 | tf_op jit(solution)/shard_map/ppermute | solution.py:466

commit v9 on v6

--- a/solution.py
+++ b/solution.py
@@ -126,7 +126,7 @@
     square[...] = total
 
 
-def centre_back_kernel(cols, own, first, second, band, control, hessian, outer, middle, done):
+def centre_back_kernel(cols, own, first, second, band, control, hessian, outer, rest, middle, done):
     members, cells, levels = own.shape
     size = ROWS * cols
     batch = 2 * ROWS
@@ -135,10 +135,12 @@
         value = (control[m, row : row + size, :].astype(F32) + value).reshape(ROWS, cols, levels)
         at = row // cols
         rows = slice(at, at + ROWS)
-        middle[m, rows, :, :] = value[:, 8 : cols - 8]
+        late = m >= members // 2
+        place = rest if late else middle
+        place[m % (members // 2), rows, :, :] = value[:, 8 : cols - 8]
         outer[m, rows, :8, :] = value[:, :8]
         outer[m, rows, 8:, :] = value[:, cols - 8 :]
-        if (at + ROWS) % batch == 0:
+        if not late and (at + ROWS) % batch == 0:
             rows = pl.ds(at + ROWS - batch, batch)
             copy = pltpu.make_async_copy(
                 middle.at[m, rows], hessian.at[m, rows, pl.ds(8, cols - 16), :], done.at[len(copies)]
@@ -388,7 +390,7 @@
     put_sums(second, value)
 
 
-def level_kernel(mine, other, ensemble, vertical, adjoint, sums):
+def level_kernel(cols, mine, other, ensemble, vertical, adjoint, sums, *out):
     sums[...] = jnp.broadcast_to(get_sums(mine) + get_sums(other), sums.shape)
     members, cells, _ = adjoint.shape
     share = cells // 8
@@ -399,17 +401,24 @@
             weighted = which[k * share : (k + 1) * share, :].astype(F32)
             for m in range(members):
                 adjoint[m, rows, :] = adjoint_of(ensemble[m, rows, :], weighted, vertical)
+    strips_kernel(cols, adjoint, *out)
 
 
 def backward_kernel(
-    cols, entries, outer, one, two, one_corner, two_corner, band, sums, far, _,
+    cols, entries, outer, rest, one, two, one_corner, two_corner, band, sums, far, _,
     hessian, curvature, result, west, east, done,
 ):
     members, tile_rows, width, levels = outer.shape
     cells = tile_rows * cols
     batch = 2 * ROWS
+    copies = []
+    for m in range(members // 2, members):
+        copy = pltpu.make_async_copy(
+            rest.at[m - members // 2], hessian.at[m, :, pl.ds(8, cols - 16), :], done.at[len(copies)]
+        )
+        copy.start()
+        copies.append(copy)
     joined((one, two), (one_corner, two_corner), (west, east), members, cols, cells)
-    copies = []
     for start in range(0, members, 2):
         pair = (start, start + 1)
         for block in range(tile_rows // ROWS):
@@ -502,30 +511,31 @@
     first, second = call(
         level_edges_kernel, "level_edges", [message_shape, message_shape], (message, other, spread, vertical)
     )
-    adjoint, sums = call(
-        level_kernel,
+    adjoint, sums, low, high = call(
+        functools.partial(level_kernel, cols),
         "level",
-        [jax.ShapeDtypeStruct(own.shape, BF), row],
+        [jax.ShapeDtypeStruct(own.shape, BF), row] + [rows(members * tile_rows * HALO)] * 2,
         (message, other, spread, vertical),
         flops=300_000_000,
         size=4_500_000,
     )
     one, two = exchange(first, second, "lat")
     far = lax.ppermute(sums, "lat", swap("lat", 2))
-    beside_it = exchange(*strips(adjoint, cols), "lon")
+    beside_it = exchange(low, high, "lon")
     *corner, sums = corners(one, two, cols, members, sums, far)
     corner = exchange(*corner, "lon")
     outer_shape = (members, tile_rows, 16, levels)
     far = lax.ppermute(sums, "lon", swap("lon", 2))
-    hessian, outer = call(
+    rest_shape = (members // 2, tile_rows, cols - 16, levels)
+    hessian, outer, rest = call(
         functools.partial(centre_back_kernel, cols),
         "centre_back",
-        [jax.ShapeDtypeStruct(control.shape, F32), jax.ShapeDtypeStruct(outer_shape, F32)],
+        [jax.ShapeDtypeStruct(control.shape, F32), jax.ShapeDtypeStruct(outer_shape, F32), jax.ShapeDtypeStruct(rest_shape, F32)],
         (adjoint, one, two, band_back, own),
-        out_specs=(pl.BlockSpec(memory_space=pl.ANY), VMEM),
+        out_specs=(pl.BlockSpec(memory_space=pl.ANY), VMEM, VMEM),
         scratch=(
-            pltpu.VMEM((members, tile_rows, cols - 16, levels), F32),
-            pltpu.SemaphoreType.DMA((members * tile_rows // (2 * ROWS),)),
+            pltpu.VMEM(rest_shape, F32),
+            pltpu.SemaphoreType.DMA((members // 2 * tile_rows // (2 * ROWS),)),
         ),
         flops=3_000_000_000,
         size=7_000_000,
@@ -534,16 +544,16 @@
         functools.partial(backward_kernel, cols, entries),
         "backward",
         [jax.ShapeDtypeStruct(control.shape, F32), jax.ShapeDtypeStruct((1, 1), F32)],
-        (outer, *beside_it, *corner, band_side_back, sums, far, hessian),
-        in_specs=[VMEM] * 8 + [pl.BlockSpec(memory_space=pl.ANY)],
+        (outer, rest, *beside_it, *corner, band_side_back, sums, far, hessian),
+        in_specs=[VMEM] * 9 + [pl.BlockSpec(memory_space=pl.ANY)],
         scratch=(
             pltpu.VMEM(outer_shape, F32),
             pltpu.VMEM(joint.shape, BF),
             pltpu.VMEM(joint.shape, BF),
-            pltpu.SemaphoreType.DMA((2 * members * tile_rows // (2 * ROWS),)),
+            pltpu.SemaphoreType.DMA((2 * members * tile_rows // (2 * ROWS) + members // 2,)),
         ),
         out_specs=(pl.BlockSpec(memory_space=pl.ANY), SMEM),
-        aliases={8: 0},
+        aliases={9: 0},
         flops=1_000_000_000,
         size=9_000_000,
     )

time: 69 us -> 69.7 us (1.010)
  waiting for transfers between devices: 17.9 us -> 19.2 us
    ppermute x12, waiting for transfers between devices: 2.49 us -> 3.24 us  [exchange(): return (lax.ppermute(first, axis, one), lax.ppermute(second, axis, two))]
    pallas_call x16 -> x15, Pallas kernels: 12.3 us -> 11.8 us  [call(): pl.pallas_call(kernel, out_shape=tuple(shapes), in_specs=in_specs or [VME...]
  transfers between devices with their start and end apart: 23 -> 23, of which waited for: 11 -> 11; matrix products, arithmetic and copies ran while one was open for 0% -> 0% of each run, Pallas kernels for 14% -> 13%
where the time goes in v9:
time: 69.7 us; the launch traced here: 69.5 us
  starting transfers between devices  34.5 us (49%)
  waiting for transfers between devices  19.2 us (28%)
  Pallas kernels  13.3 us (19%)
  local copies, waits for them, and re-layouts  1.61 us (2%)
  between operations  1 us (1%)
    ppermute x12, starting transfers between devices, exchange(): return (lax.ppermute(first, axis, one), lax.ppermute(second, axis, two))  19.6 us
    pallas_call x15, Pallas kernels, call(): pl.pallas_call(kernel, out_shape=tuple(shapes), in_specs=in_specs or [VME...  11.8 us
    ppermute x3, starting transfers between devices, per_device(): two, one, three = [lax.ppermute(zero, 'x', swap('x', k)) for k in (2, 1, 3)]  4.52 us
    ppermute x1, waiting for transfers between devices, per_device(): other = lax.ppermute(message, 'zh', swap('zh', 1))  4.45 us
    ppermute x3, waiting for transfers between devices, per_device(): two, one, three = [lax.ppermute(zero, 'x', swap('x', k)) for k in (2, 1, 3)]  4.31 us
    ppermute x3, waiting for transfers between devices, per_device(): lax.ppermute(v, 'x', swap('x', k))  4.12 us
    ppermute x3, starting transfers between devices, per_device(): lax.ppermute(v, 'x', swap('x', k))  3.58 us
    ppermute x1, starting transfers between devices, per_device(): other = lax.ppermute(message, 'zh', swap('zh', 1))  3.35 us
  transfers between devices with their start and end apart: 23, of which 11 were waited for; matrix products, arithmetic and copies ran while one was open for 0% of the time, Pallas kernels for 13%

profile of v9, /device:TPU:2, one launch (start us, length us, event | category | flops | bytes accessed | tf_op | source)
XLA Modules:
  0.0 69.5 jit_solution(15211615923116075540)
XLA Ops:
  0.6 1.6 %copy-done.1 = bf16[4,64,32,128]{3,2,1,0:T(8,128)(2,1)S(1)} copy-done((bf16[4,64,32,128]{3,2,1,0:T(8,128)(2,1)S(1)}, bf16[4,64,32,128]{3,2,1,0:T(8,128)(2,1)}, u32[]{:S(2)}) %copy-start.1) | copy-done | bytes 2097176
  2.3 2.0 %collective-permute-start = (bf16[512,128]{1,0:T(8,128)(2,1)S(1)}, bf16[512,128]{1,0:T(8,128)(2,1)S(1)}, u32[]{:S(2)}, u32[]{:S(2)}) collective-permute-start(bf16[512,128]{1,0:T(8,128)(2,1)S(1)} %get-tuple-element.35), channel_id=1, source_target_pairs={{0,4},{4,0},{8,12},{12,8},{128,132},{132,128},{136,140},{140,136},... | collective-permute-start | bytes 393224 | tf_op jit(solution)/shard_map/ppermute | solution.py:453
  4.3 4.9 %collective-permute-start.1 = (bf16[512,128]{1,0:T(8,128)(2,1)S(1)}, bf16[512,128]{1,0:T(8,128)(2,1)S(1)}, u32[]{:S(2)}, u32[]{:S(2)}) collective-permute-start(bf16[512,128]{1,0:T(8,128)(2,1)S(1)} %get-tuple-element.36), channel_id=1, source_target_pairs={{0,140},{4,8},{8,4},{12,128},{128,12},{132,136},{136,132},{140,0},... | collective-permute-start | bytes 393224 | tf_op jit(solution)/shard_map/ppermute | solution.py:453
  9.2 0.5 strips.1
  9.7 1.7 %collective-permute-start.2 = (bf16[1024,128]{1,0:T(8,128)(2,1)S(1)}, bf16[1024,128]{1,0:T(8,128)(2,1)S(1)}, u32[]{:S(2)}, u32[]{:S(2)}) collective-permute-start(bf16[1024,128]{1,0:T(8,128)(2,1)S(1)} %get-tuple-element.39), channel_id=1, source_target_pairs={{0,1},{1,0},{2,3},{3,2},{4,5},{5,4},{6,7},{7,6},{8,9},{9,8},{10,11... | collective-permute-start | bytes 786440 | tf_op jit(solution)/shard_map/ppermute | solution.py:453
  11.4 2.2 %collective-permute-start.3 = (bf16[1024,128]{1,0:T(8,128)(2,1)S(1)}, bf16[1024,128]{1,0:T(8,128)(2,1)S(1)}, u32[]{:S(2)}, u32[]{:S(2)}) collective-permute-start(bf16[1024,128]{1,0:T(8,128)(2,1)S(1)} %get-tuple-element.40), channel_id=1, source_target_pairs={{0,3},{1,2},{2,1},{3,0},{4,7},{5,6},{6,5},{7,4},{8,11},{9,10},{10,... | collective-permute-start | bytes 786440 | tf_op jit(solution)/shard_map/ppermute | solution.py:453
  13.6 0.8 %bands.1 = (bf16[512,512]{1,0:T(8,128)(2,1)S(1)}, bf16[256,128]{1,0:T(8,128)(2,1)S(1)}) custom-call(f32[9]{0:T(128)S(1)} %copy-done.5, f32[9]{0:T(128)S(1)} %copy-done.6), custom_call_target="tpu_custom_call" | custom-call | flops 2000000 | bytes 600000 | tf_op jit(solution)/shard_map/bands/pallas_call | solution.py:76
  14.3 0.2 corners.2
  14.5 0.8 %collective-permute-start.4 = (bf16[128,128]{1,0:T(8,128)(2,1)S(1)}, bf16[128,128]{1,0:T(8,128)(2,1)S(1)}, u32[]{:S(2)}, u32[]{:S(2)}) collective-permute-start(bf16[128,128]{1,0:T(8,128)(2,1)S(1)} %get-tuple-element.41), channel_id=1, source_target_pairs={{0,1},{1,0},{2,3},{3,2},{4,5},{5,4},{6,7},{7,6},{8,9},{9,8},{10,11... | collective-permute-start | bytes 98312 | tf_op jit(solution)/shard_map/ppermute | solution.py:453
  15.3 1.2 %collective-permute-start.5 = (bf16[128,128]{1,0:T(8,128)(2,1)S(1)}, bf16[128,128]{1,0:T(8,128)(2,1)S(1)}, u32[]{:S(2)}, u32[]{:S(2)}) collective-permute-start(bf16[128,128]{1,0:T(8,128)(2,1)S(1)} %get-tuple-element.42), channel_id=1, source_target_pairs={{0,3},{1,2},{2,1},{3,0},{4,7},{5,6},{6,5},{7,4},{8,11},{9,10},{10,... | collective-permute-start | bytes 98312 | tf_op jit(solution)/shard_map/ppermute | solution.py:453
  16.5 2.3 %centre.1 = (f32[4,2048,128]{2,1,0:T(8,128)S(1)}, f32[8,128]{1,0:T(8,128)S(1)}) custom-call(bf16[4,2048,128]{2,1,0:T(8,128)(2,1)S(1)} %bitcast.10, bf16[512,128]{1,0:T(8,128)(2,1)S(1)} %collective-permute-done.first, bf16[512,128]{1,0:T(8,128)(2,1)S(1)} %collective-permute-done.1.second, bf16[512,512]{1,0:T(8,128)(2,1)S(1)} %get-tuple-element.37.band), custom_call_target="tpu_custom_call" | custom-call | flops 3000000000 | bytes 7000000 | tf_op jit(solution)/shard_map/centre/pallas_call | solution.py:243
  18.9 1.6 %collective-permute-done.5.two_corner = bf16[128,128]{1,0:T(8,128)(2,1)S(1)} collective-permute-done((bf16[128,128]{1,0:T(8,128)(2,1)S(1)}, bf16[128,128]{1,0:T(8,128)(2,1)S(1)}, u32[]{:S(2)}, u32[]{:S(2)}) %collective-permute-start.5) | collective-permute-done | bytes 32800 | tf_op jit(solution)/shard_map/ppermute | solution.py:453
  20.5 0.9 %forward_send.1 = (bf16[1024,128]{1,0:T(8,128)(2,1)S(1)}, bf16[1152,128]{1,0:T(8,128)(2,1)S(1)}, bf16[1152,128]{1,0:T(8,128)(2,1)S(1)}) custom-call(f32[4,2048,128]{2,1,0:T(8,128)S(1)} %get-tuple-element.38.inner, bf16[1024,128]{1,0:T(8,128)(2,1)S(1)} %collective-permute-done.2.one, bf16[1024,128]{1,0:T(8,128)(2,1)S(1)} %collective-permute-done.3.two, ...), custom_call_target="tpu_custom_call" | custom-call | flops 700000000 | bytes 3000000 | tf_op jit(solution)/shard_map/forward_send/pallas_call | solution.py:243
  21.4 0.1 collective-permute-start.6
  21.5 0.9 %forward_keep.1.keep = bf16[1024,128]{1,0:T(8,128)(2,1)S(1)} custom-call(f32[4,2048,128]{2,1,0:T(8,128)S(1)} %get-tuple-element.38.inner, bf16[1152,128]{1,0:T(8,128)(2,1)S(1)} %get-tuple-element.44.west, bf16[1152,128]{1,0:T(8,128)(2,1)S(1)} %get-tuple-element.45.east, bf16[256,128]{1,0:T(8,128)(2,1)S(1)} %get-tuple-element.43.band, ...), custom_call_target="tpu_custom_call" | custom-call | flops 700000000 | bytes 3000000 | tf_op jit(solution)/shard_map/forward_keep/pallas_call | solution.py:243
  22.4 0.6 collective-permute-done.6.got
  23.0 0.1 shares.1
  23.1 0.6 collective-permute-start.7
  23.7 2.4 %collective-permute-start.8 = (bf16[256,128]{1,0:T(8,128)(2,1)S(1)}, bf16[256,128]{1,0:T(8,128)(2,1)S(1)}, u32[]{:S(2)}, u32[]{:S(2)}) collective-permute-start(bf16[256,128]{1,0:T(8,128)(2,1)S(1)} %get-tuple-element.49), channel_id=1, source_target_pairs={{0,64},{32,96},{64,0},{96,32},{1,65},{33,97},{65,1},{97,33},{2,66}... | collective-permute-start | bytes 196616 | tf_op jit(solution)/shard_map/ppermute | solution.py:501
  26.1 0.5 collective-permute-start.9
  26.7 0.8 %collective-permute-done.7.one = bf16[256,128]{1,0:T(8,128)(2,1)S(1)} collective-permute-done((bf16[256,128]{1,0:T(8,128)(2,1)S(1)}, bf16[256,128]{1,0:T(8,128)(2,1)S(1)}, u32[]{:S(2)}, u32[]{:S(2)}) %collective-permute-start.7) | collective-permute-done | bytes 65568 | tf_op jit(solution)/shard_map/ppermute | solution.py:501
  27.5 2.4 %collective-permute-done.8.two = bf16[256,128]{1,0:T(8,128)(2,1)S(1)} collective-permute-done((bf16[256,128]{1,0:T(8,128)(2,1)S(1)}, bf16[256,128]{1,0:T(8,128)(2,1)S(1)}, u32[]{:S(2)}, u32[]{:S(2)}) %collective-permute-start.8) | collective-permute-done | bytes 65568 | tf_op jit(solution)/shard_map/ppermute | solution.py:501
  29.9 0.9 %collective-permute-done.9.three.refs_0_ = bf16[256,128]{1,0:T(8,128)(2,1)S(1)} collective-permute-done((bf16[256,128]{1,0:T(8,128)(2,1)S(1)}, bf16[256,128]{1,0:T(8,128)(2,1)S(1)}, u32[]{:S(2)}, u32[]{:S(2)}) %collective-permute-start.9) | collective-permute-done | bytes 65568 | tf_op jit(solution)/shard_map/ppermute | solution.py:501
  30.9 3.3 %collective-permute-start.10 = (bf16[272,128]{1,0:T(8,128)(2,1)S(1)}, bf16[272,128]{1,0:T(8,128)(2,1)S(1)}, u32[]{:S(2)}, u32[]{:S(2)}) collective-permute-start(bf16[272,128]{1,0:T(8,128)(2,1)S(1)} %part.1.message), channel_id=1, source_target_pairs={{0,128},{128,0},{1,129},{129,1},{2,130},{130,2},{3,131},{131,3},{4... | collective-permute-start | bytes 208904 | tf_op jit(solution)/shard_map/ppermute | solution.py:504
  34.2 0.8 %bands_back.1 = (bf16[512,512]{1,0:T(8,128)(2,1)S(1)}, bf16[256,128]{1,0:T(8,128)(2,1)S(1)}) custom-call(f32[9]{0:T(128)S(1)} %copy-done.5, f32[9]{0:T(128)S(1)} %copy-done.6, bf16[256,128]{1,0:T(8,128)(2,1)S(1)} %collective-permute-done.9.three.refs_0_), custom_call_target="tpu_custom_call" | custom-call | flops 2000000 | bytes 600000 | tf_op jit(solution)/shard_map/bands_back/pallas_call | solution.py:76
  35.0 4.5 %collective-permute-done.10.other = bf16[272,128]{1,0:T(8,128)(2,1)S(1)} collective-permute-done((bf16[272,128]{1,0:T(8,128)(2,1)S(1)}, bf16[272,128]{1,0:T(8,128)(2,1)S(1)}, u32[]{:S(2)}, u32[]{:S(2)}) %collective-permute-start.10) | collective-permute-done | bytes 69664 | tf_op jit(solution)/shard_map/ppermute | solution.py:504
  39.4 0.1 weight.1.zero
  39.5 1.0 %collective-permute-start.13 = (bf16[272,128]{1,0:T(8,128)(2,1)S(1)}, bf16[272,128]{1,0:T(8,128)(2,1)S(1)}, u32[]{:S(2)}, u32[]{:S(2)}) collective-permute-start(bf16[272,128]{1,0:T(8,128)(2,1)S(1)} %weight.1.zero), channel_id=1, source_target_pairs={{0,96},{32,64},{64,32},{96,0},{1,97},{33,65},{65,33},{97,1},{2,98}... | collective-permute-start | bytes 208904 | tf_op jit(solution)/shard_map/ppermute | solution.py:506
  40.4 3.6 %collective-permute-start.12 = (bf16[272,128]{1,0:T(8,128)(2,1)S(1)}, bf16[272,128]{1,0:T(8,128)(2,1)S(1)}, u32[]{:S(2)}, u32[]{:S(2)}) collective-permute-start(bf16[272,128]{1,0:T(8,128)(2,1)S(1)} %weight.1.zero), channel_id=1, source_target_pairs={{0,64},{32,96},{64,0},{96,32},{1,65},{33,97},{65,1},{97,33},{2,66}... | collective-permute-start | bytes 208904 | tf_op jit(solution)/shard_map/ppermute | solution.py:506
  44.0 2.3 %collective-permute-done.12.two = bf16[272,128]{1,0:T(8,128)(2,1)S(1)} collective-permute-done((bf16[272,128]{1,0:T(8,128)(2,1)S(1)}, bf16[272,128]{1,0:T(8,128)(2,1)S(1)}, u32[]{:S(2)}, u32[]{:S(2)}) %collective-permute-start.12) | collective-permute-done | bytes 69664 | tf_op jit(solution)/shard_map/ppermute | solution.py:506
  46.3 2.0 %collective-permute-done.11.one = bf16[272,128]{1,0:T(8,128)(2,1)S(1)} collective-permute-done((bf16[272,128]{1,0:T(8,128)(2,1)S(1)}, bf16[272,128]{1,0:T(8,128)(2,1)S(1)}, u32[]{:S(2)}, u32[]{:S(2)}) %collective-permute-start.11) | collective-permute-done | bytes 69664 | tf_op jit(solution)/shard_map/ppermute | solution.py:506
  48.3 0.1 collective-permute-start.14
  48.4 1.5 %collective-permute-done.14.other = bf16[1040,128]{1,0:T(8,128)(2,1)S(1)} collective-permute-done((bf16[1040,128]{1,0:T(8,128)(2,1)S(1)}, bf16[1040,128]{1,0:T(8,128)(2,1)S(1)}, u32[]{:S(2)}, u32[]{:S(2)}) %collective-permute-start.14) | collective-permute-done | bytes 266272 | tf_op jit(solution)/shard_map/ppermute | solution.py:508
  50.0 0.3 level_edges.1
  50.3 0.1 collective-permute-start.15
  50.4 2.1 %collective-permute-start.16 = (bf16[528,128]{1,0:T(8,128)(2,1)S(1)}, bf16[528,128]{1,0:T(8,128)(2,1)S(1)}, u32[]{:S(2)}, u32[]{:S(2)}) collective-permute-start(bf16[528,128]{1,0:T(8,128)(2,1)S(1)} %get-tuple-element.55), channel_id=1, source_target_pairs={{0,140},{4,8},{8,4},{12,128},{128,12},{132,136},{136,132},{140,0},... | collective-permute-start | bytes 405512 | tf_op jit(solution)/shard_map/ppermute | solution.py:453
  52.5 1.2 %level.1 = (bf16[4,2048,128]{2,1,0:T(8,128)(2,1)S(1)}, f32[8,128]{1,0:T(8,128)S(1)}, bf16[1024,128]{1,0:T(8,128)(2,1)S(1)}, bf16[1024,128]{1,0:T(8,128)(2,1)S(1)}) custom-call(bf16[1040,128]{1,0:T(8,128)(2,1)S(1)} %gather.1.mine, bf16[1040,128]{1,0:T(8,128)(2,1)S(1)} %collective-permute-done.14.other, bf16[4,2048,128]{2,1,0:T(8,128)(2,1)S(1)} %bitcast.7, ...), custom_call_target="tpu_custom_call" | custom-call | flops 300000000 | bytes 4500000 | tf_op jit(solution)/shard_map/level/pallas_call | solution.py:243
  53.7 1.4 %collective-permute-start.19 = (f32[8,128]{1,0:T(8,128)S(1)}, f32[8,128]{1,0:T(8,128)S(1)}, u32[]{:S(2)}, u32[]{:S(2)}) collective-permute-start(f32[8,128]{1,0:T(8,128)S(1)} %get-tuple-element.61.refs_0_), channel_id=1, source_target_pairs={{0,8},{4,12},{8,0},{12,4},{1,9},{5,13},{9,1},{13,5},{2,10},{6,14},... | collective-permute-start | bytes 12296 | tf_op jit(solution)/shard_map/ppermute | solution.py:523
  55.2 0.1 collective-permute-start.17
  55.2 2.2 %collective-permute-start.18 = (bf16[1024,128]{1,0:T(8,128)(2,1)S(1)}, bf16[1024,128]{1,0:T(8,128)(2,1)S(1)}, u32[]{:S(2)}, u32[]{:S(2)}) collective-permute-start(bf16[1024,128]{1,0:T(8,128)(2,1)S(1)} %get-tuple-element.60), channel_id=1, source_target_pairs={{0,3},{1,2},{2,1},{3,0},{4,7},{5,6},{6,5},{7,4},{8,11},{9,10},{10,... | collective-permute-start | bytes 786440 | tf_op jit(solution)/shard_map/ppermute | solution.py:453
  57.4 0.9 %collective-permute-done.19.refs_1_ = f32[8,128]{1,0:T(8,128)S(1)} collective-permute-done((f32[8,128]{1,0:T(8,128)S(1)}, f32[8,128]{1,0:T(8,128)S(1)}, u32[]{:S(2)}, u32[]{:S(2)}) %collective-permute-start.19) | collective-permute-done | bytes 4128 | tf_op jit(solution)/shard_map/ppermute | solution.py:523
  58.3 0.2 corners.3
  58.5 1.8 %collective-permute-start.22 = (f32[8,128]{1,0:T(8,128)S(1)}, f32[8,128]{1,0:T(8,128)S(1)}, u32[]{:S(2)}, u32[]{:S(2)}) collective-permute-start(f32[8,128]{1,0:T(8,128)S(1)} %get-tuple-element.64.sums), channel_id=1, source_target_pairs={{0,2},{1,3},{2,0},{3,1},{4,6},{5,7},{6,4},{7,5},{8,10},{9,11},{10,... | collective-permute-start | bytes 12296 | tf_op jit(solution)/shard_map/ppermute | solution.py:528
  60.3 1.3 %collective-permute-start.20 = (bf16[144,128]{1,0:T(8,128)(2,1)S(1)}, bf16[144,128]{1,0:T(8,128)(2,1)S(1)}, u32[]{:S(2)}, u32[]{:S(2)}) collective-permute-start(bf16[144,128]{1,0:T(8,128)(2,1)S(1)} %get-tuple-element.62), channel_id=1, source_target_pairs={{0,1},{1,0},{2,3},{3,2},{4,5},{5,4},{6,7},{7,6},{8,9},{9,8},{10,11... | collective-permute-start | bytes 110600 | tf_op jit(solution)/shard_map/ppermute | solution.py:453
  61.7 1.1 %collective-permute-start.21 = (bf16[144,128]{1,0:T(8,128)(2,1)S(1)}, bf16[144,128]{1,0:T(8,128)(2,1)S(1)}, u32[]{:S(2)}, u32[]{:S(2)}) collective-permute-start(bf16[144,128]{1,0:T(8,128)(2,1)S(1)} %get-tuple-element.63), channel_id=1, source_target_pairs={{0,3},{1,2},{2,1},{3,0},{4,7},{5,6},{6,5},{7,4},{8,11},{9,10},{10,... | collective-permute-start | bytes 110600 | tf_op jit(solution)/shard_map/ppermute | solution.py:453
  62.7 2.5 %centre_back.1 = (f32[4,64,32,128]{3,2,1,0:T(8,128)}, f32[4,64,16,128]{3,2,1,0:T(8,128)S(1)}, f32[2,64,16,128]{3,2,1,0:T(8,128)S(1)}) custom-call(bf16[4,2048,128]{2,1,0:T(8,128)(2,1)S(1)} %get-tuple-element.53.own, bf16[528,128]{1,0:T(8,128)(2,1)S(1)} %collective-permute-done.15.first, bf16[528,128]{1,0:T(8,128)(2,1)S(1)} %collective-permute-done.16.second, ...), custom_call_target="tpu_custom_call" | custom-call | flops 3000000000 | bytes 7000000 | tf_op jit(solution)/shard_map/centre_back/pallas_call | solution.py:243
  65.2 1.6 %collective-permute-done.21.two_corner = bf16[144,128]{1,0:T(8,128)(2,1)S(1)} collective-permute-done((bf16[144,128]{1,0:T(8,128)(2,1)S(1)}, bf16[144,128]{1,0:T(8,128)(2,1)S(1)}, u32[]{:S(2)}, u32[]{:S(2)}) %collective-permute-start.21) | collective-permute-done | bytes 36896 | tf_op jit(solution)/shard_map/ppermute | solution.py:453
  66.8 2.5 %backward.1 = (f32[4,64,32,128]{3,2,1,0:T(8,128)}, f32[1,1]{1,0:T(1,128)}) custom-call(f32[4,64,16,128]{3,2,1,0:T(8,128)S(1)} %get-tuple-element.57.outer, f32[2,64,16,128]{3,2,1,0:T(8,128)S(1)} %get-tuple-element.58.rest, bf16[1024,128]{1,0:T(8,128)(2,1)S(1)} %collective-permute-done.17.one, ...), custom_call_target="tpu_custom_call", output_to_operand_aliasing={{0}: (9, {})} | custom-call | flops 1000000000 | bytes 9000000 | tf_op jit(solution)/shard_map/backward/pallas_call | solution.py:243
  (29 shorter events, 0.2 us)
Async XLA Ops:
  0.6 1.6 %copy-start.1 = (bf16[4,64,32,128]{3,2,1,0:T(8,128)(2,1)S(1)}, bf16[4,64,32,128]{3,2,1,0:T(8,128)(2,1)}, u32[]{:S(2)}) copy-start(bf16[4,64,32,128]{3,2,1,0:T(8,128)(2,1)} %param.6) | copy-start | bytes 6291460
  2.2 11.3 %copy-start.5 = (f32[9]{0:T(128)S(1)}, f32[9]{0:T(128)}, u32[]{:S(2)}) copy-start(f32[9]{0:T(128)} %lat_taps.3) | copy-start | bytes 112
  2.2 11.3 %copy-start.6 = (f32[9]{0:T(128)S(1)}, f32[9]{0:T(128)}, u32[]{:S(2)}) copy-start(f32[9]{0:T(128)} %lon_taps.3) | copy-start | bytes 112
  2.2 14.3 %copy-start.2 = (bf16[4,64,32,128]{3,2,1,0:T(8,128)(2,1)S(1)}, bf16[4,64,32,128]{3,2,1,0:T(8,128)(2,1)}, u32[]{:S(2)}) copy-start(bf16[4,64,32,128]{3,2,1,0:T(8,128)(2,1)} %param.6) | copy-start | bytes 6291460
  2.3 12.0 %collective-permute-start = (bf16[512,128]{1,0:T(8,128)(2,1)S(1)}, bf16[512,128]{1,0:T(8,128)(2,1)S(1)}, u32[]{:S(2)}, u32[]{:S(2)}) collective-permute-start(bf16[512,128]{1,0:T(8,128)(2,1)S(1)} %get-tuple-element.35), channel_id=1, source_target_pairs={{0,4},{4,0},{8,12},{12,8},{128,132},{132,128},{136,140},{140,136},... | collective-permute-start | bytes 393224 | tf_op jit(solution)/shard_map/ppermute | solution.py:453
  4.3 10.0 %collective-permute-start.1 = (bf16[512,128]{1,0:T(8,128)(2,1)S(1)}, bf16[512,128]{1,0:T(8,128)(2,1)S(1)}, u32[]{:S(2)}, u32[]{:S(2)}) collective-permute-start(bf16[512,128]{1,0:T(8,128)(2,1)S(1)} %get-tuple-element.36), channel_id=1, source_target_pairs={{0,140},{4,8},{8,4},{12,128},{128,12},{132,136},{136,132},{140,0},... | collective-permute-start | bytes 393224 | tf_op jit(solution)/shard_map/ppermute | solution.py:453
  9.7 10.8 %collective-permute-start.2 = (bf16[1024,128]{1,0:T(8,128)(2,1)S(1)}, bf16[1024,128]{1,0:T(8,128)(2,1)S(1)}, u32[]{:S(2)}, u32[]{:S(2)}) collective-permute-start(bf16[1024,128]{1,0:T(8,128)(2,1)S(1)} %get-tuple-element.39), channel_id=1, source_target_pairs={{0,1},{1,0},{2,3},{3,2},{4,5},{5,4},{6,7},{7,6},{8,9},{9,8},{10,11... | collective-permute-start | bytes 786440 | tf_op jit(solution)/shard_map/ppermute | solution.py:453
  11.4 9.1 %collective-permute-start.3 = (bf16[1024,128]{1,0:T(8,128)(2,1)S(1)}, bf16[1024,128]{1,0:T(8,128)(2,1)S(1)}, u32[]{:S(2)}, u32[]{:S(2)}) collective-permute-start(bf16[1024,128]{1,0:T(8,128)(2,1)S(1)} %get-tuple-element.40), channel_id=1, source_target_pairs={{0,3},{1,2},{2,1},{3,0},{4,7},{5,6},{6,5},{7,4},{8,11},{9,10},{10,... | collective-permute-start | bytes 786440 | tf_op jit(solution)/shard_map/ppermute | solution.py:453
  14.5 4.3 %collective-permute-start.4 = (bf16[128,128]{1,0:T(8,128)(2,1)S(1)}, bf16[128,128]{1,0:T(8,128)(2,1)S(1)}, u32[]{:S(2)}, u32[]{:S(2)}) collective-permute-start(bf16[128,128]{1,0:T(8,128)(2,1)S(1)} %get-tuple-element.41), channel_id=1, source_target_pairs={{0,1},{1,0},{2,3},{3,2},{4,5},{5,4},{6,7},{7,6},{8,9},{9,8},{10,11... | collective-permute-start | bytes 98312 | tf_op jit(solution)/shard_map/ppermute | solution.py:453
  15.3 5.2 %collective-permute-start.5 = (bf16[128,128]{1,0:T(8,128)(2,1)S(1)}, bf16[128,128]{1,0:T(8,128)(2,1)S(1)}, u32[]{:S(2)}, u32[]{:S(2)}) collective-permute-start(bf16[128,128]{1,0:T(8,128)(2,1)S(1)} %get-tuple-element.42), channel_id=1, source_target_pairs={{0,3},{1,2},{2,1},{3,0},{4,7},{5,6},{6,5},{7,4},{8,11},{9,10},{10,... | collective-permute-start | bytes 98312 | tf_op jit(solution)/shard_map/ppermute | solution.py:453
  16.5 4.0 %copy-start = (bf16[4,64,32,128]{3,2,1,0:T(8,128)(2,1)S(1)}, bf16[4,64,32,128]{3,2,1,0:T(8,128)(2,1)}, u32[]{:S(2)}) copy-start(bf16[4,64,32,128]{3,2,1,0:T(8,128)(2,1)} %param.7) | copy-start | bytes 6291460
  16.5 4.0 %copy-start.4 = (bf16[128,128]{1,0:T(8,128)(2,1)S(1)}, bf16[128,128]{1,0:T(8,128)(2,1)}, u32[]{:S(2)}) copy-start(bf16[128,128]{1,0:T(8,128)(2,1)} %vertical.7) | copy-start | bytes 98308
  21.4 1.6 %collective-permute-start.6 = (bf16[1024,128]{1,0:T(8,128)(2,1)S(1)}, bf16[1024,128]{1,0:T(8,128)(2,1)S(1)}, u32[]{:S(2)}, u32[]{:S(2)}) collective-permute-start(bf16[1024,128]{1,0:T(8,128)(2,1)S(1)} %get-tuple-element.46), channel_id=1, source_target_pairs={{0,16},{16,0},{1,17},{17,1},{2,18},{18,2},{3,19},{19,3},{4,20},{20... | collective-permute-start | bytes 786440 | tf_op jit(solution)/shard_map/ppermute | solution.py:499
  21.5 17.9 %copy-start.3 = (f32[64,32,128]{2,1,0:T(8,128)S(1)}, f32[64,32,128]{2,1,0:T(8,128)}, u32[]{:S(2)}) copy-start(f32[64,32,128]{2,1,0:T(8,128)} %param.8) | copy-start | bytes 3145732
  23.1 4.4 %collective-permute-start.7 = (bf16[256,128]{1,0:T(8,128)(2,1)S(1)}, bf16[256,128]{1,0:T(8,128)(2,1)S(1)}, u32[]{:S(2)}, u32[]{:S(2)}) collective-permute-start(bf16[256,128]{1,0:T(8,128)(2,1)S(1)} %get-tuple-element.48), channel_id=1, source_target_pairs={{0,32},{32,0},{64,96},{96,64},{1,33},{33,1},{65,97},{97,65},{2,34}... | collective-permute-start | bytes 196616 | tf_op jit(solution)/shard_map/ppermute | solution.py:501
  23.7 6.2 %collective-permute-start.8 = (bf16[256,128]{1,0:T(8,128)(2,1)S(1)}, bf16[256,128]{1,0:T(8,128)(2,1)S(1)}, u32[]{:S(2)}, u32[]{:S(2)}) collective-permute-start(bf16[256,128]{1,0:T(8,128)(2,1)S(1)} %get-tuple-element.49), channel_id=1, source_target_pairs={{0,64},{32,96},{64,0},{96,32},{1,65},{33,97},{65,1},{97,33},{2,66}... | collective-permute-start | bytes 196616 | tf_op jit(solution)/shard_map/ppermute | solution.py:501
  26.1 4.7 %collective-permute-start.9 = (bf16[256,128]{1,0:T(8,128)(2,1)S(1)}, bf16[256,128]{1,0:T(8,128)(2,1)S(1)}, u32[]{:S(2)}, u32[]{:S(2)}) collective-permute-start(bf16[256,128]{1,0:T(8,128)(2,1)S(1)} %get-tuple-element.50), channel_id=1, source_target_pairs={{0,96},{32,64},{64,32},{96,0},{1,97},{33,65},{65,33},{97,1},{2,98}... | collective-permute-start | bytes 196616 | tf_op jit(solution)/shard_map/ppermute | solution.py:501
  30.9 8.6 %collective-permute-start.10 = (bf16[272,128]{1,0:T(8,128)(2,1)S(1)}, bf16[272,128]{1,0:T(8,128)(2,1)S(1)}, u32[]{:S(2)}, u32[]{:S(2)}) collective-permute-start(bf16[272,128]{1,0:T(8,128)(2,1)S(1)} %part.1.message), channel_id=1, source_target_pairs={{0,128},{128,0},{1,129},{129,1},{2,130},{130,2},{3,131},{131,3},{4... | collective-permute-start | bytes 208904 | tf_op jit(solution)/shard_map/ppermute | solution.py:504
  39.5 4.5 %collective-permute-start.13 = (bf16[272,128]{1,0:T(8,128)(2,1)S(1)}, bf16[272,128]{1,0:T(8,128)(2,1)S(1)}, u32[]{:S(2)}, u32[]{:S(2)}) collective-permute-start(bf16[272,128]{1,0:T(8,128)(2,1)S(1)} %weight.1.zero), channel_id=1, source_target_pairs={{0,96},{32,64},{64,32},{96,0},{1,97},{33,65},{65,33},{97,1},{2,98}... | collective-permute-start | bytes 208904 | tf_op jit(solution)/shard_map/ppermute | solution.py:506
  40.4 5.8 %collective-permute-start.12 = (bf16[272,128]{1,0:T(8,128)(2,1)S(1)}, bf16[272,128]{1,0:T(8,128)(2,1)S(1)}, u32[]{:S(2)}, u32[]{:S(2)}) collective-permute-start(bf16[272,128]{1,0:T(8,128)(2,1)S(1)} %weight.1.zero), channel_id=1, source_target_pairs={{0,64},{32,96},{64,0},{96,32},{1,65},{33,97},{65,1},{97,33},{2,66}... | collective-permute-start | bytes 208904 | tf_op jit(solution)/shard_map/ppermute | solution.py:506
  44.0 4.3 %collective-permute-start.11 = (bf16[272,128]{1,0:T(8,128)(2,1)S(1)}, bf16[272,128]{1,0:T(8,128)(2,1)S(1)}, u32[]{:S(2)}, u32[]{:S(2)}) collective-permute-start(bf16[272,128]{1,0:T(8,128)(2,1)S(1)} %weight.1.zero), channel_id=1, source_target_pairs={{0,32},{32,0},{64,96},{96,64},{1,33},{33,1},{65,97},{97,65},{2,34}... | collective-permute-start | bytes 208904 | tf_op jit(solution)/shard_map/ppermute | solution.py:506
  48.3 1.6 %collective-permute-start.14 = (bf16[1040,128]{1,0:T(8,128)(2,1)S(1)}, bf16[1040,128]{1,0:T(8,128)(2,1)S(1)}, u32[]{:S(2)}, u32[]{:S(2)}) collective-permute-start(bf16[1040,128]{1,0:T(8,128)(2,1)S(1)} %gather.1.mine), channel_id=1, source_target_pairs={{0,16},{16,0},{1,17},{17,1},{2,18},{18,2},{3,19},{19,3},{4,20},{20... | collective-permute-start | bytes 798728 | tf_op jit(solution)/shard_map/ppermute | solution.py:508
  50.3 8.1 %collective-permute-start.15 = (bf16[528,128]{1,0:T(8,128)(2,1)S(1)}, bf16[528,128]{1,0:T(8,128)(2,1)S(1)}, u32[]{:S(2)}, u32[]{:S(2)}) collective-permute-start(bf16[528,128]{1,0:T(8,128)(2,1)S(1)} %get-tuple-element.54), channel_id=1, source_target_pairs={{0,4},{4,0},{8,12},{12,8},{128,132},{132,128},{136,140},{140,136},... | collective-permute-start | bytes 405512 | tf_op jit(solution)/shard_map/ppermute | solution.py:453
  50.4 8.0 %collective-permute-start.16 = (bf16[528,128]{1,0:T(8,128)(2,1)S(1)}, bf16[528,128]{1,0:T(8,128)(2,1)S(1)}, u32[]{:S(2)}, u32[]{:S(2)}) collective-permute-start(bf16[528,128]{1,0:T(8,128)(2,1)S(1)} %get-tuple-element.55), channel_id=1, source_target_pairs={{0,140},{4,8},{8,4},{12,128},{128,12},{132,136},{136,132},{140,0},... | collective-permute-start | bytes 405512 | tf_op jit(solution)/shard_map/ppermute | solution.py:453
  53.7 4.6 %collective-permute-start.19 = (f32[8,128]{1,0:T(8,128)S(1)}, f32[8,128]{1,0:T(8,128)S(1)}, u32[]{:S(2)}, u32[]{:S(2)}) collective-permute-start(f32[8,128]{1,0:T(8,128)S(1)} %get-tuple-element.61.refs_0_), channel_id=1, source_target_pairs={{0,8},{4,12},{8,0},{12,4},{1,9},{5,13},{9,1},{13,5},{2,10},{6,14},... | collective-permute-start | bytes 12296 | tf_op jit(solution)/shard_map/ppermute | solution.py:523
  55.2 11.7 %collective-permute-start.17 = (bf16[1024,128]{1,0:T(8,128)(2,1)S(1)}, bf16[1024,128]{1,0:T(8,128)(2,1)S(1)}, u32[]{:S(2)}, u32[]{:S(2)}) collective-permute-start(bf16[1024,128]{1,0:T(8,128)(2,1)S(1)} %get-tuple-element.59), channel_id=1, source_target_pairs={{0,1},{1,0},{2,3},{3,2},{4,5},{5,4},{6,7},{7,6},{8,9},{9,8},{10,11... | collective-permute-start | bytes 786440 | tf_op jit(solution)/shard_map/ppermute | solution.py:453
  55.2 11.6 %collective-permute-start.18 = (bf16[1024,128]{1,0:T(8,128)(2,1)S(1)}, bf16[1024,128]{1,0:T(8,128)(2,1)S(1)}, u32[]{:S(2)}, u32[]{:S(2)}) collective-permute-start(bf16[1024,128]{1,0:T(8,128)(2,1)S(1)} %get-tuple-element.60), channel_id=1, source_target_pairs={{0,3},{1,2},{2,1},{3,0},{4,7},{5,6},{6,5},{7,4},{8,11},{9,10},{10,... | collective-permute-start | bytes 786440 | tf_op jit(solution)/shard_map/ppermute | solution.py:453
  58.5 6.7 %collective-permute-start.22 = (f32[8,128]{1,0:T(8,128)S(1)}, f32[8,128]{1,0:T(8,128)S(1)}, u32[]{:S(2)}, u32[]{:S(2)}) collective-permute-start(f32[8,128]{1,0:T(8,128)S(1)} %get-tuple-element.64.sums), channel_id=1, source_target_pairs={{0,2},{1,3},{2,0},{3,1},{4,6},{5,7},{6,4},{7,5},{8,10},{9,11},{10,... | collective-permute-start | bytes 12296 | tf_op jit(solution)/shard_map/ppermute | solution.py:528
  60.3 4.9 %collective-permute-start.20 = (bf16[144,128]{1,0:T(8,128)(2,1)S(1)}, bf16[144,128]{1,0:T(8,128)(2,1)S(1)}, u32[]{:S(2)}, u32[]{:S(2)}) collective-permute-start(bf16[144,128]{1,0:T(8,128)(2,1)S(1)} %get-tuple-element.62), channel_id=1, source_target_pairs={{0,1},{1,0},{2,3},{3,2},{4,5},{5,4},{6,7},{7,6},{8,9},{9,8},{10,11... | collective-permute-start | bytes 110600 | tf_op jit(solution)/shard_map/ppermute | solution.py:453
  61.7 5.2 %collective-permute-start.21 = (bf16[144,128]{1,0:T(8,128)(2,1)S(1)}, bf16[144,128]{1,0:T(8,128)(2,1)S(1)}, u32[]{:S(2)}, u32[]{:S(2)}) collective-permute-start(bf16[144,128]{1,0:T(8,128)(2,1)S(1)} %get-tuple-element.63), channel_id=1, source_target_pairs={{0,3},{1,2},{2,1},{3,0},{4,7},{5,6},{6,5},{7,4},{8,11},{9,10},{10,... | collective-permute-start | bytes 110600 | tf_op jit(solution)/shard_map/ppermute | solution.py:453
